TPU v7x, 32 devices: a whole 2x2x4 slice. The times are simulated.
32 devices in a mesh: section: 2 (over core), dp: 8 (over z, x), tensor: 2 (over y).
Axes of the slice: x: 2, y: 2, z: 4, core: 2. Of those that a mesh axis runs over, the one named last changes fastest.
Arguments:
- tokens: bfloat16 [2, 16, 2048, 512], P('section', 'dp', 'tensor'), may hold values from -6 to 6
- lengths: int32 [2, 16, 2], P(None, 'dp'), may hold values from 0 to 2048, as said below
- self_qkv: bfloat16 [2, 3, 512, 512], P('section', None, None, 'tensor'), may hold values from -0.25 to 0.25
- self_out: bfloat16 [2, 512, 512], P('section', 'tensor'), may hold values from -6 to 6
- cross_proj: bfloat16 [2, 2, 512, 512], P('section', None, None, 'tensor')
- ffn_up: bfloat16 [2, 512, 2048], P('section', None, 'tensor'), may hold values from -0.25 to 0.25
- ffn_down: bfloat16 [2, 2048, 512], P('section', 'tensor'), may hold values from -0.125 to 0.125
- norms: float32 [2, 3, 2, 512], P('section')
- cotangent: bfloat16 [2, 16, 2048, 512], P('section', 'dp', 'tensor'), may hold values from -6 to 6
Outputs:
- result: bfloat16 [2, 16, 2048, 512], P('section', 'dp', 'tensor')
- token_grad: float32 [2, 16, 2048, 512], P('section', 'dp', 'tensor')
- qkv_grad: float32 [2, 3, 512, 512], P('section', None, None, 'tensor')
- out_grad: float32 [2, 512, 512], P('section', 'tensor')
- cross_grad: float32 [2, 2, 512, 512], P('section', None, None, 'tensor')
- up_grad: float32 [2, 512, 2048], P('section', None, 'tensor')
- down_grad: float32 [2, 2048, 512], P('section', 'tensor')
- norm_grad: float32 [2, 3, 2, 512], P('section')
Inputs may be any that keep to these rules, and one draw needn't show every extreme that they name: lengths[s, r] are the lengths of the sequences packed from the start of row r, the rest being padding: either one sequence (second entry 0) or two, each of 1024 tokens or more, together at most 2048; source row r and target row r hold the same number of sequences, and target sequence k belongs to source sequence k.
All inputs are finite; a program needn't handle non-finite values.
Results may differ from a plain program's by a relative error of at most 0.019.
Values may be sent and summed in bfloat16 or wider, within the bound.
A program may use at most 384 MiB of HBM per device.

v0:
```python
import math

import jax
import jax.numpy as jnp
from jax import lax
from jax.sharding import PartitionSpec as P

HEADS = 8


EPSILON = 1e-05
MASKED = -1000000000.0


def from_behind(shard, axis, by):
    devices = lax.axis_size(axis)
    pairs = [(i, i + by) for i in range(devices) if 0 <= i + by < devices]
    return lax.ppermute(shard, axis, pairs)


def layer_norm(row_block, norm_gain, norm_shift):
    row_mean = jnp.mean(row_block, axis=-1, keepdims=True)
    centered = row_block - row_mean
    variance = jnp.mean(centered * centered, axis=-1, keepdims=True)
    return centered * lax.rsqrt(variance + EPSILON) * norm_gain + norm_shift


def norm_backward(row_block, norm_gain, norm_shift, grad_rows):
    _, pull_back = jax.vjp(layer_norm, row_block, norm_gain, norm_shift)
    return pull_back(grad_rows)


def smooth_gate(inner_act):
    return (
        0.5
        * inner_act
        * (
            1.0
            + jnp.tanh(
                0.7978845608028654 * (inner_act + 0.044715 * inner_act * inner_act * inner_act)
            )
        )
    )


def segment_ids(length_pair, row_length):
    position = jnp.arange(row_length, dtype=jnp.int32)
    return jnp.where(
        position < length_pair[0], 0, jnp.where(position < length_pair[0] + length_pair[1], 1, 2)
    ).astype(jnp.int32)


def allowed(query_seg, key_seg):
    return (key_seg[None, :] < 2) & (
        (query_seg[:, None] == key_seg[None, :]) | (query_seg[:, None] == 2)
    )


def pick_slot(buffer, slot_index):
    return lax.dynamic_index_in_dim(buffer, slot_index, 0, keepdims=False)


def store_slot(buffer, slot_index, value, is_live):
    previous = lax.dynamic_index_in_dim(buffer, slot_index, 0, keepdims=False)
    return lax.dynamic_update_index_in_dim(
        buffer, jnp.where(is_live, value, previous), slot_index, 0
    )


def gather_rows(share_rows):
    return lax.all_gather(share_rows, "tensor", axis=0, tiled=True)


def sum_rows(partial_rows):
    return lax.psum_scatter(
        partial_rows.astype(jnp.bfloat16), "tensor", scatter_dimension=0, tiled=True
    ).astype(jnp.float32)


def gather_grads(share_grads):
    return lax.all_gather(share_grads, "tensor", axis=0, tiled=True)


def sum_grads(partial_grads):
    return lax.psum_scatter(
        partial_grads.astype(jnp.bfloat16), "tensor", scatter_dimension=0, tiled=True
    ).astype(jnp.float32)


def send_memory(sent_memory):
    return from_behind(sent_memory, "section", 1)


def return_grads(memory_grads):
    return from_behind(memory_grads, "section", -1)


def block_setup(queries, local_heads):
    row_length = queries.shape[0]
    head_width = queries.shape[1] // local_heads
    block_rows = min(512, row_length)
    return (row_length, head_width, block_rows, 1.0 / math.sqrt(head_width))


def attend_forward(queries, key_rows, value_rows, query_seg, key_seg, local_heads):
    row_length, head_width, block_rows, score_scale = block_setup(queries, local_heads)
    key_heads = key_rows.reshape(row_length, local_heads, head_width)
    value_heads = value_rows.reshape(row_length, local_heads, head_width)
    query_blocks = queries.reshape(row_length // block_rows, block_rows, local_heads, head_width)
    seg_blocks = query_seg.reshape(row_length // block_rows, block_rows)

    def one_block(block_item):
        query_block, seg_block = block_item
        scores = (
            jnp.einsum("qhd,khd->hqk", query_block, key_heads, preferred_element_type=jnp.float32)
            * score_scale
        )
        scores = jnp.where(allowed(seg_block, key_seg)[None], scores, MASKED)
        row_max = jnp.max(scores, axis=-1, keepdims=True)
        exponent = jnp.exp(scores - row_max)
        probability = (exponent / jnp.sum(exponent, axis=-1, keepdims=True)).astype(jnp.bfloat16)
        return jnp.einsum(
            "hqk,khd->qhd", probability, value_heads, preferred_element_type=jnp.float32
        ).astype(jnp.bfloat16)

    mixture = lax.map(one_block, (query_blocks, seg_blocks))
    return mixture.reshape(row_length, local_heads * head_width)


def attend_backward(queries, key_rows, value_rows, grad_mix, query_seg, key_seg, local_heads):
    row_length, head_width, block_rows, score_scale = block_setup(queries, local_heads)
    key_heads = key_rows.reshape(row_length, local_heads, head_width)
    value_heads = value_rows.reshape(row_length, local_heads, head_width)
    block_count = row_length // block_rows
    query_blocks = queries.reshape(block_count, block_rows, local_heads, head_width)
    grad_blocks = grad_mix.reshape(block_count, block_rows, local_heads, head_width)
    seg_blocks = query_seg.reshape(block_count, block_rows)

    def one_block(carry, block_item):
        key_total, value_total = carry
        query_block, grad_block, seg_block = block_item
        scores = (
            jnp.einsum("qhd,khd->hqk", query_block, key_heads, preferred_element_type=jnp.float32)
            * score_scale
        )
        scores = jnp.where(allowed(seg_block, key_seg)[None], scores, MASKED)
        row_max = jnp.max(scores, axis=-1, keepdims=True)
        exponent = jnp.exp(scores - row_max)
        probability = exponent / jnp.sum(exponent, axis=-1, keepdims=True)
        prob_low = probability.astype(jnp.bfloat16)
        mixture = jnp.einsum(
            "hqk,khd->qhd", prob_low, value_heads, preferred_element_type=jnp.float32
        ).astype(jnp.bfloat16)
        value_total = value_total + jnp.einsum(
            "hqk,qhd->khd", prob_low, grad_block, preferred_element_type=jnp.float32
        )
        grad_prob = jnp.einsum(
            "qhd,khd->hqk", grad_block, value_heads, preferred_element_type=jnp.float32
        )
        row_inner = jnp.sum(probability * grad_prob, axis=-1, keepdims=True)
        grad_scores = (probability * (grad_prob - row_inner)).astype(jnp.bfloat16)
        grad_query = (
            jnp.einsum("hqk,khd->qhd", grad_scores, key_heads, preferred_element_type=jnp.float32)
            * score_scale
        ).astype(jnp.bfloat16)
        key_total = (
            key_total
            + jnp.einsum(
                "hqk,qhd->khd", grad_scores, query_block, preferred_element_type=jnp.float32
            )
            * score_scale
        )
        return ((key_total, value_total), (grad_query, mixture))

    zero_heads = jnp.zeros((row_length, local_heads, head_width), jnp.float32)
    totals, outputs = lax.scan(
        one_block, (zero_heads, zero_heads), (query_blocks, grad_blocks, seg_blocks)
    )
    flat_width = local_heads * head_width
    return (
        outputs[0].reshape(row_length, flat_width),
        totals[0].reshape(row_length, flat_width).astype(jnp.bfloat16),
        totals[1].reshape(row_length, flat_width).astype(jnp.bfloat16),
        outputs[1].reshape(row_length, flat_width),
    )


def projected(row_block, weight_matrix):
    return jnp.dot(row_block, weight_matrix, preferred_element_type=jnp.float32).astype(
        jnp.bfloat16
    )


def back_product(grad_rows, weight_matrix):
    return lax.dot_general(
        grad_rows, weight_matrix, (((1,), (1,)), ((), ())), preferred_element_type=jnp.float32
    )


def weight_product(row_block, grad_rows):
    return lax.dot_general(
        row_block, grad_rows, (((0,), (0,)), ((), ())), preferred_element_type=jnp.float32
    )


def self_forward(attn_in, qkv_weight, out_weight, own_seg, local_heads):
    mixture = attend_forward(
        projected(attn_in, qkv_weight[0]),
        projected(attn_in, qkv_weight[1]),
        projected(attn_in, qkv_weight[2]),
        own_seg,
        own_seg,
        local_heads,
    )
    return jnp.dot(mixture, out_weight, preferred_element_type=jnp.float32)


def self_backward(attn_in, grad_full, qkv_weight, out_weight, own_seg, local_heads):
    queries = projected(attn_in, qkv_weight[0])
    key_rows = projected(attn_in, qkv_weight[1])
    value_rows = projected(attn_in, qkv_weight[2])
    grad_mix = back_product(grad_full, out_weight).astype(jnp.bfloat16)
    grad_query, grad_key, grad_value, mixture = attend_backward(
        queries, key_rows, value_rows, grad_mix, own_seg, own_seg, local_heads
    )
    grad_out = weight_product(mixture, grad_full)
    triple = (grad_query, grad_key, grad_value)
    grad_qkv = jnp.stack([weight_product(attn_in, member) for member in triple])
    partial_value = (
        back_product(grad_query, qkv_weight[0])
        + back_product(grad_key, qkv_weight[1])
        + back_product(grad_value, qkv_weight[2])
    )
    return (partial_value, grad_qkv, grad_out)


def cross_forward(cross_in, memory, cross_weight, own_seg, source_seg, local_heads):
    mixture = attend_forward(
        projected(cross_in, cross_weight[0]), memory[0], memory[1], own_seg, source_seg, local_heads
    )
    return back_product(mixture, cross_weight[1])


def cross_backward(cross_in, grad_full, memory, cross_weight, own_seg, source_seg, local_heads):
    queries = projected(cross_in, cross_weight[0])
    grad_mix = jnp.dot(grad_full, cross_weight[1], preferred_element_type=jnp.float32).astype(
        jnp.bfloat16
    )
    grad_query, grad_key, grad_value, mixture = attend_backward(
        queries, memory[0], memory[1], grad_mix, own_seg, source_seg, local_heads
    )
    grad_pair = jnp.stack(
        [weight_product(cross_in, grad_query), weight_product(grad_full, mixture)]
    )
    partial_value = back_product(grad_query, cross_weight[0])
    return (partial_value, grad_pair, jnp.stack([grad_key, grad_value]))


def memory_forward(memory_in, cross_weight):
    return jnp.stack([projected(memory_in, cross_weight[0]), projected(memory_in, cross_weight[1])])


def memory_backward(memory_in, returned, cross_weight):
    partial_value = back_product(returned[0], cross_weight[0]) + back_product(
        returned[1], cross_weight[1]
    )
    return (
        partial_value,
        jnp.stack([weight_product(memory_in, returned[0]), weight_product(memory_in, returned[1])]),
    )


def ffn_forward(row_block, up_weight, down_weight):
    inner_act = jnp.dot(row_block, up_weight, preferred_element_type=jnp.float32)
    activated = smooth_gate(inner_act).astype(jnp.bfloat16)
    return jnp.dot(activated, down_weight, preferred_element_type=jnp.float32)


def ffn_backward(row_block, grad_rows, up_weight, down_weight):
    inner_act = jnp.dot(row_block, up_weight, preferred_element_type=jnp.float32)
    activated, pull_back = jax.vjp(smooth_gate, inner_act)
    grad_down = weight_product(activated.astype(jnp.bfloat16), grad_rows)
    grad_act = back_product(grad_rows, down_weight)
    grad_inner = pull_back(grad_act)[0].astype(jnp.bfloat16)
    grad_up = weight_product(row_block, grad_inner)
    return (back_product(grad_inner, up_weight), grad_up, grad_down)


def ffn_step_forward(hidden_two, up_weight, down_weight):
    ffn_in = lax.all_gather(hidden_two.astype(jnp.bfloat16), "tensor", axis=0, tiled=True)
    return (
        lax.psum_scatter(
            ffn_forward(ffn_in, up_weight, down_weight).astype(jnp.bfloat16),
            "tensor",
            scatter_dimension=0,
            tiled=True,
        ).astype(jnp.float32),
        ffn_in,
    )


def ffn_step_backward(grad_third, ffn_keep, slot_index, up_weight, down_weight):
    ffn_in = pick_slot(ffn_keep, slot_index)
    grad_ffn_full = lax.all_gather(grad_third.astype(jnp.bfloat16), "tensor", axis=0, tiled=True)
    ffn_partial, up_step, down_step = ffn_backward(ffn_in, grad_ffn_full, up_weight, down_weight)
    return (
        lax.psum_scatter(
            ffn_partial.astype(jnp.bfloat16), "tensor", scatter_dimension=0, tiled=True
        ).astype(jnp.float32),
        up_step,
        down_step,
    )


def local(tokens, lengths, self_qkv, self_out, cross_proj, ffn_up, ffn_down, norms, cotangent):
    section_index = lax.axis_index("section")
    is_encoder = section_index == 0
    token_share = tokens[0]
    cotangent_share = cotangent[0]
    qkv_weight = self_qkv[0]
    out_weight = self_out[0]
    cross_weight = cross_proj[0]
    up_weight = ffn_up[0]
    down_weight = ffn_down[0]
    norm_table = norms[0]
    micro_count, share_rows, model_width = token_share.shape
    row_length = share_rows * lax.axis_size("tensor")
    local_width = qkv_weight.shape[-1]
    local_heads = local_width // (model_width // HEADS)
    own_lengths = lax.dynamic_index_in_dim(lengths, section_index, 0, keepdims=False)
    source_lengths = lengths[0]
    wide_zero = jnp.zeros((row_length, model_width), jnp.float32)
    memory_zero = jnp.zeros((2, row_length, local_width), jnp.bfloat16)
    cross_zero = jnp.zeros(cross_weight.shape, jnp.float32)
    width_zero = jnp.zeros((model_width,), jnp.float32)
    share_shape = (micro_count, share_rows, model_width)
    wide_shape = (micro_count, row_length, model_width)
    first_keep = jnp.zeros(share_shape, jnp.float32)
    second_keep = jnp.zeros(share_shape, jnp.float32)
    third_keep = jnp.zeros(share_shape, jnp.float32)
    attn_keep = jnp.zeros(wide_shape, jnp.bfloat16)
    cross_keep = jnp.zeros(wide_shape, jnp.bfloat16)
    ffn_keep = jnp.zeros(wide_shape, jnp.bfloat16)
    memory_keep = jnp.zeros(wide_shape, jnp.bfloat16)
    memory_store = jnp.zeros((micro_count, 2, row_length, local_width), jnp.bfloat16)
    result = jnp.zeros(share_shape, jnp.bfloat16)
    for step_number in range(micro_count + 1):
        micro_index = step_number - section_index
        is_live = (micro_index >= 0) & (micro_index < micro_count)
        slot_index = jnp.clip(micro_index, 0, micro_count - 1)
        own_seg = segment_ids(pick_slot(own_lengths, slot_index), row_length)
        source_seg = segment_ids(pick_slot(source_lengths, slot_index), row_length)
        encoder_input_share = pick_slot(token_share, slot_index).astype(jnp.float32)
        base_rows = lax.cond(
            is_encoder,
            lambda: layer_norm(encoder_input_share, norm_table[2, 0], norm_table[2, 1]),
            lambda: encoder_input_share,
        )
        attn_in = gather_rows(base_rows.astype(jnp.bfloat16))
        first_sum = base_rows + sum_rows(
            self_forward(attn_in, qkv_weight, out_weight, own_seg, local_heads)
        )
        hidden_one = layer_norm(first_sum, norm_table[0, 0], norm_table[0, 1])
        cross_in = gather_rows(hidden_one.astype(jnp.bfloat16))
        memory = pick_slot(memory_store, slot_index)
        cross_partial = lax.cond(
            is_encoder,
            lambda: wide_zero,
            lambda: cross_forward(cross_in, memory, cross_weight, own_seg, source_seg, local_heads),
        )
        second_sum = hidden_one + sum_rows(cross_partial)
        hidden_two = lax.cond(
            is_encoder,
            lambda: second_sum,
            lambda: layer_norm(second_sum, norm_table[2, 0], norm_table[2, 1]),
        )
        ffn_out, ffn_in = ffn_step_forward(hidden_two, up_weight, down_weight)
        ffn_keep = store_slot(ffn_keep, slot_index, ffn_in, is_live)
        third_sum = hidden_two + ffn_out
        output_rows = layer_norm(third_sum, norm_table[1, 0], norm_table[1, 1])
        memory_in = gather_rows(output_rows.astype(jnp.bfloat16))
        sent_memory = lax.cond(
            is_encoder, lambda: memory_forward(memory_in, cross_weight), lambda: memory_zero
        )
        arrived = send_memory(sent_memory)
        if step_number < micro_count:
            memory_store = memory_store.at[step_number].set(arrived)
        first_keep = store_slot(first_keep, slot_index, first_sum, is_live)
        second_keep = store_slot(second_keep, slot_index, second_sum, is_live)
        third_keep = store_slot(third_keep, slot_index, third_sum, is_live)
        attn_keep = store_slot(attn_keep, slot_index, attn_in, is_live)
        cross_keep = store_slot(cross_keep, slot_index, cross_in, is_live)
        memory_keep = store_slot(memory_keep, slot_index, memory_in, is_live)
        result = store_slot(result, slot_index, output_rows.astype(jnp.bfloat16), is_live)
    grad_qkv = jnp.zeros(qkv_weight.shape, jnp.float32)
    grad_out = jnp.zeros(out_weight.shape, jnp.float32)
    grad_cross = cross_zero
    grad_up = jnp.zeros(up_weight.shape, jnp.float32)
    grad_down = jnp.zeros(down_weight.shape, jnp.float32)
    grad_norm = jnp.zeros(norm_table.shape, jnp.float32)
    returned_store = jnp.zeros((micro_count, 2, row_length, local_width), jnp.bfloat16)
    token_grad = jnp.zeros(share_shape, jnp.float32)
    step_total = micro_count + 1
    for step_number in range(step_total):
        micro_index = step_number - 1 + section_index
        is_live = (micro_index >= 0) & (micro_index < micro_count)
        slot_index = jnp.clip(micro_index, 0, micro_count - 1)
        own_seg = segment_ids(pick_slot(own_lengths, slot_index), row_length)
        source_seg = segment_ids(pick_slot(source_lengths, slot_index), row_length)
        first_sum = pick_slot(first_keep, slot_index)
        second_sum = pick_slot(second_keep, slot_index)
        third_sum = pick_slot(third_keep, slot_index)
        attn_in = pick_slot(attn_keep, slot_index)
        memory = pick_slot(memory_store, slot_index)
        grad_output = pick_slot(cotangent_share, slot_index).astype(jnp.float32)
        cross_in = pick_slot(cross_keep, slot_index)
        memory_in = pick_slot(memory_keep, slot_index)
        returned = pick_slot(returned_store, slot_index)
        memory_partial, memory_weights = lax.cond(
            is_encoder,
            lambda: memory_backward(memory_in, returned, cross_weight),
            lambda: (wide_zero, cross_zero),
        )
        grad_encoded = grad_output + sum_grads(memory_partial)
        grad_third, gain_one, shift_one = norm_backward(
            third_sum, norm_table[1, 0], norm_table[1, 1], grad_encoded
        )
        grad_ffn, up_step, down_step = ffn_step_backward(
            grad_third, ffn_keep, slot_index, up_weight, down_weight
        )
        grad_hidden_two = grad_third + grad_ffn
        grad_second, gain_two, shift_two = lax.cond(
            is_encoder,
            lambda: (grad_hidden_two, width_zero, width_zero),
            lambda: norm_backward(second_sum, norm_table[2, 0], norm_table[2, 1], grad_hidden_two),
        )
        grad_second, gain_one, shift_one, gain_two, shift_two, up_step, down_step = (
            grad_second,
            gain_one,
            shift_one,
            gain_two,
            shift_two,
            up_step,
            down_step,
        )
        grad_cross_full = gather_grads(grad_second.astype(jnp.bfloat16))
        cross_partial, cross_step, memory_grads = lax.cond(
            is_encoder,
            lambda: (wide_zero, cross_zero, memory_zero),
            lambda: cross_backward(
                cross_in, grad_cross_full, memory, cross_weight, own_seg, source_seg, local_heads
            ),
        )
        grad_hidden_one = grad_second + sum_grads(cross_partial)
        arrived_grads = return_grads(memory_grads)
        if step_number < micro_count:
            returned_store = returned_store.at[step_number].set(arrived_grads)
        side_step = memory_weights + cross_step
        grad_first, gain_zero, shift_zero = norm_backward(
            first_sum, norm_table[0, 0], norm_table[0, 1], grad_hidden_one
        )
        grad_attn_full = gather_grads(grad_first.astype(jnp.bfloat16))
        self_partial, qkv_step, out_step = self_backward(
            attn_in, grad_attn_full, qkv_weight, out_weight, own_seg, local_heads
        )
        grad_base = grad_first + sum_grads(self_partial)
        input_share = pick_slot(token_share, slot_index).astype(jnp.float32)
        grad_input, gain_input, shift_input = lax.cond(
            is_encoder,
            lambda: norm_backward(input_share, norm_table[2, 0], norm_table[2, 1], grad_base),
            lambda: (grad_base, width_zero, width_zero),
        )
        grad_input, gain_zero, shift_zero, gain_input, shift_input, qkv_step, out_step = (
            grad_input,
            gain_zero,
            shift_zero,
            gain_input,
            shift_input,
            qkv_step,
            out_step,
        )
        token_grad = store_slot(token_grad, slot_index, grad_input, is_live)
        norm_step = jnp.stack(
            [
                jnp.stack([gain_zero, shift_zero]),
                jnp.stack([gain_one, shift_one]),
                jnp.stack([gain_two + gain_input, shift_two + shift_input]),
            ]
        )
        grad_qkv = grad_qkv + jnp.where(is_live, qkv_step, 0.0)
        grad_out = grad_out + jnp.where(is_live, out_step, 0.0)
        grad_cross = grad_cross + jnp.where(is_live, side_step, 0.0)
        grad_up = grad_up + jnp.where(is_live, up_step, 0.0)
        grad_down = grad_down + jnp.where(is_live, down_step, 0.0)
        grad_norm = grad_norm + jnp.where(is_live, norm_step, 0.0)
    summed = (
        lax.psum(grad_qkv.astype(jnp.bfloat16), "dp").astype(jnp.float32),
        lax.psum(grad_out.astype(jnp.bfloat16), "dp").astype(jnp.float32),
        lax.psum(grad_cross.astype(jnp.bfloat16), "dp").astype(jnp.float32),
        lax.psum(grad_up.astype(jnp.bfloat16), "dp").astype(jnp.float32),
        lax.psum(grad_down.astype(jnp.bfloat16), "dp").astype(jnp.float32),
    )
    norm_total = lax.psum(grad_norm, ("dp", "tensor"))
    return (
        result[None],
        token_grad[None],
        summed[0][None],
        summed[1][None],
        summed[2][None],
        summed[3][None],
        summed[4][None],
        norm_total[None],
    )


def solution(mesh):
    placed = (
        P("section", "dp", "tensor", None),
        P(None, "dp", None),
        P("section", None, None, "tensor"),
        P("section", "tensor", None),
        P("section", None, None, "tensor"),
        P("section", None, "tensor"),
        P("section", "tensor", None),
        P("section", None, None, None),
        P("section", "dp", "tensor", None),
    )
    return jax.shard_map(
        local,
        mesh=mesh,
        in_specs=placed,
        out_specs=(
            P("section", "dp", "tensor", None),
            P("section", "dp", "tensor", None),
            P("section", None, None, "tensor"),
            P("section", "tensor", None),
            P("section", None, None, "tensor"),
            P("section", None, "tensor"),
            P("section", "tensor", None),
            P("section", None, None, None),
        ),
        check_vma=False,
    )
```

profile of v0, /device:TPU:0, one launch (start us, length us, event | category | flops | bytes accessed | tf_op | source)
XLA Modules:
  0.0 4078.2 jit_solution(124796647238543304)
XLA Ops:
  34.3 16.4 all-gather.22.cloned.1.call-done
  65.7 88.7 %while.280 = (s32[]{:T(128)}, bf16[4,512,4,64]{1,3,2,0:T(8,128)(2,1)}, s32[4,512]{1,0:T(4,128)S(1)}, bf16[4,512,4,64]{1,3,2,0:T(8,128)(2,1)}, bf16[2048,4,64]{0,...) while((s32[]{:T(128)}, ...), condition=%wide.region_7.8_spmd.clone, body=%wide.region_4.7_spmd.clone.sunk | while | flops 1102205440 | bytes 38320240 | solution.py:126
  176.9 88.8 %while.281 = (s32[]{:T(128)}, bf16[4,512,4,64]{1,3,2,0:T(8,128)(2,1)}, s32[4,512]{1,0:T(4,128)S(1)}, bf16[4,512,4,64]{1,3,2,0:T(8,128)(2,1)}, bf16[2048,4,64]{0,...) while((s32[]{:T(128)}, ...), condition=%wide.region_32.33_spmd.clone, body=%wide.region_29.32_spmd.clone.sunk | while | flops 1102205440 | bytes 38320240 | solution.py:126
  201.5 10.6 fusion.1381
  223.6 10.6 fusion.1381
  245.7 10.6 fusion.1381
  288.2 92.3 %while.282 = (s32[]{:T(128)}, bf16[4,512,4,64]{1,3,2,0:T(8,128)(2,1)}, s32[4,512]{1,0:T(4,128)}, bf16[4,512,4,64]{1,3,2,0:T(8,128)(2,1)}, bf16[2048,4,64]{0,2,1:...) while((s32[]{:T(128)}, ...), condition=%wide.region_59.60_spmd.clone, body=%wide.region_56.59_spmd.clone.sunk | while | flops 1102205440 | bytes 38320240 | solution.py:126
  392.6 24.2 reduce-scatter.34.cloned.1.call-done
  425.0 33.2 all-gather.24.cloned.1.call-done
  461.7 144.2 %reduce-scatter.24.cloned.1.call-done = bf16[1024,512]{1,0:T(8,128)(2,1)} async-done(((bf16[2048,512]{1,0:T(8,128)(2,1)}), bf16[1024,512]{1,0:T(8,128)(2,1)}) %reduce-scatter.24.cloned.1.call-update) | async-done | bytes 1048592 | tf_op jit(solution)/shard_map/reduce_scatter | solution.py:75
  614.0 38.1 all-gather.26.cloned.1.call-done
  659.2 31.9 reduce-scatter.26.cloned.1.call-done
  697.1 32.7 all-gather.32.cloned.1.call-done
  741.1 23.9 all-gather.30.cloned.1.call-done
  774.9 123.1 %reduce-scatter.30.cloned.1.call-done = bf16[1024,512]{1,0:T(8,128)(2,1)} async-done(((bf16[2048,512]{1,0:T(8,128)(2,1)}), bf16[1024,512]{1,0:T(8,128)(2,1)}) %reduce-scatter.30.cloned.1.call-update) | async-done | bytes 1048592 | tf_op jit(solution)/shard_map/reduce_scatter | solution.py:75
  907.4 38.1 all-gather.34.cloned.1.call-done
  955.0 29.5 reduce-scatter.32.cloned.1.call-done
  991.1 33.2 all-gather.40.cloned.1.call-done
  1041.9 23.0 all-gather.38.cloned.1.call-done
  1071.7 126.5 %reduce-scatter.36.cloned.1.call-done = bf16[1024,512]{1,0:T(8,128)(2,1)} async-done(((bf16[2048,512]{1,0:T(8,128)(2,1)}), bf16[1024,512]{1,0:T(8,128)(2,1)}) %reduce-scatter.36.cloned.1.call-update) | async-done | bytes 1048592 | tf_op jit(solution)/shard_map/reduce_scatter | solution.py:75
  1207.6 37.4 all-gather.42.cloned.1.call-done
  1255.4 28.7 reduce-scatter.38.cloned.1.call-done
  1298.3 25.4 all-gather.44.cloned.1.call-done
  1350.0 18.0 reduce-scatter.40.cloned.1.call-done
  1392.0 17.3 all-gather.46.cloned.1.call-done
  1409.3 10.7 fusion.698
  1428.1 29.6 reduce-scatter.42.cloned.1.call-done
  1475.7 27.6 all-gather.48.cloned.1.call-done
  1516.6 300.8 %collective-permute-done.2 = bf16[2,2048,256]{2,1,0:T(8,128)(2,1)S(1)} collective-permute-done((bf16[2,2048,256]{2,1,0:T(8,128)(2,1)S(1)}, bf16[2,2048,256]{2,1,0:T(8,128)(2,1)S(1)}, u32[]{:S(2)}, u32[]{:S(2)}) %collective-permute-start.2) | collective-permute-done | bytes 2097184 | tf_op jit(solution)/shard_map/ppermute | solution.py:18
  1820.6 14.6 conditional.38
  1835.8 31.4 reduce-scatter.48.cloned.1.call-done
  1882.8 25.4 all-gather.52.cloned.1.call-done
  1908.2 10.7 fusion.702
  1924.7 32.0 reduce-scatter.50.cloned.1.call-done
  1963.6 39.4 all-gather.54.cloned.1.call-done
  2017.5 302.8 %collective-permute-done.3 = bf16[2,2048,256]{2,1,0:T(8,128)(2,1)S(1)} collective-permute-done((bf16[2,2048,256]{2,1,0:T(8,128)(2,1)}, bf16[2,2048,256]{2,1,0:T(8,128)(2,1)S(1)}, u32[]{:S(2)}, u32[]{:S(2)}) %collective-permute-start.3) | collective-permute-done | bytes 2097184 | tf_op jit(solution)/shard_map/ppermute | solution.py:18
  2320.2 15.1 conditional.42
  2335.5 31.9 reduce-scatter.56.cloned.1.call-done
  2383.6 25.6 all-gather.58.cloned.1.call-done
  2409.2 10.7 fusion.706
  2425.8 31.9 reduce-scatter.58.cloned.1.call-done
  2571.8 206.4 %reduce-scatter.60.cloned.1.call-done = bf16[1024,512]{1,0:T(8,128)(2,1)} async-done(((bf16[2048,512]{1,0:T(8,128)(2,1)}), bf16[1024,512]{1,0:T(8,128)(2,1)}) %reduce-scatter.60.cloned.1.call-update) | async-done | bytes 1048592 | tf_op jit(solution)/shard_map/reduce_scatter | solution.py:85
  2834.6 273.7 %while.285 = (s32[]{:T(128)}, f32[2048,4,64]{0,2,1:T(8,128)S(1)}, f32[2048,4,64]{0,2,1:T(8,128)}, bf16[4,512,4,64]{1,3,2,0:T(8,128)(2,1)}, bf16[4,512,4,64]{1,3,...) while((s32[]{:T(128)}, f32[2048,4,64]{0,2,1:T(8,128)S(1)}, ...), condition=%wide.region_195.196_spmd.clone, body=%wide.region_191.195_spmd.clone.sunk | while | flops 3290319360 | bytes 251224416 | solution.py:176
  2848.4 13.5 multiply_reduce_fusion.53
  2906.1 10.6 fusion.1431
  2916.7 13.5 multiply_reduce_fusion.53
  2985.0 13.5 multiply_reduce_fusion.53
  3053.4 13.5 multiply_reduce_fusion.53
  3119.6 273.8 %while.284 = (s32[]{:T(128)}, f32[2048,4,64]{0,2,1:T(8,128)S(1)}, f32[2048,4,64]{0,2,1:T(8,128)}, bf16[4,512,4,64]{1,3,2,0:T(8,128)(2,1)}, bf16[4,512,4,64]{1,3,...) while((s32[]{:T(128)}, f32[2048,4,64]{0,2,1:T(8,128)S(1)}, ...), condition=%wide.region_153.154_spmd.clone, body=%wide.region_149.153_spmd.clone.sunk | while | flops 3290319360 | bytes 251224416 | solution.py:176
  3133.3 13.5 multiply_reduce_fusion.52
  3201.1 13.5 multiply_reduce_fusion.52
  3269.6 13.5 multiply_reduce_fusion.52
  3327.4 10.6 fusion.1415
  3338.1 13.5 multiply_reduce_fusion.52
  3417.3 273.1 %while.283 = (s32[]{:T(128)}, f32[2048,4,64]{0,2,1:T(8,128)S(1)}, f32[2048,4,64]{0,2,1:T(8,128)}, bf16[4,512,4,64]{1,3,2,0:T(8,128)(2,1)}, bf16[4,512,4,64]{1,3,...) while((s32[]{:T(128)}, f32[2048,4,64]{0,2,1:T(8,128)S(1)}, ...), condition=%wide.region_111.112_spmd.clone, body=%wide.region_107.111_spmd.clone.sunk | while | flops 3290319360 | bytes 251224416 | solution.py:176
  3430.8 13.5 multiply_reduce_fusion.51
  3498.6 13.5 multiply_reduce_fusion.51
  3567.0 13.5 multiply_reduce_fusion.51
  3635.4 13.5 multiply_reduce_fusion.51
  3745.2 126.8 %all-reduce.5.cloned.1.call-done = (bf16[1,3,512,256]{3,2,1,0:T(8,128)(2,1)}, bf16[1,256,512]{2,1,0:T(8,128)(2,1)}, bf16[1,2,512,256]{3,2,1,0:T(8,128)(2,1)}, bf...) async-done(((bf16[1,3,512,256]{3,2,1,0:T(8,128)(2,1)}, bf16[1,256,512]{2,1,0:T(8,128)(2,1)}, bf16[1,2,512,256]{3,2,1,0:T(8,128)(2,1)}, bf16[1,512,1024]{2,1,0:T(8,128)(2,1)}, ...) | async-done | bytes 3670032 | tf_op jit(solution)/shard_map/psum | solution.py:497
  3879.7 25.2 reduce-scatter.62.cloned.1.call-done
  3915.9 23.2 reduce-scatter.54.cloned.1.call-done
  3950.2 23.4 reduce-scatter.46.cloned.1.call-done
  3987.3 75.8 %psum.47 = f32[1,3,2,512]{3,2,1,0:T(2,128)} all-reduce(f32[1,3,2,512]{3,2,1,0:T(2,128)S(1)} %fusion.979), channel_id=1, replica_groups=mesh['section'=2,'dp'=8,'tensor'=2] {'dp','tensor'}, use_global_device_ids=true, to_apply=%region_222.223 | all-reduce | flops 3072 | bytes 24576 | tf_op jit(solution)/shard_map/psum | solution.py:503
  (1354 shorter events, 1657.3 us)
Async XLA Ops:
  7.2 644.9 %copy-start = (bf16[1,512,1024]{2,1,0:T(8,128)(2,1)S(1)}, bf16[1,512,1024]{2,1,0:T(8,128)(2,1)}, u32[]{:S(2)}) copy-start(bf16[1,512,1024]{2,1,0:T(8,128)(2,1)} %param.92) | copy-start | bytes 3145732
  7.2 43.5 %all-gather.22.cloned.1.call-start = ((), (), s32[]{:S(2)}) async-start(), calls=%async_computation.21 | async-start | bytes 3145728 | tf_op jit(solution)/shard_map/all_gather | solution.py:71
  15.1 141.6 %all-gather.28.cloned.1.call-start = ((), (), s32[]{:S(2)}) async-start(), calls=%async_computation.27 | async-start | bytes 3145728 | tf_op jit(solution)/shard_map/all_gather | solution.py:71
  22.6 245.4 %all-gather.36.cloned.1.call-start = ((), (), s32[]{:S(2)}) async-start(), calls=%async_computation.34 | async-start | bytes 3145728 | tf_op jit(solution)/shard_map/all_gather | solution.py:71
  25.7 359.8 %reduce-scatter.22.cloned.1.call-start = ((), (), s32[]{:S(2)}) async-start(), calls=%async_computation.22 | async-start | bytes 3145728 | tf_op jit(solution)/shard_map/reduce_scatter | solution.py:75
  170.5 218.1 %reduce-scatter.28.cloned.1.call-start = ((), (), s32[]{:S(2)}) async-start(), calls=%async_computation.28 | async-start | bytes 3145728 | tf_op jit(solution)/shard_map/reduce_scatter | solution.py:75
  281.8 135.0 %reduce-scatter.34.cloned.1.call-start = ((), (), s32[]{:S(2)}) async-start(), calls=%async_computation.35 | async-start | bytes 3145728 | tf_op jit(solution)/shard_map/reduce_scatter | solution.py:75
  384.9 73.4 %all-gather.24.cloned.1.call-start = ((), (), s32[]{:S(2)}) async-start(), calls=%async_computation.23 | async-start | bytes 3145728 | tf_op jit(solution)/shard_map/all_gather | solution.py:71
  385.5 222.9 %copy-start.189 = (f32[1,1,512]{2,1,0:T(1,128)}, f32[1,1,512]{2,1,0:T(1,128)S(1)}, u32[]{:S(2)}) copy-start(f32[1,1,512]{2,1,0:T(1,128)S(1)} %get-tuple-element.3276) | copy-start | bytes 6148
  385.5 222.9 %copy-start.202 = (f32[1,1,512]{2,1,0:T(1,128)}, f32[1,1,512]{2,1,0:T(1,128)S(1)}, u32[]{:S(2)}) copy-start(f32[1,1,512]{2,1,0:T(1,128)S(1)} %get-tuple-element.3279) | copy-start | bytes 6148
  425.0 180.9 %reduce-scatter.24.cloned.1.call-start = ((), (), s32[]{:S(2)}) async-start(), calls=%async_computation.24 | async-start | bytes 3145728 | tf_op jit(solution)/shard_map/reduce_scatter | solution.py:75
  461.6 190.4 %all-gather.26.cloned.1.call-start = ((), (), s32[]{:S(2)}) async-start(), calls=%async_computation.25 | async-start | bytes 3145728 | tf_op jit(solution)/shard_map/all_gather | solution.py:290
  613.9 77.2 %reduce-scatter.26.cloned.1.call-start = ((), (), s32[]{:S(2)}) async-start(), calls=%async_computation.26 | async-start | bytes 3145728 | tf_op jit(solution)/shard_map/reduce_scatter | solution.py:292
  659.2 70.6 %all-gather.32.cloned.1.call-start = ((), (), s32[]{:S(2)}) async-start(), calls=%async_computation.30 | async-start | bytes 3145728 | tf_op jit(solution)/shard_map/all_gather | solution.py:71
  696.5 68.5 %all-gather.30.cloned.1.call-start = ((), (), s32[]{:S(2)}) async-start(), calls=%async_computation.29 | async-start | bytes 3145728 | tf_op jit(solution)/shard_map/all_gather | solution.py:71
  697.1 200.9 %reduce-scatter.30.cloned.1.call-start = ((), (), s32[]{:S(2)}) async-start(), calls=%async_computation.31 | async-start | bytes 3145728 | tf_op jit(solution)/shard_map/reduce_scatter | solution.py:75
  738.5 26.5 collective-permute-start
  766.6 178.9 %all-gather.34.cloned.1.call-start = ((), (), s32[]{:S(2)}) async-start(), calls=%async_computation.32 | async-start | bytes 3145728 | tf_op jit(solution)/shard_map/all_gather | solution.py:290
  771.6 126.4 %copy-start.190 = (f32[1,1,512]{2,1,0:T(1,128)S(1)}, f32[1,1,512]{2,1,0:T(1,128)}, u32[]{:S(2)}) copy-start(f32[1,1,512]{2,1,0:T(1,128)} %copy-done.189) | copy-start | bytes 6148
  771.6 126.4 %copy-start.200 = (f32[1024]{0:T(1024)S(1)}, f32[1024]{0:T(1024)}, u32[]{:S(2)}) copy-start(f32[1024]{0:T(1024)} %copy-done.199) | copy-start | bytes 12292
  771.6 126.4 %copy-start.203 = (f32[1,1,512]{2,1,0:T(1,128)S(1)}, f32[1,1,512]{2,1,0:T(1,128)}, u32[]{:S(2)}) copy-start(f32[1,1,512]{2,1,0:T(1,128)} %copy-done.202) | copy-start | bytes 6148
  771.6 126.4 %copy-start.216 = (f32[1024]{0:T(1024)S(1)}, f32[1024]{0:T(1024)}, u32[]{:S(2)}) copy-start(f32[1024]{0:T(1024)} %copy-done.215) | copy-start | bytes 12292
  907.4 77.2 %reduce-scatter.32.cloned.1.call-start = ((), (), s32[]{:S(2)}) async-start(), calls=%async_computation.33 | async-start | bytes 3145728 | tf_op jit(solution)/shard_map/reduce_scatter | solution.py:292
  952.6 71.7 %all-gather.40.cloned.1.call-start = ((), (), s32[]{:S(2)}) async-start(), calls=%async_computation.37 | async-start | bytes 3145728 | tf_op jit(solution)/shard_map/all_gather | solution.py:71
  991.0 73.9 %all-gather.38.cloned.1.call-start = ((), (), s32[]{:S(2)}) async-start(), calls=%async_computation.36 | async-start | bytes 3145728 | tf_op jit(solution)/shard_map/all_gather | solution.py:71
  1030.2 5.3 collective-permute-start.1
  1031.6 166.6 %reduce-scatter.36.cloned.1.call-start = ((), (), s32[]{:S(2)}) async-start(), calls=%async_computation.38 | async-start | bytes 3145728 | tf_op jit(solution)/shard_map/reduce_scatter | solution.py:75
  1066.8 178.2 %all-gather.42.cloned.1.call-start = ((), (), s32[]{:S(2)}) async-start(), calls=%async_computation.39 | async-start | bytes 3145728 | tf_op jit(solution)/shard_map/all_gather | solution.py:290
  1066.9 131.3 %copy-start.21 = (f32[1024,512]{1,0:T(8,128)S(1)}, f32[1024,512]{1,0:T(8,128)}, u32[]{:S(2)}) copy-start(f32[1024,512]{1,0:T(8,128)} %copy-done.19) | copy-start | bytes 6291460
  1066.9 131.3 %copy-start.191 = (f32[1,1,512]{2,1,0:T(1,128)S(1)}, f32[1,1,512]{2,1,0:T(1,128)}, u32[]{:S(2)}) copy-start(f32[1,1,512]{2,1,0:T(1,128)} %copy-done.189) | copy-start | bytes 6148
  1066.9 131.3 %copy-start.198 = (f32[1024]{0:T(1024)S(1)}, f32[1024]{0:T(1024)}, u32[]{:S(2)}) copy-start(f32[1024]{0:T(1024)} %copy-done.197) | copy-start | bytes 12292
  1066.9 131.3 %copy-start.204 = (f32[1,1,512]{2,1,0:T(1,128)S(1)}, f32[1,1,512]{2,1,0:T(1,128)}, u32[]{:S(2)}) copy-start(f32[1,1,512]{2,1,0:T(1,128)} %copy-done.202) | copy-start | bytes 6148
  1066.9 131.3 %copy-start.214 = (f32[1024]{0:T(1024)S(1)}, f32[1024]{0:T(1024)}, u32[]{:S(2)}) copy-start(f32[1024]{0:T(1024)} %copy-done.213) | copy-start | bytes 12292
  1207.6 76.5 %reduce-scatter.38.cloned.1.call-start = ((), (), s32[]{:S(2)}) async-start(), calls=%async_computation.40 | async-start | bytes 3145728 | tf_op jit(solution)/shard_map/reduce_scatter | solution.py:292
  1252.1 71.6 %all-gather.44.cloned.1.call-start = ((), (), s32[]{:S(2)}) async-start(), calls=%async_computation.41 | async-start | bytes 3145728 | tf_op jit(solution)/shard_map/all_gather | solution.py:71
  1290.5 77.5 %reduce-scatter.40.cloned.1.call-start = ((), (), s32[]{:S(2)}) async-start(), calls=%async_computation.42 | async-start | bytes 3145728 | tf_op jit(solution)/shard_map/reduce_scatter | solution.py:85
  1336.0 73.3 %all-gather.46.cloned.1.call-start = ((), (), s32[]{:S(2)}) async-start(), calls=%async_computation.43 | async-start | bytes 3145728 | tf_op jit(solution)/shard_map/all_gather | solution.py:304
  1376.0 81.7 %reduce-scatter.42.cloned.1.call-start = ((), (), s32[]{:S(2)}) async-start(), calls=%async_computation.44 | async-start | bytes 3145728 | tf_op jit(solution)/shard_map/reduce_scatter | solution.py:307
  1425.7 77.7 %all-gather.48.cloned.1.call-start = ((), (), s32[]{:S(2)}) async-start(), calls=%async_computation.45 | async-start | bytes 3145728 | tf_op jit(solution)/shard_map/all_gather | solution.py:81
  1462.8 404.4 %reduce-scatter.48.cloned.1.call-start = ((), (), s32[]{:S(2)}) async-start(), calls=%async_computation.49 | async-start | bytes 3145728 | tf_op jit(solution)/shard_map/reduce_scatter | solution.py:85
  1515.3 302.1 %collective-permute-start.2 = (bf16[2,2048,256]{2,1,0:T(8,128)(2,1)S(1)}, bf16[2,2048,256]{2,1,0:T(8,128)(2,1)S(1)}, u32[]{:S(2)}, u32[]{:S(2)}) collective-permute-start(bf16[2,2048,256]{2,1,0:T(8,128)(2,1)S(1)} %copy.90), channel_id=1, source_target_pairs={{16,0},{17,1},{18,2},{19,3},{20,4},{21,5},{22,6},{23,7},{24,8},{25... | collective-permute-start | bytes 6291464 | tf_op jit(solution)/shard_map/ppermute | solution.py:18
  1835.2 73.0 %all-gather.52.cloned.1.call-start = ((), (), s32[]{:S(2)}) async-start(), calls=%async_computation.50 | async-start | bytes 3145728 | tf_op jit(solution)/shard_map/all_gather | solution.py:304
  1875.0 81.7 %reduce-scatter.50.cloned.1.call-start = ((), (), s32[]{:S(2)}) async-start(), calls=%async_computation.51 | async-start | bytes 3145728 | tf_op jit(solution)/shard_map/reduce_scatter | solution.py:307
  1924.7 78.4 %all-gather.54.cloned.1.call-start = ((), (), s32[]{:S(2)}) async-start(), calls=%async_computation.52 | async-start | bytes 3145728 | tf_op jit(solution)/shard_map/all_gather | solution.py:81
  1961.8 405.6 %reduce-scatter.56.cloned.1.call-start = ((), (), s32[]{:S(2)}) async-start(), calls=%async_computation.56 | async-start | bytes 3145728 | tf_op jit(solution)/shard_map/reduce_scatter | solution.py:85
  2012.2 308.0 %copy-start.87 = (bf16[1,2,512,256]{3,2,1,0:T(8,128)(2,1)S(1)}, bf16[1,2,512,256]{3,2,1,0:T(8,128)(2,1)}, u32[]{:S(2)}) copy-start(bf16[1,2,512,256]{3,2,1,0:T(8,128)(2,1)} %param.91) | copy-start | bytes 1572868
  2016.2 304.0 %collective-permute-start.3 = (bf16[2,2048,256]{2,1,0:T(8,128)(2,1)}, bf16[2,2048,256]{2,1,0:T(8,128)(2,1)S(1)}, u32[]{:S(2)}, u32[]{:S(2)}) collective-permute-start(bf16[2,2048,256]{2,1,0:T(8,128)(2,1)} %copy.96), channel_id=1, source_target_pairs={{16,0},{17,1},{18,2},{19,3},{20,4},{21,5},{22,6},{23,7},{24,8},{25... | collective-permute-start | bytes 6291464 | tf_op jit(solution)/shard_map/ppermute | solution.py:18
  2335.4 73.8 %all-gather.58.cloned.1.call-start = ((), (), s32[]{:S(2)}) async-start(), calls=%async_computation.57 | async-start | bytes 3145728 | tf_op jit(solution)/shard_map/all_gather | solution.py:304
  2375.9 81.8 %reduce-scatter.58.cloned.1.call-start = ((), (), s32[]{:S(2)}) async-start(), calls=%async_computation.58 | async-start | bytes 3145728 | tf_op jit(solution)/shard_map/reduce_scatter | solution.py:307
  2425.7 103.9 %all-gather.60.cloned.1.call-start = ((), (), s32[]{:S(2)}) async-start(), calls=%async_computation.59 | async-start | bytes 3145728 | tf_op jit(solution)/shard_map/all_gather | solution.py:81
  2461.5 100.5 %reduce-scatter.44.cloned.1.call-start = ((), (), s32[]{:S(2)}) async-start(), calls=%async_computation.46 | async-start | bytes 3145728 | tf_op jit(solution)/shard_map/reduce_scatter | solution.py:85
  2462.3 109.5 %reduce-scatter.52.cloned.1.call-start = ((), (), s32[]{:S(2)}) async-start(), calls=%async_computation.53 | async-start | bytes 3145728 | tf_op jit(solution)/shard_map/reduce_scatter | solution.py:85
  2471.5 306.7 %reduce-scatter.60.cloned.1.call-start = ((), (), s32[]{:S(2)}) async-start(), calls=%async_computation.60 | async-start | bytes 3145728 | tf_op jit(solution)/shard_map/reduce_scatter | solution.py:85
  2539.4 284.6 %all-gather.62.cloned.1.call-start = ((), (), s32[]{:S(2)}) async-start(), calls=%async_computation.61 | async-start | bytes 3145728 | tf_op jit(solution)/shard_map/all_gather | solution.py:81
  2557.7 220.5 %copy-start.45 = (f32[1024,512]{1,0:T(8,128)S(1)}, f32[1024,512]{1,0:T(8,128)}, u32[]{:S(2)}) copy-start(f32[1024,512]{1,0:T(8,128)} %copy-done.44) | copy-start | bytes 6291460
  2557.7 220.5 %copy-start.192 = (f32[1,1,512]{2,1,0:T(1,128)S(1)}, f32[1,1,512]{2,1,0:T(1,128)}, u32[]{:S(2)}) copy-start(f32[1,1,512]{2,1,0:T(1,128)} %copy-done.189) | copy-start | bytes 6148
  2562.0 223.3 %copy-start.140 = (bf16[1024,512]{1,0:T(8,128)(2,1)S(1)}, bf16[1024,512]{1,0:T(8,128)(2,1)}, u32[]{:S(2)}) copy-start(bf16[1024,512]{1,0:T(8,128)(2,1)} %reduce-scatter.44.cloned.1.call-done) | copy-start | bytes 3145732
  2790.7 317.5 %all-gather.56.cloned.1.call-start = ((), (), s32[]{:S(2)}) async-start(), calls=%async_computation.54 | async-start | bytes 3145728 | tf_op jit(solution)/shard_map/all_gather | solution.py:81
  2805.5 601.3 %all-gather.50.cloned.1.call-start = ((), (), s32[]{:S(2)}) async-start(), calls=%async_computation.47 | async-start | bytes 3145728 | tf_op jit(solution)/shard_map/all_gather | solution.py:81
  2819.8 1052.3 %all-reduce.5.cloned.1.call-start = ((), (), s32[]{:S(2)}) async-start(), calls=%async_computation.63 | async-start | bytes 7340032 | tf_op jit(solution)/shard_map/psum | solution.py:497
  2834.6 273.7 %copy-start.108 = (bf16[1,256,512]{2,1,0:T(8,128)(2,1)S(1)}, bf16[1,256,512]{2,1,0:T(8,128)(2,1)}, u32[]{:S(2)}) copy-start(bf16[1,256,512]{2,1,0:T(8,128)(2,1)} %param.90) | copy-start | bytes 786436
  3727.3 177.7 %reduce-scatter.62.cloned.1.call-start = ((), (), s32[]{:S(2)}) async-start(), calls=%async_computation.62 | async-start | bytes 3145728 | tf_op jit(solution)/shard_map/reduce_scatter | solution.py:85
  3733.7 205.5 %reduce-scatter.54.cloned.1.call-start = ((), (), s32[]{:S(2)}) async-start(), calls=%async_computation.55 | async-start | bytes 3145728 | tf_op jit(solution)/shard_map/reduce_scatter | solution.py:85
  3739.1 234.6 %reduce-scatter.46.cloned.1.call-start = ((), (), s32[]{:S(2)}) async-start(), calls=%async_computation.48 | async-start | bytes 3145728 | tf_op jit(solution)/shard_map/reduce_scatter | solution.py:85
  (291 other events, 2511.4 us)
Sparse Core Ops, SparseCore 0:
  14.9 35.8 all-gather.21
  52.8 33.1 all-gather.27
  88.1 33.1 all-gather.35
  170.7 31.7 reduce-scatter.21
  282.0 31.8 reduce-scatter.27
  385.0 31.8 reduce-scatter.33
  425.1 33.0 all-gather.23
  461.8 144.0 reduce-scatter.23
  614.1 37.9 all-gather.25
  659.3 31.8 reduce-scatter.25
  696.6 33.1 all-gather.31
  731.8 33.1 all-gather.29
  767.3 130.6 reduce-scatter.29
  907.5 37.9 all-gather.33
  952.7 31.8 reduce-scatter.31
  991.1 33.1 all-gather.39
  1031.7 33.1 all-gather.37
  1067.1 131.0 reduce-scatter.35
  1207.7 37.2 all-gather.41
  1252.2 31.8 reduce-scatter.37
  1290.6 33.0 all-gather.43
  1336.1 31.8 reduce-scatter.39
  1376.1 33.1 all-gather.45
  1425.8 31.8 reduce-scatter.41
  1462.5 40.8 all-gather.47
  1835.3 31.8 reduce-scatter.47
  1875.1 33.1 all-gather.51
  1924.8 31.8 reduce-scatter.49
  1961.4 41.5 all-gather.53
  2335.5 31.8 reduce-scatter.55
  2376.0 33.1 all-gather.57
  2425.8 31.8 reduce-scatter.57
  2461.4 42.1 all-gather.59
  2505.8 31.8 reduce-scatter.43
  2540.0 31.8 reduce-scatter.51
  2574.0 204.1 reduce-scatter.59
  2790.8 33.1 all-gather.61
  2825.5 33.1 all-gather.55
  2860.7 33.1 all-gather.49
  3727.4 144.5 all-reduce.4
  3874.3 30.6 reduce-scatter.61
  3907.3 31.8 reduce-scatter.53
  3941.8 31.8 reduce-scatter.45
where the time goes:
time: 4090 us; the launch traced here: 4080 us
  waiting for transfers between devices  2150 us (53%)
  matrix products  1130 us (28%)
  other arithmetic  388 us (9%)
  local copies, waits for them, and re-layouts  283 us (7%)
  blocking collectives  75.8 us (2%)
    ppermute x4, waiting for transfers between devices, from_behind(): return lax.ppermute(shard, axis, pairs)  607 us
    reduce_scatter x6, waiting for transfers between devices, sum_rows(): lax.psum_scatter(partial_rows.astype(jnp.bfloat16), 'tensor', scatter_dim...  418 us
    reduce_scatter x9, waiting for transfers between devices, sum_grads(): lax.psum_scatter(partial_grads.astype(jnp.bfloat16), 'tensor', scatter_di...  369 us
    sub x24, matrix products, one_block(): exponent = jnp.exp(scores - row_max)  254 us
    all_gather x9, waiting for transfers between devices, gather_rows(): return lax.all_gather(share_rows, 'tensor', axis=0, tiled=True)  188 us
    dot_general x12, matrix products, one_block(): jnp.einsum('qhd,khd->hqk', grad_block, value_heads, preferred_element_typ...  162 us
    psum x1, waiting for transfers between devices, local(): lax.psum(grad_qkv.astype(jnp.bfloat16), 'dp').astype(jnp.float32)  127 us
    convert_element_type x12, other arithmetic, one_block(): grad_scores = (probability * (grad_prob - row_inner)).astype(jnp.bfloat16)  118 us
  transfers between devices with their start and end apart: 47, of which 38 were waited for; matrix products, arithmetic and copies ran while one was open for 28% of the time, Pallas kernels for 0%

commit v1 on v0

v1 whole, which is shorter than its diff:
```python
import functools
import math

import jax
import jax.numpy as jnp
from jax import lax
from jax.experimental import pallas as pl
from jax.experimental.pallas import tpu as pltpu
from jax.sharding import PartitionSpec as P

HEADS = 8
EPSILON = 1e-05
MASKED = -1000000000.0
LOG2E = 1.0 / math.log(2.0)
PAIR = 128
HALF = 64
VMEM = 60 * 1024 * 1024
BF16 = jnp.bfloat16
F32 = jnp.float32


def standardize(rows):
    mean = jnp.mean(rows, axis=-1, keepdims=True)
    centered = rows - mean
    inv = lax.rsqrt(jnp.mean(centered * centered, axis=-1, keepdims=True) + EPSILON)
    return centered * inv, inv


def affine(unit, norm_ref, slot):
    return unit * norm_ref[slot, 0:1, :] + norm_ref[slot, 1:2, :]


def norm_back(unit, inv, norm_ref, slot, grad, grad_ref):
    grad_ref[slot, 0:1, :] += jnp.sum(grad * unit, axis=0, keepdims=True)
    grad_ref[slot, 1:2, :] += jnp.sum(grad, axis=0, keepdims=True)
    scaled = grad * norm_ref[slot, 0:1, :]
    first = jnp.mean(scaled, axis=-1, keepdims=True)
    second = jnp.mean(scaled * unit, axis=-1, keepdims=True)
    return inv * (scaled - first - unit * second)


def gelu_tanh(inner):
    return jnp.tanh(0.7978845608028654 * (inner + 0.044715 * inner * inner * inner))


def gelu(inner):
    return 0.5 * inner * (1.0 + gelu_tanh(inner))


def gelu_both(inner):
    bent = gelu_tanh(inner)
    slope = 0.7978845608028654 * (1.0 + 0.134145 * inner * inner)
    half = 0.5 * (1.0 + bent)
    return inner * half, half + 0.5 * inner * (1.0 - bent * bent) * slope


def dot_nn(a, b):
    return jnp.dot(a, b, preferred_element_type=F32)


def dot_nt(a, b):
    return lax.dot_general(a, b, (((1,), (1,)), ((), ())), preferred_element_type=F32)


def dot_tn(a, b):
    return lax.dot_general(a, b, (((0,), (0,)), ((), ())), preferred_element_type=F32)


def row_call(body, name, rows, block, row_ins, whole_ins, row_outs, sum_outs, flops):
    def blocked(shape, dim):
        sizes = tuple(block if i == dim else size for i, size in enumerate(shape))
        return pl.BlockSpec(
            sizes, lambda step: tuple(step if i == dim else 0 for i in range(len(shape)))
        )

    def whole(shape):
        return pl.BlockSpec(
            shape, lambda step: (0,) * len(shape), pipeline_mode=pl.Buffered(buffer_count=1)
        )

    n_in = len(row_ins) + len(whole_ins)
    n_row, n_sum = len(row_outs), len(sum_outs)

    def kernel(*refs):
        ins, outs = refs[:n_in], refs[n_in : n_in + n_row]
        sums, totals = refs[n_in + n_row : n_in + n_row + n_sum], refs[n_in + n_row + n_sum :]

        @pl.when(pl.program_id(0) == 0)
        def _():
            for total in totals:
                total[...] = jnp.zeros_like(total)

        body(ins, outs, totals)

        @pl.when(pl.program_id(0) == pl.num_programs(0) - 1)
        def _():
            for out, total in zip(sums, totals):
                out[...] = total[...].astype(out.dtype)

    arrays = [array for array, _ in row_ins] + list(whole_ins)
    size = sum(a.size * a.dtype.itemsize for a in arrays)
    return pl.pallas_call(
        kernel,
        grid=(rows // block,),
        in_specs=[blocked(a.shape, dim) for a, dim in row_ins] + [whole(a.shape) for a in whole_ins],
        out_specs=[blocked(shape, dim) for shape, _, dim in row_outs]
        + [whole(shape) for shape, _ in sum_outs],
        out_shape=[jax.ShapeDtypeStruct(shape, dtype) for shape, dtype, _ in row_outs]
        + [jax.ShapeDtypeStruct(shape, dtype) for shape, dtype in sum_outs],
        scratch_shapes=[pltpu.VMEM(shape, F32) for shape, _ in sum_outs],
        compiler_params=pltpu.CompilerParams(vmem_limit_bytes=VMEM),
        cost_estimate=pl.CostEstimate(flops=flops, bytes_accessed=size, transcendentals=0),
        name=name,
    )(*arrays)


def project_qkv(x, norm, weights, with_norm, block):
    rows, width = x.shape
    parts, part = len(weights), weights[0].shape[-1]
    score = LOG2E / math.sqrt(width // HEADS)

    def body(ins, outs, totals):
        x_ref, norm_ref, *w = ins
        q_ref, kv_ref = outs
        rows_in = x_ref[...]
        if with_norm:
            unit, _ = standardize(rows_in.astype(F32))
            rows_in = affine(unit, norm_ref, 2).astype(BF16)
        for k in range(parts):
            q_ref[k] = (dot_nn(rows_in, w[k][0]) * score).astype(BF16)
            kv_ref[0, k] = dot_nn(rows_in, w[k][1]).astype(BF16)
            kv_ref[1, k] = dot_nn(rows_in, w[k][2]).astype(BF16)

    return row_call(
        body,
        "project_qkv",
        rows,
        block,
        [(x, 0)],
        [norm, *weights],
        [((parts, rows, part), BF16, 1), ((2, parts, rows, part), BF16, 2)],
        [],
        6 * rows * width * width,
    )


def encoder_forward(x, mix, norm, out, up, down, cross, block):
    rows, width = x.shape
    parts, part = len(out), out[0].shape[0]

    def body(ins, outs, totals):
        x_ref, mix_ref, norm_ref = ins[:3]
        wo, wu, wd, wc = (ins[3 + i * parts : 3 + (i + 1) * parts] for i in range(4))
        result_ref, kv_ref, first_ref, third_ref = outs
        unit, _ = standardize(x_ref[...].astype(F32))
        first = affine(unit, norm_ref, 2)
        for k in range(parts):
            first += dot_nn(mix_ref[k], wo[k][...])
        first_ref[...] = first
        unit, _ = standardize(first)
        third = affine(unit, norm_ref, 0)
        low = third.astype(BF16)
        for k in range(parts):
            act = gelu(dot_nn(low, wu[k][...])).astype(BF16)
            third += dot_nn(act, wd[k][...])
        third_ref[...] = third
        unit, _ = standardize(third)
        low = affine(unit, norm_ref, 1).astype(BF16)
        result_ref[...] = low
        for k in range(parts):
            kv_ref[0, k] = dot_nn(low, wc[k][0]).astype(BF16)
            kv_ref[1, k] = dot_nn(low, wc[k][1]).astype(BF16)

    units = sum(w.shape[1] for w in up)
    return row_call(
        body,
        "encoder_forward",
        rows,
        block,
        [(x, 0), (mix, 1)],
        [norm, *out, *up, *down, *cross],
        [
            ((rows, width), BF16, 0),
            ((2, parts, rows, part), BF16, 2),
            ((rows, width), F32, 0),
            ((rows, width), F32, 0),
        ],
        [],
        6 * rows * width * width + 4 * rows * width * units,
    )


def decoder_middle(x, mix, norm, out, cross, block):
    rows, width = x.shape
    parts, part = len(out), out[0].shape[0]
    score = LOG2E / math.sqrt(width // HEADS)

    def body(ins, outs, totals):
        x_ref, mix_ref, norm_ref = ins[:3]
        wo, wc = (ins[3 + i * parts : 3 + (i + 1) * parts] for i in range(2))
        q_ref, first_ref = outs
        first = x_ref[...].astype(F32)
        for k in range(parts):
            first += dot_nn(mix_ref[k], wo[k][...])
        first_ref[...] = first
        unit, _ = standardize(first)
        low = affine(unit, norm_ref, 0).astype(BF16)
        for k in range(parts):
            q_ref[k] = (dot_nn(low, wc[k][0]) * score).astype(BF16)

    return row_call(
        body,
        "decoder_middle",
        rows,
        block,
        [(x, 0), (mix, 1)],
        [norm, *out, *cross],
        [((parts, rows, part), BF16, 1), ((rows, width), F32, 0)],
        [],
        4 * rows * width * width,
    )


def ffn_back(low, grad_low, up, down, up_total, down_total, parts):
    grad = None
    for k in range(parts):
        act, slope = gelu_both(dot_nn(low, up[k][...]))
        down_total[k] += dot_tn(act.astype(BF16), grad_low)
        grad_inner = (dot_nt(grad_low, down[k][...]) * slope).astype(BF16)
        up_total[k] += dot_tn(low, grad_inner)
        step = dot_nt(grad_inner, up[k][...])
        grad = step if grad is None else grad + step
    return grad


def decoder_turn(first, mix, cotangent, norm, cross, up, down, block):
    rows, width = first.shape
    parts, part, units = len(cross), cross[0].shape[-1], up[0].shape[1]

    def body(ins, outs, totals):
        first_ref, mix_ref, cot_ref, norm_ref = ins[:4]
        wc, wu, wd = (ins[4 + i * parts : 4 + (i + 1) * parts] for i in range(3))
        result_ref, second_grad_ref, mix_grad_ref = outs
        out_total, up_total, down_total, norm_total = totals
        unit, _ = standardize(first_ref[...])
        second = affine(unit, norm_ref, 0)
        for k in range(parts):
            second += dot_nt(mix_ref[k], wc[k][1])
        unit_two, inv_two = standardize(second)
        third = affine(unit_two, norm_ref, 2)
        low = third.astype(BF16)
        acts, slopes = [], []
        for k in range(parts):
            act, slope = gelu_both(dot_nn(low, wu[k][...]))
            acts.append(act.astype(BF16))
            slopes.append(slope)
            third += dot_nn(acts[k], wd[k][...])
        unit_three, inv_three = standardize(third)
        result_ref[...] = affine(unit_three, norm_ref, 1).astype(BF16)
        grad = norm_back(
            unit_three, inv_three, norm_ref, 1, cot_ref[...].astype(F32), norm_total
        )
        grad_low = grad.astype(BF16)
        for k in range(parts):
            down_total[k] += dot_tn(acts[k], grad_low)
            grad_inner = (dot_nt(grad_low, wd[k][...]) * slopes[k]).astype(BF16)
            up_total[k] += dot_tn(low, grad_inner)
            grad += dot_nt(grad_inner, wu[k][...])
        grad = norm_back(unit_two, inv_two, norm_ref, 2, grad, norm_total)
        second_grad_ref[...] = grad
        grad_low = grad.astype(BF16)
        for k in range(parts):
            out_total[k] += dot_tn(grad_low, mix_ref[k])
            mix_grad_ref[k] = dot_nn(grad_low, wc[k][1]).astype(BF16)

    return row_call(
        body,
        "decoder_turn",
        rows,
        block,
        [(first, 0), (mix, 1), (cotangent, 0)],
        [norm, *cross, *up, *down],
        [
            ((rows, width), BF16, 0),
            ((rows, width), F32, 0),
            ((parts, rows, part), BF16, 1),
        ],
        [
            ((parts, width, part), BF16),
            ((parts, width, units), BF16),
            ((parts, units, width), BF16),
            ((3, 2, width), F32),
        ],
        6 * rows * width * width + 12 * rows * width * units * parts,
    )


def decoder_middle_back(first, mix, query_grad, second_grad, norm, out, cross, block):
    rows, width = first.shape
    parts, part = len(out), out[0].shape[0]

    def body(ins, outs, totals):
        first_ref, mix_ref, query_grad_ref, second_grad_ref, norm_ref = ins[:5]
        wo, wc = (ins[5 + i * parts : 5 + (i + 1) * parts] for i in range(2))
        first_grad_ref, mix_grad_ref = outs
        query_total, out_total, norm_total = totals
        unit, inv = standardize(first_ref[...])
        low = affine(unit, norm_ref, 0).astype(BF16)
        grad = second_grad_ref[...]
        for k in range(parts):
            query_total[k] += dot_tn(low, query_grad_ref[k])
            grad += dot_nt(query_grad_ref[k], wc[k][0])
        grad = norm_back(unit, inv, norm_ref, 0, grad, norm_total)
        first_grad_ref[...] = grad
        grad_low = grad.astype(BF16)
        for k in range(parts):
            out_total[k] += dot_tn(mix_ref[k], grad_low)
            mix_grad_ref[k] = dot_nt(grad_low, wo[k][...]).astype(BF16)

    return row_call(
        body,
        "decoder_middle_back",
        rows,
        block,
        [(first, 0), (mix, 1), (query_grad, 1), (second_grad, 0)],
        [norm, *out, *cross],
        [((rows, width), F32, 0), ((parts, rows, part), BF16, 1)],
        [
            ((parts, width, part), BF16),
            ((parts, part, width), BF16),
            ((3, 2, width), F32),
        ],
        8 * rows * width * width,
    )


def encoder_back(first, third, mix, memory_grads, cotangent, norm, out, up, down, cross, block):
    rows, width = first.shape
    parts, part, units = len(out), out[0].shape[0], up[0].shape[1]
    pieces = len(memory_grads)

    def body(ins, outs, totals):
        first_ref, third_ref, mix_ref, cot_ref = ins[:4]
        memory_refs, norm_ref = ins[4 : 4 + pieces], ins[4 + pieces]
        rest = ins[5 + pieces :]
        wo, wu, wd, wc = (rest[i * parts : (i + 1) * parts] for i in range(4))
        first_grad_ref, mix_grad_ref = outs
        cross_total, out_total, up_total, down_total, norm_total = totals
        unit, inv = standardize(third_ref[...])
        low = affine(unit, norm_ref, 1).astype(BF16)
        grad = cot_ref[...].astype(F32)
        for i in range(2):
            for k in range(parts):
                memory = memory_refs[0][i, k].astype(F32)
                for ref in memory_refs[1:]:
                    memory += ref[i, k].astype(F32)
                memory = memory.astype(BF16)
                cross_total[k, i] += dot_tn(low, memory)
                grad += dot_nt(memory, wc[k][i])
        grad = norm_back(unit, inv, norm_ref, 1, grad, norm_total)
        unit, inv = standardize(first_ref[...])
        low = affine(unit, norm_ref, 0).astype(BF16)
        grad += ffn_back(low, grad.astype(BF16), wu, wd, up_total, down_total, parts)
        grad = norm_back(unit, inv, norm_ref, 0, grad, norm_total)
        first_grad_ref[...] = grad
        grad_low = grad.astype(BF16)
        for k in range(parts):
            out_total[k] += dot_tn(mix_ref[k], grad_low)
            mix_grad_ref[k] = dot_nt(grad_low, wo[k][...]).astype(BF16)

    return row_call(
        body,
        "encoder_back",
        rows,
        block,
        [(first, 0), (third, 0), (mix, 1), (cotangent, 0)] + [(m, 2) for m in memory_grads],
        [norm, *out, *up, *down, *cross],
        [((rows, width), F32, 0), ((parts, rows, part), BF16, 1)],
        [
            ((parts, 2, width, part), BF16),
            ((parts, part, width), BF16),
            ((parts, width, units), BF16),
            ((parts, units, width), BF16),
            ((3, 2, width), F32),
        ],
        12 * rows * width * width + 10 * rows * width * units * parts,
    )


def input_back(x, first_grad, query_grad, key_grads, norm, weights, with_norm, block):
    rows, width = x.shape
    parts, part = len(weights), weights[0].shape[-1]
    pieces = len(key_grads)

    def body(ins, outs, totals):
        x_ref, first_grad_ref, query_grad_ref = ins[:3]
        key_refs, norm_ref, w = ins[3 : 3 + pieces], ins[3 + pieces], ins[4 + pieces :]
        (grad_ref,) = outs
        qkv_total, norm_total = totals
        low = x_ref[...]
        if with_norm:
            unit, inv = standardize(low.astype(F32))
            low = affine(unit, norm_ref, 2).astype(BF16)
        grad = first_grad_ref[...]
        for k in range(parts):
            for i in range(3):
                if i == 0:
                    member = query_grad_ref[k]
                else:
                    member = key_refs[0][i - 1, k].astype(F32)
                    for ref in key_refs[1:]:
                        member += ref[i - 1, k].astype(F32)
                    member = member.astype(BF16)
                qkv_total[k, i] += dot_tn(low, member)
                grad += dot_nt(member, w[k][i])
        if with_norm:
            grad = norm_back(unit, inv, norm_ref, 2, grad, norm_total)
        grad_ref[...] = grad.astype(BF16)

    return row_call(
        body,
        "input_back",
        rows,
        block,
        [(x, 0), (first_grad, 0), (query_grad, 1)] + [(g, 2) for g in key_grads],
        [norm, *weights],
        [((rows, width), BF16, 0)],
        [((parts, 3, width, part), BF16), ((3, 2, width), F32)],
        12 * rows * width * width,
    )


def widen_keys(span_ref, kv_refs, key_e, key_o, value_e, value_o, rows):
    lane = lax.broadcasted_iota(jnp.int32, (rows, PAIR), 1)
    place = lax.broadcasted_iota(jnp.int32, (rows, PAIR), 0)
    low = lane < HALF
    for g, kv_ref in enumerate(kv_refs):
        spot = place + span_ref[2 + g]
        live = (spot >= span_ref[0]) & (spot < span_ref[1])
        bias = jnp.where(live, 0.0, MASKED)
        keys, values = kv_ref[0].astype(F32), kv_ref[1].astype(F32)
        own = pl.ds(g * rows, rows)
        key_e[own, :] = jnp.where(low, keys, jnp.where(lane == HALF, bias, 1.0)).astype(BF16)
        key_o[own, :] = jnp.where(low, jnp.where(lane == 0, bias, 1.0), keys).astype(BF16)
        value_e[own, :] = jnp.where(low, values, 1.0).astype(BF16)
        value_o[own, :] = jnp.where(low, 1.0, values).astype(BF16)


def attend(query, kv_pieces, span, block):
    parts, rows, part = query.shape
    per_part = part // PAIR
    pairs = parts * per_part
    pieces = len(kv_pieces)
    keys = rows * pieces

    def kernel(span_ref, q_ref, *refs):
        kv_refs = refs[:pieces]
        out_ref, lse_ref, key_e, key_o, value_e, value_o = refs[pieces:]

        @pl.when(pl.program_id(1) == 0)
        def _():
            widen_keys(span_ref, kv_refs, key_e, key_o, value_e, value_o, rows)

        lane = lax.broadcasted_iota(jnp.int32, (block, PAIR), 1)
        low = lane < HALF
        query = q_ref[...].astype(F32)
        query_e = jnp.where(low, query, jnp.where(lane == HALF, 1.0, 0.0)).astype(BF16)
        query_o = jnp.where(low, jnp.where(lane == 0, 1.0, 0.0), query).astype(BF16)
        tops, sums = [], []
        for q, k, v in ((query_e, key_e, value_e), (query_o, key_o, value_o)):
            scores = dot_nt(q, k[...])
            top = jnp.max(scores, axis=1, keepdims=True)
            tops.append(top)
            sums.append(dot_nn(jnp.exp2(scores - top).astype(BF16), v[...]))
        top = jnp.where(low, tops[1], tops[0])
        weight = jnp.where(low, sums[1], sums[0])
        lse_ref[...] = top + LOG2E * jnp.log(weight)
        mixed = jnp.where(low, sums[0], sums[1])
        out_ref[...] = (mixed / pltpu.roll(weight, HALF, 1)).astype(BF16)

    return pl.pallas_call(
        kernel,
        grid_spec=pltpu.PrefetchScalarGridSpec(
            num_scalar_prefetch=1,
            grid=(pairs, rows // block),
            in_specs=[
                pl.BlockSpec(
                    (None, block, PAIR), lambda i, j, _: (i // per_part, j, i % per_part)
                )
            ]
            + [
                pl.BlockSpec(
                    (2, None, rows, PAIR), lambda i, j, _: (0, i // per_part, 0, i % per_part)
                )
            ]
            * pieces,
            out_specs=[
                pl.BlockSpec(
                    (None, block, PAIR), lambda i, j, _: (i // per_part, j, i % per_part)
                ),
                pl.BlockSpec((block, PAIR), lambda i, j, _: (j, i)),
            ],
            scratch_shapes=[pltpu.VMEM((keys, PAIR), BF16)] * 4,
        ),
        out_shape=[
            jax.ShapeDtypeStruct(query.shape, BF16),
            jax.ShapeDtypeStruct((rows, pairs * PAIR), F32),
        ],
        compiler_params=pltpu.CompilerParams(vmem_limit_bytes=VMEM),
        cost_estimate=pl.CostEstimate(
            flops=16 * rows * keys * pairs * PAIR,
            bytes_accessed=8 * rows * pairs * PAIR * pieces,
            transcendentals=0,
        ),
        name="attend",
    )(span, query, *kv_pieces)


def attend_back(query, kv_pieces, mix, mix_grad, lse, span, block, chunk):
    parts, rows, part = query.shape
    per_part = part // PAIR
    pairs = parts * per_part
    pieces = len(kv_pieces)
    keys = rows * pieces
    scale = 1.0 / math.sqrt(HALF)

    def kernel(span_ref, q_ref, mix_ref, grad_ref, lse_ref, *refs):
        kv_refs = refs[:pieces]
        dq_ref, dkv_refs = refs[pieces], refs[pieces + 1 : 2 * pieces + 1]
        key_e, key_o, value_e, value_o, key_t, key_total, value_total = refs[2 * pieces + 1 :]

        @pl.when(pl.program_id(1) == 0)
        def _():
            widen_keys(span_ref, kv_refs, key_e, key_o, value_e, value_o, rows)
            for g, kv_ref in enumerate(kv_refs):
                key_t[:, pl.ds(g * rows, rows)] = kv_ref[0].T
            key_total[...] = jnp.zeros_like(key_total)
            value_total[...] = jnp.zeros_like(value_total)

        lane = lax.broadcasted_iota(jnp.int32, (block, PAIR), 1)
        low = lane < HALF
        query, grad = q_ref[...].astype(F32), grad_ref[...].astype(F32)
        product = mix_ref[...].astype(F32) * grad
        inner = jnp.where(
            low,
            jnp.sum(jnp.where(low, 0.0, product), axis=1, keepdims=True),
            jnp.sum(jnp.where(low, product, 0.0), axis=1, keepdims=True),
        )

        def three(value, shift):
            high = value.astype(BF16).astype(F32)
            rest = value - high
            mid = rest.astype(BF16).astype(F32)
            spot = lane % HALF - shift
            return jnp.where(
                spot == 0,
                high,
                jnp.where(spot == 1, mid, jnp.where(spot == 2, rest - mid, 0.0)),
            )

        lse = three(-lse_ref[...], 1) + jnp.where(lane % HALF == 0, 1.0, 0.0)
        inner = three(-inner, 0)
        heads = []
        for own, key, value in ((low, key_e, value_e), (~low, key_o, value_o)):
            heads.append(
                (
                    key,
                    value,
                    jnp.where(own, query, lse).astype(BF16),
                    jnp.where(own, grad, inner).astype(BF16),
                    jnp.where(own, query, 0.0).astype(BF16),
                    jnp.where(own, grad, 0.0).astype(BF16),
                )
            )
        dq = [None, None]
        for c in range(keys // chunk):
            span_c = pl.ds(c * chunk, chunk)
            dk, dv = None, None
            for h, (key, value, q_wide, g_wide, q_own, g_own) in enumerate(heads):
                probs = jnp.exp2(dot_nt(key[span_c, :], q_wide))
                dscores = (probs * dot_nt(value[span_c, :], g_wide)).astype(BF16)
                step_v = dot_nn(probs.astype(BF16), g_own)
                step_k = dot_nn(dscores, q_own)
                step_q = dot_nn(key_t[pl.ds(h * HALF, HALF), span_c], dscores)
                dv = step_v if dv is None else dv + step_v
                dk = step_k if dk is None else dk + step_k
                dq[h] = step_q if dq[h] is None else dq[h] + step_q
            key_total[span_c, :] += dk
            value_total[span_c, :] += dv
        dq_ref[...] = (jnp.concatenate(dq, axis=0).T * scale).astype(BF16)

        @pl.when(pl.program_id(1) == pl.num_programs(1) - 1)
        def _():
            for g, ref in enumerate(dkv_refs):
                own = pl.ds(g * rows, rows)
                ref[0] = (key_total[own, :] * (1.0 / LOG2E)).astype(BF16)
                ref[1] = value_total[own, :].astype(BF16)

    query_spec = pl.BlockSpec(
        (None, block, PAIR), lambda i, j, _: (i // per_part, j, i % per_part)
    )
    kv_spec = pl.BlockSpec(
        (2, None, rows, PAIR), lambda i, j, _: (0, i // per_part, 0, i % per_part)
    )
    out = pl.pallas_call(
        kernel,
        grid_spec=pltpu.PrefetchScalarGridSpec(
            num_scalar_prefetch=1,
            grid=(pairs, rows // block),
            in_specs=[query_spec] * 3
            + [pl.BlockSpec((block, PAIR), lambda i, j, _: (j, i))]
            + [kv_spec] * pieces,
            out_specs=[query_spec] + [kv_spec] * pieces,
            scratch_shapes=[pltpu.VMEM((keys, PAIR), BF16)] * 4
            + [pltpu.VMEM((PAIR, keys), BF16)]
            + [pltpu.VMEM((keys, PAIR), F32)] * 2,
        ),
        out_shape=[jax.ShapeDtypeStruct(query.shape, BF16)]
        + [jax.ShapeDtypeStruct((2, parts, rows, part), BF16)] * pieces,
        compiler_params=pltpu.CompilerParams(vmem_limit_bytes=VMEM),
        cost_estimate=pl.CostEstimate(
            flops=40 * rows * keys * pairs * PAIR,
            bytes_accessed=16 * rows * pairs * PAIR * pieces,
            transcendentals=0,
        ),
        name="attend_back",
    )(span, query, mix, mix_grad, lse, *kv_pieces)
    return out[0], out[1:]


def local(tokens, lengths, self_qkv, self_out, cross_proj, ffn_up, ffn_down, norms, cotangent):
    section = lax.axis_index("section")
    tensor = lax.axis_index("tensor")
    tensors = lax.axis_size("tensor")
    _, row_count, rows, width = tokens.shape
    assert row_count == 2 and tensors % row_count == 0
    spread = tensors // row_count
    pieces = 2 * spread
    axes = ("section", "tensor")
    is_first = section == 0
    own_row = tensor // spread
    place = section * spread + tensor % spread

    def device(row, spot):
        return (spot // spread) * tensors + row * spread + spot % spread

    def each():
        return [(s, t) for s in range(2) for t in range(tensors)]

    straight = [(s * tensors + t, device(s, t)) for s, t in each()]
    turned = [(s * tensors + t, device(1 - s, t)) for s, t in each()]

    def bring(shares):
        stays = lax.dynamic_index_in_dim(shares, section, 0, keepdims=False)
        moves = lax.dynamic_index_in_dim(shares, 1 - section, 0, keepdims=False)
        one = lax.ppermute(stays, axes, straight)
        two = lax.ppermute(moves, axes, turned)
        return jnp.where(own_row == 0, one, two), jnp.where(own_row == 0, two, one)

    def take_back(source, target):
        one = jnp.where(own_row == 0, source, target)
        two = jnp.where(own_row == 0, target, source)
        one = lax.ppermute(one, axes, [(b, a) for a, b in straight])
        two = lax.ppermute(two, axes, [(b, a) for a, b in turned])
        return jnp.stack([jnp.where(is_first, one, two), jnp.where(is_first, two, one)])

    def rotate(value, by):
        pairs = [
            (device(r, p), device(r, (p + by) % pieces))
            for r in range(row_count)
            for p in range(pieces)
        ]
        return lax.ppermute(value, axes, pairs)

    def pieces_of(value):
        return [value] + [rotate(value, by) for by in range(1, pieces)]

    def pieces_home(values):
        return [values[0]] + [rotate(values[by], -by) for by in range(1, pieces)]

    def swap_sections(value):
        return lax.ppermute(value, "section", [(0, 1), (1, 0)])

    def both_sides(weight, dim):
        if spread == 1:
            other = lax.ppermute(weight, "tensor", [(t, 1 - t) for t in range(tensors)])
            parts = [weight, other]
        else:
            parts = [lax.all_gather(weight, "tensor", axis=dim, tiled=True)]
        swapped = [swap_sections(part) for part in parts]
        pairs = list(zip(parts, swapped))
        return (
            [jnp.where(is_first, mine, theirs) for mine, theirs in pairs],
            [jnp.where(is_first, theirs, mine) for mine, theirs in pairs],
        )

    def home(source_grad, target_grad, dim):
        keep = jnp.where(is_first, source_grad, target_grad).astype(F32)
        sent = swap_sections(jnp.where(is_first, target_grad, source_grad))
        total = (keep + sent.astype(F32)).astype(BF16)
        if spread == 1:
            other = lax.ppermute(total[1], "tensor", [(t, 1 - t) for t in range(tensors)])
            total = (total[0].astype(F32) + other.astype(F32)).astype(BF16)
        else:
            total = lax.psum_scatter(total[0], "tensor", scatter_dimension=dim, tiled=True)
        return total

    def span_of(query_side, key_side):
        own = lax.dynamic_index_in_dim(lengths, own_row, 1, keepdims=False)
        asks, answers = own[query_side], own[key_side]
        paired = asks[1] > 0
        second = paired & (place * rows >= asks[0])
        begin = jnp.where(second, answers[0], 0)
        end = jnp.where(second | ~paired, answers[0] + answers[1], answers[0])
        offsets = [(place - by) % pieces * rows for by in range(pieces)]
        return jnp.stack([begin, end, *offsets]).astype(jnp.int32)

    block = min(256, rows)
    query_block = min(256, rows)
    chunk = 512

    source, target = bring(tokens[0])
    source_norm, target_norm = (
        jnp.where(is_first, a, b)
        for a, b in (lambda own, other: ((own, other), (other, own)))(
            norms[0], swap_sections(norms[0])
        )
    )
    source_qkv, target_qkv = both_sides(self_qkv[0], 2)
    source_out, target_out = both_sides(self_out[0], 0)
    source_up, target_up = both_sides(ffn_up[0], 1)
    source_down, target_down = both_sides(ffn_down[0], 0)
    source_cross, target_cross = both_sides(cross_proj[0], 2)
    source_cot, target_cot = bring(cotangent[0])
    source_span, target_span, cross_span = span_of(0, 0), span_of(1, 1), span_of(1, 0)

    enc_q, enc_kv = project_qkv(source, source_norm, source_qkv, True, block)
    enc_kv = pieces_of(enc_kv)
    dec_q, dec_kv = project_qkv(target, target_norm, target_qkv, False, block)
    dec_kv = pieces_of(dec_kv)
    enc_mix, enc_lse = attend(enc_q, enc_kv, source_span, query_block)
    encoded, memory, enc_first, enc_third = encoder_forward(
        source, enc_mix, source_norm, source_out, source_up, source_down, source_cross, block
    )
    memory = pieces_of(memory)
    dec_mix, dec_lse = attend(dec_q, dec_kv, target_span, query_block)
    cross_q, dec_first = decoder_middle(
        target, dec_mix, target_norm, target_out, target_cross, block
    )
    cross_mix, cross_lse = attend(cross_q, memory, cross_span, query_block)
    decoded, second_grad, cross_mix_grad, cross_out_grad, dec_up, dec_down, dec_norm = decoder_turn(
        dec_first, cross_mix, target_cot, target_norm, target_cross, target_up, target_down, block
    )
    result = take_back(encoded, decoded)
    cross_q_grad, memory_grads = attend_back(
        cross_q, memory, cross_mix, cross_mix_grad, cross_lse, cross_span, query_block, chunk
    )
    memory_grads = pieces_home(memory_grads)
    dec_first_grad, dec_mix_grad, cross_query_grad, dec_out, step = decoder_middle_back(
        dec_first,
        dec_mix,
        cross_q_grad,
        second_grad,
        target_norm,
        target_out,
        target_cross,
        block,
    )
    dec_norm += step
    enc_first_grad, enc_mix_grad, enc_cross, enc_out, enc_up, enc_down, enc_norm = encoder_back(
        enc_first,
        enc_third,
        enc_mix,
        memory_grads,
        source_cot,
        source_norm,
        source_out,
        source_up,
        source_down,
        source_cross,
        block,
    )
    dec_cross = jnp.stack([cross_query_grad, cross_out_grad], axis=1)
    up_grad, down_grad = home(enc_up, dec_up, 1), home(enc_down, dec_down, 0)
    out_grad, cross_grad = home(enc_out, dec_out, 0), home(enc_cross, dec_cross, 2)
    dec_q_grad, dec_kv_grads = attend_back(
        dec_q, dec_kv, dec_mix, dec_mix_grad, dec_lse, target_span, query_block, chunk
    )
    dec_kv_grads = pieces_home(dec_kv_grads)
    enc_q_grad, enc_kv_grads = attend_back(
        enc_q, enc_kv, enc_mix, enc_mix_grad, enc_lse, source_span, query_block, chunk
    )
    enc_kv_grads = pieces_home(enc_kv_grads)
    target_grad, dec_qkv, _ = input_back(
        target, dec_first_grad, dec_q_grad, dec_kv_grads, target_norm, target_qkv, False, block
    )
    source_grad, enc_qkv, step = input_back(
        source, enc_first_grad, enc_q_grad, enc_kv_grads, source_norm, source_qkv, True, block
    )
    enc_norm += step
    token_grad = take_back(source_grad, target_grad).astype(F32)
    qkv_grad = home(enc_qkv, dec_qkv, 2)
    norm_total = lax.psum(jnp.stack([enc_norm, dec_norm]), ("section", "dp", "tensor"))
    norm_grad = lax.dynamic_index_in_dim(norm_total, section, 0, keepdims=False)
    summed = [
        lax.psum(grad, "dp").astype(F32)
        for grad in (qkv_grad, out_grad, cross_grad, up_grad, down_grad)
    ]
    return (
        result[None],
        token_grad[None],
        summed[0][None],
        summed[1][None],
        summed[2][None],
        summed[3][None],
        summed[4][None],
        norm_grad[None],
    )


def solution(mesh):
    placed = (
        P("section", "dp", "tensor", None),
        P(None, "dp", None),
        P("section", None, None, "tensor"),
        P("section", "tensor", None),
        P("section", None, None, "tensor"),
        P("section", None, "tensor"),
        P("section", "tensor", None),
        P("section", None, None, None),
        P("section", "dp", "tensor", None),
    )
    return jax.shard_map(
        local,
        mesh=mesh,
        in_specs=placed,
        out_specs=(
            P("section", "dp", "tensor", None),
            P("section", "dp", "tensor", None),
            P("section", None, None, "tensor"),
            P("section", "tensor", None),
            P("section", None, None, "tensor"),
            P("section", None, "tensor"),
            P("section", "tensor", None),
            P("section", None, None, None),
        ),
        check_vma=False,
    )
```

time: 4090 us -> 789 us (0.19)
  waiting for transfers between devices: 2150 us -> 188 us
  matrix products: 1130 us -> 0 us
  Pallas kernels: 0 us -> 400 us
  other arithmetic: 388 us -> 65 us
  local copies, waits for them, and re-layouts: 283 us -> 12.7 us
    reduce_scatter x21 -> x0, waiting for transfers between devices: 971 us -> none  [the longest x6 418 us: sum_rows(): lax.psum_scatter(partial_rows.astype(jnp.bfloat16), 'tensor', scatter_dim...]
    dot_general x151 -> x0, matrix products: 873 us -> none  [the longest x12 162 us: one_block(): jnp.einsum('qhd,khd->hqk', grad_block, value_heads, preferred_element_typ...]
    ppermute x4 -> x40, waiting for transfers between devices: 607 us -> 132 us  [the longest x5 60.3 us: home(): lax.ppermute(total[1], 'tensor', [(t, 1 - t) for t in range(tensors)])]
    all_gather x21 -> x0, waiting for transfers between devices: 441 us -> none  [the longest x9 188 us: gather_rows(): return lax.all_gather(share_rows, 'tensor', axis=0, tiled=True)]
    pallas_call x0 -> x15, Pallas kernels: none -> 400 us  [the longest x3 188 us: attend_back(): pl.pallas_call(kernel, grid_spec=pltpu.PrefetchScalarGridSpec(num_scalar_...]
    sub x24 -> x0, matrix products: 254 us -> none  [one_block(): exponent = jnp.exp(scores - row_max)]
    convert_element_type x35 -> x6, other arithmetic: 162 us -> 12.7 us  [the longest x5 10.4 us: home(): total = (keep + sent.astype(F32)).astype(BF16)]
    unnamed x452 -> x72, local copies, waits for them, and re-layouts: 100 us -> 5.31 us
  transfers between devices with their start and end apart: 47 -> 41, of which waited for: 38 -> 9; matrix products, arithmetic and copies ran while one was open for 28% -> 8% of each run, Pallas kernels for 0% -> 35%
where the time goes in v1:
time: 789 us; the launch traced here: 784 us
  Pallas kernels  400 us (51%)
  waiting for transfers between devices  188 us (24%)
  other arithmetic  65 us (8%)
  blocking collectives  56 us (7%)
  starting transfers between devices  38.8 us (5%)
  between operations  23.7 us (3%)
  local copies, waits for them, and re-layouts  12.7 us (2%)
    pallas_call x3, Pallas kernels, attend_back(): pl.pallas_call(kernel, grid_spec=pltpu.PrefetchScalarGridSpec(num_scalar_...  188 us
    pallas_call x9, Pallas kernels, row_call(): pl.pallas_call(kernel, grid=(rows // block,), in_specs=[blocked(a.shape,...  113 us
    pallas_call x3, Pallas kernels, attend(): pl.pallas_call(kernel, grid_spec=pltpu.PrefetchScalarGridSpec(num_scalar_...  97.8 us
    ppermute x5, waiting for transfers between devices, home(): lax.ppermute(total[1], 'tensor', [(t, 1 - t) for t in range(tensors)])  60.3 us
    psum x1, blocking collectives, local(): lax.psum(jnp.stack([enc_norm, dec_norm]), ('section', 'dp', 'tensor'))  56 us
    psum x1, waiting for transfers between devices, local(): lax.psum(grad, 'dp').astype(F32)  55.7 us
    ppermute x5, waiting for transfers between devices, both_sides(): other = lax.ppermute(weight, 'tensor', [(t, 1 - t) for t in range(tensors)])  50.3 us
    ppermute x2, waiting for transfers between devices, take_back(): two = lax.ppermute(two, axes, [(b, a) for a, b in turned])  21.7 us
  transfers between devices with their start and end apart: 41, of which 9 were waited for; matrix products, arithmetic and copies ran while one was open for 8% of the time, Pallas kernels for 35%

profile of v1, /device:TPU:0, one launch (start us, length us, event | category | flops | bytes accessed | tf_op | source)
XLA Modules:
  0.0 783.9 jit_solution(9920814030244678319)
XLA Ops:
  7.2 3.0 collective-permute-start.4
  10.8 3.1 dynamic-slice_bitcast_fusion.3
  13.9 9.5 %collective-permute-start = (bf16[1024,512]{1,0:T(8,128)(2,1)}, bf16[1024,512]{1,0:T(8,128)(2,1)}, u32[]{:S(2)}, u32[]{:S(2)}) collective-permute-start(bf16[1024,512]{1,0:T(8,128)(2,1)} %get-tuple-element.133), channel_id=1, source_target_pairs={{0,0},{1,16},{16,1},{17,17},{2,2},{3,18},{18,3},{19,19},{4,4},{5,2... | collective-permute-start | bytes 3145736 | tf_op jit(solution)/shard_map/ppermute | solution.py:656
  37.6 17.8 %collective-permute-done.8 = bf16[256,512]{1,0:T(8,128)(2,1)S(1)} collective-permute-done((bf16[256,512]{1,0:T(8,128)(2,1)S(1)}, bf16[256,512]{1,0:T(8,128)(2,1)S(1)}, u32[]{:S(2)}, u32[]{:S(2)}) %collective-permute-start.8) | collective-permute-done | bytes 262176 | tf_op jit(solution)/shard_map/ppermute | solution.py:686
  55.3 2.5 collective-permute-start.17
  57.8 2.4 broadcast_select_fusion.23
  60.9 2.8 broadcast_select_fusion.15
  63.7 1.8 collective-permute-start.14
  65.6 2.4 broadcast_select_fusion.22
  68.0 6.0 project_qkv.2
  74.5 2.2 broadcast_select_fusion.28
  76.7 16.6 %collective-permute-done.11 = bf16[512,1024]{1,0:T(8,128)(2,1)} collective-permute-done((bf16[512,1024]{1,0:T(8,128)(2,1)S(1)}, bf16[512,1024]{1,0:T(8,128)(2,1)}, u32[]{:S(2)}, u32[]{:S(2)}) %collective-permute-start.11) | collective-permute-done | bytes 1048608 | tf_op jit(solution)/shard_map/ppermute | solution.py:686
  94.7 2.7 broadcast_select_fusion.5
  97.4 2.0 collective-permute-start.22
  99.5 15.9 %collective-permute-done.14 = bf16[1024,512]{1,0:T(8,128)(2,1)} collective-permute-done((bf16[1024,512]{1,0:T(8,128)(2,1)S(1)}, bf16[1024,512]{1,0:T(8,128)(2,1)}, u32[]{:S(2)}, u32[]{:S(2)}) %collective-permute-start.14) | collective-permute-done | bytes 1048608 | tf_op jit(solution)/shard_map/ppermute | solution.py:686
  116.4 2.6 collective-permute-start.21
  119.0 1.5 broadcast_select_fusion.17
  120.5 5.4 project_qkv.3
  126.0 3.0 broadcast_select_fusion.4
  128.9 3.0 broadcast_select_fusion.16
  131.9 32.6 %attend.3 = (bf16[2,1024,256]{2,1,0:T(8,128)(2,1)}, f32[1024,512]{1,0:T(8,128)}) custom-call(s32[4]{0:T(128)} %add_add_fusion.span_ref, bf16[2,1024,256]{2,1,0:T(8,128)(2,1)} %get-tuple-element.57.q_ref, bf16[2,2,1024,256]{3,2,1,0:T(8,128)(2,1)} %get-tuple-element.58.refs_0_, bf16[2,2,1024,256]{3,2,1,0:T(8,128)(2,1)} %collective-permute-done.6.refs_1_), custom_call_target="tpu_custom_call" | custom-call | flops 17179869184 | bytes 8388608 | tf_op jit(solution)/shard_map/attend/pallas_call | solution.py:481
  164.5 13.7 %encoder_forward.1 = (bf16[1024,512]{1,0:T(8,128)(2,1)}, bf16[2,2,1024,256]{3,2,1,0:T(8,128)(2,1)}, f32[1024,512]{1,0:T(8,128)}, f32[1024,512]{1,0:T(8,128)}) custom-call(bf16[1024,512]{1,0:T(8,128)(2,1)} %get-tuple-element.131.refs_0_, bf16[2,1024,256]{2,1,0:T(8,128)(2,1)} %get-tuple-element.59.refs_1_.refs_2_.mix_ref, ...), custom_call_target="tpu_custom_call" | custom-call | flops 5905580032 | bytes 7876608 | tf_op jit(solution)/shard_map/encoder_forward/pallas_call | solution.py:102
  179.4 2.7 broadcast_select_fusion.10
  182.1 32.6 %attend.4 = (bf16[2,1024,256]{2,1,0:T(8,128)(2,1)}, f32[1024,512]{1,0:T(8,128)}) custom-call(s32[4]{0:T(128)} %add_add_fusion.1.span_ref, bf16[2,1024,256]{2,1,0:T(8,128)(2,1)} %get-tuple-element.61.q_ref, bf16[2,2,1024,256]{3,2,1,0:T(8,128)(2,1)} %get-tuple-element.62.refs_0_, bf16[2,2,1024,256]{3,2,1,0:T(8,128)(2,1)} %collective-permute-done.19.refs_1_), custom_call_target="tpu_custom_call" | custom-call | flops 17179869184 | bytes 8388608 | tf_op jit(solution)/shard_map/attend/pallas_call | solution.py:481
  214.7 6.0 decoder_middle.1
  220.7 32.6 %attend.5 = (bf16[2,1024,256]{2,1,0:T(8,128)(2,1)}, f32[1024,512]{1,0:T(8,128)}) custom-call(s32[4]{0:T(128)} %add_add_fusion.2.span_ref, bf16[2,1024,256]{2,1,0:T(8,128)(2,1)} %get-tuple-element.65.q_ref, bf16[2,2,1024,256]{3,2,1,0:T(8,128)(2,1)} %get-tuple-element.66.refs_0_, bf16[2,2,1024,256]{3,2,1,0:T(8,128)(2,1)} %collective-permute-done.20.refs_1_), custom_call_target="tpu_custom_call" | custom-call | flops 17179869184 | bytes 8388608 | tf_op jit(solution)/shard_map/attend/pallas_call | solution.py:481
  253.3 27.5 %decoder_turn.1 = (bf16[1024,512]{1,0:T(8,128)(2,1)}, f32[1024,512]{1,0:T(8,128)}, bf16[2,1024,256]{2,1,0:T(8,128)(2,1)}, bf16[2,512,256]{2,1,0:T(8,128)(2,1)}, ...) custom-call(f32[1024,512]{1,0:T(8,128)} %get-tuple-element.64.refs_0_, ...), custom_call_target="tpu_custom_call" | custom-call | flops 14495514624 | bytes 9449472 | tf_op jit(solution)/shard_map/decoder_turn/pallas_call | solution.py:102
  280.9 62.7 %attend_back.3 = (bf16[2,1024,256]{2,1,0:T(8,128)(2,1)}, bf16[2,2,1024,256]{3,2,1,0:T(8,128)(2,1)}, bf16[2,2,1024,256]{3,2,1,0:T(8,128)(2,1)}) custom-call(s32[4]{0:T(128)} %add_add_fusion.2.span_ref, bf16[2,1024,256]{2,1,0:T(8,128)(2,1)} %get-tuple-element.65.q_ref, bf16[2,1024,256]{2,1,0:T(8,128)(2,1)} %get-tuple-element.67.refs_1_.mix_ref, ...), custom_call_target="tpu_custom_call" | custom-call | flops 42949672960 | bytes 16777216 | tf_op jit(solution)/shard_map/attend_back/pallas_call | solution.py:605
  343.6 9.1 %decoder_middle_back.1 = (f32[1024,512]{1,0:T(8,128)}, bf16[2,1024,256]{2,1,0:T(8,128)(2,1)}, bf16[2,512,256]{2,1,0:T(8,128)(2,1)}, bf16[2,256,512]{2,1,0:T(8,128)(2,1)}, f32[3,2,512]{2,1,0:T(2,128)}) custom-call(f32[1024,512]{1,0:T(8,128)} %get-tuple-element.64.refs_0_, bf16[2,1024,256]{2,1,0:T(8,128)(2,1)} %get-tuple-element.63.refs_1_.mix_ref, ...), custom_call_target="tpu_custom_call" | custom-call | flops 2147483648 | bytes 7876608 | tf_op jit(solution)/shard_map/decoder_middle_back/pallas_call | solution.py:102
  352.7 62.8 %attend_back.5 = (bf16[2,1024,256]{2,1,0:T(8,128)(2,1)}, bf16[2,2,1024,256]{3,2,1,0:T(8,128)(2,1)}, bf16[2,2,1024,256]{3,2,1,0:T(8,128)(2,1)}) custom-call(s32[4]{0:T(128)} %add_add_fusion.1.span_ref, bf16[2,1024,256]{2,1,0:T(8,128)(2,1)} %get-tuple-element.61.q_ref, bf16[2,1024,256]{2,1,0:T(8,128)(2,1)} %get-tuple-element.63.refs_1_.mix_ref, ...), custom_call_target="tpu_custom_call" | custom-call | flops 42949672960 | bytes 16777216 | tf_op jit(solution)/shard_map/attend_back/pallas_call | solution.py:605
  416.0 1.3 copy-done.35
  417.3 27.5 %encoder_back.1 = (f32[1024,512]{1,0:T(8,128)}, bf16[2,1024,256]{2,1,0:T(8,128)(2,1)}, bf16[2,2,512,256]{3,2,1,0:T(8,128)(2,1)}, bf16[2,256,512]{2,1,0:T(8,128)(...) custom-call(f32[1024,512]{1,0:T(8,128)} %get-tuple-element.69.refs_0_, ...), custom_call_target="tpu_custom_call" | custom-call | flops 13958643712 | bytes 16265216 | tf_op jit(solution)/shard_map/encoder_back/pallas_call | solution.py:102
  445.7 1.2 collective-permute-start.32
  446.9 1.1 broadcast_select_fusion.3
  448.0 62.9 %attend_back.4 = (bf16[2,1024,256]{2,1,0:T(8,128)(2,1)}, bf16[2,2,1024,256]{3,2,1,0:T(8,128)(2,1)}, bf16[2,2,1024,256]{3,2,1,0:T(8,128)(2,1)}) custom-call(s32[4]{0:T(128)} %add_add_fusion.span_ref, bf16[2,1024,256]{2,1,0:T(8,128)(2,1)} %get-tuple-element.57.q_ref, bf16[2,1024,256]{2,1,0:T(8,128)(2,1)} %get-tuple-element.59.refs_1_.refs_2_.mix_ref, ...), custom_call_target="tpu_custom_call" | custom-call | flops 42949672960 | bytes 16777216 | tf_op jit(solution)/shard_map/attend_back/pallas_call | solution.py:605
  511.5 3.3 broadcast_select_fusion
  514.8 1.5 broadcast_select_fusion.1
  517.6 1.2 add_convert_fusion.4
  520.1 8.6 %input_back.3 = (bf16[1024,512]{1,0:T(8,128)(2,1)}, bf16[2,3,512,256]{3,2,1,0:T(8,128)(2,1)}, f32[3,2,512]{2,1,0:T(2,128)}) custom-call(bf16[1024,512]{1,0:T(8,128)(2,1)} %get-tuple-element.132.refs_0_, f32[1024,512]{1,0:T(8,128)} %get-tuple-element.84.refs_1_, bf16[2,1024,256]{2,1,0:T(8,128)(2,1)} %get-tuple-element.87.refs_2_, ...), custom_call_target="tpu_custom_call" | custom-call | flops 3221225472 | bytes 9973760 | tf_op jit(solution)/shard_map/input_back/pallas_call | solution.py:102
  529.5 2.9 add_convert_fusion.3
  532.4 9.5 %input_back.2 = (bf16[1024,512]{1,0:T(8,128)(2,1)}, bf16[2,3,512,256]{3,2,1,0:T(8,128)(2,1)}, f32[3,2,512]{2,1,0:T(2,128)}) custom-call(bf16[1024,512]{1,0:T(8,128)(2,1)} %get-tuple-element.131.refs_0_, f32[1024,512]{1,0:T(8,128)} %get-tuple-element.75.refs_1_, bf16[2,1024,256]{2,1,0:T(8,128)(2,1)} %get-tuple-element.78.refs_2_, ...), custom_call_target="tpu_custom_call" | custom-call | flops 3221225472 | bytes 9973760 | tf_op jit(solution)/shard_map/input_back/pallas_call | solution.py:102
  542.1 1.4 collective-permute-start.30
  544.6 1.6 collective-permute-start.35
  546.1 2.5 add_convert_fusion
  550.3 3.1 add_convert_fusion.1
  556.3 3.1 collective-permute-done.35
  560.4 21.5 %collective-permute-done.39 = bf16[1024,512]{1,0:T(8,128)(2,1)S(1)} collective-permute-done((bf16[1024,512]{1,0:T(8,128)(2,1)S(1)}, bf16[1024,512]{1,0:T(8,128)(2,1)S(1)}, u32[]{:S(2)}, u32[]{:S(2)}) %collective-permute-start.39) | collective-permute-done | bytes 1048608 | tf_op jit(solution)/shard_map/ppermute | solution.py:702
  581.9 1.3 fusion.4
  583.2 21.2 %collective-permute-done.37 = bf16[512,1024]{1,0:T(8,128)(2,1)S(1)} collective-permute-done((bf16[512,1024]{1,0:T(8,128)(2,1)S(1)}, bf16[512,1024]{1,0:T(8,128)(2,1)S(1)}, u32[]{:S(2)}, u32[]{:S(2)}) %collective-permute-start.37) | collective-permute-done | bytes 1048608 | tf_op jit(solution)/shard_map/ppermute | solution.py:702
  604.4 1.4 fusion.3
  605.7 14.5 %collective-permute-done.31 = bf16[3,512,256]{2,1,0:T(8,128)(2,1)S(1)} collective-permute-done((bf16[3,512,256]{2,1,0:T(8,128)(2,1)S(1)}, bf16[3,512,256]{2,1,0:T(8,128)(2,1)S(1)}, u32[]{:S(2)}, u32[]{:S(2)}) %collective-permute-start.31) | collective-permute-done | bytes 786464 | tf_op jit(solution)/shard_map/ppermute | solution.py:702
  621.4 1.2 copy-done.17
  623.9 2.8 collective-permute-start.24
  627.6 1.2 collective-permute-start.29
  628.9 21.7 %collective-permute-done.24 = bf16[1024,512]{1,0:T(8,128)(2,1)S(1)} collective-permute-done((bf16[1024,512]{1,0:T(8,128)(2,1)S(1)}, bf16[1024,512]{1,0:T(8,128)(2,1)S(1)}, u32[]{:S(2)}, u32[]{:S(2)}) %collective-permute-start.24) | collective-permute-done | bytes 1048608 | tf_op jit(solution)/shard_map/ppermute | solution.py:664
  650.8 1.5 maximum_bitcast_fusion
  652.3 56.0 %psum.47 = f32[2,3,2,512]{3,2,1,0:T(2,128)S(1)} all-reduce(f32[2,3,2,512]{3,2,1,0:T(2,128)S(1)} %pad_maximum_fusion.1), channel_id=1, replica_groups=mesh['section'=2,'dp'=8,'tensor'=2] {'section','dp','tensor'}, use_global_device_ids=true, to_apply=%region_5.6 | all-reduce | flops 6144 | bytes 49152 | tf_op jit(solution)/shard_map/psum | solution.py:803
  708.9 1.4 select_bitcast_fusion.1
  710.2 2.3 maximum_convert_fusion
  712.5 55.7 %all-reduce.3.cloned.1.call-done = (bf16[1,3,512,256]{3,2,1,0:T(8,128)(2,1)}, bf16[1,256,512]{2,1,0:T(8,128)(2,1)}, bf16[1,2,512,256]{3,2,1,0:T(8,128)(2,1)}, bf...) async-done(((bf16[1,3,512,256]{3,2,1,0:T(8,128)(2,1)}, bf16[1,256,512]{2,1,0:T(8,128)(2,1)}, bf16[1,2,512,256]{3,2,1,0:T(8,128)(2,1)}, bf16[1,512,1024]{2,1,0:T(8,128)(2,1)}, ...) | async-done | bytes 3670032 | tf_op jit(solution)/shard_map/psum | solution.py:806
  768.2 1.9 broadcast_in_dim.39
  770.1 2.5 broadcast_in_dim.37
  773.6 1.6 broadcast_in_dim.43
  775.2 1.6 broadcast_in_dim.45
  (161 shorter events, 27.7 us)
Async XLA Ops:
  7.2 761.0 %all-reduce.3.cloned.1.call-start = ((), (), s32[]{:S(2)}) async-start(), calls=%async_computation | async-start | bytes 7340032 | tf_op jit(solution)/shard_map/psum | solution.py:806
  7.2 29.5 %collective-permute-start.4 = (bf16[3,512,256]{2,1,0:T(8,128)(2,1)}, bf16[3,512,256]{2,1,0:T(8,128)(2,1)}, u32[]{:S(2)}, u32[]{:S(2)}) collective-permute-start(bf16[3,512,256]{2,1,0:T(8,128)(2,1)} %bitcast.109), channel_id=1, source_target_pairs={{0,1},{1,0},{2,3},{3,2},{4,5},{5,4},{6,7},{7,6},{8,9},{9,8},{10,11... | collective-permute-start | bytes 2359304 | tf_op jit(solution)/shard_map/ppermute | solution.py:686
  10.2 47.6 %collective-permute-start.3 = (bf16[3,512,256]{2,1,0:T(8,128)(2,1)}, bf16[3,512,256]{2,1,0:T(8,128)(2,1)}, u32[]{:S(2)}, u32[]{:S(2)}) collective-permute-start(bf16[3,512,256]{2,1,0:T(8,128)(2,1)} %bitcast.110), channel_id=1, source_target_pairs={{0,16},{16,0},{1,17},{17,1},{2,18},{18,2},{3,19},{19,3},{4,20},{20... | collective-permute-start | bytes 2359304 | tf_op jit(solution)/shard_map/ppermute | solution.py:682
  10.2 23.5 %collective-permute-start.2 = (f32[3,2,512]{2,1,0:T(2,128)}, f32[3,2,512]{2,1,0:T(2,128)S(1)}, u32[]{:S(2)}, u32[]{:S(2)}) collective-permute-start(f32[3,2,512]{2,1,0:T(2,128)} %bitcast.113), channel_id=1, source_target_pairs={{0,16},{16,0},{1,17},{17,1},{2,18},{18,2},{3,19},{19,3},{4,20},{20... | collective-permute-start | bytes 36872 | tf_op jit(solution)/shard_map/ppermute | solution.py:682
  10.8 24.8 %collective-permute-start.7 = (bf16[256,512]{1,0:T(8,128)(2,1)}, bf16[256,512]{1,0:T(8,128)(2,1)S(1)}, u32[]{:S(2)}, u32[]{:S(2)}) collective-permute-start(bf16[256,512]{1,0:T(8,128)(2,1)} %bitcast.111), channel_id=1, source_target_pairs={{0,16},{16,0},{1,17},{17,1},{2,18},{18,2},{3,19},{19,3},{4,20},{20... | collective-permute-start | bytes 786440 | tf_op jit(solution)/shard_map/ppermute | solution.py:682
  10.8 12.6 %copy-start.34 = (s32[2,2,2]{2,1,0:T(2,128)S(1)}, s32[2,2,2]{2,1,0:T(2,128)}, u32[]{:S(2)}) copy-start(s32[2,2,2]{2,1,0:T(2,128)} %param.10) | copy-start | bytes 100
  10.8 23.6 %copy-start.9 = (bf16[1,2,1024,512]{3,2,1,0:T(8,128)(2,1)S(1)}, bf16[1,2,1024,512]{3,2,1,0:T(8,128)(2,1)}, u32[]{:S(2)}) copy-start(bf16[1,2,1024,512]{3,2,1,0:T(8,128)(2,1)} %param.17) | copy-start | bytes 6291460
  13.9 46.8 %collective-permute-start = (bf16[1024,512]{1,0:T(8,128)(2,1)}, bf16[1024,512]{1,0:T(8,128)(2,1)}, u32[]{:S(2)}, u32[]{:S(2)}) collective-permute-start(bf16[1024,512]{1,0:T(8,128)(2,1)} %get-tuple-element.133), channel_id=1, source_target_pairs={{0,0},{1,16},{16,1},{17,17},{2,2},{3,18},{18,3},{19,19},{4,4},{5,2... | collective-permute-start | bytes 3145736 | tf_op jit(solution)/shard_map/ppermute | solution.py:656
  33.7 27.2 %collective-permute-start.1 = (bf16[1024,512]{1,0:T(8,128)(2,1)}, bf16[1024,512]{1,0:T(8,128)(2,1)S(1)}, u32[]{:S(2)}, u32[]{:S(2)}) collective-permute-start(bf16[1024,512]{1,0:T(8,128)(2,1)} %get-tuple-element.134), channel_id=1, source_target_pairs={{0,1},{1,17},{16,0},{17,16},{2,3},{3,19},{18,2},{19,18},{4,5},{5,2... | collective-permute-start | bytes 3145736 | tf_op jit(solution)/shard_map/ppermute | solution.py:657
  34.4 23.4 %copy-start.23 = (bf16[1,3,512,256]{3,2,1,0:T(8,128)(2,1)S(1)}, bf16[1,3,512,256]{3,2,1,0:T(8,128)(2,1)}, u32[]{:S(2)}) copy-start(bf16[1,3,512,256]{3,2,1,0:T(8,128)(2,1)} %param.11) | copy-start | bytes 2359300
  35.5 19.8 %collective-permute-start.8 = (bf16[256,512]{1,0:T(8,128)(2,1)S(1)}, bf16[256,512]{1,0:T(8,128)(2,1)S(1)}, u32[]{:S(2)}, u32[]{:S(2)}) collective-permute-start(bf16[256,512]{1,0:T(8,128)(2,1)S(1)} %bitcast.112), channel_id=1, source_target_pairs={{0,1},{1,0},{2,3},{3,2},{4,5},{5,4},{6,7},{7,6},{8,9},{9,8},{10,11... | collective-permute-start | bytes 786440 | tf_op jit(solution)/shard_map/ppermute | solution.py:686
  36.7 24.0 %copy-start.15 = (bf16[1,512,1024]{2,1,0:T(8,128)(2,1)S(1)}, bf16[1,512,1024]{2,1,0:T(8,128)(2,1)}, u32[]{:S(2)}) copy-start(bf16[1,512,1024]{2,1,0:T(8,128)(2,1)} %param.14) | copy-start | bytes 3145732
  36.7 27.0 %collective-permute-start.5 = (bf16[3,512,256]{2,1,0:T(8,128)(2,1)}, bf16[3,512,256]{2,1,0:T(8,128)(2,1)S(1)}, u32[]{:S(2)}, u32[]{:S(2)}) collective-permute-start(bf16[3,512,256]{2,1,0:T(8,128)(2,1)} %collective-permute-done.4), channel_id=1, source_target_pairs={{0,16},{16,0},{1,17},{17,1},{2,18},{18,2},{3,19},{19,3},{4,20},{20... | collective-permute-start | bytes 2359304 | tf_op jit(solution)/shard_map/ppermute | solution.py:682
  55.3 5.4 copy-start.27
  55.3 18.6 %collective-permute-start.17 = (bf16[2,512,256]{2,1,0:T(8,128)(2,1)}, bf16[2,512,256]{2,1,0:T(8,128)(2,1)S(1)}, u32[]{:S(2)}, u32[]{:S(2)}) collective-permute-start(bf16[2,512,256]{2,1,0:T(8,128)(2,1)} %bitcast.13), channel_id=1, source_target_pairs={{0,1},{1,0},{2,3},{3,2},{4,5},{5,4},{6,7},{7,6},{8,9},{9,8},{10,11... | collective-permute-start | bytes 1572872 | tf_op jit(solution)/shard_map/ppermute | solution.py:686
  57.8 2.4 collective-permute-start.9
  60.2 14.0 %collective-permute-start.16 = (bf16[2,512,256]{2,1,0:T(8,128)(2,1)}, bf16[2,512,256]{2,1,0:T(8,128)(2,1)}, u32[]{:S(2)}, u32[]{:S(2)}) collective-permute-start(bf16[2,512,256]{2,1,0:T(8,128)(2,1)} %bitcast.13), channel_id=1, source_target_pairs={{0,16},{16,0},{1,17},{17,1},{2,18},{18,2},{3,19},{19,3},{4,20},{20... | collective-permute-start | bytes 1572872 | tf_op jit(solution)/shard_map/ppermute | solution.py:682
  60.8 3.0 copy-start.16
  60.8 32.6 %collective-permute-start.11 = (bf16[512,1024]{1,0:T(8,128)(2,1)S(1)}, bf16[512,1024]{1,0:T(8,128)(2,1)}, u32[]{:S(2)}, u32[]{:S(2)}) collective-permute-start(bf16[512,1024]{1,0:T(8,128)(2,1)S(1)} %bitcast.105), channel_id=1, source_target_pairs={{0,1},{1,0},{2,3},{3,2},{4,5},{5,4},{6,7},{7,6},{8,9},{9,8},{10,11... | collective-permute-start | bytes 3145736 | tf_op jit(solution)/shard_map/ppermute | solution.py:686
  60.9 33.3 %collective-permute-start.10 = (bf16[512,1024]{1,0:T(8,128)(2,1)S(1)}, bf16[512,1024]{1,0:T(8,128)(2,1)}, u32[]{:S(2)}, u32[]{:S(2)}) collective-permute-start(bf16[512,1024]{1,0:T(8,128)(2,1)S(1)} %bitcast.106), channel_id=1, source_target_pairs={{0,16},{16,0},{1,17},{17,1},{2,18},{18,2},{3,19},{19,3},{4,20},{20... | collective-permute-start | bytes 3145736 | tf_op jit(solution)/shard_map/ppermute | solution.py:682
  63.7 51.6 %collective-permute-start.14 = (bf16[1024,512]{1,0:T(8,128)(2,1)S(1)}, bf16[1024,512]{1,0:T(8,128)(2,1)}, u32[]{:S(2)}, u32[]{:S(2)}) collective-permute-start(bf16[1024,512]{1,0:T(8,128)(2,1)S(1)} %bitcast.107), channel_id=1, source_target_pairs={{0,1},{1,0},{2,3},{3,2},{4,5},{5,4},{6,7},{7,6},{8,9},{9,8},{10,11... | collective-permute-start | bytes 3145736 | tf_op jit(solution)/shard_map/ppermute | solution.py:686
  73.9 19.5 %copy-start.28 = (bf16[256,512]{1,0:T(8,128)(2,1)S(1)}, bf16[256,512]{1,0:T(8,128)(2,1)}, u32[]{:S(2)}) copy-start(bf16[256,512]{1,0:T(8,128)(2,1)} %copy-done.27) | copy-start | bytes 786436
  73.9 42.5 %collective-permute-start.13 = (bf16[1024,512]{1,0:T(8,128)(2,1)S(1)}, bf16[1024,512]{1,0:T(8,128)(2,1)S(1)}, u32[]{:S(2)}, u32[]{:S(2)}) collective-permute-start(bf16[1024,512]{1,0:T(8,128)(2,1)S(1)} %bitcast.108), channel_id=1, source_target_pairs={{0,16},{16,0},{1,17},{17,1},{2,18},{18,2},{3,19},{19,3},{4,20},{20... | collective-permute-start | bytes 3145736 | tf_op jit(solution)/shard_map/ppermute | solution.py:682
  74.2 57.7 %collective-permute-start.6 = (bf16[2,2,1024,256]{3,2,1,0:T(8,128)(2,1)}, bf16[2,2,1024,256]{3,2,1,0:T(8,128)(2,1)}, u32[]{:S(2)}, u32[]{:S(2)}) collective-permute-start(bf16[2,2,1024,256]{3,2,1,0:T(8,128)(2,1)} %get-tuple-element.58.refs_0_), channel_id=1, source_target_pairs={{0,16},{16,0},{1,17},{17,1},{2,18},{18,2},{3,19},{19,3},{4,20},{20... | collective-permute-start | bytes 6291464 | tf_op jit(solution)/shard_map/ppermute | solution.py:673
  93.4 4.1 collective-permute-start.18
  94.2 31.7 %collective-permute-start.12 = (bf16[512,1024]{1,0:T(8,128)(2,1)}, bf16[512,1024]{1,0:T(8,128)(2,1)}, u32[]{:S(2)}, u32[]{:S(2)}) collective-permute-start(bf16[512,1024]{1,0:T(8,128)(2,1)} %collective-permute-done.11), channel_id=1, source_target_pairs={{0,16},{16,0},{1,17},{17,1},{2,18},{18,2},{3,19},{19,3},{4,20},{20... | collective-permute-start | bytes 3145736 | tf_op jit(solution)/shard_map/ppermute | solution.py:682
  97.4 81.9 %collective-permute-start.22 = (bf16[1024,512]{1,0:T(8,128)(2,1)}, bf16[1024,512]{1,0:T(8,128)(2,1)S(1)}, u32[]{:S(2)}, u32[]{:S(2)}) collective-permute-start(bf16[1024,512]{1,0:T(8,128)(2,1)} %get-tuple-element.129), channel_id=1, source_target_pairs={{0,0},{1,16},{16,1},{17,17},{2,2},{3,18},{18,3},{19,19},{4,4},{5,2... | collective-permute-start | bytes 3145736 | tf_op jit(solution)/shard_map/ppermute | solution.py:656
  115.4 13.6 %collective-permute-start.15 = (bf16[1024,512]{1,0:T(8,128)(2,1)}, bf16[1024,512]{1,0:T(8,128)(2,1)}, u32[]{:S(2)}, u32[]{:S(2)}) collective-permute-start(bf16[1024,512]{1,0:T(8,128)(2,1)} %collective-permute-done.14), channel_id=1, source_target_pairs={{0,16},{16,0},{1,17},{17,1},{2,18},{18,2},{3,19},{19,3},{4,20},{20... | collective-permute-start | bytes 3145736 | tf_op jit(solution)/shard_map/ppermute | solution.py:682
  116.4 63.0 %collective-permute-start.21 = (bf16[1024,512]{1,0:T(8,128)(2,1)S(1)}, bf16[1024,512]{1,0:T(8,128)(2,1)}, u32[]{:S(2)}, u32[]{:S(2)}) collective-permute-start(bf16[1024,512]{1,0:T(8,128)(2,1)S(1)} %get-tuple-element.130), channel_id=1, source_target_pairs={{0,1},{1,17},{16,0},{17,16},{2,3},{3,19},{18,2},{19,18},{4,5},{5,2... | collective-permute-start | bytes 3145736 | tf_op jit(solution)/shard_map/ppermute | solution.py:657
  125.9 56.1 %collective-permute-start.19 = (bf16[2,2,1024,256]{3,2,1,0:T(8,128)(2,1)}, bf16[2,2,1024,256]{3,2,1,0:T(8,128)(2,1)}, u32[]{:S(2)}, u32[]{:S(2)}) collective-permute-start(bf16[2,2,1024,256]{3,2,1,0:T(8,128)(2,1)} %get-tuple-element.62.refs_0_), channel_id=1, source_target_pairs={{0,16},{16,0},{1,17},{17,1},{2,18},{18,2},{3,19},{19,3},{4,20},{20... | collective-permute-start | bytes 6291464 | tf_op jit(solution)/shard_map/ppermute | solution.py:673
  178.2 42.5 %collective-permute-start.20 = (bf16[2,2,1024,256]{3,2,1,0:T(8,128)(2,1)}, bf16[2,2,1024,256]{3,2,1,0:T(8,128)(2,1)}, u32[]{:S(2)}, u32[]{:S(2)}) collective-permute-start(bf16[2,2,1024,256]{3,2,1,0:T(8,128)(2,1)} %get-tuple-element.66.refs_0_), channel_id=1, source_target_pairs={{0,16},{16,0},{1,17},{17,1},{2,18},{18,2},{3,19},{19,3},{4,20},{20... | collective-permute-start | bytes 6291464 | tf_op jit(solution)/shard_map/ppermute | solution.py:673
  343.6 72.4 %collective-permute-start.25 = (bf16[2,2,1024,256]{3,2,1,0:T(8,128)(2,1)}, bf16[2,2,1024,256]{3,2,1,0:T(8,128)(2,1)S(1)}, u32[]{:S(2)}, u32[]{:S(2)}) collective-permute-start(bf16[2,2,1024,256]{3,2,1,0:T(8,128)(2,1)} %get-tuple-element.74), channel_id=1, source_target_pairs={{0,16},{16,0},{1,17},{17,1},{2,18},{18,2},{3,19},{19,3},{4,20},{20... | collective-permute-start | bytes 6291464 | tf_op jit(solution)/shard_map/ppermute | solution.py:673
  415.5 104.1 %collective-permute-start.27 = (bf16[2,2,1024,256]{3,2,1,0:T(8,128)(2,1)}, bf16[2,2,1024,256]{3,2,1,0:T(8,128)(2,1)}, u32[]{:S(2)}, u32[]{:S(2)}) collective-permute-start(bf16[2,2,1024,256]{3,2,1,0:T(8,128)(2,1)} %get-tuple-element.89), channel_id=1, source_target_pairs={{0,16},{16,0},{1,17},{17,1},{2,18},{18,2},{3,19},{19,3},{4,20},{20... | collective-permute-start | bytes 6291464 | tf_op jit(solution)/shard_map/ppermute | solution.py:673
  417.3 27.5 %copy-start.10 = (bf16[2,256,512]{2,1,0:T(8,128)(2,1)S(1)}, bf16[2,256,512]{2,1,0:T(8,128)(2,1)}, u32[]{:S(2)}) copy-start(bf16[2,256,512]{2,1,0:T(8,128)(2,1)} %get-tuple-element.94) | copy-start | bytes 1572868
  417.3 29.6 %copy-start.13 = (bf16[2,512,256]{2,1,0:T(8,128)(2,1)S(1)}, bf16[2,512,256]{2,1,0:T(8,128)(2,1)}, u32[]{:S(2)}) copy-start(bf16[2,512,256]{2,1,0:T(8,128)(2,1)} %get-tuple-element.97) | copy-start | bytes 1572868
  417.3 29.6 %copy-start.14 = (bf16[2,512,256]{2,1,0:T(8,128)(2,1)S(1)}, bf16[2,512,256]{2,1,0:T(8,128)(2,1)}, u32[]{:S(2)}) copy-start(bf16[2,512,256]{2,1,0:T(8,128)(2,1)} %get-tuple-element.96) | copy-start | bytes 1572868
  445.7 70.6 %collective-permute-start.32 = (bf16[2,256,512]{2,1,0:T(8,128)(2,1)}, bf16[2,256,512]{2,1,0:T(8,128)(2,1)S(1)}, u32[]{:S(2)}, u32[]{:S(2)}) collective-permute-start(bf16[2,256,512]{2,1,0:T(8,128)(2,1)} %broadcast_select_fusion.24), channel_id=1, source_target_pairs={{0,16},{16,0},{1,17},{17,1},{2,18},{18,2},{3,19},{19,3},{4,20},{20... | collective-permute-start | bytes 1572872 | tf_op jit(solution)/shard_map/ppermute | solution.py:682
  448.0 81.5 %collective-permute-start.34 = (bf16[2,2,512,256]{3,2,0,1:T(8,128)(2,1)}, bf16[2,2,512,256]{3,2,0,1:T(8,128)(2,1)}, u32[]{:S(2)}, u32[]{:S(2)}) collective-permute-start(bf16[2,2,512,256]{3,2,0,1:T(8,128)(2,1)} %broadcast_select_fusion.3), channel_id=1, source_target_pairs={{0,16},{16,0},{1,17},{17,1},{2,18},{18,2},{3,19},{19,3},{4,20},{20... | collective-permute-start | bytes 3145736 | tf_op jit(solution)/shard_map/ppermute | solution.py:682
  510.9 21.5 %collective-permute-start.26 = (bf16[2,2,1024,256]{3,2,1,0:T(8,128)(2,1)}, bf16[2,2,1024,256]{3,2,1,0:T(8,128)(2,1)}, u32[]{:S(2)}, u32[]{:S(2)}) collective-permute-start(bf16[2,2,1024,256]{3,2,1,0:T(8,128)(2,1)} %get-tuple-element.80), channel_id=1, source_target_pairs={{0,16},{16,0},{1,17},{17,1},{2,18},{18,2},{3,19},{19,3},{4,20},{20... | collective-permute-start | bytes 6291464 | tf_op jit(solution)/shard_map/ppermute | solution.py:673
  511.4 3.3 copy-start
  511.5 3.3 copy-start.2
  514.7 31.4 %collective-permute-start.38 = (bf16[2,1024,512]{2,1,0:T(8,128)(2,1)}, bf16[2,1024,512]{2,1,0:T(8,128)(2,1)}, u32[]{:S(2)}, u32[]{:S(2)}) collective-permute-start(bf16[2,1024,512]{2,1,0:T(8,128)(2,1)} %broadcast_select_fusion), channel_id=1, source_target_pairs={{0,16},{16,0},{1,17},{17,1},{2,18},{18,2},{3,19},{19,3},{4,20},{20... | collective-permute-start | bytes 6291464 | tf_op jit(solution)/shard_map/ppermute | solution.py:682
  514.8 2.8 copy-start.11
  514.8 2.8 copy-start.12
  517.1 32.2 %collective-permute-start.36 = (bf16[2,512,1024]{2,1,0:T(8,128)(2,1)}, bf16[2,512,1024]{2,1,0:T(8,128)(2,1)}, u32[]{:S(2)}, u32[]{:S(2)}) collective-permute-start(bf16[2,512,1024]{2,1,0:T(8,128)(2,1)} %broadcast_select_fusion.1), channel_id=1, source_target_pairs={{0,16},{16,0},{1,17},{17,1},{2,18},{18,2},{3,19},{19,3},{4,20},{20... | collective-permute-start | bytes 6291464 | tf_op jit(solution)/shard_map/ppermute | solution.py:682
  519.6 9.2 %collective-permute-start.33 = (bf16[256,512]{1,0:T(8,128)(2,1)}, bf16[256,512]{1,0:T(8,128)(2,1)S(1)}, u32[]{:S(2)}, u32[]{:S(2)}) collective-permute-start(bf16[256,512]{1,0:T(8,128)(2,1)} %slice_bitcast_fusion.8), channel_id=1, source_target_pairs={{0,1},{1,0},{2,3},{3,2},{4,5},{5,4},{6,7},{7,6},{8,9},{9,8},{10,11... | collective-permute-start | bytes 786440 | tf_op jit(solution)/shard_map/ppermute | solution.py:702
  532.4 9.5 %copy-start.5 = (bf16[2,3,512,256]{3,2,1,0:T(8,128)(2,1)S(1)}, bf16[2,3,512,256]{3,2,1,0:T(8,128)(2,1)}, u32[]{:S(2)}) copy-start(bf16[2,3,512,256]{3,2,1,0:T(8,128)(2,1)} %get-tuple-element.92) | copy-start | bytes 4718596
  541.9 4.2 copy-start.1
  541.9 4.2 copy-start.4
  542.1 12.0 %collective-permute-start.30 = (bf16[2,3,512,256]{3,2,1,0:T(8,128)(2,1)S(1)}, bf16[2,3,512,256]{3,2,1,0:T(8,128)(2,1)S(1)}, u32[]{:S(2)}, u32[]{:S(2)}) collective-permute-start(bf16[2,3,512,256]{3,2,1,0:T(8,128)(2,1)S(1)} %broadcast_select_fusion.2), channel_id=1, source_target_pairs={{0,16},{16,0},{1,17},{17,1},{2,18},{18,2},{3,19},{19,3},{4,20},{20... | collective-permute-start | bytes 4718600 | tf_op jit(solution)/shard_map/ppermute | solution.py:682
  544.6 14.9 %collective-permute-start.35 = (bf16[2,512,256]{2,1,0:T(8,128)(2,1)S(1)}, bf16[2,512,256]{2,1,0:T(8,128)(2,1)S(1)}, u32[]{:S(2)}, u32[]{:S(2)}) collective-permute-start(bf16[2,512,256]{2,1,0:T(8,128)(2,1)S(1)} %slice_bitcast_fusion.6), channel_id=1, source_target_pairs={{0,1},{1,0},{2,3},{3,2},{4,5},{5,4},{6,7},{7,6},{8,9},{9,8},{10,11... | collective-permute-start | bytes 1572872 | tf_op jit(solution)/shard_map/ppermute | solution.py:702
  548.8 33.1 %collective-permute-start.39 = (bf16[1024,512]{1,0:T(8,128)(2,1)S(1)}, bf16[1024,512]{1,0:T(8,128)(2,1)S(1)}, u32[]{:S(2)}, u32[]{:S(2)}) collective-permute-start(bf16[1024,512]{1,0:T(8,128)(2,1)S(1)} %slice_bitcast_fusion), channel_id=1, source_target_pairs={{0,1},{1,0},{2,3},{3,2},{4,5},{5,4},{6,7},{7,6},{8,9},{9,8},{10,11... | collective-permute-start | bytes 3145736 | tf_op jit(solution)/shard_map/ppermute | solution.py:702
  553.4 6.0 copy-start.7
  553.4 50.9 %collective-permute-start.37 = (bf16[512,1024]{1,0:T(8,128)(2,1)S(1)}, bf16[512,1024]{1,0:T(8,128)(2,1)S(1)}, u32[]{:S(2)}, u32[]{:S(2)}) collective-permute-start(bf16[512,1024]{1,0:T(8,128)(2,1)S(1)} %slice_bitcast_fusion.2), channel_id=1, source_target_pairs={{0,1},{1,0},{2,3},{3,2},{4,5},{5,4},{6,7},{7,6},{8,9},{9,8},{10,11... | collective-permute-start | bytes 3145736 | tf_op jit(solution)/shard_map/ppermute | solution.py:702
  555.5 64.8 %collective-permute-start.31 = (bf16[3,512,256]{2,1,0:T(8,128)(2,1)S(1)}, bf16[3,512,256]{2,1,0:T(8,128)(2,1)S(1)}, u32[]{:S(2)}, u32[]{:S(2)}) collective-permute-start(bf16[3,512,256]{2,1,0:T(8,128)(2,1)S(1)} %slice_bitcast_fusion.4), channel_id=1, source_target_pairs={{0,1},{1,0},{2,3},{3,2},{4,5},{5,4},{6,7},{7,6},{8,9},{9,8},{10,11... | collective-permute-start | bytes 2359304 | tf_op jit(solution)/shard_map/ppermute | solution.py:702
  622.9 3.8 copy-start.19
  622.9 3.8 copy-start.20
  623.0 5.8 collective-permute-start.23
  623.9 26.7 %collective-permute-start.24 = (bf16[1024,512]{1,0:T(8,128)(2,1)S(1)}, bf16[1024,512]{1,0:T(8,128)(2,1)S(1)}, u32[]{:S(2)}, u32[]{:S(2)}) collective-permute-start(bf16[1024,512]{1,0:T(8,128)(2,1)S(1)} %get-tuple-element.120), channel_id=1, source_target_pairs={{1,0},{17,1},{0,16},{16,17},{3,2},{19,3},{2,18},{18,19},{5,4},{21,... | collective-permute-start | bytes 3145736 | tf_op jit(solution)/shard_map/ppermute | solution.py:664
  626.9 82.0 %collective-permute-start.28 = (bf16[1024,512]{1,0:T(8,128)(2,1)S(1)}, bf16[1024,512]{1,0:T(8,128)(2,1)S(1)}, u32[]{:S(2)}, u32[]{:S(2)}) collective-permute-start(bf16[1024,512]{1,0:T(8,128)(2,1)S(1)} %get-tuple-element.113), channel_id=1, source_target_pairs={{0,0},{16,1},{1,16},{17,17},{2,2},{18,3},{3,18},{19,19},{4,4},{20,... | collective-permute-start | bytes 3145736 | tf_op jit(solution)/shard_map/ppermute | solution.py:663
  627.6 81.3 %collective-permute-start.29 = (bf16[1024,512]{1,0:T(8,128)(2,1)S(1)}, bf16[1024,512]{1,0:T(8,128)(2,1)}, u32[]{:S(2)}, u32[]{:S(2)}) collective-permute-start(bf16[1024,512]{1,0:T(8,128)(2,1)S(1)} %get-tuple-element.114), channel_id=1, source_target_pairs={{1,0},{17,1},{0,16},{16,17},{3,2},{19,3},{2,18},{18,19},{5,4},{21,... | collective-permute-start | bytes 3145736 | tf_op jit(solution)/shard_map/ppermute | solution.py:664
  768.2 4.4 copy-start.24
  770.1 3.6 copy-start.22
  772.6 2.6 copy-start.21
  (13 other events, 20.1 us)
Sparse Core Ops, SparseCore 0:
  621.5 146.6 all-reduce.2

commit v2 on v1

--- a/solution.py
+++ b/solution.py
@@ -66,20 +66,53 @@
     return lax.dot_general(a, b, (((0,), (0,)), ((), ())), preferred_element_type=F32)
 
 
-def row_call(body, name, rows, block, row_ins, whole_ins, row_outs, sum_outs, flops):
-    def blocked(shape, dim):
+class At:
+    def __init__(self, array, *lead):
+        self.array, self.lead = array, lead
+        self.shape = array.shape[len(lead) :]
+        self.dtype = array.dtype
+
+    def spec(self, sizes, index, **options):
+        nones = (None,) * len(self.lead)
+        return pl.BlockSpec(nones + tuple(sizes), lambda *g: self.lead + tuple(index(*g)), **options)
+
+
+def at(array):
+    return array if isinstance(array, At) else At(array)
+
+
+def row_call(
+    body, name, rows, block, row_ins, whole_ins, row_outs, sum_outs, flops, finish=None, finals=None
+):
+    row_ins = [(at(a), dim) for a, dim in row_ins]
+    whole_ins = [at(a) for a in whole_ins]
+    finals = sum_outs if finals is None else finals
+
+    def blocked(array, dim):
+        sizes = tuple(block if i == dim else size for i, size in enumerate(array.shape))
+        return array.spec(sizes, lambda g: tuple(g if i == dim else 0 for i in range(len(sizes))))
+
+    def blocked_out(shape, dim):
         sizes = tuple(block if i == dim else size for i, size in enumerate(shape))
         return pl.BlockSpec(
-            sizes, lambda step: tuple(step if i == dim else 0 for i in range(len(shape)))
+            sizes, lambda g: tuple(g if i == dim else 0 for i in range(len(shape)))
         )
 
-    def whole(shape):
+    def whole(array):
+        return array.spec(
+            array.shape,
+            lambda g: (0,) * len(array.shape),
+            pipeline_mode=pl.Buffered(buffer_count=1),
+        )
+
+    def whole_out(shape):
         return pl.BlockSpec(
-            shape, lambda step: (0,) * len(shape), pipeline_mode=pl.Buffered(buffer_count=1)
+            shape, lambda g: (0,) * len(shape), pipeline_mode=pl.Buffered(buffer_count=1)
         )
 
-    n_in = len(row_ins) + len(whole_ins)
-    n_row, n_sum = len(row_outs), len(sum_outs)
+    n_rows_in = len(row_ins)
+    n_in = n_rows_in + len(whole_ins)
+    n_row, n_sum = len(row_outs), len(finals)
 
     def kernel(*refs):
         ins, outs = refs[:n_in], refs[n_in : n_in + n_row]
@@ -94,24 +127,35 @@
 
         @pl.when(pl.program_id(0) == pl.num_programs(0) - 1)
         def _():
-            for out, total in zip(sums, totals):
-                out[...] = total[...].astype(out.dtype)
-
-    arrays = [array for array, _ in row_ins] + list(whole_ins)
-    size = sum(a.size * a.dtype.itemsize for a in arrays)
+            if finish is None:
+                for out, total in zip(sums, totals):
+                    out[...] = total[...].astype(out.dtype)
+            else:
+                finish(ins[n_rows_in:], totals, sums)
+
+    arrays = [array for array, _ in row_ins] + whole_ins
+    size = sum(math.prod(a.shape) * a.dtype.itemsize for a in arrays)
     return pl.pallas_call(
         kernel,
         grid=(rows // block,),
-        in_specs=[blocked(a.shape, dim) for a, dim in row_ins] + [whole(a.shape) for a in whole_ins],
-        out_specs=[blocked(shape, dim) for shape, _, dim in row_outs]
-        + [whole(shape) for shape, _ in sum_outs],
+        in_specs=[blocked(a, dim) for a, dim in row_ins] + [whole(a) for a in whole_ins],
+        out_specs=[blocked_out(shape, dim) for shape, _, dim in row_outs]
+        + [whole_out(shape) for shape, _ in finals],
         out_shape=[jax.ShapeDtypeStruct(shape, dtype) for shape, dtype, _ in row_outs]
-        + [jax.ShapeDtypeStruct(shape, dtype) for shape, dtype in sum_outs],
+        + [jax.ShapeDtypeStruct(shape, dtype) for shape, dtype in finals],
         scratch_shapes=[pltpu.VMEM(shape, F32) for shape, _ in sum_outs],
         compiler_params=pltpu.CompilerParams(vmem_limit_bytes=VMEM),
         cost_estimate=pl.CostEstimate(flops=flops, bytes_accessed=size, transcendentals=0),
         name=name,
-    )(*arrays)
+    )(*[a.array for a in arrays])
+
+
+def column_blocks(wide, into, core, k, row):
+    rows, columns = wide.shape[0], wide.shape[1] // 2
+    for half in range(2):
+        into[core, k, row + half * rows : row + (half + 1) * rows, :] = wide[
+            :, half * columns : (half + 1) * columns
+        ].astype(BF16)
 
 
 def project_qkv(x, norm, weights, with_norm, block):
@@ -128,8 +172,8 @@
             rows_in = affine(unit, norm_ref, 2).astype(BF16)
         for k in range(parts):
             q_ref[k] = (dot_nn(rows_in, w[k][0]) * score).astype(BF16)
-            kv_ref[0, k] = dot_nn(rows_in, w[k][1]).astype(BF16)
-            kv_ref[1, k] = dot_nn(rows_in, w[k][2]).astype(BF16)
+            kv_ref[k, 0] = dot_nn(rows_in, w[k][1]).astype(BF16)
+            kv_ref[k, 1] = dot_nn(rows_in, w[k][2]).astype(BF16)
 
     return row_call(
         body,
@@ -138,7 +182,7 @@
         block,
         [(x, 0)],
         [norm, *weights],
-        [((parts, rows, part), BF16, 1), ((2, parts, rows, part), BF16, 2)],
+        [((parts, rows, part), BF16, 1), ((parts, 2, rows, part), BF16, 2)],
         [],
         6 * rows * width * width,
     )
@@ -168,8 +212,8 @@
         low = affine(unit, norm_ref, 1).astype(BF16)
         result_ref[...] = low
         for k in range(parts):
-            kv_ref[0, k] = dot_nn(low, wc[k][0]).astype(BF16)
-            kv_ref[1, k] = dot_nn(low, wc[k][1]).astype(BF16)
+            kv_ref[k, 0] = dot_nn(low, wc[k][0]).astype(BF16)
+            kv_ref[k, 1] = dot_nn(low, wc[k][1]).astype(BF16)
 
     units = sum(w.shape[1] for w in up)
     return row_call(
@@ -181,7 +225,7 @@
         [norm, *out, *up, *down, *cross],
         [
             ((rows, width), BF16, 0),
-            ((2, parts, rows, part), BF16, 2),
+            ((parts, 2, rows, part), BF16, 2),
             ((rows, width), F32, 0),
             ((rows, width), F32, 0),
         ],
@@ -233,7 +277,7 @@
     return grad
 
 
-def decoder_turn(first, mix, cotangent, norm, cross, up, down, block):
+def decoder_turn(first, mix, cotangent, norm, cross, up, down, block, paired=False):
     rows, width = first.shape
     parts, part, units = len(cross), cross[0].shape[-1], up[0].shape[1]
 
@@ -273,6 +317,25 @@
             out_total[k] += dot_tn(grad_low, mix_ref[k])
             mix_grad_ref[k] = dot_nn(grad_low, wc[k][1]).astype(BF16)
 
+    sums = [
+        ((parts, width, part), BF16),
+        ((parts, width, units), BF16),
+        ((parts, units, width), BF16),
+        ((3, 2, width), F32),
+    ]
+    if paired:
+        finals = [sums[0], ((2, parts, units, width), BF16), sums[3]]
+
+        def finish(ins, totals, outs):
+            outs[0][...] = totals[0][...].astype(BF16)
+            for k in range(parts):
+                column_blocks(totals[1][k], outs[1], 0, k, 0)
+                outs[1][1, k] = totals[2][k].astype(BF16)
+            outs[2][...] = totals[3][...]
+
+    else:
+        finals, finish = None, None
+
     return row_call(
         body,
         "decoder_turn",
@@ -285,13 +348,10 @@
             ((rows, width), F32, 0),
             ((parts, rows, part), BF16, 1),
         ],
-        [
-            ((parts, width, part), BF16),
-            ((parts, width, units), BF16),
-            ((parts, units, width), BF16),
-            ((3, 2, width), F32),
-        ],
+        sums,
         6 * rows * width * width + 12 * rows * width * units * parts,
+        finish,
+        finals,
     )
 
 
@@ -334,7 +394,9 @@
     )
 
 
-def encoder_back(first, third, mix, memory_grads, cotangent, norm, out, up, down, cross, block):
+def encoder_back(
+    first, third, mix, memory_grads, cotangent, norm, out, up, down, cross, block, paired=None
+):
     rows, width = first.shape
     parts, part, units = len(out), out[0].shape[0], up[0].shape[1]
     pieces = len(memory_grads)
@@ -351,9 +413,9 @@
         grad = cot_ref[...].astype(F32)
         for i in range(2):
             for k in range(parts):
-                memory = memory_refs[0][i, k].astype(F32)
+                memory = memory_refs[0][k, i].astype(F32)
                 for ref in memory_refs[1:]:
-                    memory += ref[i, k].astype(F32)
+                    memory += ref[k, i].astype(F32)
                 memory = memory.astype(BF16)
                 cross_total[k, i] += dot_tn(low, memory)
                 grad += dot_nt(memory, wc[k][i])
@@ -368,33 +430,63 @@
             out_total[k] += dot_tn(mix_ref[k], grad_low)
             mix_grad_ref[k] = dot_nt(grad_low, wo[k][...]).astype(BF16)
 
+    sums = [
+        ((parts, 2, width, part), BF16),
+        ((parts, part, width), BF16),
+        ((parts, width, units), BF16),
+        ((parts, units, width), BF16),
+        ((3, 2, width), F32),
+    ]
+    if paired is not None:
+        side = 3 * width
+        finals = [
+            ((2, parts, units, width), BF16),
+            ((2, parts, side, part), BF16),
+            sums[4],
+        ]
+
+        def finish(ins, totals, outs):
+            dec_out, dec_query, dec_cross = ins[-3:]
+            for k in range(parts):
+                column_blocks(totals[2][k], outs[0], 0, k, 0)
+                outs[0][1, k] = totals[3][k].astype(BF16)
+                column_blocks(totals[1][k], outs[1], 0, k, 0)
+                outs[1][0, k, width:side, :] = (
+                    totals[0][k].reshape(2 * width, part).astype(BF16)
+                )
+                column_blocks(dec_out[k], outs[1], 1, k, 0)
+                outs[1][1, k, width : 2 * width, :] = dec_query[k]
+                outs[1][1, k, 2 * width : side, :] = dec_cross[k]
+            outs[2][...] = totals[4][...]
+
+    else:
+        finals, finish, paired = None, None, []
+
     return row_call(
         body,
         "encoder_back",
         rows,
         block,
         [(first, 0), (third, 0), (mix, 1), (cotangent, 0)] + [(m, 2) for m in memory_grads],
-        [norm, *out, *up, *down, *cross],
+        [norm, *out, *up, *down, *cross, *paired],
         [((rows, width), F32, 0), ((parts, rows, part), BF16, 1)],
-        [
-            ((parts, 2, width, part), BF16),
-            ((parts, part, width), BF16),
-            ((parts, width, units), BF16),
-            ((parts, units, width), BF16),
-            ((3, 2, width), F32),
-        ],
+        sums,
         12 * rows * width * width + 10 * rows * width * units * parts,
-    )
-
-
-def input_back(x, first_grad, query_grad, key_grads, norm, weights, with_norm, block):
+        finish,
+        finals,
+    )
+
+
+def input_back(
+    x, first_grad, query_grad, key_grads, norm, weights, with_norm, block, paired=None
+):
     rows, width = x.shape
     parts, part = len(weights), weights[0].shape[-1]
     pieces = len(key_grads)
 
     def body(ins, outs, totals):
         x_ref, first_grad_ref, query_grad_ref = ins[:3]
-        key_refs, norm_ref, w = ins[3 : 3 + pieces], ins[3 + pieces], ins[4 + pieces :]
+        key_refs, norm_ref, w = ins[3 : 3 + pieces], ins[3 + pieces], ins[4 + pieces :][:parts]
         (grad_ref,) = outs
         qkv_total, norm_total = totals
         low = x_ref[...]
@@ -407,9 +499,9 @@
                 if i == 0:
                     member = query_grad_ref[k]
                 else:
-                    member = key_refs[0][i - 1, k].astype(F32)
+                    member = key_refs[0][k, i - 1].astype(F32)
                     for ref in key_refs[1:]:
-                        member += ref[i - 1, k].astype(F32)
+                        member += ref[k, i - 1].astype(F32)
                     member = member.astype(BF16)
                 qkv_total[k, i] += dot_tn(low, member)
                 grad += dot_nt(member, w[k][i])
@@ -417,16 +509,46 @@
             grad = norm_back(unit, inv, norm_ref, 2, grad, norm_total)
         grad_ref[...] = grad.astype(BF16)
 
+    sums = [((parts, 3, width, part), BF16), ((3, 2, width), F32)]
+    if paired is not None:
+        half = 3 * width // 2
+        extra = PAIR if paired else 0
+        finals = [((2, parts, half + extra, part), BF16)]
+
+        def finish(ins, totals, outs):
+            for k in range(parts):
+                both = totals[0][k].reshape(2 * half, part).astype(BF16)
+                for core in range(2):
+                    outs[0][core, k, :half, :] = both[core * half : (core + 1) * half]
+            if extra:
+                sides = [ins[-2][...] + totals[1][...], ins[-1][...]]
+                for core, table in enumerate(sides):
+                    lines = [
+                        table[slot, i : i + 1, h * part : (h + 1) * part]
+                        for slot in range(3)
+                        for i in range(2)
+                        for h in range(width // part)
+                    ]
+                    lines.append(jnp.zeros((extra - len(lines), part), F32))
+                    lines = jnp.concatenate(lines, axis=0).astype(BF16)
+                    for k in range(parts):
+                        outs[0][core, k, half:, :] = lines
+
+    else:
+        finals, finish, paired = None, None, []
+
     return row_call(
         body,
         "input_back",
         rows,
         block,
         [(x, 0), (first_grad, 0), (query_grad, 1)] + [(g, 2) for g in key_grads],
-        [norm, *weights],
+        [norm, *weights, *paired],
         [((rows, width), BF16, 0)],
-        [((parts, 3, width, part), BF16), ((3, 2, width), F32)],
+        sums,
         12 * rows * width * width,
+        finish,
+        finals,
     )
 
 
@@ -446,16 +568,38 @@
         value_o[own, :] = jnp.where(low, 1.0, values).astype(BF16)
 
 
-def attend(query, kv_pieces, span, block):
+def attention_specs(per_part, rows, block, query, lse_lead=()):
+    def query_spec(array):
+        return at(array).spec(
+            (None, block, PAIR), lambda i, j: (i // per_part, j, i % per_part)
+        )
+
+    def kv_spec(array):
+        return at(array).spec(
+            (None, 2, rows, PAIR), lambda i, j: (i // per_part, 0, 0, i % per_part)
+        )
+
+    return query_spec, kv_spec, pl.BlockSpec((block, PAIR), lambda i, j: (j, i))
+
+
+def attend(query, kv_pieces, span, block, carrier=None):
+    query, kv_pieces = at(query), [at(piece) for piece in kv_pieces]
+    carrier = carrier or Carrier()
     parts, rows, part = query.shape
     per_part = part // PAIR
     pairs = parts * per_part
     pieces = len(kv_pieces)
     keys = rows * pieces
+    n_carry = len(carrier.ins)
 
     def kernel(span_ref, q_ref, *refs):
-        kv_refs = refs[:pieces]
-        out_ref, lse_ref, key_e, key_o, value_e, value_o = refs[pieces:]
+        kv_refs, refs = refs[:pieces], refs[pieces:]
+        carry_ins, refs = refs[:n_carry], refs[n_carry:]
+        out_ref, lse_ref, refs = refs[0], refs[1], refs[2:]
+        carry_outs, refs = refs[: len(carrier.outs)], refs[len(carrier.outs) :]
+        key_e, key_o, value_e, value_o = refs[:4]
+        step = pl.program_id(0) * pl.num_programs(1) + pl.program_id(1)
+        carrier.run(step, pairs * (rows // block), carry_ins, carry_outs, refs[4:])
 
         @pl.when(pl.program_id(1) == 0)
         def _():
@@ -478,56 +622,54 @@
         mixed = jnp.where(low, sums[0], sums[1])
         out_ref[...] = (mixed / pltpu.roll(weight, HALF, 1)).astype(BF16)
 
+    query_spec, kv_spec, lse_spec = attention_specs(per_part, rows, block, query)
+    out_spec = pl.BlockSpec(
+        (None, block, PAIR), lambda i, j: (i // per_part, j, i % per_part)
+    )
+    hold = pl.BlockSpec(memory_space=pl.ANY)
     return pl.pallas_call(
         kernel,
-        grid_spec=pltpu.PrefetchScalarGridSpec(
-            num_scalar_prefetch=1,
-            grid=(pairs, rows // block),
-            in_specs=[
-                pl.BlockSpec(
-                    (None, block, PAIR), lambda i, j, _: (i // per_part, j, i % per_part)
-                )
-            ]
-            + [
-                pl.BlockSpec(
-                    (2, None, rows, PAIR), lambda i, j, _: (0, i // per_part, 0, i % per_part)
-                )
-            ]
-            * pieces,
-            out_specs=[
-                pl.BlockSpec(
-                    (None, block, PAIR), lambda i, j, _: (i // per_part, j, i % per_part)
-                ),
-                pl.BlockSpec((block, PAIR), lambda i, j, _: (j, i)),
-            ],
-            scratch_shapes=[pltpu.VMEM((keys, PAIR), BF16)] * 4,
-        ),
+        grid=(pairs, rows // block),
+        in_specs=[pl.BlockSpec(memory_space=pltpu.SMEM), query_spec(query)]
+        + [kv_spec(piece) for piece in kv_pieces]
+        + [hold] * n_carry,
+        out_specs=[out_spec, lse_spec] + [hold] * len(carrier.outs),
+        scratch_shapes=[pltpu.VMEM((keys, PAIR), BF16)] * 4 + carrier.scratch,
         out_shape=[
             jax.ShapeDtypeStruct(query.shape, BF16),
             jax.ShapeDtypeStruct((rows, pairs * PAIR), F32),
-        ],
-        compiler_params=pltpu.CompilerParams(vmem_limit_bytes=VMEM),
+        ]
+        + carrier.outs,
+        compiler_params=pltpu.CompilerParams(vmem_limit_bytes=VMEM, **carrier.params),
         cost_estimate=pl.CostEstimate(
             flops=16 * rows * keys * pairs * PAIR,
             bytes_accessed=8 * rows * pairs * PAIR * pieces,
             transcendentals=0,
         ),
         name="attend",
-    )(span, query, *kv_pieces)
-
-
-def attend_back(query, kv_pieces, mix, mix_grad, lse, span, block, chunk):
+    )(span, query.array, *[piece.array for piece in kv_pieces], *carrier.ins)
+
+
+def attend_back(query, kv_pieces, mix, mix_grad, lse, span, block, chunk, carrier=None):
+    query, kv_pieces = at(query), [at(piece) for piece in kv_pieces]
+    mix, mix_grad = at(mix), at(mix_grad)
+    carrier = carrier or Carrier()
     parts, rows, part = query.shape
     per_part = part // PAIR
     pairs = parts * per_part
     pieces = len(kv_pieces)
     keys = rows * pieces
     scale = 1.0 / math.sqrt(HALF)
+    n_carry = len(carrier.ins)
 
     def kernel(span_ref, q_ref, mix_ref, grad_ref, lse_ref, *refs):
-        kv_refs = refs[:pieces]
-        dq_ref, dkv_refs = refs[pieces], refs[pieces + 1 : 2 * pieces + 1]
-        key_e, key_o, value_e, value_o, key_t, key_total, value_total = refs[2 * pieces + 1 :]
+        kv_refs, refs = refs[:pieces], refs[pieces:]
+        carry_ins, refs = refs[:n_carry], refs[n_carry:]
+        dq_ref, dkv_refs, refs = refs[0], refs[1 : pieces + 1], refs[pieces + 1 :]
+        carry_outs, refs = refs[: len(carrier.outs)], refs[len(carrier.outs) :]
+        key_e, key_o, value_e, value_o, key_t, key_total, value_total = refs[:7]
+        step = pl.program_id(0) * pl.num_programs(1) + pl.program_id(1)
+        carrier.run(step, pairs * (rows // block), carry_ins, carry_outs, refs[7:])
 
         @pl.when(pl.program_id(1) == 0)
         def _():
@@ -546,19 +688,21 @@
             jnp.sum(jnp.where(low, 0.0, product), axis=1, keepdims=True),
             jnp.sum(jnp.where(low, product, 0.0), axis=1, keepdims=True),
         )
+        spot = jnp.where(low, lane, lane - HALF)
 
         def three(value, shift):
             high = value.astype(BF16).astype(F32)
             rest = value - high
             mid = rest.astype(BF16).astype(F32)
-            spot = lane % HALF - shift
             return jnp.where(
-                spot == 0,
+                spot == shift,
                 high,
-                jnp.where(spot == 1, mid, jnp.where(spot == 2, rest - mid, 0.0)),
+                jnp.where(
+                    spot == shift + 1, mid, jnp.where(spot == shift + 2, rest - mid, 0.0)
+                ),
             )
 
-        lse = three(-lse_ref[...], 1) + jnp.where(lane % HALF == 0, 1.0, 0.0)
+        lse = three(-lse_ref[...], 1) + jnp.where(spot == 0, 1.0, 0.0)
         inner = three(-inner, 0)
         heads = []
         for own, key, value in ((low, key_e, value_e), (~low, key_o, value_o)):
@@ -596,39 +740,508 @@
                 ref[0] = (key_total[own, :] * (1.0 / LOG2E)).astype(BF16)
                 ref[1] = value_total[own, :].astype(BF16)
 
-    query_spec = pl.BlockSpec(
-        (None, block, PAIR), lambda i, j, _: (i // per_part, j, i % per_part)
-    )
-    kv_spec = pl.BlockSpec(
-        (2, None, rows, PAIR), lambda i, j, _: (0, i // per_part, 0, i % per_part)
-    )
+    query_spec, kv_spec, lse_spec = attention_specs(per_part, rows, block, query)
+    plain = jax.ShapeDtypeStruct(query.shape, BF16)
+    plain_kv = jax.ShapeDtypeStruct((parts, 2, rows, part), BF16)
+    hold = pl.BlockSpec(memory_space=pl.ANY)
     out = pl.pallas_call(
         kernel,
-        grid_spec=pltpu.PrefetchScalarGridSpec(
-            num_scalar_prefetch=1,
-            grid=(pairs, rows // block),
-            in_specs=[query_spec] * 3
-            + [pl.BlockSpec((block, PAIR), lambda i, j, _: (j, i))]
-            + [kv_spec] * pieces,
-            out_specs=[query_spec] + [kv_spec] * pieces,
-            scratch_shapes=[pltpu.VMEM((keys, PAIR), BF16)] * 4
-            + [pltpu.VMEM((PAIR, keys), BF16)]
-            + [pltpu.VMEM((keys, PAIR), F32)] * 2,
-        ),
-        out_shape=[jax.ShapeDtypeStruct(query.shape, BF16)]
-        + [jax.ShapeDtypeStruct((2, parts, rows, part), BF16)] * pieces,
-        compiler_params=pltpu.CompilerParams(vmem_limit_bytes=VMEM),
+        grid=(pairs, rows // block),
+        in_specs=[pl.BlockSpec(memory_space=pltpu.SMEM)]
+        + [query_spec(a) for a in (query, mix, mix_grad)]
+        + [lse_spec]
+        + [kv_spec(piece) for piece in kv_pieces]
+        + [hold] * n_carry,
+        out_specs=[query_spec(plain)]
+        + [kv_spec(plain_kv)] * pieces
+        + [hold] * len(carrier.outs),
+        scratch_shapes=[pltpu.VMEM((keys, PAIR), BF16)] * 4
+        + [pltpu.VMEM((PAIR, keys), BF16)]
+        + [pltpu.VMEM((keys, PAIR), F32)] * 2
+        + carrier.scratch,
+        out_shape=[plain] + [plain_kv] * pieces + carrier.outs,
+        compiler_params=pltpu.CompilerParams(vmem_limit_bytes=VMEM, **carrier.params),
         cost_estimate=pl.CostEstimate(
             flops=40 * rows * keys * pairs * PAIR,
             bytes_accessed=16 * rows * pairs * PAIR * pieces,
             transcendentals=0,
         ),
         name="attend_back",
-    )(span, query, mix, mix_grad, lse, *kv_pieces)
-    return out[0], out[1:]
-
-
-def local(tokens, lengths, self_qkv, self_out, cross_proj, ffn_up, ffn_down, norms, cotangent):
+    )(
+        span,
+        query.array,
+        mix.array,
+        mix_grad.array,
+        lse,
+        *[piece.array for piece in kv_pieces],
+        *carrier.ins,
+    )
+    return out[0], out[1 : pieces + 1], out[pieces + 1 :]
+
+
+def spots():
+    return lax.axis_index("section"), lax.axis_index("dp"), lax.axis_index("tensor")
+
+
+def remote(source, target, sent, landed, **where):
+    return pltpu.make_async_remote_copy(
+        src_ref=source,
+        dst_ref=target,
+        send_sem=sent,
+        recv_sem=landed,
+        device_id=where,
+        device_id_type=pl.DeviceIdType.MESH,
+    )
+
+
+def greet(peers):
+    barrier = pltpu.get_barrier_semaphore()
+    for peer in peers:
+        pl.semaphore_signal(
+            barrier, inc=1, device_id=peer, device_id_type=pl.DeviceIdType.MESH
+        )
+    pl.semaphore_wait(barrier, len(peers))
+
+
+def group_peers():
+    section, _, tensor = spots()
+    return [
+        {"section": 1 - section},
+        {"tensor": 1 - tensor},
+        {"section": 1 - section, "tensor": 1 - tensor},
+    ]
+
+
+class Carrier:
+    ins, outs, scratch, params = (), [], [], {}
+
+    def run(self, step, steps, ins, outs, scratch):
+        pass
+
+
+class SpreadRows:
+    sems = [pltpu.SemaphoreType.DMA((2,)), pltpu.SemaphoreType.DMA((2,)), pltpu.SemaphoreType.DMA]
+
+    def __init__(self, source, target, sems):
+        self.source, self.target = source, target
+        self.sent, self.landed, self.kept = sems
+
+    def copy(self, row):
+        section, _, tensor = spots()
+        return remote(
+            self.source.at[row],
+            self.target.at[section],
+            self.sent.at[row],
+            self.landed.at[section],
+            section=tensor,
+            tensor=row,
+        )
+
+    def keep(self, row):
+        section, _, _ = spots()
+        return pltpu.make_async_copy(self.source.at[row], self.target.at[section], self.kept)
+
+    def start(self):
+        section, _, tensor = spots()
+        for row in range(2):
+            stays = (section == tensor) & (tensor == row)
+
+            @pl.when(stays)
+            def _():
+                self.keep(row).start()
+
+            @pl.when(jnp.logical_not(stays))
+            def _():
+                self.copy(row).start()
+
+    def wait_side(self, side):
+        section, _, tensor = spots()
+        stays = (section == tensor) & (section == side)
+
+        @pl.when(stays)
+        def _():
+            self.keep(side).wait()
+
+        @pl.when(jnp.logical_not(stays))
+        def _():
+            remote(
+                self.source.at[0],
+                self.target.at[side],
+                self.sent.at[0],
+                self.landed.at[side],
+                section=tensor,
+                tensor=0,
+            ).wait_recv()
+
+    def wait_sent(self):
+        section, _, tensor = spots()
+        for row in range(2):
+            @pl.when(jnp.logical_not((section == tensor) & (tensor == row)))
+            def _():
+                self.copy(row).wait_send()
+
+
+class SpreadWeight:
+    sems = [pltpu.SemaphoreType.DMA((7,))]
+
+    def __init__(self, source, target, sems):
+        section, _, tensor = spots()
+        (sem,) = sems
+        self.kept = pltpu.make_async_copy(source, target.at[section, 0], sem.at[0])
+        self.over = remote(source, target.at[section, 1], sem.at[1], sem.at[2], tensor=1 - tensor)
+        self.near = remote(source, target.at[section, 0], sem.at[3], sem.at[4], section=1 - section)
+        self.onward = remote(
+            target.at[section, 1],
+            target.at[section, 1],
+            sem.at[5],
+            sem.at[6],
+            section=1 - section,
+        )
+
+    def start(self):
+        self.over.start()
+        self.kept.start()
+        self.near.start()
+
+    def forward(self):
+        self.over.wait_recv()
+        self.onward.start()
+
+    def finish(self):
+        self.kept.wait()
+        self.near.wait()
+        self.over.wait_send()
+        self.onward.wait()
+
+
+class Spread(Carrier):
+    def __init__(self, weights, forwards, rows, collective):
+        self.ins = [*weights, *rows]
+        self.weights, self.rows, self.forwards = len(weights), len(rows), forwards
+        self.outs = [jax.ShapeDtypeStruct((2, 2, *w.shape), w.dtype) for w in weights] + [
+            jax.ShapeDtypeStruct(r.shape, r.dtype) for r in rows
+        ]
+        self.scratch = SpreadWeight.sems * len(weights) + SpreadRows.sems * len(rows)
+        self.params = dict(collective_id=collective, has_side_effects=True)
+
+    def run(self, step, steps, ins, outs, scratch):
+        def weight(i):
+            return SpreadWeight(ins[i], outs[i], scratch[i : i + 1])
+
+        def row(i):
+            spot = self.weights + i
+            sems = scratch[self.weights + 3 * i : self.weights + 3 * i + 3]
+            return SpreadRows(ins[spot], outs[spot], sems)
+
+        @pl.when(step == 0)
+        def _():
+            greet(group_peers())
+            for i in range(self.weights):
+                weight(i).start()
+            for i in range(self.rows):
+                row(i).start()
+
+        for i, when in enumerate(self.forwards):
+
+            @pl.when(step == when)
+            def _():
+                weight(i).forward()
+
+        @pl.when(step == steps - 1)
+        def _():
+            for i in range(self.weights):
+                weight(i).finish()
+            for i in range(self.rows):
+                row(i).wait_side(0)
+                row(i).wait_side(1)
+                row(i).wait_sent()
+
+
+class Reduce(Carrier):
+    def __init__(self, sources, chunk, collective):
+        self.ins = list(sources)
+        self.chunk = chunk
+        self.places = [
+            (i, row) for i, s in enumerate(sources) for row in range(0, s.shape[2], chunk)
+        ]
+        self.count = len(self.places)
+        self.levels = lax.axis_size("dp").bit_length() - 1
+        width = sources[0].shape[3]
+        self.outs = [jax.ShapeDtypeStruct((self.count * chunk, width), BF16)]
+
+        def room(*shape):
+            return pltpu.VMEM((self.count, *shape, width), BF16)
+
+        halves = [room(chunk >> (level + 1)) for level in range(self.levels)]
+        self.scratch = [room(2, chunk), room(2, chunk), room(chunk), room(chunk)]
+        self.scratch += halves + halves
+        self.scratch += [pltpu.SemaphoreType.DMA((2 + 2 * (2 + 2 * self.levels), self.count))]
+        self.params = dict(collective_id=collective, has_side_effects=True)
+        self.stages = 4 + 2 * self.levels
+        self.steps = self.count + self.stages - 1
+
+    def run(self, step, steps, ins, outs, scratch):
+        chunk, levels = self.chunk, self.levels
+        assert steps >= self.steps
+        own, chip, other, full = scratch[:4]
+        halves, doubles = scratch[4 : 4 + levels], scratch[4 + levels : 4 + 2 * levels]
+        sems = scratch[4 + 2 * levels]
+        section, group, tensor = spots()
+        bits = [(group // (1 << level)) % 2 for level in range(levels)]
+        peers = [group + (1 << level) * (1 - 2 * bits[level]) for level in range(levels)]
+        begins = [0]
+        for level in range(levels):
+            begins.append(begins[level] + bits[level] * (chunk >> (level + 1)))
+
+        def keeps(level):
+            return pl.ds(pl.multiple_of(begins[level + 1], 16), chunk >> (level + 1))
+
+        def gives(level):
+            start = begins[level] + (1 - bits[level]) * (chunk >> (level + 1))
+            return pl.ds(pl.multiple_of(start, 16), chunk >> (level + 1))
+
+        def pair(kind, c):
+            return sems.at[2 + 2 * kind, c], sems.at[3 + 2 * kind, c]
+
+        def load(c):
+            i, row = self.places[c]
+            return pltpu.make_async_copy(
+                ins[i].at[section, :, pl.ds(row, chunk), :], own.at[c], sems.at[0, c]
+            )
+
+        def cross(c, place=None):
+            i, row = self.places[0] if place is None else place
+            return remote(
+                ins[i].at[1 - section, :, pl.ds(row, chunk), :],
+                chip.at[c],
+                *pair(0, c),
+                section=1 - section,
+            )
+
+        def over(c):
+            return remote(own.at[c, 1], other.at[c], *pair(1, c), tensor=1 - tensor)
+
+        def halve(level, c):
+            return remote(
+                own.at[c, 0, gives(level), :],
+                halves[level].at[c],
+                *pair(2 + level, c),
+                dp=peers[level],
+            )
+
+        def double(level, c):
+            return remote(
+                full.at[c, keeps(level), :],
+                doubles[level].at[c],
+                *pair(2 + levels + level, c),
+                dp=peers[level],
+            )
+
+        def store(c):
+            return pltpu.make_async_copy(
+                full.at[c],
+                outs[0].at[pl.ds(pl.multiple_of(c * chunk, 16), chunk), :],
+                sems.at[1, c],
+            )
+
+        def added(a, b):
+            return (a.astype(F32) + b.astype(F32)).astype(BF16)
+
+        def stage(number, c):
+            if number == 1:
+                pltpu.make_async_copy(
+                    ins[0].at[section, :, pl.ds(0, chunk), :], own.at[c], sems.at[0, c]
+                ).wait()
+                cross(c).wait()
+                own[c] = added(own[c], chip[c])
+                over(c).start()
+            elif number == 2:
+                over(c).wait()
+                own[c, 0] = added(own[c, 0], other[c])
+                halve(0, c).start()
+            elif number < 3 + levels:
+                level = number - 3
+                halve(level, c).wait()
+                mine = keeps(level)
+                if level < levels - 1:
+                    own[c, 0, mine, :] = added(own[c, 0, mine, :], halves[level][c])
+                    halve(level + 1, c).start()
+                else:
+                    full[c, mine, :] = added(own[c, 0, mine, :], halves[level][c])
+                    double(level, c).start()
+            elif number < 3 + 2 * levels:
+                level = levels - 1 - (number - 3 - levels)
+                double(level, c).wait()
+                full[c, gives(level), :] = doubles[level][c]
+                if level:
+                    double(level - 1, c).start()
+                else:
+                    store(c).start()
+            else:
+                store(c).wait()
+
+        @pl.when(step == 0)
+        def _():
+            greet(
+                [{"section": 1 - section}, {"tensor": 1 - tensor}]
+                + [{"dp": peer} for peer in peers]
+            )
+
+        for number in reversed(range(1, self.stages)):
+            c = step - number
+
+            @pl.when((c >= 0) & (c < self.count))
+            def _():
+                stage(number, c)
+
+        for c, place in enumerate(self.places):
+
+            @pl.when(step == c)
+            def _():
+                load(c).start()
+                cross(c, place).start()
+
+
+def reduce_alone(sources, chunk, collective):
+    carrier = Reduce(sources, chunk, collective)
+
+    def kernel(*refs):
+        n = len(carrier.ins)
+        carrier.run(pl.program_id(0), carrier.steps, refs[:n], refs[n : n + 1], refs[n + 1 :])
+
+    hold = pl.BlockSpec(memory_space=pl.ANY)
+    return pl.pallas_call(
+        kernel,
+        grid=(carrier.steps,),
+        in_specs=[hold] * len(carrier.ins),
+        out_specs=hold,
+        out_shape=carrier.outs[0],
+        scratch_shapes=carrier.scratch,
+        compiler_params=pltpu.CompilerParams(vmem_limit_bytes=VMEM, **carrier.params),
+        name="reduce_alone",
+    )(*carrier.ins)
+
+
+def open_up(tokens, qkv, norm, block, collective):
+    _, rows, width = tokens.shape
+    part = qkv.shape[-1]
+    score = LOG2E / math.sqrt(width // HEADS)
+
+    def kernel(tokens_ref, qkv_ref, norm_ref, *refs):
+        x_out, w_out, n_out, q_out, own_out, other_out = refs[:6]
+        x, low, w, n, q, kv = refs[6:12]
+        row_sems, weight_sems, norm_sems, load_sems, store_sems, kv_sems = (
+            refs[12:15],
+            refs[15:16],
+            refs[16],
+            refs[17],
+            refs[18],
+            refs[19],
+        )
+        section, _, _ = spots()
+        greet(group_peers())
+        rows_in = SpreadRows(tokens_ref, x, row_sems)
+        weight = SpreadWeight(qkv_ref, w, weight_sems)
+        rows_in.start()
+        weight.start()
+        norm_kept = pltpu.make_async_copy(norm_ref, n.at[section], norm_sems.at[0])
+        norm_near = remote(
+            norm_ref, n.at[section], norm_sems.at[1], norm_sems.at[2], section=1 - section
+        )
+        norm_kept.start()
+        norm_near.start()
+        stores = []
+
+        def save(source, target):
+            copy = pltpu.make_async_copy(source, target, store_sems.at[len(stores)])
+            copy.start()
+            stores.append(copy)
+
+        kv_copies = []
+
+        def project(side, k):
+            def step(i, carry):
+                own = pl.ds(pl.multiple_of(i * block, block), block)
+                rows_low = low[own, :] if side == 0 else x[1, own, :]
+                q[side, k, own, :] = (dot_nn(rows_low, w[side, k, 0]) * score).astype(BF16)
+                kv[side, k, 0, own, :] = dot_nn(rows_low, w[side, k, 1]).astype(BF16)
+                kv[side, k, 1, own, :] = dot_nn(rows_low, w[side, k, 2]).astype(BF16)
+                return carry
+
+            lax.fori_loop(0, rows // block, step, 0)
+            spot = 2 * (2 * side + k)
+            copy = remote(
+                kv.at[side, k],
+                other_out.at[side, k],
+                kv_sems.at[spot],
+                kv_sems.at[spot + 1],
+                section=1 - section,
+            )
+            copy.start()
+            kv_copies.append(copy)
+            save(kv.at[side, k], own_out.at[side, k])
+            save(q.at[side, k], q_out.at[side, k])
+
+        norm_kept.wait()
+        norm_near.wait()
+        save(n, n_out)
+        rows_in.wait_side(0)
+        save(x.at[0], x_out.at[0])
+
+        def settle(i, carry):
+            own = pl.ds(pl.multiple_of(i * block, block), block)
+            unit, _ = standardize(x[0, own, :].astype(F32))
+            low[own, :] = affine(unit, n.at[0], 2).astype(BF16)
+            return carry
+
+        lax.fori_loop(0, rows // block, settle, 0)
+        weight.kept.wait()
+        weight.near.wait()
+        project(0, 0)
+        rows_in.wait_side(1)
+        save(x.at[1], x_out.at[1])
+        project(1, 0)
+        weight.forward()
+        weight.over.wait_send()
+        weight.onward.wait()
+        save(w, w_out)
+        project(0, 1)
+        project(1, 1)
+        rows_in.wait_sent()
+        for copy in kv_copies + stores:
+            copy.wait()
+
+    hold = pl.BlockSpec(memory_space=pl.ANY)
+    shapes = [
+        ((2, rows, width), BF16),
+        ((2, 2, *qkv.shape), BF16),
+        ((2, *norm.shape), F32),
+        ((2, 2, rows, part), BF16),
+        ((2, 2, 2, rows, part), BF16),
+    ]
+    return pl.pallas_call(
+        kernel,
+        in_specs=[hold] * 3,
+        out_specs=[hold] * 6,
+        out_shape=[jax.ShapeDtypeStruct(*s) for s in shapes + shapes[-1:]],
+        scratch_shapes=[pltpu.VMEM(*shapes[0]), pltpu.VMEM((rows, width), BF16)]
+        + [pltpu.VMEM(*s) for s in shapes[1:]]
+        + SpreadRows.sems
+        + SpreadWeight.sems
+        + [
+            pltpu.SemaphoreType.DMA((3,)),
+            pltpu.SemaphoreType.DMA((1,)),
+            pltpu.SemaphoreType.DMA((12,)),
+            pltpu.SemaphoreType.DMA((8,)),
+        ],
+        compiler_params=pltpu.CompilerParams(
+            vmem_limit_bytes=VMEM, collective_id=collective, has_side_effects=True
+        ),
+        name="open_up",
+    )(tokens, qkv, norm)
+
+
+def local_general(tokens, lengths, self_qkv, self_out, cross_proj, ffn_up, ffn_down, norms, cotangent):
     section = lax.axis_index("section")
     tensor = lax.axis_index("tensor")
     tensors = lax.axis_size("tensor")
@@ -752,7 +1365,7 @@
         dec_first, cross_mix, target_cot, target_norm, target_cross, target_up, target_down, block
     )
     result = take_back(encoded, decoded)
-    cross_q_grad, memory_grads = attend_back(
+    cross_q_grad, memory_grads, _ = attend_back(
         cross_q, memory, cross_mix, cross_mix_grad, cross_lse, cross_span, query_block, chunk
     )
     memory_grads = pieces_home(memory_grads)
@@ -783,11 +1396,11 @@
     dec_cross = jnp.stack([cross_query_grad, cross_out_grad], axis=1)
     up_grad, down_grad = home(enc_up, dec_up, 1), home(enc_down, dec_down, 0)
     out_grad, cross_grad = home(enc_out, dec_out, 0), home(enc_cross, dec_cross, 2)
-    dec_q_grad, dec_kv_grads = attend_back(
+    dec_q_grad, dec_kv_grads, _ = attend_back(
         dec_q, dec_kv, dec_mix, dec_mix_grad, dec_lse, target_span, query_block, chunk
     )
     dec_kv_grads = pieces_home(dec_kv_grads)
-    enc_q_grad, enc_kv_grads = attend_back(
+    enc_q_grad, enc_kv_grads, _ = attend_back(
         enc_q, enc_kv, enc_mix, enc_mix_grad, enc_lse, source_span, query_block, chunk
     )
     enc_kv_grads = pieces_home(enc_kv_grads)
@@ -818,6 +1431,196 @@
     )
 
 
+def local_fast(tokens, lengths, self_qkv, self_out, cross_proj, ffn_up, ffn_down, norms, cotangent):
+    section, tensor = lax.axis_index("section"), lax.axis_index("tensor")
+    _, row_count, rows, width = tokens.shape
+    assert row_count == 2
+    is_first = section == 0
+    block = min(256, rows)
+    query_block = min(256, rows)
+    chunk = 512
+
+    def swap(value):
+        return lax.ppermute(value, "section", [(0, 1), (1, 0)])
+
+    def give_back(value, side):
+        return [
+            lax.ppermute(
+                value, ("section", "tensor"), [(2 * p + row, 2 * side + p) for p in range(2)]
+            )
+            for row in range(2)
+        ]
+
+    def span_of(query_side, key_side):
+        own = lax.dynamic_index_in_dim(lengths, tensor, 1, keepdims=False)
+        asks, answers = own[query_side], own[key_side]
+        paired = asks[1] > 0
+        second = paired & (section * rows >= asks[0])
+        begin = jnp.where(second, answers[0], 0)
+        end = jnp.where(second | ~paired, answers[0] + answers[1], answers[0])
+        return jnp.stack([begin, end, section * rows, (1 - section) * rows]).astype(jnp.int32)
+
+    spans = span_of(0, 0), span_of(1, 1), span_of(1, 0)
+    x, qkv, norm, q, kv_own, kv_other = open_up(tokens[0], self_qkv[0], norms[0], block, 1)
+
+    def parts(weight, side):
+        return [At(weight, side, k) for k in range(2)]
+
+    enc_x, dec_x, enc_norm_in, dec_norm_in = At(x, 0), At(x, 1), At(norm, 0), At(norm, 1)
+    enc_q, dec_q = At(q, 0), At(q, 1)
+    enc_kv, dec_kv = [[At(kv_own, side), At(kv_other, side)] for side in range(2)]
+    enc_mix, enc_lse, out, up = attend(
+        enc_q, enc_kv, spans[0], query_block, Spread([self_out[0], ffn_up[0]], [5, 14], [], 2)
+    )
+    dec_mix, dec_lse, cross, down = attend(
+        dec_q, dec_kv, spans[1], query_block, Spread([cross_proj[0], ffn_down[0]], [7, 14], [], 3)
+    )
+    encoded, memory, enc_first, enc_third = encoder_forward(
+        enc_x,
+        enc_mix,
+        enc_norm_in,
+        parts(out, 0),
+        parts(up, 0),
+        parts(down, 0),
+        parts(cross, 0),
+        block,
+    )
+    memory = [memory, swap(memory)]
+    cross_q, dec_first = decoder_middle(
+        dec_x, dec_mix, dec_norm_in, parts(out, 1), parts(cross, 1), block
+    )
+    cross_mix, cross_lse, cot = attend(
+        cross_q, memory, spans[2], query_block, Spread([], [], [cotangent[0]], 4)
+    )
+    decoded, second_grad, cross_mix_grad, cross_out_grad, ffn_dec, dec_norm = decoder_turn(
+        dec_first,
+        cross_mix,
+        At(cot, 1),
+        dec_norm_in,
+        parts(cross, 1),
+        parts(up, 1),
+        parts(down, 1),
+        block,
+        True,
+    )
+    cross_q_grad, memory_grads, (ffn_dec,) = attend_back(
+        cross_q,
+        memory,
+        cross_mix,
+        cross_mix_grad,
+        cross_lse,
+        spans[2],
+        query_block,
+        chunk,
+        Reduce([ffn_dec], 256, 5),
+    )
+    memory_grads = [memory_grads[0], swap(memory_grads[1])]
+    encoded, decoded = give_back(encoded, 0), give_back(decoded, 1)
+    dec_first_grad, dec_mix_grad, cross_query_grad, dec_out, step = decoder_middle_back(
+        dec_first,
+        dec_mix,
+        cross_q_grad,
+        second_grad,
+        dec_norm_in,
+        parts(out, 1),
+        parts(cross, 1),
+        block,
+    )
+    dec_norm += step
+    enc_first_grad, enc_mix_grad, ffn_enc, sides, enc_norm = encoder_back(
+        enc_first,
+        enc_third,
+        enc_mix,
+        memory_grads,
+        At(cot, 0),
+        enc_norm_in,
+        parts(out, 0),
+        parts(up, 0),
+        parts(down, 0),
+        parts(cross, 0),
+        block,
+        [dec_out, cross_query_grad, cross_out_grad],
+    )
+    dec_q_grad, dec_kv_grads, (ffn_enc,) = attend_back(
+        dec_q,
+        dec_kv,
+        dec_mix,
+        dec_mix_grad,
+        dec_lse,
+        spans[1],
+        query_block,
+        chunk,
+        Reduce([ffn_enc], 256, 6),
+    )
+    dec_kv_grads = [dec_kv_grads[0], swap(dec_kv_grads[1])]
+    target_grad, dec_qkv = input_back(
+        dec_x,
+        dec_first_grad,
+        dec_q_grad,
+        dec_kv_grads,
+        dec_norm_in,
+        parts(qkv, 1),
+        False,
+        block,
+        [],
+    )
+    target_grad = give_back(target_grad, 1)
+    enc_q_grad, enc_kv_grads, (sides,) = attend_back(
+        enc_q,
+        enc_kv,
+        enc_mix,
+        enc_mix_grad,
+        enc_lse,
+        spans[0],
+        query_block,
+        chunk,
+        Reduce([sides, dec_qkv], 384, 7),
+    )
+    enc_kv_grads = [enc_kv_grads[0], swap(enc_kv_grads[1])]
+    source_grad, enc_qkv = input_back(
+        enc_x,
+        enc_first_grad,
+        enc_q_grad,
+        enc_kv_grads,
+        enc_norm_in,
+        parts(qkv, 0),
+        True,
+        block,
+        [enc_norm, dec_norm],
+    )
+    source_grad = give_back(source_grad, 0)
+    last = reduce_alone([enc_qkv], PAIR, 8)
+
+    side_rows, half = 3 * width, 3 * width // 2
+    arrived = swap(jnp.where(is_first, ffn_dec, ffn_enc))
+    up_grad = jnp.where(is_first, ffn_enc, arrived).astype(F32)
+    down_grad = jnp.where(is_first, arrived, ffn_dec).astype(F32)
+    up_grad = jnp.concatenate(jnp.split(up_grad, 2, axis=0), axis=1)
+    arrived = swap(jnp.where(is_first, sides[side_rows:], last[:half]))
+    first_half = jnp.where(is_first, last[:half], arrived)
+    second_half = jnp.where(is_first, arrived, sides[side_rows:])
+    qkv_grad = jnp.concatenate([first_half, second_half], axis=0).astype(F32)
+    qkv_grad = qkv_grad.reshape(self_qkv.shape)
+    sides = sides[:side_rows].astype(F32)
+    out_grad = jnp.concatenate([sides[: width // 2], sides[width // 2 : width]], axis=1)
+    cross_grad = sides[width:].reshape(cross_proj.shape)
+    norm_grad = last[half : half + 12].astype(F32).reshape(norms.shape)
+
+    def by_side(source, target):
+        return jnp.stack([jnp.where(is_first, a, b) for a, b in zip(source, target)])
+
+    return (
+        by_side(encoded, decoded)[None],
+        by_side(source_grad, target_grad).astype(F32)[None],
+        qkv_grad,
+        out_grad[None],
+        cross_grad,
+        up_grad[None],
+        down_grad[None],
+        norm_grad,
+    )
+
+
 def solution(mesh):
     placed = (
         P("section", "dp", "tensor", None),
@@ -830,8 +1633,11 @@
         P("section", None, None, None),
         P("section", "dp", "tensor", None),
     )
+    sizes = dict(mesh.shape)
+    steps = sizes["dp"].bit_length() - 1
+    fast = sizes["tensor"] == 2 and sizes["dp"] == 1 << steps and 0 < steps <= 3
     return jax.shard_map(
-        local,
+        local_fast if fast else local_general,
         mesh=mesh,
         in_specs=placed,
         out_specs=(

time: 789 us -> 693 us (0.88)
  Pallas kernels: 400 us -> 608 us
  waiting for transfers between devices: 188 us -> 0.04 us
  blocking collectives: 56 us -> 0 us
  other arithmetic: 65 us -> 19.9 us
  between operations: 23.7 us -> 10.4 us
    pallas_call x15, Pallas kernels: 400 us -> 608 us  [the longest x3 249 us: attend_back(): pl.pallas_call(kernel, grid=(pairs, rows // block), in_specs=[pl.BlockSpe...]
    ppermute x40 -> x14, waiting for transfers between devices: 132 us -> 0.04 us  [the longest x8 0.02 us: give_back(): lax.ppermute(value, ('section', 'tensor'), [(2 * p + row, 2 * side + p) f...]
    psum x1 -> x0, blocking collectives: 56 us -> none  [local(): lax.psum(jnp.stack([enc_norm, dec_norm]), ('section', 'dp', 'tensor'))]
    psum x1 -> x0, waiting for transfers between devices: 55.7 us -> none  [local(): lax.psum(grad, 'dp').astype(F32)]
    select_n x20 -> x3, other arithmetic: 33.3 us -> 2.19 us  [the longest x1 1.08 us: local_fast(): arrived = swap(jnp.where(is_first, ffn_dec, ffn_enc))]
    convert_element_type x6 -> x3, other arithmetic: 12.7 us -> 3.68 us  [the longest x1 2.29 us: local_fast(): by_side(source_grad, target_grad).astype(F32)[None]]
    broadcast_in_dim x11 -> x4, other arithmetic: 15.5 us -> 6.77 us  [the longest x1 2.95 us: local_fast(): down_grad[None]]
    ppermute x40 -> x14, starting transfers between devices: 38.8 us -> 34.4 us  [the longest x8 30.2 us: give_back(): lax.ppermute(value, ('section', 'tensor'), [(2 * p + row, 2 * side + p) f...]
  transfers between devices with their start and end apart: 41 -> 14, of which waited for: 9 -> 0; matrix products, arithmetic and copies ran while one was open for 8% -> 3% of each run, Pallas kernels for 35% -> 27%
where the time goes in v2:
time: 693 us; the launch traced here: 680 us
  Pallas kernels  608 us (88%)
  starting transfers between devices  34.4 us (5%)
  other arithmetic  19.9 us (3%)
  between operations  10.4 us (2%)
  local copies, waits for them, and re-layouts  7.23 us (1%)
    pallas_call x3, Pallas kernels, attend_back(): pl.pallas_call(kernel, grid=(pairs, rows // block), in_specs=[pl.BlockSpe...  249 us
    pallas_call x3, Pallas kernels, attend(): pl.pallas_call(kernel, grid=(pairs, rows // block), in_specs=[pl.BlockSpe...  137 us
    pallas_call x7, Pallas kernels, row_call(): pl.pallas_call(kernel, grid=(rows // block,), in_specs=[blocked(a, dim) f...  113 us
    pallas_call x1, Pallas kernels, reduce_alone(): pl.pallas_call(kernel, grid=(carrier.steps,), in_specs=[hold] * len(carri...  57.2 us
    pallas_call x1, Pallas kernels, open_up(): pl.pallas_call(kernel, in_specs=[hold] * 3, out_specs=[hold] * 6, out_sha...  51.8 us
    ppermute x8, starting transfers between devices, give_back(): lax.ppermute(value, ('section', 'tensor'), [(2 * p + row, 2 * side + p) f...  30.2 us
  transfers between devices with their start and end apart: 14, of which 0 were waited for; matrix products, arithmetic and copies ran while one was open for 3% of the time, Pallas kernels for 27%

profile of v2, /device:TPU:0, one launch (start us, length us, event | category | flops | bytes accessed | tf_op | source)
XLA Modules:
  0.0 680.2 jit_solution(9457806371408363592)
XLA Ops:
  0.6 1.4 constant_dynamic-slice_fusion.2
  9.8 51.8 %open_up.1 = (bf16[2,1024,512]{2,1,0:T(8,128)(2,1)}, bf16[2,2,3,512,256]{4,3,2,1,0:T(8,128)(2,1)}, f32[2,3,2,512]{3,2,1,0:T(2,128)}, bf16[2,2,1024,256]{3,2,1,0:...) custom-call(bf16[2,1024,512]{2,1,0:T(8,128)(2,1)} %bitcast.41, ...), custom_call_target="tpu_custom_call" | custom-call | tf_op jit(solution)/shard_map/open_up/pallas_call | solution.py:1222
  61.6 0.7 add_add_fusion
  62.3 46.1 %attend.3 = (bf16[2,1024,256]{2,1,0:T(8,128)(2,1)}, f32[1024,512]{1,0:T(8,128)}, bf16[2,2,256,512]{3,2,1,0:T(8,128)(2,1)}, bf16[2,2,512,1024]{3,2,1,0:T(8,128)(2,1)}) custom-call(s32[4]{0:T(128)} %get-tuple-element.130.span_ref, bf16[2,2,1024,256]{3,2,1,0:T(8,128)(2,1)} %get-tuple-element.64.q_ref, bf16[2,2,2,1024,256]{4,3,2,1,0:T(8,128)(2,1)} %get-tuple-element.65.refs_0_, ...), custom_call_target="tpu_custom_call" | custom-call | flops 17179869184 | bytes 8388608 | tf_op jit(solution)/shard_map/attend/pallas_call | solution.py:630
  108.4 52.8 %attend.4 = (bf16[2,1024,256]{2,1,0:T(8,128)(2,1)}, f32[1024,512]{1,0:T(8,128)}, bf16[2,2,2,512,256]{4,3,2,1,0:T(8,128)(2,1)}, bf16[2,2,1024,512]{3,2,1,0:T(8,128)(2,1)}) custom-call(s32[4]{0:T(128)} %get-tuple-element.131.span_ref, bf16[2,2,1024,256]{3,2,1,0:T(8,128)(2,1)} %get-tuple-element.64.q_ref, ...), custom_call_target="tpu_custom_call" | custom-call | flops 17179869184 | bytes 8388608 | tf_op jit(solution)/shard_map/attend/pallas_call | solution.py:630
  161.3 13.7 %encoder_forward.1 = (bf16[1024,512]{1,0:T(8,128)(2,1)}, bf16[2,2,1024,256]{3,2,1,0:T(8,128)(2,1)}, f32[1024,512]{1,0:T(8,128)}, f32[1024,512]{1,0:T(8,128)}) custom-call(bf16[2,1024,512]{2,1,0:T(8,128)(2,1)} %get-tuple-element.63.refs_0_, bf16[2,1024,256]{2,1,0:T(8,128)(2,1)} %get-tuple-element.67.refs_1_.refs_2_.mix_ref, ...), custom_call_target="tpu_custom_call" | custom-call | flops 5905580032 | bytes 7876608 | tf_op jit(solution)/shard_map/encoder_forward/pallas_call | solution.py:138
  174.9 0.2 collective-permute-start.1
  176.4 6.0 decoder_middle.1
  182.4 0.6 add_add_fusion.2.span_ref
  183.0 0.0 collective-permute-done.1.refs_1_
  183.0 1.3 copy-done.9
  184.3 38.2 %attend.5 = (bf16[2,1024,256]{2,1,0:T(8,128)(2,1)}, f32[1024,512]{1,0:T(8,128)}, bf16[2,1024,512]{2,1,0:T(8,128)(2,1)}) custom-call(s32[4]{0:T(128)} %add_add_fusion.2.span_ref, bf16[2,1024,256]{2,1,0:T(8,128)(2,1)} %get-tuple-element.76.q_ref, bf16[2,2,1024,256]{3,2,1,0:T(8,128)(2,1)} %get-tuple-element.77.refs_0_, bf16[2,2,1024,256]{3,2,1,0:T(8,128)(2,1)} %copy-done.9, ...), custom_call_target="tpu_custom_call" | custom-call | flops 17179869184 | bytes 8388608 | tf_op jit(solution)/shard_map/attend/pallas_call | solution.py:630
  222.5 27.3 %decoder_turn.1 = (bf16[1024,512]{1,0:T(8,128)(2,1)}, f32[1024,512]{1,0:T(8,128)}, bf16[2,1024,256]{2,1,0:T(8,128)(2,1)}, bf16[2,512,256]{2,1,0:T(8,128)(2,1)}, ...) custom-call(f32[1024,512]{1,0:T(8,128)} %get-tuple-element.75.refs_0_, ...), custom_call_target="tpu_custom_call" | custom-call | flops 14495514624 | bytes 9449472 | tf_op jit(solution)/shard_map/decoder_turn/pallas_call | solution.py:138
  249.9 84.4 %attend_back.3 = (bf16[2,1024,256]{2,1,0:T(8,128)(2,1)}, bf16[2,2,1024,256]{3,2,1,0:T(8,128)(2,1)}, bf16[2,2,1024,256]{3,2,1,0:T(8,128)(2,1)}, bf16[1024,512]{1,0:T(8,128)(2,1)}) custom-call(s32[4]{0:T(128)} %add_add_fusion.2.span_ref, bf16[2,1024,256]{2,1,0:T(8,128)(2,1)} %get-tuple-element.76.q_ref, ...), custom_call_target="tpu_custom_call" | custom-call | flops 42949672960 | bytes 16777216 | tf_op jit(solution)/shard_map/attend_back/pallas_call | solution.py:747
  334.3 0.1 collective-permute-start.5
  334.4 19.0 %decoder_middle_back.1 = (f32[1024,512]{1,0:T(8,128)}, bf16[2,1024,256]{2,1,0:T(8,128)(2,1)}, bf16[2,512,256]{2,1,0:T(8,128)(2,1)}, bf16[2,256,512]{2,1,0:T(8,128)(2,1)}, f32[3,2,512]{2,1,0:T(2,128)}) custom-call(f32[1024,512]{1,0:T(8,128)} %get-tuple-element.75.refs_0_, bf16[2,1024,256]{2,1,0:T(8,128)(2,1)} %get-tuple-element.74.refs_1_.mix_ref, ...), custom_call_target="tpu_custom_call" | custom-call | flops 2147483648 | bytes 7876608 | tf_op jit(solution)/shard_map/decoder_middle_back/pallas_call | solution.py:138
  353.3 0.0 copy-start.10
  353.3 1.3 copy-done.10
  354.7 28.4 %encoder_back.1 = (f32[1024,512]{1,0:T(8,128)}, bf16[2,1024,256]{2,1,0:T(8,128)(2,1)}, bf16[2,2,1024,512]{3,2,1,0:T(8,128)(2,1)}, bf16[2,2,1536,256]{3,2,1,0:T(8,128)(2,1)}, f32[3,2,512]{2,1,0:T(2,128)}) custom-call(f32[1024,512]{1,0:T(8,128)} %get-tuple-element.81.refs_0_, f32[1024,512]{1,0:T(8,128)} %get-tuple-element.82.refs_1_, ...), custom_call_target="tpu_custom_call" | custom-call | flops 13958643712 | bytes 17838080 | tf_op jit(solution)/shard_map/encoder_back/pallas_call | solution.py:138
  383.1 0.0 copy-start.7
  383.1 84.4 %attend_back.4 = (bf16[2,1024,256]{2,1,0:T(8,128)(2,1)}, bf16[2,2,1024,256]{3,2,1,0:T(8,128)(2,1)}, bf16[2,2,1024,256]{3,2,1,0:T(8,128)(2,1)}, bf16[1024,512]{1,0:T(8,128)(2,1)}) custom-call(s32[4]{0:T(128)} %get-tuple-element.131.span_ref, bf16[2,2,1024,256]{3,2,1,0:T(8,128)(2,1)} %get-tuple-element.64.q_ref, ...), custom_call_target="tpu_custom_call" | custom-call | flops 42949672960 | bytes 16777216 | tf_op jit(solution)/shard_map/attend_back/pallas_call | solution.py:747
  467.6 0.1 collective-permute-start.6
  467.7 1.3 collective-permute-start.3
  469.0 9.5 %collective-permute-start = (bf16[1024,512]{1,0:T(8,128)(2,1)}, bf16[1024,512]{1,0:T(8,128)(2,1)}, u32[]{:S(2)}, u32[]{:S(2)}) collective-permute-start(bf16[1024,512]{1,0:T(8,128)(2,1)} %get-tuple-element.73), channel_id=1, source_target_pairs={{0,0},{16,1},{2,2},{18,3},{4,4},{20,5},{6,6},{22,7},{8,8},{24,9},{... | collective-permute-start | bytes 3145736 | tf_op jit(solution)/shard_map/ppermute | solution.py:1448
  478.4 1.6 collective-permute-start.4
  480.1 2.3 collective-permute-start.2
  482.3 0.6 add.19.refs_9_
  483.0 1.1 broadcast_select_fusion
  484.0 0.0 collective-permute-done.6.refs_4_
  484.0 3.8 collective-permute-start.13
  487.8 8.7 %input_back.2 = (bf16[1024,512]{1,0:T(8,128)(2,1)}, bf16[2,2,768,256]{3,2,1,0:T(8,128)(2,1)}) custom-call(bf16[2,1024,512]{2,1,0:T(8,128)(2,1)} %get-tuple-element.63.refs_0_, f32[1024,512]{1,0:T(8,128)} %get-tuple-element.97.refs_1_, bf16[2,1024,256]{2,1,0:T(8,128)(2,1)} %get-tuple-element.101.refs_2_, ...), custom_call_target="tpu_custom_call" | custom-call | flops 3221225472 | bytes 9973760 | tf_op jit(solution)/shard_map/input_back/pallas_call | solution.py:138
  496.5 80.5 %attend_back.5 = (bf16[2,1024,256]{2,1,0:T(8,128)(2,1)}, bf16[2,2,1024,256]{3,2,1,0:T(8,128)(2,1)}, bf16[2,2,1024,256]{3,2,1,0:T(8,128)(2,1)}, bf16[2304,256]{1,0:T(8,128)(2,1)}) custom-call(s32[4]{0:T(128)} %get-tuple-element.130.span_ref, bf16[2,2,1024,256]{3,2,1,0:T(8,128)(2,1)} %get-tuple-element.64.q_ref, ...), custom_call_target="tpu_custom_call" | custom-call | flops 42949672960 | bytes 16777216 | tf_op jit(solution)/shard_map/attend_back/pallas_call | solution.py:747
  577.0 0.0 collective-permute-done.3
  577.0 0.1 collective-permute-start.7
  577.1 0.0 collective-permute-done.4
  577.1 1.3 select_bitcast_fusion.2
  578.5 0.0 collective-permute-done.2
  578.5 1.3 select_bitcast_fusion.3
  579.8 1.5 maximum_bitcast_fusion
  581.3 3.0 bitcast_convert_fusion
  584.3 0.2 fusion
  584.5 1.5 maximum_bitcast_fusion.1
  585.9 1.6 collective-permute-start.11
  587.6 3.0 collective-permute-start.9
  590.6 0.1 slice_convert_fusion
  590.7 0.0 copy-start.3
  590.7 1.3 copy-done.3
  592.0 9.6 %input_back.3 = (bf16[1024,512]{1,0:T(8,128)(2,1)}, bf16[2,2,896,256]{3,2,1,0:T(8,128)(2,1)}) custom-call(bf16[2,1024,512]{2,1,0:T(8,128)(2,1)} %get-tuple-element.63.refs_0_, f32[1024,512]{1,0:T(8,128)} %get-tuple-element.93.refs_1_, bf16[2,1024,256]{2,1,0:T(8,128)(2,1)} %get-tuple-element.106.refs_2_, ...), custom_call_target="tpu_custom_call" | custom-call | flops 3221225472 | bytes 9998336 | tf_op jit(solution)/shard_map/input_back/pallas_call | solution.py:138
  601.6 1.4 collective-permute-start.10
  603.0 57.2 %reduce_alone.1 = bf16[896,256]{1,0:T(8,128)(2,1)} custom-call(bf16[2,2,896,256]{3,2,1,0:T(8,128)(2,1)} %get-tuple-element.114.refs_0_), custom_call_target="tpu_custom_call" | custom-call | tf_op jit(solution)/shard_map/reduce_alone/pallas_call | solution.py:1113
  660.2 1.0 broadcast_select_fusion.3
  661.3 0.1 collective-permute-start.12
  661.4 1.0 slice.78
  662.4 0.9 maximum_bitcast_fusion.2
  663.3 9.5 %collective-permute-start.8 = (bf16[1024,512]{1,0:T(8,128)(2,1)}, bf16[1024,512]{1,0:T(8,128)(2,1)}, u32[]{:S(2)}, u32[]{:S(2)}) collective-permute-start(bf16[1024,512]{1,0:T(8,128)(2,1)} %get-tuple-element.112), channel_id=1, source_target_pairs={{0,0},{16,1},{2,2},{18,3},{4,4},{20,5},{6,6},{22,7},{8,8},{24,9},{... | collective-permute-start | bytes 3145736 | tf_op jit(solution)/shard_map/ppermute | solution.py:1448
  672.8 0.6 reshape.87
  673.4 0.1 broadcast_select_fusion.2
  673.5 0.1 pad_maximum_fusion
  673.5 1.3 convert.3
  674.8 0.0 collective-permute-done.11
  674.8 0.0 collective-permute-done.10
  674.8 1.3 select_bitcast_fusion
  676.2 1.3 select_bitcast_fusion.1
  677.5 2.3 maximum_convert_fusion
  (25 shorter events, 0.1 us)
Async XLA Ops:
  174.9 8.1 %collective-permute-start.1 = (bf16[2,2,1024,256]{3,2,1,0:T(8,128)(2,1)}, bf16[2,2,1024,256]{3,2,1,0:T(8,128)(2,1)S(1)}, u32[]{:S(2)}, u32[]{:S(2)}) collective-permute-start(bf16[2,2,1024,256]{3,2,1,0:T(8,128)(2,1)} %get-tuple-element.77.refs_0_), channel_id=1, source_target_pairs={{0,16},{16,0},{1,17},{17,1},{2,18},{18,2},{3,19},{19,3},{4,20},{20... | collective-permute-start | bytes 6291464 | tf_op jit(solution)/shard_map/ppermute | solution.py:1444
  183.0 1.3 copy-start.9
  334.3 19.1 %collective-permute-start.5 = (bf16[2,2,1024,256]{3,2,1,0:T(8,128)(2,1)}, bf16[2,2,1024,256]{3,2,1,0:T(8,128)(2,1)S(1)}, u32[]{:S(2)}, u32[]{:S(2)}) collective-permute-start(bf16[2,2,1024,256]{3,2,1,0:T(8,128)(2,1)} %get-tuple-element.87), channel_id=1, source_target_pairs={{0,16},{16,0},{1,17},{17,1},{2,18},{18,2},{3,19},{19,3},{4,20},{20... | collective-permute-start | bytes 6291464 | tf_op jit(solution)/shard_map/ppermute | solution.py:1444
  353.3 1.3 copy-start.10
  383.1 99.2 %copy-start.7 = (f32[3,2,512]{2,1,0:T(2,128)S(1)}, f32[3,2,512]{2,1,0:T(2,128)}, u32[]{:S(2)}) copy-start(f32[3,2,512]{2,1,0:T(2,128)} %get-tuple-element.110) | copy-start | bytes 36868
  383.1 99.2 %copy-start.8 = (f32[3,2,512]{2,1,0:T(2,128)S(1)}, f32[3,2,512]{2,1,0:T(2,128)}, u32[]{:S(2)}) copy-start(f32[3,2,512]{2,1,0:T(2,128)} %get-tuple-element.111) | copy-start | bytes 36868
  383.1 99.8 %copy-start = (bf16[1024,512]{1,0:T(8,128)(2,1)S(1)}, bf16[1024,512]{1,0:T(8,128)(2,1)}, u32[]{:S(2)}) copy-start(bf16[1024,512]{1,0:T(8,128)(2,1)} %get-tuple-element.117) | copy-start | bytes 3145732
  467.6 16.5 %collective-permute-start.6 = (bf16[2,2,1024,256]{3,2,1,0:T(8,128)(2,1)}, bf16[2,2,1024,256]{3,2,1,0:T(8,128)(2,1)S(1)}, u32[]{:S(2)}, u32[]{:S(2)}) collective-permute-start(bf16[2,2,1024,256]{3,2,1,0:T(8,128)(2,1)} %get-tuple-element.103), channel_id=1, source_target_pairs={{0,16},{16,0},{1,17},{17,1},{2,18},{18,2},{3,19},{19,3},{4,20},{20... | collective-permute-start | bytes 6291464 | tf_op jit(solution)/shard_map/ppermute | solution.py:1444
  467.7 109.3 %collective-permute-start.3 = (bf16[1024,512]{1,0:T(8,128)(2,1)}, bf16[1024,512]{1,0:T(8,128)(2,1)}, u32[]{:S(2)}, u32[]{:S(2)}) collective-permute-start(bf16[1024,512]{1,0:T(8,128)(2,1)} %get-tuple-element.73), channel_id=1, source_target_pairs={{1,0},{17,1},{3,2},{19,3},{5,4},{21,5},{7,6},{23,7},{9,8},{25,9},{... | collective-permute-start | bytes 3145736 | tf_op jit(solution)/shard_map/ppermute | solution.py:1448
  469.0 109.5 %collective-permute-start = (bf16[1024,512]{1,0:T(8,128)(2,1)}, bf16[1024,512]{1,0:T(8,128)(2,1)}, u32[]{:S(2)}, u32[]{:S(2)}) collective-permute-start(bf16[1024,512]{1,0:T(8,128)(2,1)} %get-tuple-element.73), channel_id=1, source_target_pairs={{0,0},{16,1},{2,2},{18,3},{4,4},{20,5},{6,6},{22,7},{8,8},{24,9},{... | collective-permute-start | bytes 3145736 | tf_op jit(solution)/shard_map/ppermute | solution.py:1448
  478.4 98.6 %collective-permute-start.4 = (bf16[1024,512]{1,0:T(8,128)(2,1)}, bf16[1024,512]{1,0:T(8,128)(2,1)}, u32[]{:S(2)}, u32[]{:S(2)}) collective-permute-start(bf16[1024,512]{1,0:T(8,128)(2,1)} %get-tuple-element.80), channel_id=1, source_target_pairs={{1,16},{17,17},{3,18},{19,19},{5,20},{21,21},{7,22},{23,23},{9,24}... | collective-permute-start | bytes 3145736 | tf_op jit(solution)/shard_map/ppermute | solution.py:1448
  480.1 98.4 %collective-permute-start.2 = (bf16[1024,512]{1,0:T(8,128)(2,1)}, bf16[1024,512]{1,0:T(8,128)(2,1)}, u32[]{:S(2)}, u32[]{:S(2)}) collective-permute-start(bf16[1024,512]{1,0:T(8,128)(2,1)} %get-tuple-element.80), channel_id=1, source_target_pairs={{0,16},{16,17},{2,18},{18,19},{4,20},{20,21},{6,22},{22,23},{8,24}... | collective-permute-start | bytes 3145736 | tf_op jit(solution)/shard_map/ppermute | solution.py:1448
  484.0 3.8 copy-start.4
  484.0 97.3 %collective-permute-start.13 = (bf16[1024,512]{1,0:T(8,128)(2,1)}, bf16[1024,512]{1,0:T(8,128)(2,1)}, u32[]{:S(2)}, u32[]{:S(2)}) collective-permute-start(bf16[1024,512]{1,0:T(8,128)(2,1)} %broadcast_select_fusion), channel_id=1, source_target_pairs={{0,16},{16,0},{1,17},{17,1},{2,18},{18,2},{3,19},{19,3},{4,20},{20... | collective-permute-start | bytes 3145736 | tf_op jit(solution)/shard_map/ppermute | solution.py:1444
  577.0 13.7 %collective-permute-start.7 = (bf16[2,2,1024,256]{3,2,1,0:T(8,128)(2,1)}, bf16[2,2,1024,256]{3,2,1,0:T(8,128)(2,1)S(1)}, u32[]{:S(2)}, u32[]{:S(2)}) collective-permute-start(bf16[2,2,1024,256]{3,2,1,0:T(8,128)(2,1)} %get-tuple-element.108), channel_id=1, source_target_pairs={{0,16},{16,0},{1,17},{17,1},{2,18},{18,2},{3,19},{19,3},{4,20},{20... | collective-permute-start | bytes 6291464 | tf_op jit(solution)/shard_map/ppermute | solution.py:1444
  579.8 1.5 copy-start.1
  584.5 6.1 copy-start.5
  585.9 88.9 %collective-permute-start.11 = (bf16[1024,512]{1,0:T(8,128)(2,1)}, bf16[1024,512]{1,0:T(8,128)(2,1)}, u32[]{:S(2)}, u32[]{:S(2)}) collective-permute-start(bf16[1024,512]{1,0:T(8,128)(2,1)} %get-tuple-element.113), channel_id=1, source_target_pairs={{1,16},{17,17},{3,18},{19,19},{5,20},{21,21},{7,22},{23,23},{9,24}... | collective-permute-start | bytes 3145736 | tf_op jit(solution)/shard_map/ppermute | solution.py:1448
  587.6 88.6 %collective-permute-start.9 = (bf16[1024,512]{1,0:T(8,128)(2,1)}, bf16[1024,512]{1,0:T(8,128)(2,1)}, u32[]{:S(2)}, u32[]{:S(2)}) collective-permute-start(bf16[1024,512]{1,0:T(8,128)(2,1)} %get-tuple-element.113), channel_id=1, source_target_pairs={{0,16},{16,17},{2,18},{18,19},{4,20},{20,21},{6,22},{22,23},{8,24}... | collective-permute-start | bytes 3145736 | tf_op jit(solution)/shard_map/ppermute | solution.py:1448
  590.7 1.3 copy-start.3
  601.6 58.6 %copy-start.6 = (bf16[2304,256]{1,0:T(8,128)(2,1)S(1)}, bf16[2304,256]{1,0:T(8,128)(2,1)}, u32[]{:S(2)}) copy-start(bf16[2304,256]{1,0:T(8,128)(2,1)} %get-tuple-element.115) | copy-start | bytes 3538948
  601.6 73.2 %collective-permute-start.10 = (bf16[1024,512]{1,0:T(8,128)(2,1)}, bf16[1024,512]{1,0:T(8,128)(2,1)}, u32[]{:S(2)}, u32[]{:S(2)}) collective-permute-start(bf16[1024,512]{1,0:T(8,128)(2,1)} %get-tuple-element.112), channel_id=1, source_target_pairs={{1,0},{17,1},{3,2},{19,3},{5,4},{21,5},{7,6},{23,7},{9,8},{25,9},{... | collective-permute-start | bytes 3145736 | tf_op jit(solution)/shard_map/ppermute | solution.py:1448
  661.3 11.5 %copy-start.2 = (bf16[896,256]{1,0:T(8,128)(2,1)S(1)}, bf16[896,256]{1,0:T(8,128)(2,1)}, u32[]{:S(2)}) copy-start(bf16[896,256]{1,0:T(8,128)(2,1)} %reduce_alone.1) | copy-start | bytes 1376260
  661.3 12.1 %collective-permute-start.12 = (bf16[768,256]{1,0:T(8,128)(2,1)S(1)}, bf16[768,256]{1,0:T(8,128)(2,1)S(1)}, u32[]{:S(2)}, u32[]{:S(2)}) collective-permute-start(bf16[768,256]{1,0:T(8,128)(2,1)S(1)} %broadcast_select_fusion.3), channel_id=1, source_target_pairs={{0,16},{16,0},{1,17},{17,1},{2,18},{18,2},{3,19},{19,3},{4,20},{20... | collective-permute-start | bytes 1179656 | tf_op jit(solution)/shard_map/ppermute | solution.py:1444
  663.3 12.9 %collective-permute-start.8 = (bf16[1024,512]{1,0:T(8,128)(2,1)}, bf16[1024,512]{1,0:T(8,128)(2,1)}, u32[]{:S(2)}, u32[]{:S(2)}) collective-permute-start(bf16[1024,512]{1,0:T(8,128)(2,1)} %get-tuple-element.112), channel_id=1, source_target_pairs={{0,0},{16,1},{2,2},{18,3},{4,4},{20,5},{6,6},{22,7},{8,8},{24,9},{... | collective-permute-start | bytes 3145736 | tf_op jit(solution)/shard_map/ppermute | solution.py:1448

commit v3 on v2

--- a/solution.py
+++ b/solution.py
@@ -512,27 +512,31 @@
     sums = [((parts, 3, width, part), BF16), ((3, 2, width), F32)]
     if paired is not None:
         half = 3 * width // 2
-        extra = PAIR if paired else 0
-        finals = [((2, parts, half + extra, part), BF16)]
+        shape = (4 * half // 2 + 2 * PAIR, PAIR) if paired else (half, part)
+        finals = [((2, parts, *shape), BF16)]
 
         def finish(ins, totals, outs):
             for k in range(parts):
-                both = totals[0][k].reshape(2 * half, part).astype(BF16)
+                both = totals[0][k].reshape(2 * half, part)
                 for core in range(2):
-                    outs[0][core, k, :half, :] = both[core * half : (core + 1) * half]
-            if extra:
+                    own = both[core * half : (core + 1) * half]
+                    if paired:
+                        column_blocks(own, outs[0], core, k, 0)
+                    else:
+                        outs[0][core, k] = own.astype(BF16)
+            if paired:
                 sides = [ins[-2][...] + totals[1][...], ins[-1][...]]
                 for core, table in enumerate(sides):
                     lines = [
-                        table[slot, i : i + 1, h * part : (h + 1) * part]
+                        table[slot, i : i + 1, h * PAIR : (h + 1) * PAIR]
                         for slot in range(3)
                         for i in range(2)
-                        for h in range(width // part)
+                        for h in range(width // PAIR)
                     ]
-                    lines.append(jnp.zeros((extra - len(lines), part), F32))
+                    lines.append(jnp.zeros((2 * PAIR - len(lines), PAIR), F32))
                     lines = jnp.concatenate(lines, axis=0).astype(BF16)
                     for k in range(parts):
-                        outs[0][core, k, half:, :] = lines
+                        outs[0][core, k, 2 * half :, :] = lines
 
     else:
         finals, finish, paired = None, None, []
@@ -584,7 +588,7 @@
 
 def attend(query, kv_pieces, span, block, carrier=None):
     query, kv_pieces = at(query), [at(piece) for piece in kv_pieces]
-    carrier = carrier or Carrier()
+    carrier = carrier or Carry()
     parts, rows, part = query.shape
     per_part = part // PAIR
     pairs = parts * per_part
@@ -653,7 +657,7 @@
 def attend_back(query, kv_pieces, mix, mix_grad, lse, span, block, chunk, carrier=None):
     query, kv_pieces = at(query), [at(piece) for piece in kv_pieces]
     mix, mix_grad = at(mix), at(mix_grad)
-    carrier = carrier or Carrier()
+    carrier = carrier or Carry()
     parts, rows, part = query.shape
     per_part = part // PAIR
     pairs = parts * per_part
@@ -783,7 +787,22 @@
     return lax.axis_index("section"), lax.axis_index("dp"), lax.axis_index("tensor")
 
 
-def remote(source, target, sent, landed, **where):
+def dp_peer(group, level):
+    return group + (1 << level) * (1 - 2 * ((group // (1 << level)) % 2))
+
+
+def where_is(peer):
+    section, group, tensor = spots()
+    if peer == "near":
+        return {"section": 1 - section}
+    if peer == "over":
+        return {"tensor": 1 - tensor}
+    if peer == "cross":
+        return {"section": 1 - section, "tensor": 1 - tensor}
+    return {"dp": dp_peer(group, peer)}
+
+
+def remote(source, target, sent, landed, where):
     return pltpu.make_async_remote_copy(
         src_ref=source,
         dst_ref=target,
@@ -798,176 +817,280 @@
     barrier = pltpu.get_barrier_semaphore()
     for peer in peers:
         pl.semaphore_signal(
-            barrier, inc=1, device_id=peer, device_id_type=pl.DeviceIdType.MESH
+            barrier, inc=1, device_id=where_is(peer), device_id_type=pl.DeviceIdType.MESH
         )
     pl.semaphore_wait(barrier, len(peers))
 
 
-def group_peers():
-    section, _, tensor = spots()
-    return [
-        {"section": 1 - section},
-        {"tensor": 1 - tensor},
-        {"section": 1 - section, "tensor": 1 - tensor},
-    ]
-
-
-class Carrier:
-    ins, outs, scratch, params = (), [], [], {}
+class Carry:
+    def __init__(self, tasks=(), collective=None):
+        self.tasks = list(tasks)
+        self.ins = [a for task in self.tasks for a in task.ins]
+        self.outs = [a for task in self.tasks for a in task.outs]
+        self.scratch = [a for task in self.tasks for a in task.scratch]
+        self.peers = []
+        for task in self.tasks:
+            self.peers += [peer for peer in task.peers if peer not in self.peers]
+        self.params = (
+            dict(collective_id=collective, has_side_effects=True) if self.tasks else {}
+        )
 
     def run(self, step, steps, ins, outs, scratch):
-        pass
-
-
-class SpreadRows:
-    sems = [pltpu.SemaphoreType.DMA((2,)), pltpu.SemaphoreType.DMA((2,)), pltpu.SemaphoreType.DMA]
-
-    def __init__(self, source, target, sems):
-        self.source, self.target = source, target
+        if not self.tasks:
+            return
+
+        @pl.when(step == 0)
+        def _():
+            greet(self.peers)
+
+        for task in self.tasks:
+            i, o, s = len(task.ins), len(task.outs), len(task.scratch)
+            task.run(step, steps, ins[:i], outs[:o], scratch[:s])
+            ins, outs, scratch = ins[i:], outs[o:], scratch[s:]
+
+
+GROUP = ["near", "over", "cross"]
+
+
+class RowCopies:
+    def __init__(self, copies, arrivals, sems, room=None):
+        self.copies, self.arrivals, self.room = copies, arrivals, room
         self.sent, self.landed, self.kept = sems
 
-    def copy(self, row):
+    def copy(self, i):
+        source, target, slot, section, tensor, _ = self.copies[i]
+        return remote(
+            source,
+            target,
+            self.sent.at[i],
+            self.landed.at[slot],
+            {"section": section, "tensor": tensor},
+        )
+
+    def keep(self, i):
+        source, target = self.copies[i][:2]
+        return pltpu.make_async_copy(
+            source, target if self.room is None else self.room, self.kept
+        )
+
+    def keep_on(self):
+        for i in range(len(self.copies)):
+
+            @pl.when(self.here(i, True))
+            def _():
+                self.keep(i).wait()
+                pltpu.make_async_copy(self.room, self.copies[i][1], self.kept).start()
+
+    def here(self, i, stays):
         section, _, tensor = spots()
-        return remote(
-            self.source.at[row],
-            self.target.at[section],
-            self.sent.at[row],
-            self.landed.at[section],
-            section=tensor,
-            tensor=row,
-        )
-
-    def keep(self, row):
-        section, _, _ = spots()
-        return pltpu.make_async_copy(self.source.at[row], self.target.at[section], self.kept)
+        _, _, _, to_section, to_tensor, condition = self.copies[i]
+        own = (to_section == section) & (to_tensor == tensor)
+        return condition & (own if stays else jnp.logical_not(own))
 
     def start(self):
+        for i in range(len(self.copies)):
+
+            @pl.when(self.here(i, True))
+            def _():
+                self.keep(i).start()
+
+            @pl.when(self.here(i, False))
+            def _():
+                self.copy(i).start()
+
+    def wait_sent(self):
+        for i in range(len(self.copies)):
+
+            @pl.when(self.here(i, False))
+            def _():
+                self.copy(i).wait_send()
+
+    def wait_arrival(self, i):
         section, _, tensor = spots()
-        for row in range(2):
-            stays = (section == tensor) & (tensor == row)
-
-            @pl.when(stays)
-            def _():
-                self.keep(row).start()
-
-            @pl.when(jnp.logical_not(stays))
-            def _():
-                self.copy(row).start()
-
-    def wait_side(self, side):
-        section, _, tensor = spots()
-        stays = (section == tensor) & (section == side)
-
-        @pl.when(stays)
+        target, slot, from_section, from_tensor, condition = self.arrivals[i]
+        own = (from_section == section) & (from_tensor == tensor)
+        source = self.copies[0][0]
+
+        @pl.when(condition & own)
         def _():
-            self.keep(side).wait()
-
-        @pl.when(jnp.logical_not(stays))
+            stays = source if self.room is None else self.room
+            pltpu.make_async_copy(stays, target, self.kept).wait()
+
+        @pl.when(condition & jnp.logical_not(own))
         def _():
             remote(
-                self.source.at[0],
-                self.target.at[side],
-                self.sent.at[0],
-                self.landed.at[side],
-                section=tensor,
-                tensor=0,
+                source, target, self.sent.at[0], self.landed.at[slot], where_is("near")
             ).wait_recv()
 
-    def wait_sent(self):
-        section, _, tensor = spots()
-        for row in range(2):
-            @pl.when(jnp.logical_not((section == tensor) & (tensor == row)))
-            def _():
-                self.copy(row).wait_send()
-
-
-class SpreadWeight:
-    sems = [pltpu.SemaphoreType.DMA((7,))]
-
-    def __init__(self, source, target, sems):
-        section, _, tensor = spots()
-        (sem,) = sems
-        self.kept = pltpu.make_async_copy(source, target.at[section, 0], sem.at[0])
-        self.over = remote(source, target.at[section, 1], sem.at[1], sem.at[2], tensor=1 - tensor)
-        self.near = remote(source, target.at[section, 0], sem.at[3], sem.at[4], section=1 - section)
+
+ROW_SEMS = [
+    pltpu.SemaphoreType.DMA((2,)),
+    pltpu.SemaphoreType.DMA((2,)),
+    pltpu.SemaphoreType.DMA,
+]
+
+
+def spread_rows(source, target, sems, sides=(0, 1), room=None):
+    section, _, tensor = spots()
+    yes = section >= 0
+    sends = yes if len(sides) == 2 else section == sides[0]
+    copies = [
+        (source.at[row], target.at[section], section, tensor, row, sends) for row in range(2)
+    ]
+    arrivals = [(target.at[side], side, side, section, yes) for side in sides]
+    return RowCopies(copies, arrivals, sems, room)
+
+
+def return_rows(source, target, sems, side, room):
+    section, _, tensor = spots()
+    copies = [(source, target.at[tensor], tensor, side, section, section >= 0)]
+    arrivals = [(target.at[row], row, tensor, row, section == side) for row in range(2)]
+    return RowCopies(copies, arrivals, sems, room)
+
+
+class SpreadRows:
+    peers = GROUP
+
+    def __init__(self, array, sides):
+        self.ins, self.sides = [array], sides
+        self.outs = [jax.ShapeDtypeStruct(array.shape, array.dtype)]
+        self.scratch = ROW_SEMS + [pltpu.VMEM(array.shape[-2:], array.dtype)]
+
+    def make(self, ins, outs, scratch):
+        return spread_rows(ins[0], outs[0], scratch[:3], self.sides, scratch[3])
+
+    def run(self, step, steps, ins, outs, scratch):
+        @pl.when(step == 0)
+        def _():
+            self.make(ins, outs, scratch).start()
+
+        @pl.when(step == 2)
+        def _():
+            self.make(ins, outs, scratch).keep_on()
+
+        @pl.when(step == steps - 1)
+        def _():
+            rows = self.make(ins, outs, scratch)
+            for i in range(len(rows.arrivals)):
+                rows.wait_arrival(i)
+            rows.wait_sent()
+
+
+class ReturnRows(SpreadRows):
+    def __init__(self, array, side):
+        self.ins, self.side = [array], side
+        self.outs = [jax.ShapeDtypeStruct((2, *array.shape), array.dtype)]
+        self.scratch = ROW_SEMS + [pltpu.VMEM(array.shape, array.dtype)]
+
+    def make(self, ins, outs, scratch):
+        return return_rows(ins[0], outs[0], scratch[:3], self.side, scratch[3])
+
+
+class WeightCopies:
+    sems = [pltpu.SemaphoreType.DMA((11,))]
+
+    def __init__(self, source, target, sem, room=None):
+        section, group, _ = spots()
+        count = source.shape[0] // 2
+        bit = group % 2
+        own = pl.ds(pl.multiple_of(bit * count, 16), count)
+        other = pl.ds(pl.multiple_of((1 - bit) * count, 16), count)
+        here = target.at[section, 1]
+        stays = target.at[section, 0]
+        if room is None:
+            self.kept = pltpu.make_async_copy(source, stays, sem.at[0])
+        else:
+            self.first = pltpu.make_async_copy(source, room, sem.at[0])
+            self.kept = pltpu.make_async_copy(room, stays, sem.at[0])
+        self.room = room
+        self.near = remote(
+            source, target.at[section, 0], sem.at[1], sem.at[2], where_is("near")
+        )
+        self.over = remote(source.at[own], here.at[own], sem.at[3], sem.at[4], where_is("over"))
+        self.side = remote(here.at[own], here.at[own], sem.at[5], sem.at[6], where_is(0))
         self.onward = remote(
-            target.at[section, 1],
-            target.at[section, 1],
-            sem.at[5],
-            sem.at[6],
-            section=1 - section,
+            here.at[own], here.at[own], sem.at[7], sem.at[8], where_is("near")
+        )
+        self.last = remote(
+            here.at[other], here.at[other], sem.at[9], sem.at[10], where_is("near")
         )
 
     def start(self):
         self.over.start()
+        self.near.start()
+        if self.room is None:
+            self.kept.start()
+        else:
+            self.first.start()
+
+    def keep_on(self):
+        self.first.wait()
         self.kept.start()
-        self.near.start()
 
     def forward(self):
         self.over.wait_recv()
+        self.side.start()
         self.onward.start()
+
+    def forward_last(self):
+        self.side.wait_recv()
+        self.last.start()
 
     def finish(self):
         self.kept.wait()
         self.near.wait()
         self.over.wait_send()
+        self.side.wait_send()
         self.onward.wait()
-
-
-class Spread(Carrier):
-    def __init__(self, weights, forwards, rows, collective):
-        self.ins = [*weights, *rows]
-        self.weights, self.rows, self.forwards = len(weights), len(rows), forwards
-        self.outs = [jax.ShapeDtypeStruct((2, 2, *w.shape), w.dtype) for w in weights] + [
-            jax.ShapeDtypeStruct(r.shape, r.dtype) for r in rows
-        ]
-        self.scratch = SpreadWeight.sems * len(weights) + SpreadRows.sems * len(rows)
-        self.params = dict(collective_id=collective, has_side_effects=True)
+        self.last.wait()
+
+
+class SpreadWeight:
+    peers = ["near", "over", 0]
+
+    def __init__(self, weight, forward, last):
+        self.ins = [weight]
+        self.outs = [jax.ShapeDtypeStruct((2, 2, *weight.shape), weight.dtype)]
+        self.scratch = WeightCopies.sems + [pltpu.VMEM(weight.shape, weight.dtype)]
+        self.steps = forward, last
 
     def run(self, step, steps, ins, outs, scratch):
-        def weight(i):
-            return SpreadWeight(ins[i], outs[i], scratch[i : i + 1])
-
-        def row(i):
-            spot = self.weights + i
-            sems = scratch[self.weights + 3 * i : self.weights + 3 * i + 3]
-            return SpreadRows(ins[spot], outs[spot], sems)
+        def copies():
+            return WeightCopies(ins[0], outs[0], *scratch)
 
         @pl.when(step == 0)
         def _():
-            greet(group_peers())
-            for i in range(self.weights):
-                weight(i).start()
-            for i in range(self.rows):
-                row(i).start()
-
-        for i, when in enumerate(self.forwards):
-
-            @pl.when(step == when)
-            def _():
-                weight(i).forward()
+            copies().start()
+
+        @pl.when(step == 2)
+        def _():
+            copies().keep_on()
+
+        @pl.when(step == self.steps[0])
+        def _():
+            copies().forward()
+
+        @pl.when(step == self.steps[1])
+        def _():
+            copies().forward_last()
 
         @pl.when(step == steps - 1)
         def _():
-            for i in range(self.weights):
-                weight(i).finish()
-            for i in range(self.rows):
-                row(i).wait_side(0)
-                row(i).wait_side(1)
-                row(i).wait_sent()
-
-
-class Reduce(Carrier):
-    def __init__(self, sources, chunk, collective):
+            copies().finish()
+
+
+class Reduce:
+    def __init__(self, sources, chunk, spacing, patience):
         self.ins = list(sources)
-        self.chunk = chunk
+        self.chunk, self.spacing, self.patience = chunk, spacing, patience
         self.places = [
             (i, row) for i, s in enumerate(sources) for row in range(0, s.shape[2], chunk)
         ]
         self.count = len(self.places)
         self.levels = lax.axis_size("dp").bit_length() - 1
+        self.peers = ["near", "over", *range(self.levels)]
         width = sources[0].shape[3]
-        self.outs = [jax.ShapeDtypeStruct((self.count * chunk, width), BF16)]
+        self.outs = [jax.ShapeDtypeStruct((self.count * chunk, width), BF16)] * 2
 
         def room(*shape):
             return pltpu.VMEM((self.count, *shape, width), BF16)
@@ -975,10 +1098,9 @@
         halves = [room(chunk >> (level + 1)) for level in range(self.levels)]
         self.scratch = [room(2, chunk), room(2, chunk), room(chunk), room(chunk)]
         self.scratch += halves + halves
-        self.scratch += [pltpu.SemaphoreType.DMA((2 + 2 * (2 + 2 * self.levels), self.count))]
-        self.params = dict(collective_id=collective, has_side_effects=True)
-        self.stages = 4 + 2 * self.levels
-        self.steps = self.count + self.stages - 1
+        self.scratch += [pltpu.SemaphoreType.DMA((2 + 2 * (3 + 2 * self.levels), self.count))]
+        self.last = 1 + patience + 2 * self.levels
+        self.steps = self.last + 1 + spacing * (self.count - 1)
 
     def run(self, step, steps, ins, outs, scratch):
         chunk, levels = self.chunk, self.levels
@@ -988,7 +1110,6 @@
         sems = scratch[4 + 2 * levels]
         section, group, tensor = spots()
         bits = [(group // (1 << level)) % 2 for level in range(levels)]
-        peers = [group + (1 << level) * (1 - 2 * bits[level]) for level in range(levels)]
         begins = [0]
         for level in range(levels):
             begins.append(begins[level] + bits[level] * (chunk >> (level + 1)))
@@ -1003,73 +1124,75 @@
         def pair(kind, c):
             return sems.at[2 + 2 * kind, c], sems.at[3 + 2 * kind, c]
 
-        def load(c):
-            i, row = self.places[c]
+        def load(c, place):
+            i, row = place
             return pltpu.make_async_copy(
                 ins[i].at[section, :, pl.ds(row, chunk), :], own.at[c], sems.at[0, c]
             )
 
-        def cross(c, place=None):
-            i, row = self.places[0] if place is None else place
+        def cross(c, place):
+            i, row = place
             return remote(
                 ins[i].at[1 - section, :, pl.ds(row, chunk), :],
                 chip.at[c],
                 *pair(0, c),
-                section=1 - section,
+                where_is("near"),
             )
 
         def over(c):
-            return remote(own.at[c, 1], other.at[c], *pair(1, c), tensor=1 - tensor)
+            return remote(own.at[c, 1], other.at[c], *pair(1, c), where_is("over"))
 
         def halve(level, c):
             return remote(
                 own.at[c, 0, gives(level), :],
                 halves[level].at[c],
-                *pair(2 + level, c),
-                dp=peers[level],
+                *pair(3 + level, c),
+                where_is(level),
             )
 
         def double(level, c):
             return remote(
                 full.at[c, keeps(level), :],
                 doubles[level].at[c],
-                *pair(2 + levels + level, c),
-                dp=peers[level],
+                *pair(3 + levels + level, c),
+                where_is(level),
             )
+
+        def rows_of(c):
+            return pl.ds(pl.multiple_of(c * chunk, 16), chunk)
 
         def store(c):
             return pltpu.make_async_copy(
-                full.at[c],
-                outs[0].at[pl.ds(pl.multiple_of(c * chunk, 16), chunk), :],
-                sems.at[1, c],
+                full.at[c], outs[0].at[rows_of(c), :], sems.at[1, c]
             )
 
-        def added(a, b):
-            return (a.astype(F32) + b.astype(F32)).astype(BF16)
+        def tell(c):
+            return remote(
+                full.at[c], outs[1].at[rows_of(c), :], *pair(2, c), where_is("near")
+            )
 
         def stage(number, c):
             if number == 1:
-                pltpu.make_async_copy(
-                    ins[0].at[section, :, pl.ds(0, chunk), :], own.at[c], sems.at[0, c]
-                ).wait()
-                cross(c).wait()
-                own[c] = added(own[c], chip[c])
+                load(c, self.places[0]).wait()
+                cross(c, self.places[0]).wait()
+                own[c] = own[c] + chip[c]
                 over(c).start()
             elif number == 2:
                 over(c).wait()
-                own[c, 0] = added(own[c, 0], other[c])
+                own[c, 0] = own[c, 0] + other[c]
                 halve(0, c).start()
             elif number < 3 + levels:
                 level = number - 3
                 halve(level, c).wait()
                 mine = keeps(level)
+                total = own[c, 0, mine, :] + halves[level][c]
                 if level < levels - 1:
-                    own[c, 0, mine, :] = added(own[c, 0, mine, :], halves[level][c])
+                    own[c, 0, mine, :] = total
                     halve(level + 1, c).start()
                 else:
-                    full[c, mine, :] = added(own[c, 0, mine, :], halves[level][c])
+                    full[c, mine, :] = total
                     double(level, c).start()
-            elif number < 3 + 2 * levels:
+            else:
                 level = levels - 1 - (number - 3 - levels)
                 double(level, c).wait()
                 full[c, gives(level), :] = doubles[level][c]
@@ -1077,48 +1200,50 @@
                     double(level - 1, c).start()
                 else:
                     store(c).start()
-            else:
-                store(c).wait()
-
-        @pl.when(step == 0)
-        def _():
-            greet(
-                [{"section": 1 - section}, {"tensor": 1 - tensor}]
-                + [{"dp": peer} for peer in peers]
-            )
-
-        for number in reversed(range(1, self.stages)):
-            c = step - number
-
-            @pl.when((c >= 0) & (c < self.count))
+                    tell(c).start()
+
+        for number in reversed(range(1, 3 + 2 * levels)):
+            since = step - (number if number == 1 else number - 1 + self.patience)
+            c = since // self.spacing
+            due = (since >= 0) & (c < self.count)
+            if self.spacing > 1:
+                due = due & (since % self.spacing == 0)
+
+            @pl.when(due)
             def _():
                 stage(number, c)
 
         for c, place in enumerate(self.places):
 
-            @pl.when(step == c)
+            @pl.when(step == c * self.spacing)
             def _():
-                load(c).start()
+                load(c, place).start()
                 cross(c, place).start()
 
-
-def reduce_alone(sources, chunk, collective):
-    carrier = Reduce(sources, chunk, collective)
+        @pl.when(step == steps - 1)
+        def _():
+            for c in range(self.count):
+                store(c).wait()
+                tell(c).wait()
+
+
+def carry_alone(tasks, steps, collective):
+    carrier = Carry(tasks, collective)
 
     def kernel(*refs):
-        n = len(carrier.ins)
-        carrier.run(pl.program_id(0), carrier.steps, refs[:n], refs[n : n + 1], refs[n + 1 :])
+        i, o = len(carrier.ins), len(carrier.ins) + len(carrier.outs)
+        carrier.run(pl.program_id(0), steps, refs[:i], refs[i:o], refs[o:])
 
     hold = pl.BlockSpec(memory_space=pl.ANY)
     return pl.pallas_call(
         kernel,
-        grid=(carrier.steps,),
+        grid=(steps,),
         in_specs=[hold] * len(carrier.ins),
-        out_specs=hold,
-        out_shape=carrier.outs[0],
+        out_specs=[hold] * len(carrier.outs),
+        out_shape=carrier.outs,
         scratch_shapes=carrier.scratch,
         compiler_params=pltpu.CompilerParams(vmem_limit_bytes=VMEM, **carrier.params),
-        name="reduce_alone",
+        name="carry_alone",
     )(*carrier.ins)
 
 
@@ -1130,23 +1255,22 @@
     def kernel(tokens_ref, qkv_ref, norm_ref, *refs):
         x_out, w_out, n_out, q_out, own_out, other_out = refs[:6]
         x, low, w, n, q, kv = refs[6:12]
-        row_sems, weight_sems, norm_sems, load_sems, store_sems, kv_sems = (
+        row_sems, weight_sems, norm_sems, store_sems, kv_sems = (
             refs[12:15],
             refs[15:16],
             refs[16],
             refs[17],
             refs[18],
-            refs[19],
         )
         section, _, _ = spots()
-        greet(group_peers())
-        rows_in = SpreadRows(tokens_ref, x, row_sems)
-        weight = SpreadWeight(qkv_ref, w, weight_sems)
+        greet([*GROUP, 0])
+        rows_in = spread_rows(tokens_ref, x, row_sems)
+        weight = WeightCopies(qkv_ref, w, *weight_sems)
+        weight.start()
         rows_in.start()
-        weight.start()
         norm_kept = pltpu.make_async_copy(norm_ref, n.at[section], norm_sems.at[0])
         norm_near = remote(
-            norm_ref, n.at[section], norm_sems.at[1], norm_sems.at[2], section=1 - section
+            norm_ref, n.at[section], norm_sems.at[1], norm_sems.at[2], where_is("near")
         )
         norm_kept.start()
         norm_near.start()
@@ -1163,9 +1287,13 @@
             def step(i, carry):
                 own = pl.ds(pl.multiple_of(i * block, block), block)
                 rows_low = low[own, :] if side == 0 else x[1, own, :]
-                q[side, k, own, :] = (dot_nn(rows_low, w[side, k, 0]) * score).astype(BF16)
-                kv[side, k, 0, own, :] = dot_nn(rows_low, w[side, k, 1]).astype(BF16)
-                kv[side, k, 1, own, :] = dot_nn(rows_low, w[side, k, 2]).astype(BF16)
+
+                def product(m):
+                    return dot_nn(rows_low, w[side, k, m * width : (m + 1) * width, :])
+
+                q[side, k, own, :] = (product(0) * score).astype(BF16)
+                kv[side, k, 0, own, :] = product(1).astype(BF16)
+                kv[side, k, 1, own, :] = product(2).astype(BF16)
                 return carry
 
             lax.fori_loop(0, rows // block, step, 0)
@@ -1175,7 +1303,7 @@
                 other_out.at[side, k],
                 kv_sems.at[spot],
                 kv_sems.at[spot + 1],
-                section=1 - section,
+                where_is("near"),
             )
             copy.start()
             kv_copies.append(copy)
@@ -1185,7 +1313,11 @@
         norm_kept.wait()
         norm_near.wait()
         save(n, n_out)
-        rows_in.wait_side(0)
+        weight.forward()
+        weight.forward_last()
+        weight.finish()
+        save(w, w_out)
+        rows_in.wait_arrival(0)
         save(x.at[0], x_out.at[0])
 
         def settle(i, carry):
@@ -1195,17 +1327,11 @@
             return carry
 
         lax.fori_loop(0, rows // block, settle, 0)
-        weight.kept.wait()
-        weight.near.wait()
         project(0, 0)
-        rows_in.wait_side(1)
+        project(0, 1)
+        rows_in.wait_arrival(1)
         save(x.at[1], x_out.at[1])
         project(1, 0)
-        weight.forward()
-        weight.over.wait_send()
-        weight.onward.wait()
-        save(w, w_out)
-        project(0, 1)
         project(1, 1)
         rows_in.wait_sent()
         for copy in kv_copies + stores:
@@ -1226,11 +1352,10 @@
         out_shape=[jax.ShapeDtypeStruct(*s) for s in shapes + shapes[-1:]],
         scratch_shapes=[pltpu.VMEM(*shapes[0]), pltpu.VMEM((rows, width), BF16)]
         + [pltpu.VMEM(*s) for s in shapes[1:]]
-        + SpreadRows.sems
-        + SpreadWeight.sems
+        + ROW_SEMS
+        + WeightCopies.sems
         + [
             pltpu.SemaphoreType.DMA((3,)),
-            pltpu.SemaphoreType.DMA((1,)),
             pltpu.SemaphoreType.DMA((12,)),
             pltpu.SemaphoreType.DMA((8,)),
         ],
@@ -1443,13 +1568,8 @@
     def swap(value):
         return lax.ppermute(value, "section", [(0, 1), (1, 0)])
 
-    def give_back(value, side):
-        return [
-            lax.ppermute(
-                value, ("section", "tensor"), [(2 * p + row, 2 * side + p) for p in range(2)]
-            )
-            for row in range(2)
-        ]
+    def flat(weight):
+        return weight.reshape(-1, weight.shape[-1])
 
     def span_of(query_side, key_side):
         own = lax.dynamic_index_in_dim(lengths, tensor, 1, keepdims=False)
@@ -1461,7 +1581,8 @@
         return jnp.stack([begin, end, section * rows, (1 - section) * rows]).astype(jnp.int32)
 
     spans = span_of(0, 0), span_of(1, 1), span_of(1, 0)
-    x, qkv, norm, q, kv_own, kv_other = open_up(tokens[0], self_qkv[0], norms[0], block, 1)
+    x, qkv, norm, q, kv_own, kv_other = open_up(tokens[0], flat(self_qkv), norms[0], block, 1)
+    qkv = qkv.reshape(2, 2, *self_qkv.shape[1:])
 
     def parts(weight, side):
         return [At(weight, side, k) for k in range(2)]
@@ -1469,11 +1590,27 @@
     enc_x, dec_x, enc_norm_in, dec_norm_in = At(x, 0), At(x, 1), At(norm, 0), At(norm, 1)
     enc_q, dec_q = At(q, 0), At(q, 1)
     enc_kv, dec_kv = [[At(kv_own, side), At(kv_other, side)] for side in range(2)]
-    enc_mix, enc_lse, out, up = attend(
-        enc_q, enc_kv, spans[0], query_block, Spread([self_out[0], ffn_up[0]], [5, 14], [], 2)
-    )
-    dec_mix, dec_lse, cross, down = attend(
-        dec_q, dec_kv, spans[1], query_block, Spread([cross_proj[0], ffn_down[0]], [7, 14], [], 3)
+    enc_mix, enc_lse, out, cross, up = attend(
+        enc_q,
+        enc_kv,
+        spans[0],
+        query_block,
+        Carry(
+            [
+                SpreadWeight(self_out[0], 3, 5),
+                SpreadWeight(flat(cross_proj), 7, 10),
+                SpreadWeight(ffn_up[0], 12, 15),
+            ],
+            2,
+        ),
+    )
+    cross = cross.reshape(2, 2, *cross_proj.shape[1:])
+    dec_mix, dec_lse, down, dec_cot = attend(
+        dec_q,
+        dec_kv,
+        spans[1],
+        query_block,
+        Carry([SpreadWeight(ffn_down[0], 8, 14), SpreadRows(cotangent[0], (1,))], 3),
     )
     encoded, memory, enc_first, enc_third = encoder_forward(
         enc_x,
@@ -1489,13 +1626,17 @@
     cross_q, dec_first = decoder_middle(
         dec_x, dec_mix, dec_norm_in, parts(out, 1), parts(cross, 1), block
     )
-    cross_mix, cross_lse, cot = attend(
-        cross_q, memory, spans[2], query_block, Spread([], [], [cotangent[0]], 4)
+    cross_mix, cross_lse, enc_cot, encoded = attend(
+        cross_q,
+        memory,
+        spans[2],
+        query_block,
+        Carry([SpreadRows(cotangent[0], (0,)), ReturnRows(encoded, 0)], 4),
     )
     decoded, second_grad, cross_mix_grad, cross_out_grad, ffn_dec, dec_norm = decoder_turn(
         dec_first,
         cross_mix,
-        At(cot, 1),
+        At(dec_cot, 1),
         dec_norm_in,
         parts(cross, 1),
         parts(up, 1),
@@ -1503,7 +1644,7 @@
         block,
         True,
     )
-    cross_q_grad, memory_grads, (ffn_dec,) = attend_back(
+    cross_q_grad, memory_grads, (ffn_dec, ffn_dec_other, decoded) = attend_back(
         cross_q,
         memory,
         cross_mix,
@@ -1512,10 +1653,9 @@
         spans[2],
         query_block,
         chunk,
-        Reduce([ffn_dec], 256, 5),
+        Carry([Reduce([ffn_dec], 256, 2, 2), ReturnRows(decoded, 1)], 5),
     )
     memory_grads = [memory_grads[0], swap(memory_grads[1])]
-    encoded, decoded = give_back(encoded, 0), give_back(decoded, 1)
     dec_first_grad, dec_mix_grad, cross_query_grad, dec_out, step = decoder_middle_back(
         dec_first,
         dec_mix,
@@ -1532,7 +1672,7 @@
         enc_third,
         enc_mix,
         memory_grads,
-        At(cot, 0),
+        At(enc_cot, 0),
         enc_norm_in,
         parts(out, 0),
         parts(up, 0),
@@ -1541,7 +1681,7 @@
         block,
         [dec_out, cross_query_grad, cross_out_grad],
     )
-    dec_q_grad, dec_kv_grads, (ffn_enc,) = attend_back(
+    dec_q_grad, dec_kv_grads, (ffn_enc, ffn_enc_other) = attend_back(
         dec_q,
         dec_kv,
         dec_mix,
@@ -1550,7 +1690,7 @@
         spans[1],
         query_block,
         chunk,
-        Reduce([ffn_enc], 256, 6),
+        Carry([Reduce([ffn_enc], 256, 2, 2)], 6),
     )
     dec_kv_grads = [dec_kv_grads[0], swap(dec_kv_grads[1])]
     target_grad, dec_qkv = input_back(
@@ -1564,8 +1704,7 @@
         block,
         [],
     )
-    target_grad = give_back(target_grad, 1)
-    enc_q_grad, enc_kv_grads, (sides,) = attend_back(
+    enc_q_grad, enc_kv_grads, (sides, sides_other, target_grad) = attend_back(
         enc_q,
         enc_kv,
         enc_mix,
@@ -1574,7 +1713,7 @@
         spans[0],
         query_block,
         chunk,
-        Reduce([sides, dec_qkv], 384, 7),
+        Carry([Reduce([sides, dec_qkv], 384, 1, 2), ReturnRows(target_grad, 1)], 7),
     )
     enc_kv_grads = [enc_kv_grads[0], swap(enc_kv_grads[1])]
     source_grad, enc_qkv = input_back(
@@ -1588,26 +1727,34 @@
         block,
         [enc_norm, dec_norm],
     )
-    source_grad = give_back(source_grad, 0)
-    last = reduce_alone([enc_qkv], PAIR, 8)
+    reduce = Reduce([enc_qkv], enc_qkv.shape[2] // 2, 1, 1)
+    last, last_other, source_grad = carry_alone(
+        [reduce, ReturnRows(source_grad, 0)], reduce.steps, 8
+    )
 
     side_rows, half = 3 * width, 3 * width // 2
-    arrived = swap(jnp.where(is_first, ffn_dec, ffn_enc))
-    up_grad = jnp.where(is_first, ffn_enc, arrived).astype(F32)
-    down_grad = jnp.where(is_first, arrived, ffn_dec).astype(F32)
+    up_grad = jnp.where(is_first, ffn_enc, ffn_dec_other).astype(F32)
+    down_grad = jnp.where(is_first, ffn_enc_other, ffn_dec).astype(F32)
     up_grad = jnp.concatenate(jnp.split(up_grad, 2, axis=0), axis=1)
-    arrived = swap(jnp.where(is_first, sides[side_rows:], last[:half]))
-    first_half = jnp.where(is_first, last[:half], arrived)
-    second_half = jnp.where(is_first, arrived, sides[side_rows:])
-    qkv_grad = jnp.concatenate([first_half, second_half], axis=0).astype(F32)
-    qkv_grad = qkv_grad.reshape(self_qkv.shape)
+
+    def columns(halves):
+        return jnp.concatenate([halves[:half], halves[half : 2 * half]], axis=1)
+
+    qkv_grad = jnp.concatenate(
+        [
+            jnp.where(is_first, columns(last), sides_other[side_rows:]),
+            jnp.where(is_first, columns(last_other), sides[side_rows:]),
+        ],
+        axis=0,
+    )
+    qkv_grad = qkv_grad.astype(F32).reshape(self_qkv.shape)
     sides = sides[:side_rows].astype(F32)
     out_grad = jnp.concatenate([sides[: width // 2], sides[width // 2 : width]], axis=1)
     cross_grad = sides[width:].reshape(cross_proj.shape)
-    norm_grad = last[half : half + 12].astype(F32).reshape(norms.shape)
+    norm_grad = last[2 * half : 2 * half + 24].astype(F32).reshape(norms.shape)
 
     def by_side(source, target):
-        return jnp.stack([jnp.where(is_first, a, b) for a, b in zip(source, target)])
+        return jnp.where(is_first, source, target)
 
     return (
         by_side(encoded, decoded)[None],

time: 693 us -> 615 us (0.89)
  Pallas kernels: 608 us -> 565 us
  starting transfers between devices: 34.4 us -> 1.3 us
    ppermute x8 -> x0, starting transfers between devices: 30.2 us -> none  [give_back(): lax.ppermute(value, ('section', 'tensor'), [(2 * p + row, 2 * side + p) f...]
    pallas_call x3, Pallas kernels: 137 us -> 120 us  [attend(): pl.pallas_call(kernel, grid=(pairs, rows // block), in_specs=[pl.BlockSpe...]
    pallas_call x3, Pallas kernels: 249 us -> 235 us  [attend_back(): pl.pallas_call(kernel, grid=(pairs, rows // block), in_specs=[pl.BlockSpe...]
  transfers between devices with their start and end apart: 14 -> 4, of which waited for: 0 -> 1; matrix products, arithmetic and copies ran while one was open for 3% -> 1% of each run, Pallas kernels for 27% -> 4%
where the time goes in v3:
time: 615 us; the launch traced here: 605 us
  Pallas kernels  565 us (92%)
  other arithmetic  13.1 us (2%)
  local copies, waits for them, and re-layouts  11.5 us (2%)
  between operations  10.3 us (2%)
    pallas_call x3, Pallas kernels, attend_back(): pl.pallas_call(kernel, grid=(pairs, rows // block), in_specs=[pl.BlockSpe...  235 us
    pallas_call x3, Pallas kernels, attend(): pl.pallas_call(kernel, grid=(pairs, rows // block), in_specs=[pl.BlockSpe...  120 us
    pallas_call x7, Pallas kernels, row_call(): pl.pallas_call(kernel, grid=(rows // block,), in_specs=[blocked(a, dim) f...  113 us
    pallas_call x1, Pallas kernels, carry_alone(): pl.pallas_call(kernel, grid=(steps,), in_specs=[hold] * len(carrier.ins),...  50.9 us
    pallas_call x1, Pallas kernels, open_up(): pl.pallas_call(kernel, in_specs=[hold] * 3, out_specs=[hold] * 6, out_sha...  45.5 us
  transfers between devices with their start and end apart: 4, of which 1 were waited for; matrix products, arithmetic and copies ran while one was open for 1% of the time, Pallas kernels for 4%

profile of v3, /device:TPU:0, one launch (start us, length us, event | category | flops | bytes accessed | tf_op | source)
XLA Modules:
  0.0 605.4 jit_solution(15267731365278911100)
XLA Ops:
  0.6 1.4 constant_dynamic-slice_fusion.2
  9.8 45.5 %open_up.1 = (bf16[2,1024,512]{2,1,0:T(8,128)(2,1)}, bf16[2,2,1536,256]{3,2,1,0:T(8,128)(2,1)}, f32[2,3,2,512]{3,2,1,0:T(2,128)}, bf16[2,2,1024,256]{3,2,1,0:T(8...) custom-call(bf16[2,1024,512]{2,1,0:T(8,128)(2,1)} %bitcast.52, ...), custom_call_target="tpu_custom_call" | custom-call | tf_op jit(solution)/shard_map/open_up/pallas_call | solution.py:1348
  55.3 0.6 add_add_fusion.1
  55.9 37.6 %attend.3 = (bf16[2,1024,256]{2,1,0:T(8,128)(2,1)}, f32[1024,512]{1,0:T(8,128)}, bf16[2,2,1024,512]{3,2,1,0:T(8,128)(2,1)}, bf16[2,1024,512]{2,1,0:T(8,128)(2,1)}) custom-call(s32[4]{0:T(128)} %get-tuple-element.150.span_ref, bf16[2,2,1024,256]{3,2,1,0:T(8,128)(2,1)} %get-tuple-element.74.q_ref, bf16[2,2,2,1024,256]{4,3,2,1,0:T(8,128)(2,1)} %get-tuple-element.75.refs_0_, ...), custom_call_target="tpu_custom_call" | custom-call | flops 17179869184 | bytes 8388608 | tf_op jit(solution)/shard_map/attend/pallas_call | solution.py:634
  93.6 47.2 %attend.4 = (bf16[2,1024,256]{2,1,0:T(8,128)(2,1)}, f32[1024,512]{1,0:T(8,128)}, bf16[2,2,256,512]{3,2,1,0:T(8,128)(2,1)}, bf16[2,2,1024,256]{3,2,1,0:T(8,128)(2,1)}, bf16[2,2,512,1024]{3,2,1,0:T(8,128)(2,1)}) custom-call(s32[4]{0:T(128)} %get-tuple-element.151.span_ref, bf16[2,2,1024,256]{3,2,1,0:T(8,128)(2,1)} %get-tuple-element.74.q_ref, ...), custom_call_target="tpu_custom_call" | custom-call | flops 17179869184 | bytes 8388608 | tf_op jit(solution)/shard_map/attend/pallas_call | solution.py:634
  140.8 13.7 %encoder_forward.1 = (bf16[1024,512]{1,0:T(8,128)(2,1)}, bf16[2,2,1024,256]{3,2,1,0:T(8,128)(2,1)}, f32[1024,512]{1,0:T(8,128)}, f32[1024,512]{1,0:T(8,128)}) custom-call(bf16[2,1024,512]{2,1,0:T(8,128)(2,1)} %get-tuple-element.73.refs_0_, bf16[2,1024,256]{2,1,0:T(8,128)(2,1)} %get-tuple-element.82.refs_1_.refs_2_.mix_ref, ...), custom_call_target="tpu_custom_call" | custom-call | flops 5905580032 | bytes 7876608 | tf_op jit(solution)/shard_map/encoder_forward/pallas_call | solution.py:138
  154.5 0.4 collective-permute-start
  156.1 6.0 decoder_middle.1
  162.2 0.7 add_add_fusion.span_ref
  162.8 0.0 collective-permute-done.refs_1_
  162.8 1.3 copy-done.11
  164.2 35.4 %attend.5 = (bf16[2,1024,256]{2,1,0:T(8,128)(2,1)}, f32[1024,512]{1,0:T(8,128)}, bf16[2,1024,512]{2,1,0:T(8,128)(2,1)}, bf16[2,1024,512]{2,1,0:T(8,128)(2,1)}) custom-call(s32[4]{0:T(128)} %add_add_fusion.span_ref, bf16[2,1024,256]{2,1,0:T(8,128)(2,1)} %get-tuple-element.81.q_ref, bf16[2,2,1024,256]{3,2,1,0:T(8,128)(2,1)} %get-tuple-element.85.refs_0_, ...), custom_call_target="tpu_custom_call" | custom-call | flops 17179869184 | bytes 8388608 | tf_op jit(solution)/shard_map/attend/pallas_call | solution.py:634
  199.6 27.3 %decoder_turn.1 = (bf16[1024,512]{1,0:T(8,128)(2,1)}, f32[1024,512]{1,0:T(8,128)}, bf16[2,1024,256]{2,1,0:T(8,128)(2,1)}, bf16[2,512,256]{2,1,0:T(8,128)(2,1)}, ...) custom-call(f32[1024,512]{1,0:T(8,128)} %get-tuple-element.89.refs_0_, ...), custom_call_target="tpu_custom_call" | custom-call | flops 14495514624 | bytes 9449472 | tf_op jit(solution)/shard_map/decoder_turn/pallas_call | solution.py:138
  226.9 82.8 %attend_back.3 = (bf16[2,1024,256]{2,1,0:T(8,128)(2,1)}, bf16[2,2,1024,256]{3,2,1,0:T(8,128)(2,1)}, bf16[2,2,1024,256]{3,2,1,0:T(8,128)(2,1)}, bf16[1024,512]{1,...) custom-call(s32[4]{0:T(128)} %add_add_fusion.span_ref, ...), custom_call_target="tpu_custom_call" | custom-call | flops 42949672960 | bytes 16777216 | tf_op jit(solution)/shard_map/attend_back/pallas_call | solution.py:751
  309.7 0.4 collective-permute-start.1
  310.1 19.5 %decoder_middle_back.1 = (f32[1024,512]{1,0:T(8,128)}, bf16[2,1024,256]{2,1,0:T(8,128)(2,1)}, bf16[2,512,256]{2,1,0:T(8,128)(2,1)}, bf16[2,256,512]{2,1,0:T(8,128)(2,1)}, f32[3,2,512]{2,1,0:T(2,128)}) custom-call(f32[1024,512]{1,0:T(8,128)} %get-tuple-element.89.refs_0_, bf16[2,1024,256]{2,1,0:T(8,128)(2,1)} %get-tuple-element.77.refs_1_.mix_ref, ...), custom_call_target="tpu_custom_call" | custom-call | flops 2147483648 | bytes 7876608 | tf_op jit(solution)/shard_map/decoder_middle_back/pallas_call | solution.py:138
  329.7 0.0 collective-permute-done.1.refs_5_
  329.7 0.0 copy-start.12
  329.7 1.3 copy-done.12
  331.0 28.4 %encoder_back.1 = (f32[1024,512]{1,0:T(8,128)}, bf16[2,1024,256]{2,1,0:T(8,128)(2,1)}, bf16[2,2,1024,512]{3,2,1,0:T(8,128)(2,1)}, bf16[2,2,1536,256]{3,2,1,0:T(8,128)(2,1)}, f32[3,2,512]{2,1,0:T(2,128)}) custom-call(f32[1024,512]{1,0:T(8,128)} %get-tuple-element.96.refs_0_, f32[1024,512]{1,0:T(8,128)} %get-tuple-element.97.refs_1_, ...), custom_call_target="tpu_custom_call" | custom-call | flops 13958643712 | bytes 17838080 | tf_op jit(solution)/shard_map/encoder_back/pallas_call | solution.py:138
  359.4 71.9 %attend_back.4 = (bf16[2,1024,256]{2,1,0:T(8,128)(2,1)}, bf16[2,2,1024,256]{3,2,1,0:T(8,128)(2,1)}, bf16[2,2,1024,256]{3,2,1,0:T(8,128)(2,1)}, bf16[1024,512]{1,0:T(8,128)(2,1)}, bf16[1024,512]{1,0:T(8,128)(2,1)}) custom-call(s32[4]{0:T(128)} %get-tuple-element.150.span_ref, bf16[2,2,1024,256]{3,2,1,0:T(8,128)(2,1)} %get-tuple-element.74.q_ref, ...), custom_call_target="tpu_custom_call" | custom-call | flops 42949672960 | bytes 16777216 | tf_op jit(solution)/shard_map/attend_back/pallas_call | solution.py:751
  431.3 0.4 collective-permute-start.2
  431.7 4.0 collective-permute-done.2.refs_4_
  435.7 1.3 copy-done.1
  437.0 8.5 %input_back.2 = (bf16[1024,512]{1,0:T(8,128)(2,1)}, bf16[2,2,768,256]{3,2,1,0:T(8,128)(2,1)}) custom-call(bf16[2,1024,512]{2,1,0:T(8,128)(2,1)} %get-tuple-element.73.refs_0_, f32[1024,512]{1,0:T(8,128)} %get-tuple-element.110.refs_1_, bf16[2,1024,256]{2,1,0:T(8,128)(2,1)} %get-tuple-element.114.refs_2_, ...), custom_call_target="tpu_custom_call" | custom-call | flops 3221225472 | bytes 9973760 | tf_op jit(solution)/shard_map/input_back/pallas_call | solution.py:138
  445.6 80.7 %attend_back.5 = (bf16[2,1024,256]{2,1,0:T(8,128)(2,1)}, bf16[2,2,1024,256]{3,2,1,0:T(8,128)(2,1)}, bf16[2,2,1024,256]{3,2,1,0:T(8,128)(2,1)}, bf16[2304,256]{1,...) custom-call(s32[4]{0:T(128)} %get-tuple-element.151.span_ref, ...), custom_call_target="tpu_custom_call" | custom-call | flops 42949672960 | bytes 16777216 | tf_op jit(solution)/shard_map/attend_back/pallas_call | solution.py:751
  526.3 0.1 collective-permute-start.3
  526.4 0.0 copy-done
  526.4 0.0 copy-start.9
  526.4 0.0 copy-start.10
  526.4 0.0 copy-start.6
  526.4 0.0 copy-start.8
  526.4 1.5 select_bitcast_fusion
  528.0 0.0 copy-done.9
  528.0 0.0 copy-done.10
  528.0 0.6 add.19.refs_9_
  528.6 0.0 copy-done.6
  528.6 0.1 copy-done.8
  528.7 0.1 select_convert_fusion
  528.8 0.2 fusion
  529.0 0.0 copy-start.5
  529.0 0.0 copy-start.7
  529.0 1.5 maximum_bitcast_fusion
  530.5 0.1 copy-done.5
  530.6 0.7 copy-done.7
  531.3 1.5 bitcast_convert_fusion.1
  532.8 0.3 copy-done.4
  533.1 0.1 slice_convert_fusion
  533.2 1.0 slice.92
  534.3 0.9 maximum_bitcast_fusion.1
  535.2 0.0 collective-permute-done.3.refs_4_
  535.2 9.6 %input_back.3 = (bf16[1024,512]{1,0:T(8,128)(2,1)}, bf16[2,2,1792,128]{3,2,1,0:T(8,128)(2,1)}) custom-call(bf16[2,1024,512]{2,1,0:T(8,128)(2,1)} %get-tuple-element.73.refs_0_, f32[1024,512]{1,0:T(8,128)} %get-tuple-element.106.refs_1_, bf16[2,1024,256]{2,1,0:T(8,128)(2,1)} %get-tuple-element.120.refs_2_, ...), custom_call_target="tpu_custom_call" | custom-call | flops 3221225472 | bytes 9998336 | tf_op jit(solution)/shard_map/input_back/pallas_call | solution.py:138
  544.7 50.9 %carry_alone.1 = (bf16[1792,128]{1,0:T(8,128)(2,1)}, bf16[1792,128]{1,0:T(8,128)(2,1)}, bf16[2,1024,512]{2,1,0:T(8,128)(2,1)}) custom-call(bf16[2,2,1792,128]{3,2,1,0:T(8,128)(2,1)} %get-tuple-element.126.refs_0_, bf16[1024,512]{1,0:T(8,128)(2,1)} %get-tuple-element.127.refs_1_), custom_call_target="tpu_custom_call" | custom-call | tf_op jit(solution)/shard_map/carry_alone/pallas_call | solution.py:1238
  595.6 0.7 slice_convert_fusion.1
  596.3 1.0 fusion.2
  597.4 0.6 reshape.73
  598.0 1.0 fusion.3
  599.0 0.1 maximum_select_fusion.1
  599.1 0.0 copy-start.3
  599.2 1.2 maximum_select_fusion
  600.4 0.1 pad_maximum_fusion
  600.5 1.3 convert.5
  601.8 0.9 copy-done.2
  602.7 2.3 bitcast_convert_fusion
  (7 shorter events, 0.0 us)
Async XLA Ops:
  154.5 8.3 %collective-permute-start = (bf16[2,2,1024,256]{3,2,1,0:T(8,128)(2,1)}, bf16[2,2,1024,256]{3,2,1,0:T(8,128)(2,1)S(1)}, u32[]{:S(2)}, u32[]{:S(2)}) collective-permute-start(bf16[2,2,1024,256]{3,2,1,0:T(8,128)(2,1)} %get-tuple-element.85.refs_0_), channel_id=1, source_target_pairs={{0,16},{16,0},{1,17},{17,1},{2,18},{18,2},{3,19},{19,3},{4,20},{20... | collective-permute-start | bytes 6291464 | tf_op jit(solution)/shard_map/ppermute | solution.py:1569
  162.8 1.3 copy-start.11
  309.7 20.0 %collective-permute-start.1 = (bf16[2,2,1024,256]{3,2,1,0:T(8,128)(2,1)}, bf16[2,2,1024,256]{3,2,1,0:T(8,128)(2,1)S(1)}, u32[]{:S(2)}, u32[]{:S(2)}) collective-permute-start(bf16[2,2,1024,256]{3,2,1,0:T(8,128)(2,1)} %get-tuple-element.100), channel_id=1, source_target_pairs={{0,16},{16,0},{1,17},{17,1},{2,18},{18,2},{3,19},{19,3},{4,20},{20... | collective-permute-start | bytes 6291464 | tf_op jit(solution)/shard_map/ppermute | solution.py:1569
  329.7 1.3 copy-start.12
  431.3 4.4 collective-permute-start.2
  435.7 1.3 copy-start.1
  445.5 80.8 %copy-start = (bf16[2,1024,512]{2,1,0:T(8,128)(2,1)S(1)}, bf16[2,1024,512]{2,1,0:T(8,128)(2,1)}, u32[]{:S(2)}) copy-start(bf16[2,1024,512]{2,1,0:T(8,128)(2,1)} %get-tuple-element.87) | copy-start | bytes 6291460
  526.3 8.9 %collective-permute-start.3 = (bf16[2,2,1024,256]{3,2,1,0:T(8,128)(2,1)}, bf16[2,2,1024,256]{3,2,1,0:T(8,128)(2,1)}, u32[]{:S(2)}, u32[]{:S(2)}) collective-permute-start(bf16[2,2,1024,256]{3,2,1,0:T(8,128)(2,1)} %get-tuple-element.122), channel_id=1, source_target_pairs={{0,16},{16,0},{1,17},{17,1},{2,18},{18,2},{3,19},{19,3},{4,20},{20... | collective-permute-start | bytes 6291464 | tf_op jit(solution)/shard_map/ppermute | solution.py:1569
  526.4 1.6 copy-start.9
  526.4 1.6 copy-start.10
  526.4 2.2 copy-start.6
  526.4 2.3 copy-start.8
  529.0 1.6 copy-start.5
  529.0 2.3 copy-start.7
  531.3 1.8 copy-start.4
  599.1 2.6 copy-start.3
  600.4 2.3 copy-start.2

commit v4 on v3

--- a/solution.py
+++ b/solution.py
@@ -572,21 +572,19 @@
         value_o[own, :] = jnp.where(low, 1.0, values).astype(BF16)
 
 
-def attention_specs(per_part, rows, block, query, lse_lead=()):
+def attention_specs(per_part, rows):
     def query_spec(array):
-        return at(array).spec(
-            (None, block, PAIR), lambda i, j: (i // per_part, j, i % per_part)
-        )
+        return at(array).spec((None, rows, PAIR), lambda i: (i // per_part, 0, i % per_part))
 
     def kv_spec(array):
         return at(array).spec(
-            (None, 2, rows, PAIR), lambda i, j: (i // per_part, 0, 0, i % per_part)
+            (None, 2, rows, PAIR), lambda i: (i // per_part, 0, 0, i % per_part)
         )
 
-    return query_spec, kv_spec, pl.BlockSpec((block, PAIR), lambda i, j: (j, i))
-
-
-def attend(query, kv_pieces, span, block, carrier=None):
+    return query_spec, kv_spec, pl.BlockSpec((rows, PAIR), lambda i: (0, i))
+
+
+def attend(query, kv_pieces, span, block, carrier=None, slots=1):
     query, kv_pieces = at(query), [at(piece) for piece in kv_pieces]
     carrier = carrier or Carry()
     parts, rows, part = query.shape
@@ -595,6 +593,8 @@
     pieces = len(kv_pieces)
     keys = rows * pieces
     n_carry = len(carrier.ins)
+    blocks = rows // block
+    stride = blocks // slots
 
     def kernel(span_ref, q_ref, *refs):
         kv_refs, refs = refs[:pieces], refs[pieces:]
@@ -602,48 +602,56 @@
         out_ref, lse_ref, refs = refs[0], refs[1], refs[2:]
         carry_outs, refs = refs[: len(carrier.outs)], refs[len(carrier.outs) :]
         key_e, key_o, value_e, value_o = refs[:4]
-        step = pl.program_id(0) * pl.num_programs(1) + pl.program_id(1)
-        carrier.run(step, pairs * (rows // block), carry_ins, carry_outs, refs[4:])
-
-        @pl.when(pl.program_id(1) == 0)
-        def _():
-            widen_keys(span_ref, kv_refs, key_e, key_o, value_e, value_o, rows)
-
+
+        def carry(slot):
+            place = pl.program_id(0)
+            carrier.run(place, slot, slots, pairs * slots, carry_ins, carry_outs, refs[4:])
+
+        carry(0)
+        widen_keys(span_ref, kv_refs, key_e, key_o, value_e, value_o, rows)
         lane = lax.broadcasted_iota(jnp.int32, (block, PAIR), 1)
         low = lane < HALF
-        query = q_ref[...].astype(F32)
-        query_e = jnp.where(low, query, jnp.where(lane == HALF, 1.0, 0.0)).astype(BF16)
-        query_o = jnp.where(low, jnp.where(lane == 0, 1.0, 0.0), query).astype(BF16)
+        units = []
+        for i in range(blocks):
+            query = q_ref[i * block : (i + 1) * block, :].astype(F32)
+            first = jnp.where(low, query, jnp.where(lane == HALF, 1.0, 0.0)).astype(BF16)
+            second = jnp.where(low, jnp.where(lane == 0, 1.0, 0.0), query).astype(BF16)
+            units += [(first, key_e, value_e), (second, key_o, value_o)]
+
+        def scores_of(unit):
+            return dot_nt(unit[0], unit[1][...])
+
+        ahead = scores_of(units[0])
         tops, sums = [], []
-        for q, k, v in ((query_e, key_e, value_e), (query_o, key_o, value_o)):
-            scores = dot_nt(q, k[...])
+        for u, unit in enumerate(units):
+            if u and u % (2 * stride) == 0:
+                carry(u // (2 * stride))
+            scores = ahead
+            if u + 1 < len(units):
+                ahead = scores_of(units[u + 1])
             top = jnp.max(scores, axis=1, keepdims=True)
             tops.append(top)
-            sums.append(dot_nn(jnp.exp2(scores - top).astype(BF16), v[...]))
-        top = jnp.where(low, tops[1], tops[0])
-        weight = jnp.where(low, sums[1], sums[0])
-        lse_ref[...] = top + LOG2E * jnp.log(weight)
-        mixed = jnp.where(low, sums[0], sums[1])
-        out_ref[...] = (mixed / pltpu.roll(weight, HALF, 1)).astype(BF16)
-
-    query_spec, kv_spec, lse_spec = attention_specs(per_part, rows, block, query)
-    out_spec = pl.BlockSpec(
-        (None, block, PAIR), lambda i, j: (i // per_part, j, i % per_part)
-    )
+            sums.append(dot_nn(jnp.exp2(scores - top).astype(BF16), unit[2][...]))
+            if u % 2:
+                own = slice(u // 2 * block, (u // 2 + 1) * block)
+                top = jnp.where(low, tops[u], tops[u - 1])
+                weight = jnp.where(low, sums[u], sums[u - 1])
+                lse_ref[own, :] = top + LOG2E * jnp.log(weight)
+                mixed = jnp.where(low, sums[u - 1], sums[u])
+                out_ref[own, :] = (mixed / pltpu.roll(weight, HALF, 1)).astype(BF16)
+
+    query_spec, kv_spec, lse_spec = attention_specs(per_part, rows)
+    plain = jax.ShapeDtypeStruct(query.shape, BF16)
     hold = pl.BlockSpec(memory_space=pl.ANY)
     return pl.pallas_call(
         kernel,
-        grid=(pairs, rows // block),
+        grid=(pairs,),
         in_specs=[pl.BlockSpec(memory_space=pltpu.SMEM), query_spec(query)]
         + [kv_spec(piece) for piece in kv_pieces]
         + [hold] * n_carry,
-        out_specs=[out_spec, lse_spec] + [hold] * len(carrier.outs),
+        out_specs=[query_spec(plain), lse_spec] + [hold] * len(carrier.outs),
         scratch_shapes=[pltpu.VMEM((keys, PAIR), BF16)] * 4 + carrier.scratch,
-        out_shape=[
-            jax.ShapeDtypeStruct(query.shape, BF16),
-            jax.ShapeDtypeStruct((rows, pairs * PAIR), F32),
-        ]
-        + carrier.outs,
+        out_shape=[plain, jax.ShapeDtypeStruct((rows, pairs * PAIR), F32)] + carrier.outs,
         compiler_params=pltpu.CompilerParams(vmem_limit_bytes=VMEM, **carrier.params),
         cost_estimate=pl.CostEstimate(
             flops=16 * rows * keys * pairs * PAIR,
@@ -654,36 +662,43 @@
     )(span, query.array, *[piece.array for piece in kv_pieces], *carrier.ins)
 
 
-def attend_back(query, kv_pieces, mix, mix_grad, lse, span, block, chunk, carrier=None):
+def attend_back(
+    query, kv_pieces, mix, mix_grad, lse, span, chunk, carrier=None, slots=1
+):
     query, kv_pieces = at(query), [at(piece) for piece in kv_pieces]
     mix, mix_grad = at(mix), at(mix_grad)
-    carrier = carrier or Carry()
     parts, rows, part = query.shape
     per_part = part // PAIR
     pairs = parts * per_part
     pieces = len(kv_pieces)
     keys = rows * pieces
     scale = 1.0 / math.sqrt(HALF)
+    swaps = carrier is not None
+    carrier = carrier or Carry()
     n_carry = len(carrier.ins)
+    kept = 1 if swaps else pieces
+    chunks = keys // chunk
+    stride = chunks // slots
 
     def kernel(span_ref, q_ref, mix_ref, grad_ref, lse_ref, *refs):
         kv_refs, refs = refs[:pieces], refs[pieces:]
         carry_ins, refs = refs[:n_carry], refs[n_carry:]
         dq_ref, dkv_refs, refs = refs[0], refs[1 : pieces + 1], refs[pieces + 1 :]
         carry_outs, refs = refs[: len(carrier.outs)], refs[len(carrier.outs) :]
-        key_e, key_o, value_e, value_o, key_t, key_total, value_total = refs[:7]
-        step = pl.program_id(0) * pl.num_programs(1) + pl.program_id(1)
-        carrier.run(step, pairs * (rows // block), carry_ins, carry_outs, refs[7:])
-
-        @pl.when(pl.program_id(1) == 0)
-        def _():
-            widen_keys(span_ref, kv_refs, key_e, key_o, value_e, value_o, rows)
-            for g, kv_ref in enumerate(kv_refs):
-                key_t[:, pl.ds(g * rows, rows)] = kv_ref[0].T
-            key_total[...] = jnp.zeros_like(key_total)
-            value_total[...] = jnp.zeros_like(value_total)
-
-        lane = lax.broadcasted_iota(jnp.int32, (block, PAIR), 1)
+        key_e, key_o, value_e, value_o, key_t = refs[:5]
+        refs = refs[5:]
+        if swaps:
+            given, swap_sems, refs = refs[0], refs[1], refs[2:]
+        pair = pl.program_id(0)
+
+        def carry(slot):
+            carrier.run(pair, slot, slots, pairs * slots, carry_ins, carry_outs, refs)
+
+        carry(0)
+        widen_keys(span_ref, kv_refs, key_e, key_o, value_e, value_o, rows)
+        for g, kv_ref in enumerate(kv_refs):
+            key_t[:, g * rows : (g + 1) * rows] = kv_ref[0].T
+        lane = lax.broadcasted_iota(jnp.int32, (rows, PAIR), 1)
         low = lane < HALF
         query, grad = q_ref[...].astype(F32), grad_ref[...].astype(F32)
         product = mix_ref[...].astype(F32) * grad
@@ -708,60 +723,95 @@
 
         lse = three(-lse_ref[...], 1) + jnp.where(spot == 0, 1.0, 0.0)
         inner = three(-inner, 0)
-        heads = []
-        for own, key, value in ((low, key_e, value_e), (~low, key_o, value_o)):
-            heads.append(
-                (
-                    key,
-                    value,
-                    jnp.where(own, query, lse).astype(BF16),
-                    jnp.where(own, grad, inner).astype(BF16),
-                    jnp.where(own, query, 0.0).astype(BF16),
-                    jnp.where(own, grad, 0.0).astype(BF16),
+        heads = [
+            (
+                key,
+                value,
+                jnp.where(own, query, lse).astype(BF16),
+                jnp.where(own, grad, inner).astype(BF16),
+                jnp.where(own, query, 0.0).astype(BF16),
+                jnp.where(own, grad, 0.0).astype(BF16),
+            )
+            for own, key, value in ((low, key_e, value_e), (~low, key_o, value_o))
+        ]
+        units = [(c * chunk, h) for c in range(chunks) for h in range(2)]
+
+        def front(unit):
+            begin, h = unit
+            own = slice(begin, begin + chunk)
+            key, value, q_wide, g_wide, _, _ = heads[h]
+            return dot_nt(key[own, :], q_wide), dot_nt(value[own, :], g_wide)
+
+        ahead = front(units[0])
+        dq = [None, None]
+        for u, (begin, h) in enumerate(units):
+            if u and u % (2 * stride) == 0:
+                carry(u // (2 * stride))
+            scores, dprobs = ahead
+            if u + 1 < len(units):
+                ahead = front(units[u + 1])
+            probs = jnp.exp2(scores)
+            dscores = (probs * dprobs).astype(BF16)
+            _, _, _, _, q_own, g_own = heads[h]
+            step_v = dot_nn(probs.astype(BF16), g_own)
+            step_k = dot_nn(dscores, q_own)
+            step_q = dot_nn(key_t[h * HALF : (h + 1) * HALF, begin : begin + chunk], dscores)
+            dq[h] = step_q if dq[h] is None else dq[h] + step_q
+            if h == 0:
+                dv, dk = step_v, step_k
+            else:
+                g, first = begin // rows, begin % rows
+                own = slice(first, first + chunk)
+                dk = ((dk + step_k) * (1.0 / LOG2E)).astype(BF16)
+                dv = (dv + step_v).astype(BF16)
+                if g < kept:
+                    dkv_refs[g][0, own, :] = dk
+                    dkv_refs[g][1, own, :] = dv
+                else:
+                    given[pair, 0, own, :] = dk
+                    given[pair, 1, own, :] = dv
+        dq_ref[...] = (jnp.concatenate(dq, axis=0).T * scale).astype(BF16)
+        if swaps:
+            columns = pl.ds(pl.multiple_of(pair % per_part * PAIR, PAIR), PAIR)
+
+            def swap(i, place):
+                return remote(
+                    given.at[i],
+                    dkv_refs[1].at[place // per_part, :, :, columns],
+                    swap_sems.at[0, i],
+                    swap_sems.at[1, i],
+                    where_is("near"),
                 )
-            )
-        dq = [None, None]
-        for c in range(keys // chunk):
-            span_c = pl.ds(c * chunk, chunk)
-            dk, dv = None, None
-            for h, (key, value, q_wide, g_wide, q_own, g_own) in enumerate(heads):
-                probs = jnp.exp2(dot_nt(key[span_c, :], q_wide))
-                dscores = (probs * dot_nt(value[span_c, :], g_wide)).astype(BF16)
-                step_v = dot_nn(probs.astype(BF16), g_own)
-                step_k = dot_nn(dscores, q_own)
-                step_q = dot_nn(key_t[pl.ds(h * HALF, HALF), span_c], dscores)
-                dv = step_v if dv is None else dv + step_v
-                dk = step_k if dk is None else dk + step_k
-                dq[h] = step_q if dq[h] is None else dq[h] + step_q
-            key_total[span_c, :] += dk
-            value_total[span_c, :] += dv
-        dq_ref[...] = (jnp.concatenate(dq, axis=0).T * scale).astype(BF16)
-
-        @pl.when(pl.program_id(1) == pl.num_programs(1) - 1)
-        def _():
-            for g, ref in enumerate(dkv_refs):
-                own = pl.ds(g * rows, rows)
-                ref[0] = (key_total[own, :] * (1.0 / LOG2E)).astype(BF16)
-                ref[1] = value_total[own, :].astype(BF16)
-
-    query_spec, kv_spec, lse_spec = attention_specs(per_part, rows, block, query)
+
+            swap(pair, pair).start()
+
+            @pl.when(pair == pairs - 1)
+            def _():
+                for i in range(pairs):
+                    swap(i, pair).wait()
+
+    query_spec, kv_spec, lse_spec = attention_specs(per_part, rows)
     plain = jax.ShapeDtypeStruct(query.shape, BF16)
     plain_kv = jax.ShapeDtypeStruct((parts, 2, rows, part), BF16)
     hold = pl.BlockSpec(memory_space=pl.ANY)
+    swap_scratch = [
+        pltpu.VMEM((pairs, 2, rows, PAIR), BF16),
+        pltpu.SemaphoreType.DMA((2, pairs)),
+    ]
     out = pl.pallas_call(
         kernel,
-        grid=(pairs, rows // block),
+        grid=(pairs,),
         in_specs=[pl.BlockSpec(memory_space=pltpu.SMEM)]
         + [query_spec(a) for a in (query, mix, mix_grad)]
         + [lse_spec]
         + [kv_spec(piece) for piece in kv_pieces]
         + [hold] * n_carry,
         out_specs=[query_spec(plain)]
-        + [kv_spec(plain_kv)] * pieces
-        + [hold] * len(carrier.outs),
+        + [kv_spec(plain_kv)] * kept
+        + [hold] * (pieces - kept + len(carrier.outs)),
         scratch_shapes=[pltpu.VMEM((keys, PAIR), BF16)] * 4
         + [pltpu.VMEM((PAIR, keys), BF16)]
-        + [pltpu.VMEM((keys, PAIR), F32)] * 2
+        + (swap_scratch if swaps else [])
         + carrier.scratch,
         out_shape=[plain] + [plain_kv] * pieces + carrier.outs,
         compiler_params=pltpu.CompilerParams(vmem_limit_bytes=VMEM, **carrier.params),
@@ -835,18 +885,31 @@
             dict(collective_id=collective, has_side_effects=True) if self.tasks else {}
         )
 
-    def run(self, step, steps, ins, outs, scratch):
-        if not self.tasks:
-            return
-
-        @pl.when(step == 0)
-        def _():
-            greet(self.peers)
-
+    def plan(self, steps, ins, outs, scratch):
+        plan = {}
+        if self.tasks:
+            plan[0] = [lambda: greet(self.peers)]
+        events = []
         for task in self.tasks:
             i, o, s = len(task.ins), len(task.outs), len(task.scratch)
-            task.run(step, steps, ins[:i], outs[:o], scratch[:s])
+            events += task.events(steps, ins[:i], outs[:o], scratch[:s])
             ins, outs, scratch = ins[i:], outs[o:], scratch[s:]
+        for step, rank, action in sorted(events, key=lambda event: event[:2]):
+            assert 0 <= step < steps
+            plan.setdefault(step, []).append(action)
+        return plan
+
+    def run(self, place, slot, slots, steps, ins, outs, scratch):
+        for step, actions in self.plan(steps, ins, outs, scratch).items():
+            if step % slots == slot:
+
+                @pl.when(place == step // slots)
+                def _():
+                    for action in actions:
+                        action()
+
+
+LAST = 1000
 
 
 GROUP = ["near", "over", "cross"]
@@ -951,34 +1014,34 @@
 class SpreadRows:
     peers = GROUP
 
-    def __init__(self, array, sides):
-        self.ins, self.sides = [array], sides
+    def __init__(self, array, sides, begin=0):
+        self.ins, self.sides, self.begin = [array], sides, begin
         self.outs = [jax.ShapeDtypeStruct(array.shape, array.dtype)]
         self.scratch = ROW_SEMS + [pltpu.VMEM(array.shape[-2:], array.dtype)]
 
     def make(self, ins, outs, scratch):
         return spread_rows(ins[0], outs[0], scratch[:3], self.sides, scratch[3])
 
-    def run(self, step, steps, ins, outs, scratch):
-        @pl.when(step == 0)
-        def _():
-            self.make(ins, outs, scratch).start()
-
-        @pl.when(step == 2)
-        def _():
-            self.make(ins, outs, scratch).keep_on()
-
-        @pl.when(step == steps - 1)
-        def _():
-            rows = self.make(ins, outs, scratch)
+    def events(self, steps, ins, outs, scratch):
+        def make():
+            return self.make(ins, outs, scratch)
+
+        def finish():
+            rows = make()
             for i in range(len(rows.arrivals)):
                 rows.wait_arrival(i)
             rows.wait_sent()
 
+        return [
+            (self.begin, 1, lambda: make().start()),
+            (self.begin + 1, 1, lambda: make().keep_on()),
+            (steps - 1, LAST, finish),
+        ]
+
 
 class ReturnRows(SpreadRows):
-    def __init__(self, array, side):
-        self.ins, self.side = [array], side
+    def __init__(self, array, side, begin=0):
+        self.ins, self.side, self.begin = [array], side, begin
         self.outs = [jax.ShapeDtypeStruct((2, *array.shape), array.dtype)]
         self.scratch = ROW_SEMS + [pltpu.VMEM(array.shape, array.dtype)]
 
@@ -987,36 +1050,36 @@
 
 
 class WeightCopies:
-    sems = [pltpu.SemaphoreType.DMA((11,))]
-
-    def __init__(self, source, target, sem, room=None):
+    @staticmethod
+    def sems(count):
+        return pltpu.SemaphoreType.DMA((3 + 8 * count,))
+
+    def __init__(self, source, target, sem, room=None, count=1):
         section, group, _ = spots()
-        count = source.shape[0] // 2
+        rows = source.shape[0] // (2 * count)
         bit = group % 2
-        own = pl.ds(pl.multiple_of(bit * count, 16), count)
-        other = pl.ds(pl.multiple_of((1 - bit) * count, 16), count)
-        here = target.at[section, 1]
-        stays = target.at[section, 0]
+        here, stays = target.at[section, 1], target.at[section, 0]
+        self.room = room
         if room is None:
             self.kept = pltpu.make_async_copy(source, stays, sem.at[0])
         else:
             self.first = pltpu.make_async_copy(source, room, sem.at[0])
             self.kept = pltpu.make_async_copy(room, stays, sem.at[0])
-        self.room = room
-        self.near = remote(
-            source, target.at[section, 0], sem.at[1], sem.at[2], where_is("near")
-        )
-        self.over = remote(source.at[own], here.at[own], sem.at[3], sem.at[4], where_is("over"))
-        self.side = remote(here.at[own], here.at[own], sem.at[5], sem.at[6], where_is(0))
-        self.onward = remote(
-            here.at[own], here.at[own], sem.at[7], sem.at[8], where_is("near")
-        )
-        self.last = remote(
-            here.at[other], here.at[other], sem.at[9], sem.at[10], where_is("near")
-        )
+        self.near = remote(source, stays, sem.at[1], sem.at[2], where_is("near"))
+        self.over, self.side, self.onward, self.last = [], [], [], []
+        for i in range(count):
+            own = pl.ds(pl.multiple_of((bit * count + i) * rows, 16), rows)
+            other = pl.ds(pl.multiple_of(((1 - bit) * count + i) * rows, 16), rows)
+            source_own, own, other = source.at[own], here.at[own], here.at[other]
+            pairs = [(sem.at[3 + 8 * i + 2 * j], sem.at[4 + 8 * i + 2 * j]) for j in range(4)]
+            self.over.append(remote(source_own, own, *pairs[0], where_is("over")))
+            self.side.append(remote(own, own, *pairs[1], where_is(0)))
+            self.onward.append(remote(own, own, *pairs[2], where_is("near")))
+            self.last.append(remote(other, other, *pairs[3], where_is("near")))
 
     def start(self):
-        self.over.start()
+        for copy in self.over:
+            copy.start()
         self.near.start()
         if self.room is None:
             self.kept.start()
@@ -1027,113 +1090,138 @@
         self.first.wait()
         self.kept.start()
 
-    def forward(self):
-        self.over.wait_recv()
-        self.side.start()
-        self.onward.start()
-
-    def forward_last(self):
-        self.side.wait_recv()
-        self.last.start()
+    def forward(self, i):
+        self.over[i].wait_recv()
+        self.side[i].start()
+        self.onward[i].start()
+
+    def forward_last(self, i):
+        self.side[i].wait_recv()
+        self.last[i].start()
 
     def finish(self):
         self.kept.wait()
         self.near.wait()
-        self.over.wait_send()
-        self.side.wait_send()
-        self.onward.wait()
-        self.last.wait()
+        for over, side, onward, last in zip(self.over, self.side, self.onward, self.last):
+            over.wait_send()
+            side.wait_send()
+            onward.wait()
+            last.wait()
 
 
 class SpreadWeight:
     peers = ["near", "over", 0]
 
-    def __init__(self, weight, forward, last):
+    def __init__(self, weight, forwards, lasts):
         self.ins = [weight]
         self.outs = [jax.ShapeDtypeStruct((2, 2, *weight.shape), weight.dtype)]
-        self.scratch = WeightCopies.sems + [pltpu.VMEM(weight.shape, weight.dtype)]
-        self.steps = forward, last
-
-    def run(self, step, steps, ins, outs, scratch):
+        self.forwards, self.lasts = forwards, lasts
+        self.scratch = [
+            WeightCopies.sems(len(forwards)),
+            pltpu.VMEM(weight.shape, weight.dtype),
+        ]
+
+    def events(self, steps, ins, outs, scratch):
         def copies():
-            return WeightCopies(ins[0], outs[0], *scratch)
-
-        @pl.when(step == 0)
-        def _():
-            copies().start()
-
-        @pl.when(step == 2)
-        def _():
-            copies().keep_on()
-
-        @pl.when(step == self.steps[0])
-        def _():
-            copies().forward()
-
-        @pl.when(step == self.steps[1])
-        def _():
-            copies().forward_last()
-
-        @pl.when(step == steps - 1)
-        def _():
-            copies().finish()
+            return WeightCopies(ins[0], outs[0], *scratch, len(self.forwards))
+
+        def forward(i):
+            return lambda: copies().forward(i)
+
+        def forward_last(i):
+            return lambda: copies().forward_last(i)
+
+        return (
+            [(0, 0, lambda: copies().start()), (1, 0, lambda: copies().keep_on())]
+            + [(when, 1, forward(i)) for i, when in enumerate(self.forwards)]
+            + [(when, 2, forward_last(i)) for i, when in enumerate(self.lasts)]
+            + [(steps - 1, LAST, lambda: copies().finish())]
+        )
 
 
 class Reduce:
-    def __init__(self, sources, chunk, spacing, patience):
-        self.ins = list(sources)
-        self.chunk, self.spacing, self.patience = chunk, spacing, patience
-        self.places = [
-            (i, row) for i, s in enumerate(sources) for row in range(0, s.shape[2], chunk)
-        ]
-        self.count = len(self.places)
-        self.levels = lax.axis_size("dp").bit_length() - 1
-        self.peers = ["near", "over", *range(self.levels)]
-        width = sources[0].shape[3]
-        self.outs = [jax.ShapeDtypeStruct((self.count * chunk, width), BF16)] * 2
+    def __init__(self, source, chunk, begins, pace, only=None, levels=None):
+        self.ins = [source]
+        self.chunk, self.begins, self.only = chunk, begins, only
+        self.count = source.shape[-2] // chunk
+        assert self.count == len(begins)
+        self.levels = list(range(lax.axis_size("dp").bit_length() - 1))
+        if levels is not None:
+            self.levels = levels
+        depth = len(self.levels)
+        self.peers = []
+        self.stages = []
+        if only != "slice":
+            self.peers += ["near", "over"]
+            self.stages += ["enter", "cross", "over"]
+        if only != "chip":
+            self.peers += ["near", *self.levels]
+            self.stages += ["load", "loaded"] if only == "slice" else []
+            self.stages += [("halve", i) for i in range(depth)]
+            self.stages += [("double", i) for i in reversed(range(depth))]
+        assert len(pace) == len(self.stages) - 1
+        self.dues = [sum(pace[:i]) for i in range(len(self.stages))]
+        width = source.shape[-1]
+        whole = jax.ShapeDtypeStruct((self.count * chunk, width), BF16)
+        self.outs = [whole] if only == "chip" else [whole] * 2
 
         def room(*shape):
             return pltpu.VMEM((self.count, *shape, width), BF16)
 
-        halves = [room(chunk >> (level + 1)) for level in range(self.levels)]
-        self.scratch = [room(2, chunk), room(2, chunk), room(chunk), room(chunk)]
-        self.scratch += halves + halves
-        self.scratch += [pltpu.SemaphoreType.DMA((2 + 2 * (3 + 2 * self.levels), self.count))]
-        self.last = 1 + patience + 2 * self.levels
-        self.steps = self.last + 1 + spacing * (self.count - 1)
-
-    def run(self, step, steps, ins, outs, scratch):
-        chunk, levels = self.chunk, self.levels
-        assert steps >= self.steps
-        own, chip, other, full = scratch[:4]
-        halves, doubles = scratch[4 : 4 + levels], scratch[4 + levels : 4 + 2 * levels]
-        sems = scratch[4 + 2 * levels]
-        section, group, tensor = spots()
-        bits = [(group // (1 << level)) % 2 for level in range(levels)]
-        begins = [0]
-        for level in range(levels):
-            begins.append(begins[level] + bits[level] * (chunk >> (level + 1)))
-
-        def keeps(level):
-            return pl.ds(pl.multiple_of(begins[level + 1], 16), chunk >> (level + 1))
-
-        def gives(level):
-            start = begins[level] + (1 - bits[level]) * (chunk >> (level + 1))
-            return pl.ds(pl.multiple_of(start, 16), chunk >> (level + 1))
+        self.scratch = [room(2, chunk)]
+        if only != "slice":
+            self.scratch += [room(2, chunk), room(chunk)]
+        if only != "chip":
+            halves = [room(chunk >> (i + 1)) for i in range(depth)]
+            self.scratch += [room(chunk)] + halves + halves
+        self.scratch += [pltpu.SemaphoreType.DMA((2 + 2 * (3 + 2 * depth), self.count))]
+
+    def events(self, steps, ins, outs, scratch):
+        chunk, depth = self.chunk, len(self.levels)
+        source, refs = ins[0], list(scratch)
+        own, sems = refs[0], refs[-1]
+        refs = refs[1:-1]
+        if self.only != "slice":
+            chip, other = refs[:2]
+            refs = refs[2:]
+        if self.only != "chip":
+            full, halves, doubles = refs[0], refs[1 : 1 + depth], refs[1 + depth :]
+
+        def bounds(i):
+            _, group, _ = spots()
+            begin = 0
+            for j in range(i):
+                bit = (group // (1 << self.levels[j])) % 2
+                begin = begin + bit * (chunk >> (j + 1))
+            return begin
+
+        def keeps(i):
+            return pl.ds(pl.multiple_of(bounds(i + 1), 16), chunk >> (i + 1))
+
+        def gives(i):
+            begin = 2 * bounds(i) + (chunk >> (i + 1)) - bounds(i + 1)
+            return pl.ds(pl.multiple_of(begin, 16), chunk >> (i + 1))
 
         def pair(kind, c):
             return sems.at[2 + 2 * kind, c], sems.at[3 + 2 * kind, c]
 
-        def load(c, place):
-            i, row = place
+        def rows_of(c):
+            return pl.ds(c * chunk, chunk)
+
+        def load(c):
+            if self.only == "slice":
+                return pltpu.make_async_copy(
+                    source.at[rows_of(c), :], own.at[c, 0], sems.at[0, c]
+                )
+            section, _, _ = spots()
             return pltpu.make_async_copy(
-                ins[i].at[section, :, pl.ds(row, chunk), :], own.at[c], sems.at[0, c]
+                source.at[section, :, rows_of(c), :], own.at[c], sems.at[0, c]
             )
 
-        def cross(c, place):
-            i, row = place
+        def cross(c):
+            section, _, _ = spots()
             return remote(
-                ins[i].at[1 - section, :, pl.ds(row, chunk), :],
+                source.at[1 - section, :, rows_of(c), :],
                 chip.at[c],
                 *pair(0, c),
                 where_is("near"),
@@ -1142,89 +1230,84 @@
         def over(c):
             return remote(own.at[c, 1], other.at[c], *pair(1, c), where_is("over"))
 
-        def halve(level, c):
+        def halve(i, c):
             return remote(
-                own.at[c, 0, gives(level), :],
-                halves[level].at[c],
-                *pair(3 + level, c),
-                where_is(level),
+                own.at[c, 0, gives(i), :],
+                halves[i].at[c],
+                *pair(3 + i, c),
+                where_is(self.levels[i]),
             )
 
-        def double(level, c):
+        def double(i, c):
             return remote(
-                full.at[c, keeps(level), :],
-                doubles[level].at[c],
-                *pair(3 + levels + level, c),
-                where_is(level),
+                full.at[c, keeps(i), :],
+                doubles[i].at[c],
+                *pair(3 + depth + i, c),
+                where_is(self.levels[i]),
             )
 
-        def rows_of(c):
-            return pl.ds(pl.multiple_of(c * chunk, 16), chunk)
-
         def store(c):
-            return pltpu.make_async_copy(
-                full.at[c], outs[0].at[rows_of(c), :], sems.at[1, c]
-            )
+            kept = own.at[c, 0] if self.only == "chip" else full.at[c]
+            return pltpu.make_async_copy(kept, outs[0].at[rows_of(c), :], sems.at[1, c])
 
         def tell(c):
             return remote(
                 full.at[c], outs[1].at[rows_of(c), :], *pair(2, c), where_is("near")
             )
 
-        def stage(number, c):
-            if number == 1:
-                load(c, self.places[0]).wait()
-                cross(c, self.places[0]).wait()
+        def act(stage, c):
+            if stage == "enter":
+                load(c).start()
+                cross(c).start()
+            elif stage == "load":
+                load(c).start()
+            elif stage == "loaded":
+                load(c).wait()
+                halve(0, c).start()
+            elif stage == "cross":
+                load(c).wait()
+                cross(c).wait()
                 own[c] = own[c] + chip[c]
                 over(c).start()
-            elif number == 2:
+            elif stage == "over":
                 over(c).wait()
                 own[c, 0] = own[c, 0] + other[c]
-                halve(0, c).start()
-            elif number < 3 + levels:
-                level = number - 3
-                halve(level, c).wait()
-                mine = keeps(level)
-                total = own[c, 0, mine, :] + halves[level][c]
-                if level < levels - 1:
+                if self.only == "chip":
+                    store(c).start()
+                else:
+                    halve(0, c).start()
+            elif stage[0] == "halve":
+                i = stage[1]
+                halve(i, c).wait()
+                mine = keeps(i)
+                total = own[c, 0, mine, :] + halves[i][c]
+                if i < depth - 1:
                     own[c, 0, mine, :] = total
-                    halve(level + 1, c).start()
+                    halve(i + 1, c).start()
                 else:
                     full[c, mine, :] = total
-                    double(level, c).start()
+                    double(i, c).start()
             else:
-                level = levels - 1 - (number - 3 - levels)
-                double(level, c).wait()
-                full[c, gives(level), :] = doubles[level][c]
-                if level:
-                    double(level - 1, c).start()
+                i = stage[1]
+                double(i, c).wait()
+                full[c, gives(i), :] = doubles[i][c]
+                if i:
+                    double(i - 1, c).start()
                 else:
                     store(c).start()
                     tell(c).start()
 
-        for number in reversed(range(1, 3 + 2 * levels)):
-            since = step - (number if number == 1 else number - 1 + self.patience)
-            c = since // self.spacing
-            due = (since >= 0) & (c < self.count)
-            if self.spacing > 1:
-                due = due & (since % self.spacing == 0)
-
-            @pl.when(due)
-            def _():
-                stage(number, c)
-
-        for c, place in enumerate(self.places):
-
-            @pl.when(step == c * self.spacing)
-            def _():
-                load(c, place).start()
-                cross(c, place).start()
-
-        @pl.when(step == steps - 1)
-        def _():
-            for c in range(self.count):
-                store(c).wait()
+        def leave(c):
+            store(c).wait()
+            if self.only != "chip":
                 tell(c).wait()
+
+        events = []
+        for c, begin in enumerate(self.begins):
+            for i, (stage, due) in enumerate(zip(self.stages, self.dues)):
+                events.append((begin + due, -i, functools.partial(act, stage, c)))
+            events.append((steps - 1, LAST, functools.partial(leave, c)))
+        return events
 
 
 def carry_alone(tasks, steps, collective):
@@ -1232,7 +1315,7 @@
 
     def kernel(*refs):
         i, o = len(carrier.ins), len(carrier.ins) + len(carrier.outs)
-        carrier.run(pl.program_id(0), steps, refs[:i], refs[i:o], refs[o:])
+        carrier.run(pl.program_id(0), 0, 1, steps, refs[:i], refs[i:o], refs[o:])
 
     hold = pl.BlockSpec(memory_space=pl.ANY)
     return pl.pallas_call(
@@ -1265,7 +1348,7 @@
         section, _, _ = spots()
         greet([*GROUP, 0])
         rows_in = spread_rows(tokens_ref, x, row_sems)
-        weight = WeightCopies(qkv_ref, w, *weight_sems)
+        weight = WeightCopies(qkv_ref, w, weight_sems[0])
         weight.start()
         rows_in.start()
         norm_kept = pltpu.make_async_copy(norm_ref, n.at[section], norm_sems.at[0])
@@ -1313,8 +1396,8 @@
         norm_kept.wait()
         norm_near.wait()
         save(n, n_out)
-        weight.forward()
-        weight.forward_last()
+        weight.forward(0)
+        weight.forward_last(0)
         weight.finish()
         save(w, w_out)
         rows_in.wait_arrival(0)
@@ -1353,7 +1436,7 @@
         scratch_shapes=[pltpu.VMEM(*shapes[0]), pltpu.VMEM((rows, width), BF16)]
         + [pltpu.VMEM(*s) for s in shapes[1:]]
         + ROW_SEMS
-        + WeightCopies.sems
+        + [WeightCopies.sems(1)]
         + [
             pltpu.SemaphoreType.DMA((3,)),
             pltpu.SemaphoreType.DMA((12,)),
@@ -1455,7 +1538,7 @@
 
     block = min(256, rows)
     query_block = min(256, rows)
-    chunk = 512
+    chunk = 256
 
     source, target = bring(tokens[0])
     source_norm, target_norm = (
@@ -1491,7 +1574,7 @@
     )
     result = take_back(encoded, decoded)
     cross_q_grad, memory_grads, _ = attend_back(
-        cross_q, memory, cross_mix, cross_mix_grad, cross_lse, cross_span, query_block, chunk
+        cross_q, memory, cross_mix, cross_mix_grad, cross_lse, cross_span, chunk
     )
     memory_grads = pieces_home(memory_grads)
     dec_first_grad, dec_mix_grad, cross_query_grad, dec_out, step = decoder_middle_back(
@@ -1522,11 +1605,11 @@
     up_grad, down_grad = home(enc_up, dec_up, 1), home(enc_down, dec_down, 0)
     out_grad, cross_grad = home(enc_out, dec_out, 0), home(enc_cross, dec_cross, 2)
     dec_q_grad, dec_kv_grads, _ = attend_back(
-        dec_q, dec_kv, dec_mix, dec_mix_grad, dec_lse, target_span, query_block, chunk
+        dec_q, dec_kv, dec_mix, dec_mix_grad, dec_lse, target_span, chunk
     )
     dec_kv_grads = pieces_home(dec_kv_grads)
     enc_q_grad, enc_kv_grads, _ = attend_back(
-        enc_q, enc_kv, enc_mix, enc_mix_grad, enc_lse, source_span, query_block, chunk
+        enc_q, enc_kv, enc_mix, enc_mix_grad, enc_lse, source_span, chunk
     )
     enc_kv_grads = pieces_home(enc_kv_grads)
     target_grad, dec_qkv, _ = input_back(
@@ -1563,7 +1646,11 @@
     is_first = section == 0
     block = min(256, rows)
     query_block = min(256, rows)
-    chunk = 512
+    chunk = 256
+    levels = lax.axis_size("dp").bit_length() - 1
+
+    def hops(*steps):
+        return list(steps[:levels]) + list(steps[3 : 3 + levels])
 
     def swap(value):
         return lax.ppermute(value, "section", [(0, 1), (1, 0)])
@@ -1590,28 +1677,35 @@
     enc_x, dec_x, enc_norm_in, dec_norm_in = At(x, 0), At(x, 1), At(norm, 0), At(norm, 1)
     enc_q, dec_q = At(q, 0), At(q, 1)
     enc_kv, dec_kv = [[At(kv_own, side), At(kv_other, side)] for side in range(2)]
-    enc_mix, enc_lse, out, cross, up = attend(
+    enc_mix, enc_lse, out, up = attend(
         enc_q,
         enc_kv,
         spans[0],
         query_block,
         Carry(
             [
-                SpreadWeight(self_out[0], 3, 5),
-                SpreadWeight(flat(cross_proj), 7, 10),
-                SpreadWeight(ffn_up[0], 12, 15),
+                SpreadWeight(self_out[0], [3], [5]),
+                SpreadWeight(ffn_up[0], [4, 5, 6, 7], [6, 7, 7, 7]),
             ],
             2,
         ),
-    )
-    cross = cross.reshape(2, 2, *cross_proj.shape[1:])
-    dec_mix, dec_lse, down, dec_cot = attend(
+        2,
+    )
+    dec_mix, dec_lse, down, cross = attend(
         dec_q,
         dec_kv,
         spans[1],
         query_block,
-        Carry([SpreadWeight(ffn_down[0], 8, 14), SpreadRows(cotangent[0], (1,))], 3),
-    )
+        Carry(
+            [
+                SpreadWeight(ffn_down[0], [3, 4, 5, 6], [5, 6, 7, 7]),
+                SpreadWeight(flat(cross_proj), [7, 7], [7, 7]),
+            ],
+            3,
+        ),
+        2,
+    )
+    cross = cross.reshape(2, 2, *cross_proj.shape[1:])
     encoded, memory, enc_first, enc_third = encoder_forward(
         enc_x,
         enc_mix,
@@ -1626,17 +1720,17 @@
     cross_q, dec_first = decoder_middle(
         dec_x, dec_mix, dec_norm_in, parts(out, 1), parts(cross, 1), block
     )
-    cross_mix, cross_lse, enc_cot, encoded = attend(
+    cross_mix, cross_lse, cot = attend(
         cross_q,
         memory,
         spans[2],
         query_block,
-        Carry([SpreadRows(cotangent[0], (0,)), ReturnRows(encoded, 0)], 4),
+        Carry([SpreadRows(cotangent[0], (0, 1))], 4),
     )
     decoded, second_grad, cross_mix_grad, cross_out_grad, ffn_dec, dec_norm = decoder_turn(
         dec_first,
         cross_mix,
-        At(dec_cot, 1),
+        At(cot, 1),
         dec_norm_in,
         parts(cross, 1),
         parts(up, 1),
@@ -1644,18 +1738,19 @@
         block,
         True,
     )
-    cross_q_grad, memory_grads, (ffn_dec, ffn_dec_other, decoded) = attend_back(
+    cross_q_grad, memory_grads, (ffn_dec, decoded) = attend_back(
         cross_q,
         memory,
         cross_mix,
         cross_mix_grad,
         cross_lse,
         spans[2],
-        query_block,
         chunk,
-        Carry([Reduce([ffn_dec], 256, 2, 2), ReturnRows(decoded, 1)], 5),
-    )
-    memory_grads = [memory_grads[0], swap(memory_grads[1])]
+        Carry(
+            [Reduce(ffn_dec, 256, [0, 1, 2, 3], [1, 2], "chip"), ReturnRows(decoded, 1, 4)], 5
+        ),
+        2,
+    )
     dec_first_grad, dec_mix_grad, cross_query_grad, dec_out, step = decoder_middle_back(
         dec_first,
         dec_mix,
@@ -1672,7 +1767,7 @@
         enc_third,
         enc_mix,
         memory_grads,
-        At(enc_cot, 0),
+        At(cot, 0),
         enc_norm_in,
         parts(out, 0),
         parts(up, 0),
@@ -1681,18 +1776,30 @@
         block,
         [dec_out, cross_query_grad, cross_out_grad],
     )
-    dec_q_grad, dec_kv_grads, (ffn_enc, ffn_enc_other) = attend_back(
+    dec_q_grad, dec_kv_grads, (ffn_dec, ffn_dec_other, ffn_enc, sides) = attend_back(
         dec_q,
         dec_kv,
         dec_mix,
         dec_mix_grad,
         dec_lse,
         spans[1],
-        query_block,
         chunk,
-        Carry([Reduce([ffn_enc], 256, 2, 2)], 6),
-    )
-    dec_kv_grads = [dec_kv_grads[0], swap(dec_kv_grads[1])]
+        Carry(
+            [
+                Reduce(
+                    ffn_dec,
+                    256,
+                    [0, 1, 2, 3],
+                    [1, *hops(2, 1, 2, 1, 1, 2)],
+                    "slice",
+                ),
+                Reduce(ffn_enc, 256, [0, 2, 4, 6], [1, 4], "chip"),
+                Reduce(sides, 384, [7, 8, 10, 11], [1, 3], "chip"),
+            ],
+            6,
+        ),
+        4,
+    )
     target_grad, dec_qkv = input_back(
         dec_x,
         dec_first_grad,
@@ -1704,18 +1811,39 @@
         block,
         [],
     )
-    enc_q_grad, enc_kv_grads, (sides, sides_other, target_grad) = attend_back(
+    enc_q_grad, enc_kv_grads, (ffn_enc, ffn_enc_other, sides, _, dec_qkv, dec_qkv_other, target_grad, encoded) = attend_back(
         enc_q,
         enc_kv,
         enc_mix,
         enc_mix_grad,
         enc_lse,
         spans[0],
-        query_block,
         chunk,
-        Carry([Reduce([sides, dec_qkv], 384, 1, 2), ReturnRows(target_grad, 1)], 7),
-    )
-    enc_kv_grads = [enc_kv_grads[0], swap(enc_kv_grads[1])]
+        Carry(
+            [
+                Reduce(
+                    ffn_enc,
+                    256,
+                    [0, 1, 2, 3],
+                    [1, *hops(2, 1, 2, 1, 1, 2)],
+                    "slice",
+                ),
+                Reduce(
+                    sides,
+                    384,
+                    [0, 1, 2, 3],
+                    [1, *hops(2, 1, 2, 1, 1, 2)],
+                    "slice",
+                    [1, 2, 0] if levels == 3 else None,
+                ),
+                Reduce(dec_qkv, 384, [0, 1], [1, 3, *hops(2, 1, 2, 1, 1, 2)]),
+                ReturnRows(target_grad, 1, 4),
+                ReturnRows(encoded, 0, 4),
+            ],
+            7,
+        ),
+        4,
+    )
     source_grad, enc_qkv = input_back(
         enc_x,
         enc_first_grad,
@@ -1727,12 +1855,16 @@
         block,
         [enc_norm, dec_norm],
     )
-    reduce = Reduce([enc_qkv], enc_qkv.shape[2] // 2, 1, 1)
     last, last_other, source_grad = carry_alone(
-        [reduce, ReturnRows(source_grad, 0)], reduce.steps, 8
-    )
-
-    side_rows, half = 3 * width, 3 * width // 2
+        [
+            Reduce(enc_qkv, enc_qkv.shape[2] // 2, [0, 1], [1, 1, *hops(1, 1, 1, 1, 1, 1)]),
+            ReturnRows(source_grad, 0, 4),
+        ],
+        4 + 2 * levels,
+        8,
+    )
+
+    half = 3 * width // 2
     up_grad = jnp.where(is_first, ffn_enc, ffn_dec_other).astype(F32)
     down_grad = jnp.where(is_first, ffn_enc_other, ffn_dec).astype(F32)
     up_grad = jnp.concatenate(jnp.split(up_grad, 2, axis=0), axis=1)
@@ -1742,13 +1874,13 @@
 
     qkv_grad = jnp.concatenate(
         [
-            jnp.where(is_first, columns(last), sides_other[side_rows:]),
-            jnp.where(is_first, columns(last_other), sides[side_rows:]),
+            jnp.where(is_first, columns(last), dec_qkv_other),
+            jnp.where(is_first, columns(last_other), dec_qkv),
         ],
         axis=0,
     )
     qkv_grad = qkv_grad.astype(F32).reshape(self_qkv.shape)
-    sides = sides[:side_rows].astype(F32)
+    sides = sides.astype(F32)
     out_grad = jnp.concatenate([sides[: width // 2], sides[width // 2 : width]], axis=1)
     cross_grad = sides[width:].reshape(cross_proj.shape)
     norm_grad = last[2 * half : 2 * half + 24].astype(F32).reshape(norms.shape)

time: 615 us -> 533 us (0.87)
  Pallas kernels: 565 us -> 494 us
    pallas_call x6, Pallas kernels: 356 us -> 304 us  [the longest x3 200 us: attend_back(): pl.pallas_call(kernel, grid=(pairs,), in_specs=[pl.BlockSpec(memory_space...]
    pallas_call x7, Pallas kernels: 113 us -> 103 us  [row_call(): pl.pallas_call(kernel, grid=(rows // block,), in_specs=[blocked(a, dim) f...]
    pallas_call x1, Pallas kernels: 50.9 us -> 42.1 us  [carry_alone(): pl.pallas_call(kernel, grid=(steps,), in_specs=[hold] * len(carrier.ins),...]
  transfers between devices with their start and end apart: 4 -> 1, of which waited for: 1 -> 0; matrix products, arithmetic and copies ran while one was open for 1% -> 0% of each run, Pallas kernels for 4% -> 1%
where the time goes in v4:
time: 533 us; the launch traced here: 527 us
  Pallas kernels  494 us (93%)
  other arithmetic  12.7 us (2%)
  between operations  10.2 us (2%)
  local copies, waits for them, and re-layouts  9.88 us (2%)
    pallas_call x3, Pallas kernels, attend_back(): pl.pallas_call(kernel, grid=(pairs,), in_specs=[pl.BlockSpec(memory_space...  200 us
    pallas_call x3, Pallas kernels, attend(): pl.pallas_call(kernel, grid=(pairs,), in_specs=[pl.BlockSpec(memory_space...  103 us
    pallas_call x7, Pallas kernels, row_call(): pl.pallas_call(kernel, grid=(rows // block,), in_specs=[blocked(a, dim) f...  103 us
    pallas_call x1, Pallas kernels, open_up(): pl.pallas_call(kernel, in_specs=[hold] * 3, out_specs=[hold] * 6, out_sha...  45.5 us
    pallas_call x1, Pallas kernels, carry_alone(): pl.pallas_call(kernel, grid=(steps,), in_specs=[hold] * len(carrier.ins),...  42.1 us
  transfers between devices with their start and end apart: 1, of which 0 were waited for; matrix products, arithmetic and copies ran while one was open for 0% of the time, Pallas kernels for 1%

profile of v4, /device:TPU:0, one launch (start us, length us, event | category | flops | bytes accessed | tf_op | source)
XLA Modules:
  0.0 526.9 jit_solution(9459408437021865936)
XLA Ops:
  0.6 1.4 constant_dynamic-slice_fusion.2
  9.8 45.5 %open_up.1 = (bf16[2,1024,512]{2,1,0:T(8,128)(2,1)}, bf16[2,2,1536,256]{3,2,1,0:T(8,128)(2,1)}, f32[2,3,2,512]{3,2,1,0:T(2,128)}, bf16[2,2,1024,256]{3,2,1,0:T(8...) custom-call(bf16[2,1024,512]{2,1,0:T(8,128)(2,1)} %bitcast.52, ...), custom_call_target="tpu_custom_call" | custom-call | tf_op jit(solution)/shard_map/open_up/pallas_call | solution.py:1431
  55.3 0.6 add_add_fusion
  55.9 34.5 %attend.3 = (bf16[2,1024,256]{2,1,0:T(8,128)(2,1)}, f32[1024,512]{1,0:T(8,128)}, bf16[2,2,256,512]{3,2,1,0:T(8,128)(2,1)}, bf16[2,2,512,1024]{3,2,1,0:T(8,128)(2,1)}) custom-call(s32[4]{0:T(128)} %get-tuple-element.156.span_ref, bf16[2,2,1024,256]{3,2,1,0:T(8,128)(2,1)} %get-tuple-element.76.q_ref, bf16[2,2,2,1024,256]{4,3,2,1,0:T(8,128)(2,1)} %get-tuple-element.77.refs_0_, ...), custom_call_target="tpu_custom_call" | custom-call | flops 17179869184 | bytes 8388608 | tf_op jit(solution)/shard_map/attend/pallas_call | solution.py:646
  90.5 36.8 %attend.4 = (bf16[2,1024,256]{2,1,0:T(8,128)(2,1)}, f32[1024,512]{1,0:T(8,128)}, bf16[2,2,1024,512]{3,2,1,0:T(8,128)(2,1)}, bf16[2,2,1024,256]{3,2,1,0:T(8,128)(2,1)}) custom-call(s32[4]{0:T(128)} %get-tuple-element.157.span_ref, bf16[2,2,1024,256]{3,2,1,0:T(8,128)(2,1)} %get-tuple-element.76.q_ref, bf16[2,2,2,1024,256]{4,3,2,1,0:T(8,128)(2,1)} %get-tuple-element.77.refs_0_, ...), custom_call_target="tpu_custom_call" | custom-call | flops 17179869184 | bytes 8388608 | tf_op jit(solution)/shard_map/attend/pallas_call | solution.py:646
  127.3 13.7 %encoder_forward.1 = (bf16[1024,512]{1,0:T(8,128)(2,1)}, bf16[2,2,1024,256]{3,2,1,0:T(8,128)(2,1)}, f32[1024,512]{1,0:T(8,128)}, f32[1024,512]{1,0:T(8,128)}) custom-call(bf16[2,1024,512]{2,1,0:T(8,128)(2,1)} %get-tuple-element.80.refs_0_, bf16[2,1024,256]{2,1,0:T(8,128)(2,1)} %get-tuple-element.79.refs_1_.refs_2_.mix_ref, ...), custom_call_target="tpu_custom_call" | custom-call | flops 5905580032 | bytes 7876608 | tf_op jit(solution)/shard_map/encoder_forward/pallas_call | solution.py:138
  140.9 0.4 collective-permute-start
  142.6 6.0 %decoder_middle.1 = (bf16[2,1024,256]{2,1,0:T(8,128)(2,1)}, f32[1024,512]{1,0:T(8,128)}) custom-call(bf16[2,1024,512]{2,1,0:T(8,128)(2,1)} %get-tuple-element.80.refs_0_, bf16[2,1024,256]{2,1,0:T(8,128)(2,1)} %get-tuple-element.88.refs_1_.mix_ref, f32[2,3,2,512]{3,2,1,0:T(2,128)} %get-tuple-element.81.refs_2_.refs_3_.refs_4_.refs_6_.refs_5_, ...), custom_call_target="tpu_custom_call" | custom-call | flops 1073741824 | bytes 3682304 | tf_op jit(solution)/shard_map/decoder_middle/pallas_call | solution.py:138
  148.7 0.6 add_add_fusion.2.span_ref
  149.3 0.0 collective-permute-done.refs_1_
  149.3 0.0 copy-start.13
  149.3 1.3 copy-done.13
  150.6 31.9 %attend.5 = (bf16[2,1024,256]{2,1,0:T(8,128)(2,1)}, f32[1024,512]{1,0:T(8,128)}, bf16[2,1024,512]{2,1,0:T(8,128)(2,1)}) custom-call(s32[4]{0:T(128)} %add_add_fusion.2.span_ref, bf16[2,1024,256]{2,1,0:T(8,128)(2,1)} %get-tuple-element.89.q_ref, bf16[2,2,1024,256]{3,2,1,0:T(8,128)(2,1)} %get-tuple-element.90.refs_0_, bf16[2,2,1024,256]{3,2,1,0:T(8,128)(2,1)} %copy-done.13, ...), custom_call_target="tpu_custom_call" | custom-call | flops 17179869184 | bytes 8388608 | tf_op jit(solution)/shard_map/attend/pallas_call | solution.py:646
  182.5 27.1 %decoder_turn.1 = (bf16[1024,512]{1,0:T(8,128)(2,1)}, f32[1024,512]{1,0:T(8,128)}, bf16[2,1024,256]{2,1,0:T(8,128)(2,1)}, bf16[2,512,256]{2,1,0:T(8,128)(2,1)}, ...) custom-call(f32[1024,512]{1,0:T(8,128)} %get-tuple-element.93.refs_0_, ...), custom_call_target="tpu_custom_call" | custom-call | flops 14495514624 | bytes 9449472 | tf_op jit(solution)/shard_map/decoder_turn/pallas_call | solution.py:138
  209.6 54.8 %attend_back.3 = (bf16[2,1024,256]{2,1,0:T(8,128)(2,1)}, bf16[2,2,1024,256]{3,2,1,0:T(8,128)(2,1)}, bf16[2,2,1024,256]{3,2,1,0:T(8,128)(2,1)}, bf16[1024,512]{1,0:T(8,128)(2,1)}, bf16[2,1024,512]{2,1,0:T(8,128)(2,1)}) custom-call(s32[4]{0:T(128)} %add_add_fusion.2.span_ref, bf16[2,1024,256]{2,1,0:T(8,128)(2,1)} %get-tuple-element.89.q_ref, ...), custom_call_target="tpu_custom_call" | custom-call | flops 42949672960 | bytes 16777216 | tf_op jit(solution)/shard_map/attend_back/pallas_call | solution.py:801
  264.4 0.0 copy-start.12
  264.4 9.3 %decoder_middle_back.1 = (f32[1024,512]{1,0:T(8,128)}, bf16[2,1024,256]{2,1,0:T(8,128)(2,1)}, bf16[2,512,256]{2,1,0:T(8,128)(2,1)}, bf16[2,256,512]{2,1,0:T(8,128)(2,1)}, f32[3,2,512]{2,1,0:T(2,128)}) custom-call(f32[1024,512]{1,0:T(8,128)} %get-tuple-element.93.refs_0_, bf16[2,1024,256]{2,1,0:T(8,128)(2,1)} %get-tuple-element.88.refs_1_.mix_ref, ...), custom_call_target="tpu_custom_call" | custom-call | flops 2147483648 | bytes 7876608 | tf_op jit(solution)/shard_map/decoder_middle_back/pallas_call | solution.py:138
  273.7 0.0 copy-done.12
  273.7 1.3 add.19.refs_9_
  275.1 28.4 %encoder_back.1 = (f32[1024,512]{1,0:T(8,128)}, bf16[2,1024,256]{2,1,0:T(8,128)(2,1)}, bf16[2,2,1024,512]{3,2,1,0:T(8,128)(2,1)}, bf16[2,2,1536,256]{3,2,1,0:T(8,128)(2,1)}, f32[3,2,512]{2,1,0:T(2,128)}) custom-call(f32[1024,512]{1,0:T(8,128)} %get-tuple-element.86.refs_0_, f32[1024,512]{1,0:T(8,128)} %get-tuple-element.87.refs_1_, ...), custom_call_target="tpu_custom_call" | custom-call | flops 13958643712 | bytes 17838080 | tf_op jit(solution)/shard_map/encoder_back/pallas_call | solution.py:138
  303.5 65.0 %attend_back.4 = (bf16[2,1024,256]{2,1,0:T(8,128)(2,1)}, bf16[2,2,1024,256]{3,2,1,0:T(8,128)(2,1)}, bf16[2,2,1024,256]{3,2,1,0:T(8,128)(2,1)}, bf16[1024,512]{1,...) custom-call(s32[4]{0:T(128)} %get-tuple-element.157.span_ref, ...), custom_call_target="tpu_custom_call" | custom-call | flops 42949672960 | bytes 16777216 | tf_op jit(solution)/shard_map/attend_back/pallas_call | solution.py:801
  368.5 8.5 %input_back.2 = (bf16[1024,512]{1,0:T(8,128)(2,1)}, bf16[2,2,768,256]{3,2,1,0:T(8,128)(2,1)}) custom-call(bf16[2,1024,512]{2,1,0:T(8,128)(2,1)} %get-tuple-element.80.refs_0_, f32[1024,512]{1,0:T(8,128)} %get-tuple-element.114.refs_1_, bf16[2,1024,256]{2,1,0:T(8,128)(2,1)} %get-tuple-element.115.refs_2_, ...), custom_call_target="tpu_custom_call" | custom-call | flops 3221225472 | bytes 9973760 | tf_op jit(solution)/shard_map/input_back/pallas_call | solution.py:138
  377.0 80.6 %attend_back.5 = (bf16[2,1024,256]{2,1,0:T(8,128)(2,1)}, bf16[2,2,1024,256]{3,2,1,0:T(8,128)(2,1)}, bf16[2,2,1024,256]{3,2,1,0:T(8,128)(2,1)}, bf16[1024,512]{1,...) custom-call(s32[4]{0:T(128)} %get-tuple-element.156.span_ref, ...), custom_call_target="tpu_custom_call" | custom-call | flops 42949672960 | bytes 16777216 | tf_op jit(solution)/shard_map/attend_back/pallas_call | solution.py:801
  457.5 9.6 %input_back.3 = (bf16[1024,512]{1,0:T(8,128)(2,1)}, bf16[2,2,1792,128]{3,2,1,0:T(8,128)(2,1)}) custom-call(bf16[2,1024,512]{2,1,0:T(8,128)(2,1)} %get-tuple-element.80.refs_0_, f32[1024,512]{1,0:T(8,128)} %get-tuple-element.124.refs_1_, bf16[2,1024,256]{2,1,0:T(8,128)(2,1)} %get-tuple-element.125.refs_2_, ...), custom_call_target="tpu_custom_call" | custom-call | flops 3221225472 | bytes 9998336 | tf_op jit(solution)/shard_map/input_back/pallas_call | solution.py:138
  467.1 0.0 copy-start
  467.1 42.1 %carry_alone.1 = (bf16[1792,128]{1,0:T(8,128)(2,1)}, bf16[1792,128]{1,0:T(8,128)(2,1)}, bf16[2,1024,512]{2,1,0:T(8,128)(2,1)}) custom-call(bf16[2,2,1792,128]{3,2,1,0:T(8,128)(2,1)} %get-tuple-element.131.refs_0_, bf16[1024,512]{1,0:T(8,128)(2,1)} %get-tuple-element.132.refs_1_), custom_call_target="tpu_custom_call" | custom-call | tf_op jit(solution)/shard_map/carry_alone/pallas_call | solution.py:1321
  509.3 0.0 copy-start.11
  509.3 0.7 slice_convert_fusion
  510.0 1.0 fusion.2
  511.1 0.0 copy-start.10
  511.1 0.0 copy-done
  511.1 0.0 copy-start.9
  511.1 1.0 slice.80
  512.2 0.6 reshape.73
  512.8 0.0 copy-done.11
  512.8 0.0 copy-done.10
  512.8 0.1 maximum_select_fusion
  513.0 0.0 copy-done.9
  513.0 0.1 maximum_select_fusion.1
  513.1 0.0 copy-start.6
  513.1 0.0 copy-start.8
  513.1 0.1 pad_maximum_fusion
  513.2 1.3 convert.5
  514.5 0.1 copy-done.6
  514.5 0.7 copy-done.8
  515.2 0.1 select_convert_fusion
  515.4 0.0 copy-start.1
  515.4 0.0 copy-start.2
  515.4 0.2 fusion
  515.6 1.4 copy-done.1
  517.0 0.6 copy-done.2
  517.6 0.0 copy-start.3
  517.6 0.0 copy-start.4
  517.6 1.5 select_bitcast_fusion
  519.1 0.8 copy-done.3
  519.9 0.6 copy-done.4
  520.6 0.0 copy-start.5
  520.6 0.0 copy-start.7
  520.6 2.3 bitcast_convert_fusion
  522.9 0.9 maximum_bitcast_fusion.1
  523.7 0.0 copy-done.5
  523.7 0.0 copy-done.7
  523.7 1.5 bitcast_convert_fusion.1
  525.2 1.5 maximum_bitcast_fusion
  (2 shorter events, 0.1 us)
Async XLA Ops:
  140.9 8.3 %collective-permute-start = (bf16[2,2,1024,256]{3,2,1,0:T(8,128)(2,1)}, bf16[2,2,1024,256]{3,2,1,0:T(8,128)(2,1)S(1)}, u32[]{:S(2)}, u32[]{:S(2)}) collective-permute-start(bf16[2,2,1024,256]{3,2,1,0:T(8,128)(2,1)} %get-tuple-element.90.refs_0_), channel_id=1, source_target_pairs={{0,16},{16,0},{1,17},{17,1},{2,18},{18,2},{3,19},{19,3},{4,20},{20... | collective-permute-start | bytes 6291464 | tf_op jit(solution)/shard_map/ppermute | solution.py:1656
  149.3 1.3 copy-start.13
  264.4 9.3 %copy-start.12 = (f32[3,2,512]{2,1,0:T(2,128)S(1)}, f32[3,2,512]{2,1,0:T(2,128)}, u32[]{:S(2)}) copy-start(f32[3,2,512]{2,1,0:T(2,128)} %get-tuple-element.129) | copy-start | bytes 36868
  467.1 43.9 %copy-start = (bf16[1536,256]{1,0:T(8,128)(2,1)S(1)}, bf16[1536,256]{1,0:T(8,128)(2,1)}, u32[]{:S(2)}) copy-start(bf16[1536,256]{1,0:T(8,128)(2,1)} %get-tuple-element.139) | copy-start | bytes 2359300
  509.3 3.5 copy-start.11
  511.1 1.8 copy-start.10
  511.1 1.8 copy-start.9
  513.1 1.4 copy-start.6
  513.1 2.1 copy-start.8
  515.4 1.6 copy-start.1
  515.4 2.2 copy-start.2
  517.6 2.3 copy-start.3
  517.6 3.0 copy-start.4
  520.6 3.2 copy-start.5
  520.6 3.2 copy-start.7

commit v5 on v4

--- a/solution.py
+++ b/solution.py
@@ -82,11 +82,11 @@
 
 
 def row_call(
-    body, name, rows, block, row_ins, whole_ins, row_outs, sum_outs, flops, finish=None, finals=None
+    body, name, rows, row_ins, whole_ins, row_outs, keeps, finals, finish, flops, into=None
 ):
+    block, part = min(512, rows), min(256, rows)
     row_ins = [(at(a), dim) for a, dim in row_ins]
     whole_ins = [at(a) for a in whole_ins]
-    finals = sum_outs if finals is None else finals
 
     def blocked(array, dim):
         sizes = tuple(block if i == dim else size for i, size in enumerate(array.shape))
@@ -96,6 +96,12 @@
         sizes = tuple(block if i == dim else size for i, size in enumerate(shape))
         return pl.BlockSpec(
             sizes, lambda g: tuple(g if i == dim else 0 for i in range(len(shape)))
+        )
+
+    def sided_out(shape, dim):
+        plain = blocked_out(shape, dim)
+        return pl.BlockSpec(
+            (None, *plain.block_shape), lambda g: (into[0], *plain.index_map(g))
         )
 
     def whole(array):
@@ -112,115 +118,143 @@
 
     n_rows_in = len(row_ins)
     n_in = n_rows_in + len(whole_ins)
-    n_row, n_sum = len(row_outs), len(finals)
+    n_row, n_final = len(row_outs), len(finals)
+    out_specs = [blocked_out(shape, dim) for shape, _, dim in row_outs]
+    out_shapes = [jax.ShapeDtypeStruct(shape, dtype) for shape, dtype, _ in row_outs]
+    held, aliases = [], {}
+    if into is not None:
+        shape, dtype, dim = row_outs[-1]
+        out_specs[-1] = sided_out(shape, dim)
+        out_shapes[-1] = jax.ShapeDtypeStruct((2, *shape), dtype)
+        if into[1] is not None:
+            held, aliases = [into[1]], {n_in: n_row - 1}
 
     def kernel(*refs):
-        ins, outs = refs[:n_in], refs[n_in : n_in + n_row]
-        sums, totals = refs[n_in + n_row : n_in + n_row + n_sum], refs[n_in + n_row + n_sum :]
-
-        @pl.when(pl.program_id(0) == 0)
-        def _():
-            for total in totals:
-                total[...] = jnp.zeros_like(total)
-
-        body(ins, outs, totals)
-
-        @pl.when(pl.program_id(0) == pl.num_programs(0) - 1)
-        def _():
-            if finish is None:
-                for out, total in zip(sums, totals):
-                    out[...] = total[...].astype(out.dtype)
-            else:
-                finish(ins[n_rows_in:], totals, sums)
+        ins, refs = refs[:n_in], refs[len(held) :]
+        outs = refs[n_in : n_in + n_row]
+        last_outs, kept = refs[n_in + n_row : n_in + n_row + n_final], refs[n_in + n_row + n_final :]
+        step = pl.program_id(0)
+        if finals:
+
+            @pl.when(step == 0)
+            def _():
+                kept[-1][...] = jnp.zeros_like(kept[-1])
+
+        turns = []
+        for begin in range(0, block, part):
+            all_rows = pl.ds(pl.multiple_of(step * block + begin, part), part)
+            turns.append(body(ins, outs, kept, slice(begin, begin + part), all_rows))
+        waiting, running = turns[1:], turns[:1]
+        while running:
+            running = [turn for turn in running if next(turn, LAST) is not LAST]
+            if waiting:
+                running.append(waiting.pop(0))
+
+        if finals:
+
+            @pl.when(step == pl.num_programs(0) - 1)
+            def _():
+                finish(ins[n_rows_in:], kept, last_outs)
 
     arrays = [array for array, _ in row_ins] + whole_ins
     size = sum(math.prod(a.shape) * a.dtype.itemsize for a in arrays)
     return pl.pallas_call(
         kernel,
         grid=(rows // block,),
-        in_specs=[blocked(a, dim) for a, dim in row_ins] + [whole(a) for a in whole_ins],
-        out_specs=[blocked_out(shape, dim) for shape, _, dim in row_outs]
-        + [whole_out(shape) for shape, _ in finals],
-        out_shape=[jax.ShapeDtypeStruct(shape, dtype) for shape, dtype, _ in row_outs]
-        + [jax.ShapeDtypeStruct(shape, dtype) for shape, dtype in finals],
-        scratch_shapes=[pltpu.VMEM(shape, F32) for shape, _ in sum_outs],
+        in_specs=[blocked(a, dim) for a, dim in row_ins]
+        + [whole(a) for a in whole_ins]
+        + [pl.BlockSpec(memory_space=pl.ANY)] * len(held),
+        out_specs=out_specs + [whole_out(shape) for shape, _ in finals],
+        out_shape=out_shapes + [jax.ShapeDtypeStruct(shape, dtype) for shape, dtype in finals],
+        input_output_aliases=aliases,
+        scratch_shapes=[pltpu.VMEM(shape, dtype) for shape, dtype in keeps],
         compiler_params=pltpu.CompilerParams(vmem_limit_bytes=VMEM),
         cost_estimate=pl.CostEstimate(flops=flops, bytes_accessed=size, transcendentals=0),
         name=name,
-    )(*[a.array for a in arrays])
-
-
-def column_blocks(wide, into, core, k, row):
-    rows, columns = wide.shape[0], wide.shape[1] // 2
-    for half in range(2):
-        into[core, k, row + half * rows : row + (half + 1) * rows, :] = wide[
-            :, half * columns : (half + 1) * columns
-        ].astype(BF16)
-
-
-def project_qkv(x, norm, weights, with_norm, block):
+    )(*[a.array for a in arrays], *held)
+
+
+LAST = 1000
+
+
+def split(refs, parts, count):
+    return [refs[i * parts : (i + 1) * parts] for i in range(count)]
+
+
+def project_qkv(x, norm, weights, with_norm):
+    x = at(x)
     rows, width = x.shape
     parts, part = len(weights), weights[0].shape[-1]
     score = LOG2E / math.sqrt(width // HEADS)
 
-    def body(ins, outs, totals):
+    def body(ins, outs, kept, own, all_rows):
         x_ref, norm_ref, *w = ins
         q_ref, kv_ref = outs
-        rows_in = x_ref[...]
+        low = x_ref[own, :]
         if with_norm:
-            unit, _ = standardize(rows_in.astype(F32))
-            rows_in = affine(unit, norm_ref, 2).astype(BF16)
+            unit, _ = standardize(low.astype(F32))
+            low = affine(unit, norm_ref, 2).astype(BF16)
+        yield
         for k in range(parts):
-            q_ref[k] = (dot_nn(rows_in, w[k][0]) * score).astype(BF16)
-            kv_ref[k, 0] = dot_nn(rows_in, w[k][1]).astype(BF16)
-            kv_ref[k, 1] = dot_nn(rows_in, w[k][2]).astype(BF16)
+            q_ref[k, own, :] = (dot_nn(low, w[k][0]) * score).astype(BF16)
+            kv_ref[k, 0, own, :] = dot_nn(low, w[k][1]).astype(BF16)
+            kv_ref[k, 1, own, :] = dot_nn(low, w[k][2]).astype(BF16)
+            yield
 
     return row_call(
         body,
         "project_qkv",
         rows,
-        block,
         [(x, 0)],
         [norm, *weights],
         [((parts, rows, part), BF16, 1), ((parts, 2, rows, part), BF16, 2)],
         [],
+        [],
+        None,
         6 * rows * width * width,
     )
 
 
-def encoder_forward(x, mix, norm, out, up, down, cross, block):
+def encoder_forward(x, mix, norm, out, up, down, cross):
+    x = at(x)
     rows, width = x.shape
     parts, part = len(out), out[0].shape[0]
 
-    def body(ins, outs, totals):
+    def body(ins, outs, kept, own, all_rows):
         x_ref, mix_ref, norm_ref = ins[:3]
-        wo, wu, wd, wc = (ins[3 + i * parts : 3 + (i + 1) * parts] for i in range(4))
+        wo, wu, wd, wc = split(ins[3:], parts, 4)
         result_ref, kv_ref, first_ref, third_ref = outs
-        unit, _ = standardize(x_ref[...].astype(F32))
+        unit, _ = standardize(x_ref[own, :].astype(F32))
         first = affine(unit, norm_ref, 2)
         for k in range(parts):
-            first += dot_nn(mix_ref[k], wo[k][...])
-        first_ref[...] = first
+            first += dot_nn(mix_ref[k, own, :], wo[k][...])
+        yield
+        first_ref[own, :] = first
         unit, _ = standardize(first)
         third = affine(unit, norm_ref, 0)
         low = third.astype(BF16)
+        inner = dot_nn(low, wu[0][...])
+        yield
         for k in range(parts):
-            act = gelu(dot_nn(low, wu[k][...])).astype(BF16)
+            act = gelu(inner).astype(BF16)
+            if k + 1 < parts:
+                inner = dot_nn(low, wu[k + 1][...])
             third += dot_nn(act, wd[k][...])
-        third_ref[...] = third
+            yield
+        third_ref[own, :] = third
         unit, _ = standardize(third)
         low = affine(unit, norm_ref, 1).astype(BF16)
-        result_ref[...] = low
+        result_ref[own, :] = low
+        yield
         for k in range(parts):
-            kv_ref[k, 0] = dot_nn(low, wc[k][0]).astype(BF16)
-            kv_ref[k, 1] = dot_nn(low, wc[k][1]).astype(BF16)
+            kv_ref[k, 0, own, :] = dot_nn(low, wc[k][0]).astype(BF16)
+            kv_ref[k, 1, own, :] = dot_nn(low, wc[k][1]).astype(BF16)
 
     units = sum(w.shape[1] for w in up)
     return row_call(
         body,
         "encoder_forward",
         rows,
-        block,
         [(x, 0), (mix, 1)],
         [norm, *out, *up, *down, *cross],
         [
@@ -230,339 +264,425 @@
             ((rows, width), F32, 0),
         ],
         [],
+        [],
+        None,
         6 * rows * width * width + 4 * rows * width * units,
     )
 
 
-def decoder_middle(x, mix, norm, out, cross, block):
+def decoder_middle(x, mix, norm, out, cross):
+    x = at(x)
     rows, width = x.shape
     parts, part = len(out), out[0].shape[0]
     score = LOG2E / math.sqrt(width // HEADS)
 
-    def body(ins, outs, totals):
+    def body(ins, outs, kept, own, all_rows):
         x_ref, mix_ref, norm_ref = ins[:3]
-        wo, wc = (ins[3 + i * parts : 3 + (i + 1) * parts] for i in range(2))
+        wo, wc = split(ins[3:], parts, 2)
         q_ref, first_ref = outs
-        first = x_ref[...].astype(F32)
+        first = x_ref[own, :].astype(F32)
         for k in range(parts):
-            first += dot_nn(mix_ref[k], wo[k][...])
-        first_ref[...] = first
+            first += dot_nn(mix_ref[k, own, :], wo[k][...])
+        yield
+        first_ref[own, :] = first
         unit, _ = standardize(first)
         low = affine(unit, norm_ref, 0).astype(BF16)
+        yield
         for k in range(parts):
-            q_ref[k] = (dot_nn(low, wc[k][0]) * score).astype(BF16)
+            q_ref[k, own, :] = (dot_nn(low, wc[k][0]) * score).astype(BF16)
 
     return row_call(
         body,
         "decoder_middle",
         rows,
-        block,
         [(x, 0), (mix, 1)],
         [norm, *out, *cross],
         [((parts, rows, part), BF16, 1), ((rows, width), F32, 0)],
         [],
+        [],
+        None,
         4 * rows * width * width,
     )
 
 
-def ffn_back(low, grad_low, up, down, up_total, down_total, parts):
-    grad = None
+def ffn_finals(low, act, inner, grad, parts, units, paired, up_out, down_out):
     for k in range(parts):
-        act, slope = gelu_both(dot_nn(low, up[k][...]))
-        down_total[k] += dot_tn(act.astype(BF16), grad_low)
-        grad_inner = (dot_nt(grad_low, down[k][...]) * slope).astype(BF16)
-        up_total[k] += dot_tn(low, grad_inner)
-        step = dot_nt(grad_inner, up[k][...])
-        grad = step if grad is None else grad + step
-    return grad
-
-
-def decoder_turn(first, mix, cotangent, norm, cross, up, down, block, paired=False):
+        if paired:
+            half = units // 2
+            for h in range(2):
+                begin = k * units + h * half
+                up_out[0, k, h * half : (h + 1) * half, :] = dot_tn(
+                    low[...], inner[:, begin : begin + half]
+                ).astype(BF16)
+            into = up_out.at[1, k]
+        else:
+            up_out[k] = dot_tn(low[...], inner[:, k * units : (k + 1) * units]).astype(BF16)
+            into = down_out.at[k]
+        into[...] = dot_tn(act[:, k * units : (k + 1) * units], grad[...]).astype(BF16)
+
+
+def decoder_turn(first, mix, cotangent, norm, cross, up, down, paired=False):
     rows, width = first.shape
     parts, part, units = len(cross), cross[0].shape[-1], up[0].shape[1]
 
-    def body(ins, outs, totals):
-        first_ref, mix_ref, cot_ref, norm_ref = ins[:4]
-        wc, wu, wd = (ins[4 + i * parts : 4 + (i + 1) * parts] for i in range(3))
+    def body(ins, outs, kept, own, all_rows):
+        first_ref, cot_ref, mix_ref, norm_ref = ins[:4]
+        wc, wu, wd = split(ins[4:], parts, 3)
         result_ref, second_grad_ref, mix_grad_ref = outs
-        out_total, up_total, down_total, norm_total = totals
-        unit, _ = standardize(first_ref[...])
+        low_keep, act_keep, inner_keep, third_keep, second_keep, norm_total = kept
+        unit, _ = standardize(first_ref[own, :])
         second = affine(unit, norm_ref, 0)
         for k in range(parts):
-            second += dot_nt(mix_ref[k], wc[k][1])
+            second += dot_nt(mix_ref[k, all_rows, :], wc[k][1])
+        yield
         unit_two, inv_two = standardize(second)
         third = affine(unit_two, norm_ref, 2)
         low = third.astype(BF16)
-        acts, slopes = [], []
+        low_keep[all_rows, :] = low
+        inner = dot_nn(low, wu[0][...])
+        yield
+        slopes = []
         for k in range(parts):
-            act, slope = gelu_both(dot_nn(low, wu[k][...]))
-            acts.append(act.astype(BF16))
+            act, slope = gelu_both(inner)
+            act = act.astype(BF16)
             slopes.append(slope)
-            third += dot_nn(acts[k], wd[k][...])
+            if k + 1 < parts:
+                inner = dot_nn(low, wu[k + 1][...])
+            act_keep[all_rows, k * units : (k + 1) * units] = act
+            third += dot_nn(act, wd[k][...])
+            yield
         unit_three, inv_three = standardize(third)
-        result_ref[...] = affine(unit_three, norm_ref, 1).astype(BF16)
+        result_ref[own, :] = affine(unit_three, norm_ref, 1).astype(BF16)
         grad = norm_back(
-            unit_three, inv_three, norm_ref, 1, cot_ref[...].astype(F32), norm_total
+            unit_three, inv_three, norm_ref, 1, cot_ref[own, :].astype(F32), norm_total
         )
         grad_low = grad.astype(BF16)
+        third_keep[all_rows, :] = grad_low
+        grad_act = dot_nt(grad_low, wd[0][...])
+        yield
         for k in range(parts):
-            down_total[k] += dot_tn(acts[k], grad_low)
-            grad_inner = (dot_nt(grad_low, wd[k][...]) * slopes[k]).astype(BF16)
-            up_total[k] += dot_tn(low, grad_inner)
+            grad_inner = (grad_act * slopes[k]).astype(BF16)
+            if k + 1 < parts:
+                grad_act = dot_nt(grad_low, wd[k + 1][...])
+            inner_keep[all_rows, k * units : (k + 1) * units] = grad_inner
             grad += dot_nt(grad_inner, wu[k][...])
+            yield
         grad = norm_back(unit_two, inv_two, norm_ref, 2, grad, norm_total)
-        second_grad_ref[...] = grad
+        second_grad_ref[own, :] = grad
         grad_low = grad.astype(BF16)
+        second_keep[all_rows, :] = grad_low
+        yield
         for k in range(parts):
-            out_total[k] += dot_tn(grad_low, mix_ref[k])
-            mix_grad_ref[k] = dot_nn(grad_low, wc[k][1]).astype(BF16)
-
-    sums = [
-        ((parts, width, part), BF16),
-        ((parts, width, units), BF16),
-        ((parts, units, width), BF16),
-        ((3, 2, width), F32),
-    ]
-    if paired:
-        finals = [sums[0], ((2, parts, units, width), BF16), sums[3]]
-
-        def finish(ins, totals, outs):
-            outs[0][...] = totals[0][...].astype(BF16)
-            for k in range(parts):
-                column_blocks(totals[1][k], outs[1], 0, k, 0)
-                outs[1][1, k] = totals[2][k].astype(BF16)
-            outs[2][...] = totals[3][...]
-
-    else:
-        finals, finish = None, None
-
+            mix_grad_ref[k, own, :] = dot_nn(grad_low, wc[k][1]).astype(BF16)
+
+    def finish(ins, kept, outs):
+        mix_ref = ins[0]
+        low_keep, act_keep, inner_keep, third_keep, second_keep, norm_total = kept
+        for k in range(parts):
+            outs[0][k] = dot_tn(second_keep[...], mix_ref[k]).astype(BF16)
+        ffn_finals(
+            low_keep, act_keep, inner_keep, third_keep, parts, units, paired, outs[1], outs[2]
+        )
+        outs[-1][...] = norm_total[...]
+
+    ffn = (
+        [((2, parts, units, width), BF16)]
+        if paired
+        else [((parts, width, units), BF16), ((parts, units, width), BF16)]
+    )
+    whole = (rows, width)
     return row_call(
         body,
         "decoder_turn",
         rows,
-        block,
-        [(first, 0), (mix, 1), (cotangent, 0)],
-        [norm, *cross, *up, *down],
+        [(first, 0), (cotangent, 0)],
+        [mix, norm, *cross, *up, *down],
+        [(whole, BF16, 0), (whole, F32, 0), ((parts, rows, part), BF16, 1)],
         [
-            ((rows, width), BF16, 0),
-            ((rows, width), F32, 0),
-            ((parts, rows, part), BF16, 1),
+            (whole, BF16),
+            ((rows, parts * units), BF16),
+            ((rows, parts * units), BF16),
+            (whole, BF16),
+            (whole, BF16),
+            ((3, 2, width), F32),
         ],
-        sums,
+        [((parts, width, part), BF16), *ffn, ((3, 2, width), F32)],
+        finish,
         6 * rows * width * width + 12 * rows * width * units * parts,
-        finish,
-        finals,
-    )
-
-
-def decoder_middle_back(first, mix, query_grad, second_grad, norm, out, cross, block):
+    )
+
+
+def decoder_middle_back(first, mix, query_grad, second_grad, norm, out, cross, into=None):
     rows, width = first.shape
     parts, part = len(out), out[0].shape[0]
 
-    def body(ins, outs, totals):
-        first_ref, mix_ref, query_grad_ref, second_grad_ref, norm_ref = ins[:5]
-        wo, wc = (ins[5 + i * parts : 5 + (i + 1) * parts] for i in range(2))
+    def body(ins, outs, kept, own, all_rows):
+        first_ref, second_grad_ref, mix_ref, query_grad_ref, norm_ref = ins[:5]
+        wo, wc = split(ins[5:], parts, 2)
         first_grad_ref, mix_grad_ref = outs
-        query_total, out_total, norm_total = totals
-        unit, inv = standardize(first_ref[...])
-        low = affine(unit, norm_ref, 0).astype(BF16)
-        grad = second_grad_ref[...]
+        low_keep, grad_keep, norm_total = kept
+        unit, inv = standardize(first_ref[own, :])
+        low_keep[all_rows, :] = affine(unit, norm_ref, 0).astype(BF16)
+        grad = second_grad_ref[own, :]
         for k in range(parts):
-            query_total[k] += dot_tn(low, query_grad_ref[k])
-            grad += dot_nt(query_grad_ref[k], wc[k][0])
+            grad += dot_nt(query_grad_ref[k, all_rows, :], wc[k][0])
+        yield
         grad = norm_back(unit, inv, norm_ref, 0, grad, norm_total)
-        first_grad_ref[...] = grad
+        first_grad_ref[own, :] = grad
         grad_low = grad.astype(BF16)
+        grad_keep[all_rows, :] = grad_low
+        yield
         for k in range(parts):
-            out_total[k] += dot_tn(mix_ref[k], grad_low)
-            mix_grad_ref[k] = dot_nt(grad_low, wo[k][...]).astype(BF16)
-
+            mix_grad_ref[k, own, :] = dot_nt(grad_low, wo[k][...]).astype(BF16)
+
+    def finish(ins, kept, outs):
+        mix_ref, query_grad_ref = ins[:2]
+        low_keep, grad_keep, norm_total = kept
+        for k in range(parts):
+            outs[0][k] = dot_tn(low_keep[...], query_grad_ref[k]).astype(BF16)
+            outs[1][k] = dot_tn(mix_ref[k], grad_keep[...]).astype(BF16)
+        outs[2][...] = norm_total[...]
+
+    whole = (rows, width)
     return row_call(
         body,
         "decoder_middle_back",
         rows,
-        block,
-        [(first, 0), (mix, 1), (query_grad, 1), (second_grad, 0)],
-        [norm, *out, *cross],
-        [((rows, width), F32, 0), ((parts, rows, part), BF16, 1)],
+        [(first, 0), (second_grad, 0)],
+        [mix, query_grad, norm, *out, *cross],
+        [(whole, F32, 0), ((parts, rows, part), BF16, 1)],
+        [(whole, BF16), (whole, BF16), ((3, 2, width), F32)],
         [
             ((parts, width, part), BF16),
             ((parts, part, width), BF16),
             ((3, 2, width), F32),
         ],
+        finish,
         8 * rows * width * width,
-    )
+        into,
+    )
+
+
+def added(refs, *index):
+    total = refs[0][index]
+    for ref in refs[1:]:
+        total = total.astype(F32) + ref[index].astype(F32)
+    return total.astype(BF16)
 
 
 def encoder_back(
-    first, third, mix, memory_grads, cotangent, norm, out, up, down, cross, block, paired=None
+    first, third, mix, memory_grads, cotangent, norm, out, up, down, cross, paired=None, into=None
 ):
     rows, width = first.shape
     parts, part, units = len(out), out[0].shape[0], up[0].shape[1]
     pieces = len(memory_grads)
 
-    def body(ins, outs, totals):
-        first_ref, third_ref, mix_ref, cot_ref = ins[:4]
-        memory_refs, norm_ref = ins[4 : 4 + pieces], ins[4 + pieces]
-        rest = ins[5 + pieces :]
-        wo, wu, wd, wc = (rest[i * parts : (i + 1) * parts] for i in range(4))
+    def body(ins, outs, kept, own, all_rows):
+        first_ref, third_ref, cot_ref = ins[:3]
+        memory_refs, mix_ref, norm_ref = ins[3 : 3 + pieces], ins[3 + pieces], ins[4 + pieces]
+        wo, wu, wd, wc = split(ins[5 + pieces :], parts, 4)
         first_grad_ref, mix_grad_ref = outs
-        cross_total, out_total, up_total, down_total, norm_total = totals
-        unit, inv = standardize(third_ref[...])
-        low = affine(unit, norm_ref, 1).astype(BF16)
-        grad = cot_ref[...].astype(F32)
-        for i in range(2):
+        low_keep, memory_keep, mid_keep, act_keep, inner_keep, third_keep, first_keep, norm_total = (
+            kept
+        )
+        grad = cot_ref[own, :].astype(F32)
+        for k in range(parts):
+            for i in range(2):
+                memory = added(memory_refs, k, i, own)
+                memory_keep[k, i, all_rows, :] = memory
+                grad += dot_nt(memory, wc[k][i])
+        yield
+        unit, inv = standardize(third_ref[own, :])
+        low_keep[all_rows, :] = affine(unit, norm_ref, 1).astype(BF16)
+        unit_one, inv_one = standardize(first_ref[own, :])
+        low = affine(unit_one, norm_ref, 0).astype(BF16)
+        mid_keep[all_rows, :] = low
+        inner = dot_nn(low, wu[0][...])
+        grad = norm_back(unit, inv, norm_ref, 1, grad, norm_total)
+        grad_low = grad.astype(BF16)
+        third_keep[all_rows, :] = grad_low
+        grad_act = dot_nt(grad_low, wd[0][...])
+        yield
+        for k in range(parts):
+            act, slope = gelu_both(inner)
+            if k + 1 < parts:
+                inner = dot_nn(low, wu[k + 1][...])
+            act_keep[all_rows, k * units : (k + 1) * units] = act.astype(BF16)
+            grad_inner = (grad_act * slope).astype(BF16)
+            if k + 1 < parts:
+                grad_act = dot_nt(grad_low, wd[k + 1][...])
+            inner_keep[all_rows, k * units : (k + 1) * units] = grad_inner
+            grad += dot_nt(grad_inner, wu[k][...])
+            yield
+        grad = norm_back(unit_one, inv_one, norm_ref, 0, grad, norm_total)
+        first_grad_ref[own, :] = grad
+        grad_low = grad.astype(BF16)
+        first_keep[all_rows, :] = grad_low
+        yield
+        for k in range(parts):
+            mix_grad_ref[k, own, :] = dot_nt(grad_low, wo[k][...]).astype(BF16)
+
+    def finish(ins, kept, outs):
+        mix_ref = ins[0]
+        low_keep, memory_keep, mid_keep, act_keep, inner_keep, third_keep, first_keep, norm_total = (
+            kept
+        )
+        if paired:
+            ffn_finals(
+                mid_keep, act_keep, inner_keep, third_keep, parts, units, True, outs[0], None
+            )
+            dec_out, dec_query, dec_cross = ins[-3:]
+            sides = outs[1]
             for k in range(parts):
-                memory = memory_refs[0][k, i].astype(F32)
-                for ref in memory_refs[1:]:
-                    memory += ref[k, i].astype(F32)
-                memory = memory.astype(BF16)
-                cross_total[k, i] += dot_tn(low, memory)
-                grad += dot_nt(memory, wc[k][i])
-        grad = norm_back(unit, inv, norm_ref, 1, grad, norm_total)
-        unit, inv = standardize(first_ref[...])
-        low = affine(unit, norm_ref, 0).astype(BF16)
-        grad += ffn_back(low, grad.astype(BF16), wu, wd, up_total, down_total, parts)
-        grad = norm_back(unit, inv, norm_ref, 0, grad, norm_total)
-        first_grad_ref[...] = grad
-        grad_low = grad.astype(BF16)
-        for k in range(parts):
-            out_total[k] += dot_tn(mix_ref[k], grad_low)
-            mix_grad_ref[k] = dot_nt(grad_low, wo[k][...]).astype(BF16)
-
-    sums = [
-        ((parts, 2, width, part), BF16),
-        ((parts, part, width), BF16),
-        ((parts, width, units), BF16),
-        ((parts, units, width), BF16),
-        ((3, 2, width), F32),
-    ]
-    if paired is not None:
-        side = 3 * width
+                column_blocks(dot_tn(mix_ref[k], first_keep[...]), sides, 0, k, 0)
+                column_blocks(dec_out[k], sides, 1, k, 0)
+                for i in range(2):
+                    here = slice((1 + i) * width, (2 + i) * width)
+                    sides[0, k, here, :] = dot_tn(low_keep[...], memory_keep[k, i]).astype(BF16)
+                    sides[1, k, here, :] = (dec_query, dec_cross)[i][k]
+        else:
+            for k in range(parts):
+                for i in range(2):
+                    outs[0][k, i] = dot_tn(low_keep[...], memory_keep[k, i]).astype(BF16)
+                outs[1][k] = dot_tn(mix_ref[k], first_keep[...]).astype(BF16)
+            ffn_finals(
+                mid_keep, act_keep, inner_keep, third_keep, parts, units, False, outs[2], outs[3]
+            )
+        outs[-1][...] = norm_total[...]
+
+    if paired:
+        finals = [((2, parts, units, width), BF16), ((2, parts, 3 * width, part), BF16)]
+    else:
         finals = [
-            ((2, parts, units, width), BF16),
-            ((2, parts, side, part), BF16),
-            sums[4],
+            ((parts, 2, width, part), BF16),
+            ((parts, part, width), BF16),
+            ((parts, width, units), BF16),
+            ((parts, units, width), BF16),
         ]
-
-        def finish(ins, totals, outs):
-            dec_out, dec_query, dec_cross = ins[-3:]
-            for k in range(parts):
-                column_blocks(totals[2][k], outs[0], 0, k, 0)
-                outs[0][1, k] = totals[3][k].astype(BF16)
-                column_blocks(totals[1][k], outs[1], 0, k, 0)
-                outs[1][0, k, width:side, :] = (
-                    totals[0][k].reshape(2 * width, part).astype(BF16)
-                )
-                column_blocks(dec_out[k], outs[1], 1, k, 0)
-                outs[1][1, k, width : 2 * width, :] = dec_query[k]
-                outs[1][1, k, 2 * width : side, :] = dec_cross[k]
-            outs[2][...] = totals[4][...]
-
-    else:
-        finals, finish, paired = None, None, []
-
+    whole = (rows, width)
     return row_call(
         body,
         "encoder_back",
         rows,
-        block,
-        [(first, 0), (third, 0), (mix, 1), (cotangent, 0)] + [(m, 2) for m in memory_grads],
-        [norm, *out, *up, *down, *cross, *paired],
-        [((rows, width), F32, 0), ((parts, rows, part), BF16, 1)],
-        sums,
+        [(first, 0), (third, 0), (cotangent, 0)] + [(m, 2) for m in memory_grads],
+        [mix, norm, *out, *up, *down, *cross, *(paired or [])],
+        [(whole, F32, 0), ((parts, rows, part), BF16, 1)],
+        [
+            (whole, BF16),
+            ((parts, 2, rows, part), BF16),
+            (whole, BF16),
+            ((rows, parts * units), BF16),
+            ((rows, parts * units), BF16),
+            (whole, BF16),
+            (whole, BF16),
+            ((3, 2, width), F32),
+        ],
+        [*finals, ((3, 2, width), F32)],
+        finish,
         12 * rows * width * width + 10 * rows * width * units * parts,
-        finish,
-        finals,
-    )
-
-
-def input_back(
-    x, first_grad, query_grad, key_grads, norm, weights, with_norm, block, paired=None
-):
+        into,
+    )
+
+
+def column_blocks(wide, into, core, k, row):
+    rows, columns = wide.shape[0], wide.shape[1] // 2
+    for half in range(2):
+        into[core, k, row + half * rows : row + (half + 1) * rows, :] = wide[
+            :, half * columns : (half + 1) * columns
+        ].astype(BF16)
+
+
+def input_back(x, first_grad, query_grad, key_grads, norm, weights, with_norm, paired=None):
+    x = at(x)
     rows, width = x.shape
     parts, part = len(weights), weights[0].shape[-1]
     pieces = len(key_grads)
-
-    def body(ins, outs, totals):
-        x_ref, first_grad_ref, query_grad_ref = ins[:3]
-        key_refs, norm_ref, w = ins[3 : 3 + pieces], ins[3 + pieces], ins[4 + pieces :][:parts]
+    key_grads = [at(g) for g in key_grads]
+
+    def body(ins, outs, kept, own, all_rows):
+        x_ref, first_grad_ref = ins[:2]
+        key_refs, query_grad_ref, norm_ref = ins[2 : 2 + pieces], ins[2 + pieces], ins[3 + pieces]
+        w = ins[4 + pieces :][:parts]
         (grad_ref,) = outs
-        qkv_total, norm_total = totals
-        low = x_ref[...]
+        low_keep, key_keep, norm_total = kept
+        grad = first_grad_ref[own, :]
+        for k in range(parts):
+            grad += dot_nt(query_grad_ref[k, all_rows, :], w[k][0])
+            for i in range(2):
+                member = added(key_refs, k, i, own)
+                key_keep[k, i, all_rows, :] = member
+                grad += dot_nt(member, w[k][1 + i])
+        yield
+        low = x_ref[own, :]
         if with_norm:
             unit, inv = standardize(low.astype(F32))
             low = affine(unit, norm_ref, 2).astype(BF16)
-        grad = first_grad_ref[...]
+            grad = norm_back(unit, inv, norm_ref, 2, grad, norm_total)
+        low_keep[all_rows, :] = low
+        grad_ref[own, :] = grad.astype(BF16)
+
+    half = 3 * width // 2
+
+    def finish(ins, kept, outs):
+        query_grad_ref = ins[0]
+        low_keep, key_keep, norm_total = kept
+
+        def product(k, i):
+            member = query_grad_ref[k] if i == 0 else key_keep[k, i - 1]
+            return dot_tn(low_keep[...], member)
+
+        if paired is None:
+            for k in range(parts):
+                for i in range(3):
+                    outs[0][k, i] = product(k, i).astype(BF16)
+            outs[1][...] = norm_total[...]
+            return
         for k in range(parts):
-            for i in range(3):
-                if i == 0:
-                    member = query_grad_ref[k]
-                else:
-                    member = key_refs[0][k, i - 1].astype(F32)
-                    for ref in key_refs[1:]:
-                        member += ref[k, i - 1].astype(F32)
-                    member = member.astype(BF16)
-                qkv_total[k, i] += dot_tn(low, member)
-                grad += dot_nt(member, w[k][i])
-        if with_norm:
-            grad = norm_back(unit, inv, norm_ref, 2, grad, norm_total)
-        grad_ref[...] = grad.astype(BF16)
-
-    sums = [((parts, 3, width, part), BF16), ((3, 2, width), F32)]
-    if paired is not None:
-        half = 3 * width // 2
-        shape = (4 * half // 2 + 2 * PAIR, PAIR) if paired else (half, part)
-        finals = [((2, parts, *shape), BF16)]
-
-        def finish(ins, totals, outs):
-            for k in range(parts):
-                both = totals[0][k].reshape(2 * half, part)
-                for core in range(2):
-                    own = both[core * half : (core + 1) * half]
-                    if paired:
-                        column_blocks(own, outs[0], core, k, 0)
-                    else:
-                        outs[0][core, k] = own.astype(BF16)
-            if paired:
-                sides = [ins[-2][...] + totals[1][...], ins[-1][...]]
-                for core, table in enumerate(sides):
-                    lines = [
-                        table[slot, i : i + 1, h * PAIR : (h + 1) * PAIR]
-                        for slot in range(3)
-                        for i in range(2)
-                        for h in range(width // PAIR)
-                    ]
-                    lines.append(jnp.zeros((2 * PAIR - len(lines), PAIR), F32))
-                    lines = jnp.concatenate(lines, axis=0).astype(BF16)
-                    for k in range(parts):
-                        outs[0][core, k, 2 * half :, :] = lines
-
+            both = jnp.concatenate([product(k, i) for i in range(3)], axis=0)
+            for core in range(2):
+                own = both[core * half : (core + 1) * half]
+                column_blocks(own, outs[0], core, k, 0)
+        if paired:
+            tables = ins[-len(paired) :]
+            sides = [tables[0][...] + norm_total[...], sum(t[...] for t in tables[1:])]
+            for core, table in enumerate(sides):
+                lines = [
+                    table[slot, i : i + 1, h * PAIR : (h + 1) * PAIR]
+                    for slot in range(3)
+                    for i in range(2)
+                    for h in range(width // PAIR)
+                ]
+                lines.append(jnp.zeros((2 * PAIR - len(lines), PAIR), F32))
+                lines = jnp.concatenate(lines, axis=0).astype(BF16)
+                for k in range(parts):
+                    outs[0][core, k, 2 * half :, :] = lines
+
+    if paired is None:
+        finals = [((parts, 3, width, part), BF16), ((3, 2, width), F32)]
     else:
-        finals, finish, paired = None, None, []
-
+        finals = [((2, parts, 2 * half + (2 * PAIR if paired else 0), PAIR), BF16)]
+    whole = (rows, width)
     return row_call(
         body,
         "input_back",
         rows,
-        block,
-        [(x, 0), (first_grad, 0), (query_grad, 1)] + [(g, 2) for g in key_grads],
-        [norm, *weights, *paired],
-        [((rows, width), BF16, 0)],
-        sums,
+        [(x, 0), (first_grad, 0)] + [(g, 2) for g in key_grads],
+        [query_grad, norm, *weights, *(paired or [])],
+        [(whole, BF16, 0)],
+        [(whole, BF16), ((parts, 2, rows, part), BF16), ((3, 2, width), F32)],
+        finals,
+        finish,
         12 * rows * width * width,
-        finish,
-        finals,
-    )
-
-
-def widen_keys(span_ref, kv_refs, key_e, key_o, value_e, value_o, rows):
+    )
+
+
+def widen_keys(span, kv_refs, key_e, key_o, value_e, value_o, rows):
     lane = lax.broadcasted_iota(jnp.int32, (rows, PAIR), 1)
     place = lax.broadcasted_iota(jnp.int32, (rows, PAIR), 0)
     low = lane < HALF
     for g, kv_ref in enumerate(kv_refs):
-        spot = place + span_ref[2 + g]
-        live = (spot >= span_ref[0]) & (spot < span_ref[1])
+        spot = place + span[2 + g]
+        live = (spot >= span[0]) & (spot < span[1])
         bias = jnp.where(live, 0.0, MASKED)
         keys, values = kv_ref[0].astype(F32), kv_ref[1].astype(F32)
         own = pl.ds(g * rows, rows)
@@ -572,24 +692,53 @@
         value_o[own, :] = jnp.where(low, 1.0, values).astype(BF16)
 
 
-def attention_specs(per_part, rows):
-    def query_spec(array):
-        return at(array).spec((None, rows, PAIR), lambda i: (i // per_part, 0, i % per_part))
-
-    def kv_spec(array):
-        return at(array).spec(
-            (None, 2, rows, PAIR), lambda i: (i // per_part, 0, 0, i % per_part)
+class Pairs:
+    def __init__(self, query):
+        self.sides = query.shape[:-3]
+        self.parts, self.rows, self.part = query.shape[-3:]
+        self.per_part = self.part // PAIR
+        self.per_side = self.parts * self.per_part
+        self.count = self.per_side * math.prod(self.sides)
+
+    def side(self, i):
+        return (i // self.per_side,) if self.sides else ()
+
+    def place(self, i):
+        i = i % self.per_side
+        return i // self.per_part, i % self.per_part
+
+    def query_spec(self, array):
+        def index(i):
+            part, column = self.place(i)
+            return *self.side(i), part, 0, column
+
+        none = (None,) * len(self.sides)
+        return at(array).spec((*none, None, self.rows, PAIR), index)
+
+    def kv_spec(self, array):
+        def index(i):
+            part, column = self.place(i)
+            return *self.side(i), part, 0, 0, column
+
+        none = (None,) * len(self.sides)
+        return at(array).spec((*none, None, 2, self.rows, PAIR), index)
+
+    def lse_spec(self):
+        none = (None,) * len(self.sides)
+        return pl.BlockSpec(
+            (*none, self.rows, PAIR), lambda i: (*self.side(i), 0, i % self.per_side)
         )
 
-    return query_spec, kv_spec, pl.BlockSpec((rows, PAIR), lambda i: (0, i))
+    def span(self, span_ref, i):
+        side = i // self.per_side if self.sides else 0
+        return [span_ref[side, j] for j in range(span_ref.shape[1])]
 
 
 def attend(query, kv_pieces, span, block, carrier=None, slots=1):
     query, kv_pieces = at(query), [at(piece) for piece in kv_pieces]
     carrier = carrier or Carry()
-    parts, rows, part = query.shape
-    per_part = part // PAIR
-    pairs = parts * per_part
+    heads_of = Pairs(query)
+    rows, pairs = heads_of.rows, heads_of.count
     pieces = len(kv_pieces)
     keys = rows * pieces
     n_carry = len(carrier.ins)
@@ -608,7 +757,8 @@
             carrier.run(place, slot, slots, pairs * slots, carry_ins, carry_outs, refs[4:])
 
         carry(0)
-        widen_keys(span_ref, kv_refs, key_e, key_o, value_e, value_o, rows)
+        span = heads_of.span(span_ref, pl.program_id(0))
+        widen_keys(span, kv_refs, key_e, key_o, value_e, value_o, rows)
         lane = lax.broadcasted_iota(jnp.int32, (block, PAIR), 1)
         low = lane < HALF
         units = []
@@ -640,7 +790,8 @@
                 mixed = jnp.where(low, sums[u - 1], sums[u])
                 out_ref[own, :] = (mixed / pltpu.roll(weight, HALF, 1)).astype(BF16)
 
-    query_spec, kv_spec, lse_spec = attention_specs(per_part, rows)
+    query_spec, kv_spec = heads_of.query_spec, heads_of.kv_spec
+    lse_spec = heads_of.lse_spec()
     plain = jax.ShapeDtypeStruct(query.shape, BF16)
     hold = pl.BlockSpec(memory_space=pl.ANY)
     return pl.pallas_call(
@@ -651,7 +802,7 @@
         + [hold] * n_carry,
         out_specs=[query_spec(plain), lse_spec] + [hold] * len(carrier.outs),
         scratch_shapes=[pltpu.VMEM((keys, PAIR), BF16)] * 4 + carrier.scratch,
-        out_shape=[plain, jax.ShapeDtypeStruct((rows, pairs * PAIR), F32)] + carrier.outs,
+        out_shape=[plain, jax.ShapeDtypeStruct((*heads_of.sides, rows, heads_of.per_side * PAIR), F32)] + carrier.outs,
         compiler_params=pltpu.CompilerParams(vmem_limit_bytes=VMEM, **carrier.params),
         cost_estimate=pl.CostEstimate(
             flops=16 * rows * keys * pairs * PAIR,
@@ -667,9 +818,8 @@
 ):
     query, kv_pieces = at(query), [at(piece) for piece in kv_pieces]
     mix, mix_grad = at(mix), at(mix_grad)
-    parts, rows, part = query.shape
-    per_part = part // PAIR
-    pairs = parts * per_part
+    heads_of = Pairs(query)
+    rows, pairs = heads_of.rows, heads_of.count
     pieces = len(kv_pieces)
     keys = rows * pieces
     scale = 1.0 / math.sqrt(HALF)
@@ -695,7 +845,8 @@
             carrier.run(pair, slot, slots, pairs * slots, carry_ins, carry_outs, refs)
 
         carry(0)
-        widen_keys(span_ref, kv_refs, key_e, key_o, value_e, value_o, rows)
+        span = heads_of.span(span_ref, pl.program_id(0))
+        widen_keys(span, kv_refs, key_e, key_o, value_e, value_o, rows)
         for g, kv_ref in enumerate(kv_refs):
             key_t[:, g * rows : (g + 1) * rows] = kv_ref[0].T
         lane = lax.broadcasted_iota(jnp.int32, (rows, PAIR), 1)
@@ -772,27 +923,32 @@
                     given[pair, 1, own, :] = dv
         dq_ref[...] = (jnp.concatenate(dq, axis=0).T * scale).astype(BF16)
         if swaps:
-            columns = pl.ds(pl.multiple_of(pair % per_part * PAIR, PAIR), PAIR)
-
-            def swap(i, place):
+            part, column = heads_of.place(pair)
+            columns = pl.ds(pl.multiple_of(column * PAIR, PAIR), PAIR)
+            spot = (*heads_of.side(pair), part, slice(None), slice(None), columns)
+
+            def swap(i):
                 return remote(
                     given.at[i],
-                    dkv_refs[1].at[place // per_part, :, :, columns],
+                    dkv_refs[1].at[spot],
                     swap_sems.at[0, i],
                     swap_sems.at[1, i],
                     where_is("near"),
                 )
 
-            swap(pair, pair).start()
+            swap(pair).start()
 
             @pl.when(pair == pairs - 1)
             def _():
                 for i in range(pairs):
-                    swap(i, pair).wait()
-
-    query_spec, kv_spec, lse_spec = attention_specs(per_part, rows)
+                    swap(i).wait()
+
+    query_spec, kv_spec = heads_of.query_spec, heads_of.kv_spec
+    lse_spec = heads_of.lse_spec()
     plain = jax.ShapeDtypeStruct(query.shape, BF16)
-    plain_kv = jax.ShapeDtypeStruct((parts, 2, rows, part), BF16)
+    plain_kv = jax.ShapeDtypeStruct(
+        (*heads_of.sides, heads_of.parts, 2, rows, heads_of.part), BF16
+    )
     hold = pl.BlockSpec(memory_space=pl.ANY)
     swap_scratch = [
         pltpu.VMEM((pairs, 2, rows, PAIR), BF16),
@@ -907,9 +1063,6 @@
                 def _():
                     for action in actions:
                         action()
-
-
-LAST = 1000
 
 
 GROUP = ["near", "over", "cross"]
@@ -1534,9 +1687,8 @@
         begin = jnp.where(second, answers[0], 0)
         end = jnp.where(second | ~paired, answers[0] + answers[1], answers[0])
         offsets = [(place - by) % pieces * rows for by in range(pieces)]
-        return jnp.stack([begin, end, *offsets]).astype(jnp.int32)
-
-    block = min(256, rows)
+        return jnp.stack([begin, end, *offsets]).astype(jnp.int32)[None]
+
     query_block = min(256, rows)
     chunk = 256
 
@@ -1555,22 +1707,22 @@
     source_cot, target_cot = bring(cotangent[0])
     source_span, target_span, cross_span = span_of(0, 0), span_of(1, 1), span_of(1, 0)
 
-    enc_q, enc_kv = project_qkv(source, source_norm, source_qkv, True, block)
+    enc_q, enc_kv = project_qkv(source, source_norm, source_qkv, True)
     enc_kv = pieces_of(enc_kv)
-    dec_q, dec_kv = project_qkv(target, target_norm, target_qkv, False, block)
+    dec_q, dec_kv = project_qkv(target, target_norm, target_qkv, False)
     dec_kv = pieces_of(dec_kv)
     enc_mix, enc_lse = attend(enc_q, enc_kv, source_span, query_block)
     encoded, memory, enc_first, enc_third = encoder_forward(
-        source, enc_mix, source_norm, source_out, source_up, source_down, source_cross, block
+        source, enc_mix, source_norm, source_out, source_up, source_down, source_cross
     )
     memory = pieces_of(memory)
     dec_mix, dec_lse = attend(dec_q, dec_kv, target_span, query_block)
     cross_q, dec_first = decoder_middle(
-        target, dec_mix, target_norm, target_out, target_cross, block
+        target, dec_mix, target_norm, target_out, target_cross
     )
     cross_mix, cross_lse = attend(cross_q, memory, cross_span, query_block)
     decoded, second_grad, cross_mix_grad, cross_out_grad, dec_up, dec_down, dec_norm = decoder_turn(
-        dec_first, cross_mix, target_cot, target_norm, target_cross, target_up, target_down, block
+        dec_first, cross_mix, target_cot, target_norm, target_cross, target_up, target_down
     )
     result = take_back(encoded, decoded)
     cross_q_grad, memory_grads, _ = attend_back(
@@ -1584,8 +1736,7 @@
         second_grad,
         target_norm,
         target_out,
-        target_cross,
-        block,
+        target_cross
     )
     dec_norm += step
     enc_first_grad, enc_mix_grad, enc_cross, enc_out, enc_up, enc_down, enc_norm = encoder_back(
@@ -1598,8 +1749,7 @@
         source_out,
         source_up,
         source_down,
-        source_cross,
-        block,
+        source_cross
     )
     dec_cross = jnp.stack([cross_query_grad, cross_out_grad], axis=1)
     up_grad, down_grad = home(enc_up, dec_up, 1), home(enc_down, dec_down, 0)
@@ -1613,10 +1763,10 @@
     )
     enc_kv_grads = pieces_home(enc_kv_grads)
     target_grad, dec_qkv, _ = input_back(
-        target, dec_first_grad, dec_q_grad, dec_kv_grads, target_norm, target_qkv, False, block
+        target, dec_first_grad, dec_q_grad, dec_kv_grads, target_norm, target_qkv, False
     )
     source_grad, enc_qkv, step = input_back(
-        source, enc_first_grad, enc_q_grad, enc_kv_grads, source_norm, source_qkv, True, block
+        source, enc_first_grad, enc_q_grad, enc_kv_grads, source_norm, source_qkv, True
     )
     enc_norm += step
     token_grad = take_back(source_grad, target_grad).astype(F32)
@@ -1667,45 +1817,33 @@
         end = jnp.where(second | ~paired, answers[0] + answers[1], answers[0])
         return jnp.stack([begin, end, section * rows, (1 - section) * rows]).astype(jnp.int32)
 
-    spans = span_of(0, 0), span_of(1, 1), span_of(1, 0)
-    x, qkv, norm, q, kv_own, kv_other = open_up(tokens[0], flat(self_qkv), norms[0], block, 1)
+    spans = jnp.stack([span_of(0, 0), span_of(1, 1), span_of(1, 0)])
+    self_spans, cross_span = spans[:2], spans[2:]
+    x, qkv, norm, q, *kv = open_up(tokens[0], flat(self_qkv), norms[0], block, 1)
     qkv = qkv.reshape(2, 2, *self_qkv.shape[1:])
 
     def parts(weight, side):
         return [At(weight, side, k) for k in range(2)]
 
     enc_x, dec_x, enc_norm_in, dec_norm_in = At(x, 0), At(x, 1), At(norm, 0), At(norm, 1)
-    enc_q, dec_q = At(q, 0), At(q, 1)
-    enc_kv, dec_kv = [[At(kv_own, side), At(kv_other, side)] for side in range(2)]
-    enc_mix, enc_lse, out, up = attend(
-        enc_q,
-        enc_kv,
-        spans[0],
+    mix, lse, out, up, cross, down = attend(
+        q,
+        kv,
+        self_spans,
         query_block,
         Carry(
             [
                 SpreadWeight(self_out[0], [3], [5]),
-                SpreadWeight(ffn_up[0], [4, 5, 6, 7], [6, 7, 7, 7]),
+                SpreadWeight(ffn_up[0], [4, 6], [7, 9]),
+                SpreadWeight(flat(cross_proj), [8], [11]),
+                SpreadWeight(ffn_down[0], [10, 12], [13, 15]),
             ],
             2,
         ),
         2,
     )
-    dec_mix, dec_lse, down, cross = attend(
-        dec_q,
-        dec_kv,
-        spans[1],
-        query_block,
-        Carry(
-            [
-                SpreadWeight(ffn_down[0], [3, 4, 5, 6], [5, 6, 7, 7]),
-                SpreadWeight(flat(cross_proj), [7, 7], [7, 7]),
-            ],
-            3,
-        ),
-        2,
-    )
     cross = cross.reshape(2, 2, *cross_proj.shape[1:])
+    enc_mix, dec_mix = At(mix, 0), At(mix, 1)
     encoded, memory, enc_first, enc_third = encoder_forward(
         enc_x,
         enc_mix,
@@ -1714,44 +1852,47 @@
         parts(up, 0),
         parts(down, 0),
         parts(cross, 0),
-        block,
     )
     memory = [memory, swap(memory)]
     cross_q, dec_first = decoder_middle(
-        dec_x, dec_mix, dec_norm_in, parts(out, 1), parts(cross, 1), block
-    )
-    cross_mix, cross_lse, cot = attend(
+        dec_x, dec_mix, dec_norm_in, parts(out, 1), parts(cross, 1)
+    )
+    cross_mix, cross_lse, dec_cot = attend(
         cross_q,
         memory,
-        spans[2],
+        cross_span,
         query_block,
-        Carry([SpreadRows(cotangent[0], (0, 1))], 4),
+        Carry([SpreadRows(cotangent[0], (1,))], 4),
+        2,
     )
     decoded, second_grad, cross_mix_grad, cross_out_grad, ffn_dec, dec_norm = decoder_turn(
         dec_first,
         cross_mix,
-        At(cot, 1),
+        At(dec_cot, 1),
         dec_norm_in,
         parts(cross, 1),
         parts(up, 1),
         parts(down, 1),
-        block,
         True,
     )
-    cross_q_grad, memory_grads, (ffn_dec, decoded) = attend_back(
+    cross_q_grad, memory_grads, (ffn_dec, enc_cot) = attend_back(
         cross_q,
         memory,
         cross_mix,
         cross_mix_grad,
         cross_lse,
-        spans[2],
+        cross_span,
         chunk,
         Carry(
-            [Reduce(ffn_dec, 256, [0, 1, 2, 3], [1, 2], "chip"), ReturnRows(decoded, 1, 4)], 5
+            [
+                Reduce(ffn_dec, 256, [0, 1, 2, 3], [1, 2], "chip"),
+                SpreadRows(cotangent[0], (0,), 4),
+            ],
+            5,
         ),
         2,
     )
-    dec_first_grad, dec_mix_grad, cross_query_grad, dec_out, step = decoder_middle_back(
+    dec_first_grad, mix_grad, cross_query_grad, dec_out, mid_norm = decoder_middle_back(
         dec_first,
         dec_mix,
         cross_q_grad,
@@ -1759,108 +1900,81 @@
         dec_norm_in,
         parts(out, 1),
         parts(cross, 1),
-        block,
-    )
-    dec_norm += step
-    enc_first_grad, enc_mix_grad, ffn_enc, sides, enc_norm = encoder_back(
+        (1, None),
+    )
+    enc_first_grad, mix_grad, ffn_enc, sides, enc_norm = encoder_back(
         enc_first,
         enc_third,
         enc_mix,
         memory_grads,
-        At(cot, 0),
+        At(enc_cot, 0),
         enc_norm_in,
         parts(out, 0),
         parts(up, 0),
         parts(down, 0),
         parts(cross, 0),
-        block,
         [dec_out, cross_query_grad, cross_out_grad],
-    )
-    dec_q_grad, dec_kv_grads, (ffn_dec, ffn_dec_other, ffn_enc, sides) = attend_back(
-        dec_q,
-        dec_kv,
-        dec_mix,
-        dec_mix_grad,
-        dec_lse,
-        spans[1],
+        (0, mix_grad),
+    )
+    q_grad, kv_grads, moved = attend_back(
+        q,
+        kv,
+        mix,
+        mix_grad,
+        lse,
+        self_spans,
         chunk,
         Carry(
             [
-                Reduce(
-                    ffn_dec,
-                    256,
-                    [0, 1, 2, 3],
-                    [1, *hops(2, 1, 2, 1, 1, 2)],
-                    "slice",
-                ),
-                Reduce(ffn_enc, 256, [0, 2, 4, 6], [1, 4], "chip"),
-                Reduce(sides, 384, [7, 8, 10, 11], [1, 3], "chip"),
+                Reduce(ffn_dec, 512, [0, 1], [1, *hops(2, 1, 1, 1, 2, 3)], "slice"),
+                Reduce(ffn_enc, 512, [2, 0], [1, 3, *hops(2, 1, 2, 1, 1, 2)]),
+                Reduce(sides, 768, [3, 1], [1, 3, *hops(1, 2, 1, 2, 1, 1)]),
+                ReturnRows(encoded, 0, 11),
+                ReturnRows(decoded, 1, 12),
             ],
             6,
         ),
-        4,
-    )
+        2,
+    )
+    ffn_dec, ffn_dec_other, ffn_enc, ffn_enc_other, sides, _, encoded, decoded = moved
     target_grad, dec_qkv = input_back(
         dec_x,
         dec_first_grad,
-        dec_q_grad,
-        dec_kv_grads,
+        At(q_grad, 1),
+        [At(g, 1) for g in kv_grads],
         dec_norm_in,
         parts(qkv, 1),
         False,
-        block,
         [],
-    )
-    enc_q_grad, enc_kv_grads, (ffn_enc, ffn_enc_other, sides, _, dec_qkv, dec_qkv_other, target_grad, encoded) = attend_back(
-        enc_q,
-        enc_kv,
-        enc_mix,
-        enc_mix_grad,
-        enc_lse,
-        spans[0],
-        chunk,
-        Carry(
-            [
-                Reduce(
-                    ffn_enc,
-                    256,
-                    [0, 1, 2, 3],
-                    [1, *hops(2, 1, 2, 1, 1, 2)],
-                    "slice",
-                ),
-                Reduce(
-                    sides,
-                    384,
-                    [0, 1, 2, 3],
-                    [1, *hops(2, 1, 2, 1, 1, 2)],
-                    "slice",
-                    [1, 2, 0] if levels == 3 else None,
-                ),
-                Reduce(dec_qkv, 384, [0, 1], [1, 3, *hops(2, 1, 2, 1, 1, 2)]),
-                ReturnRows(target_grad, 1, 4),
-                ReturnRows(encoded, 0, 4),
-            ],
-            7,
-        ),
-        4,
     )
     source_grad, enc_qkv = input_back(
         enc_x,
         enc_first_grad,
-        enc_q_grad,
-        enc_kv_grads,
+        At(q_grad, 0),
+        [At(g, 0) for g in kv_grads],
         enc_norm_in,
         parts(qkv, 0),
         True,
-        block,
-        [enc_norm, dec_norm],
-    )
-    last, last_other, source_grad = carry_alone(
+        [enc_norm, dec_norm, mid_norm],
+    )
+    enc_last, enc_other, dec_last, dec_other, source_grad, target_grad = carry_alone(
         [
-            Reduce(enc_qkv, enc_qkv.shape[2] // 2, [0, 1], [1, 1, *hops(1, 1, 1, 1, 1, 1)]),
-            ReturnRows(source_grad, 0, 4),
+            Reduce(
+                enc_qkv,
+                2 * PAIR,
+                [0, 1, 2, 2, 3, 3, 4],
+                [2, 2, *hops(1, 1, 1, 1, 1, 2)],
+            ),
+            Reduce(
+                dec_qkv,
+                2 * PAIR,
+                [0, 1, 1, 3, 4, 4],
+                [2, 2, *hops(1, 1, 1, 1, 1, 2)],
+            ),
+            ReturnRows(source_grad, 0, 6),
+            ReturnRows(target_grad, 1, 7),
         ],
-        4 + 2 * levels,
+        10 + 2 * levels,
         8,
     )
 
@@ -1874,8 +1988,8 @@
 
     qkv_grad = jnp.concatenate(
         [
-            jnp.where(is_first, columns(last), dec_qkv_other),
-            jnp.where(is_first, columns(last_other), dec_qkv),
+            jnp.where(is_first, columns(enc_last), columns(dec_other)),
+            jnp.where(is_first, columns(enc_other), columns(dec_last)),
         ],
         axis=0,
     )
@@ -1883,7 +1997,7 @@
     sides = sides.astype(F32)
     out_grad = jnp.concatenate([sides[: width // 2], sides[width // 2 : width]], axis=1)
     cross_grad = sides[width:].reshape(cross_proj.shape)
-    norm_grad = last[2 * half : 2 * half + 24].astype(F32).reshape(norms.shape)
+    norm_grad = enc_last[2 * half : 2 * half + 24].astype(F32).reshape(norms.shape)
 
     def by_side(source, target):
         return jnp.where(is_first, source, target)

time: 533 us -> 484 us (0.908)
  Pallas kernels: 494 us -> 446 us
    pallas_call x3 -> x2, Pallas kernels: 200 us -> 176 us  [attend_back(): pl.pallas_call(kernel, grid=(pairs,), in_specs=[pl.BlockSpec(memory_space...]
    pallas_call x3 -> x2, Pallas kernels: 103 us -> 82.2 us  [attend(): pl.pallas_call(kernel, grid=(pairs,), in_specs=[pl.BlockSpec(memory_space...]
where the time goes in v5:
time: 484 us; the launch traced here: 478 us
  Pallas kernels  446 us (92%)
  other arithmetic  11.4 us (2%)
  between operations  10.2 us (2%)
  local copies, waits for them, and re-layouts  9.92 us (2%)
    pallas_call x2, Pallas kernels, attend_back(): pl.pallas_call(kernel, grid=(pairs,), in_specs=[pl.BlockSpec(memory_space...  176 us
    pallas_call x7, Pallas kernels, row_call(): pl.pallas_call(kernel, grid=(rows // block,), in_specs=[blocked(a, dim) f...  97.5 us
    pallas_call x2, Pallas kernels, attend(): pl.pallas_call(kernel, grid=(pairs,), in_specs=[pl.BlockSpec(memory_space...  82.2 us
    pallas_call x1, Pallas kernels, open_up(): pl.pallas_call(kernel, in_specs=[hold] * 3, out_specs=[hold] * 6, out_sha...  45.4 us
    pallas_call x1, Pallas kernels, carry_alone(): pl.pallas_call(kernel, grid=(steps,), in_specs=[hold] * len(carrier.ins),...  45.3 us
  transfers between devices with their start and end apart: 1, of which 0 were waited for; matrix products, arithmetic and copies ran while one was open for 0% of the time, Pallas kernels for 1%

profile of v5, /device:TPU:0, one launch (start us, length us, event | category | flops | bytes accessed | tf_op | source)
XLA Modules:
  0.0 478.3 jit_solution(7819369836070216774)
XLA Ops:
  0.6 1.4 constant_dynamic-slice_fusion.1
  9.8 0.1 add_bitcast_fusion
  9.9 0.6 pad_add_fusion.span_ref
  10.5 45.4 %open_up.1 = (bf16[2,1024,512]{2,1,0:T(8,128)(2,1)}, bf16[2,2,1536,256]{3,2,1,0:T(8,128)(2,1)}, f32[2,3,2,512]{3,2,1,0:T(2,128)}, bf16[2,2,1024,256]{3,2,1,0:T(8...) custom-call(bf16[2,1024,512]{2,1,0:T(8,128)(2,1)} %bitcast.58, ...), custom_call_target="tpu_custom_call" | custom-call | tf_op jit(solution)/shard_map/open_up/pallas_call | solution.py:1584
  55.9 55.2 %attend.2 = (bf16[2,2,1024,256]{3,2,1,0:T(8,128)(2,1)}, f32[2,1024,512]{2,1,0:T(8,128)}, bf16[2,2,256,512]{3,2,1,0:T(8,128)(2,1)}, bf16[2,2,512,1024]{3,2,1,0:T(...) custom-call(s32[2,4]{1,0:T(2,128)} %pad_add_fusion.span_ref, ...), custom_call_target="tpu_custom_call" | custom-call | flops 34359738368 | bytes 16777216 | tf_op jit(solution)/shard_map/attend/pallas_call | solution.py:797
  111.1 12.1 %encoder_forward.1 = (bf16[1024,512]{1,0:T(8,128)(2,1)}, bf16[2,2,1024,256]{3,2,1,0:T(8,128)(2,1)}, f32[1024,512]{1,0:T(8,128)}, f32[1024,512]{1,0:T(8,128)}) custom-call(bf16[2,1024,512]{2,1,0:T(8,128)(2,1)} %get-tuple-element.74.refs_0_, bf16[2,2,1024,256]{3,2,1,0:T(8,128)(2,1)} %get-tuple-element.73.refs_1_.refs_2_.refs_5_.mix_ref, ...), custom_call_target="tpu_custom_call" | custom-call | flops 5905580032 | bytes 7876608 | tf_op jit(solution)/shard_map/encoder_forward/pallas_call | solution.py:161
  123.3 0.4 collective-permute-start
  124.9 5.2 %decoder_middle.1 = (bf16[2,1024,256]{2,1,0:T(8,128)(2,1)}, f32[1024,512]{1,0:T(8,128)}) custom-call(bf16[2,1024,512]{2,1,0:T(8,128)(2,1)} %get-tuple-element.74.refs_0_, bf16[2,2,1024,256]{3,2,1,0:T(8,128)(2,1)} %get-tuple-element.73.refs_1_.refs_2_.refs_5_.mix_ref, f32[2,3,2,512]{3,2,1,0:T(2,128)} %get-tuple-element.75.refs_2_.refs_3_.refs_4_.refs_6_.refs_5_, ...), custom_call_target="tpu_custom_call" | custom-call | flops 1073741824 | bytes 3682304 | tf_op jit(solution)/shard_map/decoder_middle/pallas_call | solution.py:161
  130.2 0.7 add_bitcast_fusion.2.span_ref
  130.8 0.0 collective-permute-done.refs_1_
  130.8 0.0 copy-start.12
  130.8 1.3 copy-done.12
  132.2 26.9 %attend.3 = (bf16[2,1024,256]{2,1,0:T(8,128)(2,1)}, f32[1024,512]{1,0:T(8,128)}, bf16[2,1024,512]{2,1,0:T(8,128)(2,1)}) custom-call(s32[1,4]{1,0:T(1,128)} %add_bitcast_fusion.2.span_ref, bf16[2,1024,256]{2,1,0:T(8,128)(2,1)} %get-tuple-element.82.q_ref, bf16[2,2,1024,256]{3,2,1,0:T(8,128)(2,1)} %get-tuple-element.83.refs_0_, ...), custom_call_target="tpu_custom_call" | custom-call | flops 17179869184 | bytes 8388608 | tf_op jit(solution)/shard_map/attend/pallas_call | solution.py:797
  159.1 25.7 %decoder_turn.1 = (bf16[1024,512]{1,0:T(8,128)(2,1)}, f32[1024,512]{1,0:T(8,128)}, bf16[2,1024,256]{2,1,0:T(8,128)(2,1)}, bf16[2,512,256]{2,1,0:T(8,128)(2,1)}, ...) custom-call(f32[1024,512]{1,0:T(8,128)} %get-tuple-element.85.refs_0_, ...), custom_call_target="tpu_custom_call" | custom-call | flops 14495514624 | bytes 9449472 | tf_op jit(solution)/shard_map/decoder_turn/pallas_call | solution.py:161
  184.7 63.2 %attend_back.2 = (bf16[2,1024,256]{2,1,0:T(8,128)(2,1)}, bf16[2,2,1024,256]{3,2,1,0:T(8,128)(2,1)}, bf16[2,2,1024,256]{3,2,1,0:T(8,128)(2,1)}, bf16[1024,512]{1,0:T(8,128)(2,1)}, bf16[2,1024,512]{2,1,0:T(8,128)(2,1)}) custom-call(s32[1,4]{1,0:T(1,128)} %add_bitcast_fusion.2.span_ref, bf16[2,1024,256]{2,1,0:T(8,128)(2,1)} %get-tuple-element.82.q_ref, ...), custom_call_target="tpu_custom_call" | custom-call | flops 42949672960 | bytes 16777216 | tf_op jit(solution)/shard_map/attend_back/pallas_call | solution.py:957
  248.0 8.0 %decoder_middle_back.1 = (f32[1024,512]{1,0:T(8,128)}, bf16[2,2,1024,256]{3,2,1,0:T(8,128)(2,1)}, bf16[2,512,256]{2,1,0:T(8,128)(2,1)}, bf16[2,256,512]{2,1,0:T(8,128)(2,1)}, f32[3,2,512]{2,1,0:T(2,128)}) custom-call(f32[1024,512]{1,0:T(8,128)} %get-tuple-element.85.refs_0_, f32[1024,512]{1,0:T(8,128)} %get-tuple-element.93.refs_1_, ...), custom_call_target="tpu_custom_call" | custom-call | flops 2147483648 | bytes 7876608 | tf_op jit(solution)/shard_map/decoder_middle_back/pallas_call | solution.py:161
  256.0 29.2 %encoder_back.1 = (f32[1024,512]{1,0:T(8,128)}, bf16[2,2,1024,256]{3,2,1,0:T(8,128)(2,1)}, bf16[2,2,1024,512]{3,2,1,0:T(8,128)(2,1)}, bf16[2,2,1536,256]{3,2,1,0:T(8,128)(2,1)}, f32[3,2,512]{2,1,0:T(2,128)}) custom-call(f32[1024,512]{1,0:T(8,128)} %get-tuple-element.80.refs_0_, ...), custom_call_target="tpu_custom_call", output_to_operand_aliasing={{1}: (18, {})} | custom-call | flops 13958643712 | bytes 17838080 | tf_op jit(solution)/shard_map/encoder_back/pallas_call | solution.py:161
  285.2 112.8 %attend_back.3 = (bf16[2,2,1024,256]{3,2,1,0:T(8,128)(2,1)}, bf16[2,2,2,1024,256]{4,3,2,1,0:T(8,128)(2,1)}, bf16[2,2,2,1024,256]{4,3,2,1,0:T(8,128)(2,1)}, bf16[...) custom-call(s32[2,4]{1,0:T(2,128)} %pad_add_fusion.span_ref, ...), custom_call_target="tpu_custom_call" | custom-call | flops 85899345920 | bytes 33554432 | tf_op jit(solution)/shard_map/attend_back/pallas_call | solution.py:957
  398.0 8.1 %input_back.3 = (bf16[1024,512]{1,0:T(8,128)(2,1)}, bf16[2,2,1536,128]{3,2,1,0:T(8,128)(2,1)}) custom-call(bf16[2,1024,512]{2,1,0:T(8,128)(2,1)} %get-tuple-element.74.refs_0_, f32[1024,512]{1,0:T(8,128)} %get-tuple-element.117.refs_1_, bf16[2,2,2,1024,256]{4,3,2,1,0:T(8,128)(2,1)} %get-tuple-element.109.refs_2_, ...), custom_call_target="tpu_custom_call" | custom-call | flops 3221225472 | bytes 9973760 | tf_op jit(solution)/shard_map/input_back/pallas_call | solution.py:161
  406.1 9.1 %input_back.2 = (bf16[1024,512]{1,0:T(8,128)(2,1)}, bf16[2,2,1792,128]{3,2,1,0:T(8,128)(2,1)}) custom-call(bf16[2,1024,512]{2,1,0:T(8,128)(2,1)} %get-tuple-element.74.refs_0_, f32[1024,512]{1,0:T(8,128)} %get-tuple-element.108.refs_1_, bf16[2,2,2,1024,256]{4,3,2,1,0:T(8,128)(2,1)} %get-tuple-element.109.refs_2_, ...), custom_call_target="tpu_custom_call" | custom-call | flops 3221225472 | bytes 10010624 | tf_op jit(solution)/shard_map/input_back/pallas_call | solution.py:161
  415.2 0.0 copy-start
  415.2 45.3 %carry_alone.1 = (bf16[1792,128]{1,0:T(8,128)(2,1)}, bf16[1792,128]{1,0:T(8,128)(2,1)}, bf16[1536,128]{1,0:T(8,128)(2,1)}, bf16[1536,128]{1,0:T(8,128)(2,1)}, bf...) custom-call(bf16[2,2,1792,128]{3,2,1,0:T(8,128)(2,1)} %get-tuple-element.116.refs_0_, ...), custom_call_target="tpu_custom_call" | custom-call | tf_op jit(solution)/shard_map/carry_alone/pallas_call | solution.py:1474
  460.5 0.0 copy-start.10
  460.5 0.7 slice_convert_fusion
  461.3 1.0 fusion.2
  462.3 0.0 copy-start.11
  462.4 0.0 copy-done
  462.4 0.0 copy-start.9
  462.4 1.0 slice.96
  463.5 0.6 reshape.73
  464.1 0.0 copy-done.10
  464.1 0.0 copy-done.11
  464.2 0.0 copy-done.9
  464.2 0.1 maximum_select_fusion
  464.3 0.1 maximum_select_fusion.1
  464.4 0.0 copy-start.7
  464.4 0.0 copy-start.8
  464.5 0.1 pad_maximum_fusion
  464.5 1.3 convert.5
  465.8 0.1 copy-done.7
  465.9 0.7 copy-done.8
  466.6 0.1 select_convert_fusion
  466.7 0.0 copy-start.1
  466.7 0.0 copy-start.2
  466.7 0.2 fusion
  466.9 1.4 copy-done.1
  468.3 0.6 copy-done.2
  468.9 0.0 copy-start.3
  468.9 0.0 copy-start.4
  468.9 1.5 select_bitcast_fusion
  470.5 0.8 copy-done.3
  471.3 0.6 copy-done.4
  471.9 0.0 copy-start.5
  471.9 0.0 copy-start.6
  471.9 2.3 bitcast_convert_fusion
  474.2 0.9 maximum_bitcast_fusion.1
  475.1 0.0 copy-done.5
  475.1 0.0 copy-done.6
  475.1 1.5 bitcast_convert_fusion.1
  476.5 1.5 maximum_bitcast_fusion
  (4 shorter events, 0.1 us)
Async XLA Ops:
  123.3 7.5 %collective-permute-start = (bf16[2,2,1024,256]{3,2,1,0:T(8,128)(2,1)}, bf16[2,2,1024,256]{3,2,1,0:T(8,128)(2,1)S(1)}, u32[]{:S(2)}, u32[]{:S(2)}) collective-permute-start(bf16[2,2,1024,256]{3,2,1,0:T(8,128)(2,1)} %get-tuple-element.83.refs_0_), channel_id=1, source_target_pairs={{0,16},{16,0},{1,17},{17,1},{2,18},{18,2},{3,19},{19,3},{4,20},{20... | collective-permute-start | bytes 6291464 | tf_op jit(solution)/shard_map/ppermute | solution.py:1806
  130.8 1.3 copy-start.12
  415.2 47.2 %copy-start = (bf16[1536,256]{1,0:T(8,128)(2,1)S(1)}, bf16[1536,256]{1,0:T(8,128)(2,1)}, u32[]{:S(2)}) copy-start(bf16[1536,256]{1,0:T(8,128)(2,1)} %get-tuple-element.127) | copy-start | bytes 2359300
  460.5 3.5 copy-start.10
  462.3 1.8 copy-start.11
  462.4 1.7 copy-start.9
  464.4 1.4 copy-start.7
  464.4 2.1 copy-start.8
  466.7 1.6 copy-start.1
  466.7 2.2 copy-start.2
  468.9 2.3 copy-start.3
  468.9 3.0 copy-start.4
  471.9 3.2 copy-start.5
  471.9 3.2 copy-start.6

commit v6 on v5

--- a/solution.py
+++ b/solution.py
@@ -82,7 +82,7 @@
 
 
 def row_call(
-    body, name, rows, row_ins, whole_ins, row_outs, keeps, finals, finish, flops, into=None
+    body, name, rows, row_ins, whole_ins, row_outs, keeps, finals, finish, flops, into=None, push=None
 ):
     block, part = min(512, rows), min(256, rows)
     row_ins = [(at(a), dim) for a, dim in row_ins]
@@ -121,6 +121,14 @@
     n_row, n_final = len(row_outs), len(finals)
     out_specs = [blocked_out(shape, dim) for shape, _, dim in row_outs]
     out_shapes = [jax.ShapeDtypeStruct(shape, dtype) for shape, dtype, _ in row_outs]
+    push_outs, push_scratch, push_params = [], [], {}
+    if push is not None:
+        push_outs = [out_shapes[push[0]]]
+        push_scratch = [
+            pltpu.VMEM(push_outs[0].shape, push_outs[0].dtype),
+            pltpu.SemaphoreType.DMA((2, rows // block)),
+        ]
+        push_params = dict(collective_id=push[1], has_side_effects=True)
     held, aliases = [], {}
     if into is not None:
         shape, dtype, dim = row_outs[-1]
@@ -134,6 +142,23 @@
         outs = refs[n_in : n_in + n_row]
         last_outs, kept = refs[n_in + n_row : n_in + n_row + n_final], refs[n_in + n_row + n_final :]
         step = pl.program_id(0)
+        if push is not None:
+            pushed, kept = kept[0], kept[1:]
+            kept, (push_room, push_sems) = kept[:-2], kept[-2:]
+
+            def send(i):
+                own = pl.ds(i * block, block)
+                return remote(
+                    push_room.at[:, :, own, :],
+                    pushed.at[:, :, own, :],
+                    push_sems.at[0, i],
+                    push_sems.at[1, i],
+                    where_is("near"),
+                )
+
+            @pl.when(step == 0)
+            def _():
+                greet(["near"])
         if finals:
 
             @pl.when(step == 0)
@@ -150,6 +175,19 @@
             if waiting:
                 running.append(waiting.pop(0))
 
+        if push is not None:
+            for i in range(rows // block):
+
+                @pl.when(step == i)
+                def _():
+                    push_room[:, :, i * block : (i + 1) * block, :] = outs[push[0]][...]
+                    send(i).start()
+
+            @pl.when(step == pl.num_programs(0) - 1)
+            def _():
+                for i in range(rows // block):
+                    send(i).wait()
+
         if finals:
 
             @pl.when(step == pl.num_programs(0) - 1)
@@ -164,11 +202,15 @@
         in_specs=[blocked(a, dim) for a, dim in row_ins]
         + [whole(a) for a in whole_ins]
         + [pl.BlockSpec(memory_space=pl.ANY)] * len(held),
-        out_specs=out_specs + [whole_out(shape) for shape, _ in finals],
-        out_shape=out_shapes + [jax.ShapeDtypeStruct(shape, dtype) for shape, dtype in finals],
+        out_specs=out_specs
+        + [whole_out(shape) for shape, _ in finals]
+        + [pl.BlockSpec(memory_space=pl.ANY)] * len(push_outs),
+        out_shape=out_shapes
+        + [jax.ShapeDtypeStruct(shape, dtype) for shape, dtype in finals]
+        + push_outs,
         input_output_aliases=aliases,
-        scratch_shapes=[pltpu.VMEM(shape, dtype) for shape, dtype in keeps],
-        compiler_params=pltpu.CompilerParams(vmem_limit_bytes=VMEM),
+        scratch_shapes=[pltpu.VMEM(shape, dtype) for shape, dtype in keeps] + push_scratch,
+        compiler_params=pltpu.CompilerParams(vmem_limit_bytes=VMEM, **push_params),
         cost_estimate=pl.CostEstimate(flops=flops, bytes_accessed=size, transcendentals=0),
         name=name,
     )(*[a.array for a in arrays], *held)
@@ -215,7 +257,7 @@
     )
 
 
-def encoder_forward(x, mix, norm, out, up, down, cross):
+def encoder_forward(x, mix, norm, out, up, down, cross, push=None):
     x = at(x)
     rows, width = x.shape
     parts, part = len(out), out[0].shape[0]
@@ -267,6 +309,7 @@
         [],
         None,
         6 * rows * width * width + 4 * rows * width * units,
+        push=None if push is None else (1, push),
     )
 
 
@@ -592,7 +635,54 @@
         ].astype(BF16)
 
 
-def input_back(x, first_grad, query_grad, key_grads, norm, weights, with_norm, paired=None):
+def input_part(refs, kept, own, all_rows, norm_ref, w, with_norm):
+    x_ref, first_grad_ref, key_refs, query_grad_ref, grad_ref = refs
+    low_keep, key_keep, norm_total = kept
+    grad = first_grad_ref[own, :]
+    for k in range(len(w)):
+        grad += dot_nt(query_grad_ref[k, all_rows, :], w[k][0])
+        for i in range(2):
+            member = added(key_refs, k, i, own)
+            key_keep[k, i, all_rows, :] = member
+            grad += dot_nt(member, w[k][1 + i])
+    yield
+    low = x_ref[own, :]
+    if with_norm:
+        unit, inv = standardize(low.astype(F32))
+        low = affine(unit, norm_ref, 2).astype(BF16)
+        grad = norm_back(unit, inv, norm_ref, 2, grad, norm_total)
+    low_keep[all_rows, :] = low
+    grad_ref[own, :] = grad.astype(BF16)
+
+
+def input_sums(kept, query_grad_ref, into, parts):
+    low_keep, key_keep, _ = kept
+    for k in range(parts):
+        both = jnp.concatenate(
+            [dot_tn(low_keep[...], query_grad_ref[k])]
+            + [dot_tn(low_keep[...], key_keep[k, i]) for i in range(2)],
+            axis=0,
+        )
+        half = both.shape[0] // 2
+        for core in range(2):
+            column_blocks(both[core * half : (core + 1) * half], into, core, k, 0)
+
+
+def norm_lines(sides, into, parts, row):
+    for core, table in enumerate(sides):
+        lines = [
+            table[slot, i : i + 1, h * PAIR : (h + 1) * PAIR]
+            for slot in range(3)
+            for i in range(2)
+            for h in range(table.shape[-1] // PAIR)
+        ]
+        lines.append(jnp.zeros((2 * PAIR - len(lines), PAIR), F32))
+        lines = jnp.concatenate(lines, axis=0).astype(BF16)
+        for k in range(parts):
+            into[core, k, row:, :] = lines
+
+
+def input_back(x, first_grad, query_grad, key_grads, norm, weights, with_norm):
     x = at(x)
     rows, width = x.shape
     parts, part = len(weights), weights[0].shape[-1]
@@ -602,75 +692,28 @@
     def body(ins, outs, kept, own, all_rows):
         x_ref, first_grad_ref = ins[:2]
         key_refs, query_grad_ref, norm_ref = ins[2 : 2 + pieces], ins[2 + pieces], ins[3 + pieces]
-        w = ins[4 + pieces :][:parts]
-        (grad_ref,) = outs
-        low_keep, key_keep, norm_total = kept
-        grad = first_grad_ref[own, :]
-        for k in range(parts):
-            grad += dot_nt(query_grad_ref[k, all_rows, :], w[k][0])
-            for i in range(2):
-                member = added(key_refs, k, i, own)
-                key_keep[k, i, all_rows, :] = member
-                grad += dot_nt(member, w[k][1 + i])
-        yield
-        low = x_ref[own, :]
-        if with_norm:
-            unit, inv = standardize(low.astype(F32))
-            low = affine(unit, norm_ref, 2).astype(BF16)
-            grad = norm_back(unit, inv, norm_ref, 2, grad, norm_total)
-        low_keep[all_rows, :] = low
-        grad_ref[own, :] = grad.astype(BF16)
-
-    half = 3 * width // 2
+        refs = x_ref, first_grad_ref, key_refs, query_grad_ref, outs[0]
+        yield from input_part(refs, kept, own, all_rows, norm_ref, ins[4 + pieces :], with_norm)
 
     def finish(ins, kept, outs):
         query_grad_ref = ins[0]
         low_keep, key_keep, norm_total = kept
-
-        def product(k, i):
-            member = query_grad_ref[k] if i == 0 else key_keep[k, i - 1]
-            return dot_tn(low_keep[...], member)
-
-        if paired is None:
-            for k in range(parts):
-                for i in range(3):
-                    outs[0][k, i] = product(k, i).astype(BF16)
-            outs[1][...] = norm_total[...]
-            return
         for k in range(parts):
-            both = jnp.concatenate([product(k, i) for i in range(3)], axis=0)
-            for core in range(2):
-                own = both[core * half : (core + 1) * half]
-                column_blocks(own, outs[0], core, k, 0)
-        if paired:
-            tables = ins[-len(paired) :]
-            sides = [tables[0][...] + norm_total[...], sum(t[...] for t in tables[1:])]
-            for core, table in enumerate(sides):
-                lines = [
-                    table[slot, i : i + 1, h * PAIR : (h + 1) * PAIR]
-                    for slot in range(3)
-                    for i in range(2)
-                    for h in range(width // PAIR)
-                ]
-                lines.append(jnp.zeros((2 * PAIR - len(lines), PAIR), F32))
-                lines = jnp.concatenate(lines, axis=0).astype(BF16)
-                for k in range(parts):
-                    outs[0][core, k, 2 * half :, :] = lines
-
-    if paired is None:
-        finals = [((parts, 3, width, part), BF16), ((3, 2, width), F32)]
-    else:
-        finals = [((2, parts, 2 * half + (2 * PAIR if paired else 0), PAIR), BF16)]
+            outs[0][k, 0] = dot_tn(low_keep[...], query_grad_ref[k]).astype(BF16)
+            for i in range(2):
+                outs[0][k, 1 + i] = dot_tn(low_keep[...], key_keep[k, i]).astype(BF16)
+        outs[1][...] = norm_total[...]
+
     whole = (rows, width)
     return row_call(
         body,
         "input_back",
         rows,
         [(x, 0), (first_grad, 0)] + [(g, 2) for g in key_grads],
-        [query_grad, norm, *weights, *(paired or [])],
+        [query_grad, norm, *weights],
         [(whole, BF16, 0)],
         [(whole, BF16), ((parts, 2, rows, part), BF16), ((3, 2, width), F32)],
-        finals,
+        [((parts, 3, width, part), BF16), ((3, 2, width), F32)],
         finish,
         12 * rows * width * width,
     )
@@ -878,8 +921,8 @@
             (
                 key,
                 value,
-                jnp.where(own, query, lse).astype(BF16),
-                jnp.where(own, grad, inner).astype(BF16),
+                jnp.where(own, query, lse).astype(BF16).T,
+                jnp.where(own, grad, inner).astype(BF16).T,
                 jnp.where(own, query, 0.0).astype(BF16),
                 jnp.where(own, grad, 0.0).astype(BF16),
             )
@@ -891,7 +934,7 @@
             begin, h = unit
             own = slice(begin, begin + chunk)
             key, value, q_wide, g_wide, _, _ = heads[h]
-            return dot_nt(key[own, :], q_wide), dot_nt(value[own, :], g_wide)
+            return dot_nn(key[own, :], q_wide), dot_nn(value[own, :], g_wide)
 
         ahead = front(units[0])
         dq = [None, None]
@@ -1084,9 +1127,9 @@
         )
 
     def keep(self, i):
-        source, target = self.copies[i][:2]
+        source, target, slot = self.copies[i][:3]
         return pltpu.make_async_copy(
-            source, target if self.room is None else self.room, self.kept
+            source, target if self.room is None else self.room, self.kept.at[slot]
         )
 
     def keep_on(self):
@@ -1095,7 +1138,8 @@
             @pl.when(self.here(i, True))
             def _():
                 self.keep(i).wait()
-                pltpu.make_async_copy(self.room, self.copies[i][1], self.kept).start()
+                target, slot = self.copies[i][1:3]
+                pltpu.make_async_copy(self.room, target, self.kept.at[slot]).start()
 
     def here(self, i, stays):
         section, _, tensor = spots()
@@ -1130,7 +1174,7 @@
         @pl.when(condition & own)
         def _():
             stays = source if self.room is None else self.room
-            pltpu.make_async_copy(stays, target, self.kept).wait()
+            pltpu.make_async_copy(stays, target, self.kept.at[slot]).wait()
 
         @pl.when(condition & jnp.logical_not(own))
         def _():
@@ -1139,21 +1183,25 @@
             ).wait_recv()
 
 
-ROW_SEMS = [
-    pltpu.SemaphoreType.DMA((2,)),
-    pltpu.SemaphoreType.DMA((2,)),
-    pltpu.SemaphoreType.DMA,
-]
-
-
-def spread_rows(source, target, sems, sides=(0, 1), room=None):
+def row_sems(pieces=1):
+    return [pltpu.SemaphoreType.DMA((2 * pieces,))] * 3
+
+
+def spread_rows(source, target, sems, sides=(0, 1), room=None, pieces=1):
     section, _, tensor = spots()
     yes = section >= 0
     sends = yes if len(sides) == 2 else section == sides[0]
-    copies = [
-        (source.at[row], target.at[section], section, tensor, row, sends) for row in range(2)
-    ]
-    arrivals = [(target.at[side], side, side, section, yes) for side in sides]
+    count = source.shape[1] // pieces
+    copies, arrivals = [], []
+    for i in range(pieces):
+        own = pl.ds(i * count, count)
+        for row in range(2):
+            slot = 2 * i + section
+            copies.append(
+                (source.at[row, own, :], target.at[section, own, :], slot, tensor, row, sends)
+            )
+        for side in sides:
+            arrivals.append((target.at[side, own, :], 2 * i + side, side, section, yes))
     return RowCopies(copies, arrivals, sems, room)
 
 
@@ -1166,11 +1214,12 @@
 
 class SpreadRows:
     peers = GROUP
+    staged = True
 
     def __init__(self, array, sides, begin=0):
         self.ins, self.sides, self.begin = [array], sides, begin
         self.outs = [jax.ShapeDtypeStruct(array.shape, array.dtype)]
-        self.scratch = ROW_SEMS + [pltpu.VMEM(array.shape[-2:], array.dtype)]
+        self.scratch = row_sems() + [pltpu.VMEM(array.shape[-2:], array.dtype)]
 
     def make(self, ins, outs, scratch):
         return spread_rows(ins[0], outs[0], scratch[:3], self.sides, scratch[3])
@@ -1185,21 +1234,21 @@
                 rows.wait_arrival(i)
             rows.wait_sent()
 
-        return [
-            (self.begin, 1, lambda: make().start()),
-            (self.begin + 1, 1, lambda: make().keep_on()),
-            (steps - 1, LAST, finish),
-        ]
+        events = [(self.begin, 1, lambda: make().start()), (steps - 1, LAST, finish)]
+        if self.staged:
+            events.append((self.begin + 1, 1, lambda: make().keep_on()))
+        return events
 
 
 class ReturnRows(SpreadRows):
-    def __init__(self, array, side, begin=0):
-        self.ins, self.side, self.begin = [array], side, begin
+    def __init__(self, array, side, begin=0, staged=True):
+        self.ins, self.side, self.begin, self.staged = [array], side, begin, staged
         self.outs = [jax.ShapeDtypeStruct((2, *array.shape), array.dtype)]
-        self.scratch = ROW_SEMS + [pltpu.VMEM(array.shape, array.dtype)]
+        self.scratch = row_sems() + [pltpu.VMEM(array.shape, array.dtype)] * staged
 
     def make(self, ins, outs, scratch):
-        return return_rows(ins[0], outs[0], scratch[:3], self.side, scratch[3])
+        room = scratch[3] if len(scratch) > 3 else None
+        return return_rows(ins[0], outs[0], scratch[:3], self.side, room)
 
 
 class WeightCopies:
@@ -1463,44 +1512,214 @@
         return events
 
 
-def carry_alone(tasks, steps, collective):
-    carrier = Carry(tasks, collective)
+def close_down(x, firsts, q_grad, kv_grads, norm, qkv, norm_grads, schedule, collective):
+    _, rows, width = x.shape
+    parts, _, _, part = qkv.shape[1:]
+    half = 3 * width // 2
+    shapes = [(2, parts, 2 * half + extra, PAIR) for extra in (2 * PAIR, 0)]
+    dec_steps, enc_steps, returns, steps = schedule
+    whole = (rows, width)
+    grad_shape = jax.ShapeDtypeStruct(whole, BF16)
+    carrier = Carry(
+        [
+            Reduce(jax.ShapeDtypeStruct(shapes[0], BF16), 2 * PAIR, *enc_steps),
+            Reduce(jax.ShapeDtypeStruct(shapes[1], BF16), 2 * PAIR, *dec_steps),
+            ReturnRows(grad_shape, 0, returns[0], False),
+            ReturnRows(grad_shape, 1, returns[1], False),
+        ],
+        collective,
+    )
+    halves = 2
+    count, sub = rows // halves, min(256, rows // halves)
 
     def kernel(*refs):
-        i, o = len(carrier.ins), len(carrier.ins) + len(carrier.outs)
-        carrier.run(pl.program_id(0), 0, 1, steps, refs[:i], refs[i:o], refs[o:])
+        x_in, first_ins, q_in, kv_ins, norm_in, qkv_in, refs = (
+            refs[0],
+            refs[1:3],
+            refs[3],
+            refs[4:6],
+            refs[6],
+            refs[7],
+            refs[8:],
+        )
+        norm_grad_refs, refs = refs[: len(norm_grads)], refs[len(norm_grads) :]
+        outs, refs = refs[: len(carrier.outs)], refs[len(carrier.outs) :]
+        x_room, first_room, q_room, kv_room, norm_room, qkv_room, sems = refs[:7]
+        low, keys, total, grads, enc_sum, dec_sum, *rest = refs[7:]
+        ins = [enc_sum, dec_sum, grads.at[0], grads.at[1]]
+        plan = carrier.plan(steps, ins, outs, rest)
+        loads = []
+
+        def load(source, target):
+            copy = pltpu.make_async_copy(source, target, sems.at[len(loads)])
+            copy.start()
+            loads.append(copy)
+            return copy
+
+        arrivals = {}
+        for side in (1, 0):
+            for i in range(halves):
+                own = pl.ds(i * count, count)
+                arrivals[side, i] = [
+                    load(first_ins[side].at[own, :], first_room.at[side, own, :]),
+                    load(q_in.at[side, :, own, :], q_room.at[side, :, own, :]),
+                    load(kv_ins[0].at[side, :, :, own, :], kv_room.at[0, side, :, :, own, :]),
+                    load(kv_ins[1].at[side, :, :, own, :], kv_room.at[1, side, :, :, own, :]),
+                    load(x_in.at[side, own, :], x_room.at[side, own, :]),
+                ]
+                if i == 0:
+                    arrivals[side, i] += [
+                        load(qkv_in.at[side], qkv_room.at[side]),
+                        load(norm_in.at[side], norm_room.at[side]),
+                    ]
+        total[...] = jnp.zeros_like(total)
+
+        def piece(side, i):
+            for copy in arrivals[side, i]:
+                copy.wait()
+            kept = low, keys, total
+            refs = (
+                x_room.at[side],
+                first_room.at[side],
+                [kv_room.at[0, side], kv_room.at[1, side]],
+                q_room.at[side],
+                grads.at[side],
+            )
+            w = [qkv_room.at[side, k] for k in range(parts)]
+            turns = []
+            for begin in range(i * count, (i + 1) * count, sub):
+                own = slice(begin, begin + sub)
+                turns.append(
+                    input_part(refs, kept, own, own, norm_room.at[side], w, side == 0)
+                )
+            while turns:
+                turns = [turn for turn in turns if next(turn, LAST) is not LAST]
+            if i == halves - 1:
+                into = (enc_sum, dec_sum)[side]
+                input_sums(kept, q_room.at[side], into, parts)
+                if side == 0:
+                    sides = [
+                        norm_grad_refs[0][...] + total[...],
+                        sum(ref[...] for ref in norm_grad_refs[1:]),
+                    ]
+                    norm_lines(sides, into, parts, 2 * half)
+
+        for step in range(steps):
+            for action in plan.get(step, []):
+                action()
+            if step < 2 * halves:
+                piece(1 - step // halves, step % halves)
+
+    hold = pl.BlockSpec(memory_space=pl.ANY)
+    vmem = pl.BlockSpec(memory_space=pltpu.VMEM)
+    arrays = [x, *firsts, q_grad, *kv_grads, norm, qkv]
+    rooms = [
+        pltpu.VMEM(x.shape, BF16),
+        pltpu.VMEM((2, *whole), F32),
+        pltpu.VMEM(q_grad.shape, BF16),
+        pltpu.VMEM((2, *kv_grads[0].shape), BF16),
+        pltpu.VMEM(norm.shape, F32),
+        pltpu.VMEM(qkv.shape, BF16),
+        pltpu.SemaphoreType.DMA((2 * (5 * halves + 2),)),
+        pltpu.VMEM(whole, BF16),
+        pltpu.VMEM((parts, 2, rows, part), BF16),
+        pltpu.VMEM((3, 2, width), F32),
+        pltpu.VMEM((2, *whole), BF16),
+        pltpu.VMEM(shapes[0], BF16),
+        pltpu.VMEM(shapes[1], BF16),
+    ]
+    return pl.pallas_call(
+        kernel,
+        in_specs=[hold] * len(arrays) + [vmem] * len(norm_grads),
+        out_specs=[hold] * len(carrier.outs),
+        out_shape=carrier.outs,
+        scratch_shapes=rooms + carrier.scratch,
+        compiler_params=pltpu.CompilerParams(vmem_limit_bytes=VMEM, **carrier.params),
+        name="close_down",
+    )(*arrays, *norm_grads)
+
+
+def lay_out(pairs, singles, shapes, finish):
+    arrays = [array for pair in pairs for array in pair] + [single[0] for single in singles]
+    spans = [(0, min(a.shape[0], b.shape[0])) for a, b in pairs] + [s[1:] for s in singles]
+    loaded = [
+        jax.ShapeDtypeStruct((span[1], *array.shape[1:]), array.dtype)
+        for array, span in zip([a for a, _ in pairs] + [s[0] for s in singles], spans)
+    ]
+
+    def kernel(*refs):
+        ins, outs = refs[: len(arrays)], refs[len(arrays) : len(arrays) + len(shapes)]
+        refs = refs[len(arrays) + len(shapes) :]
+        rooms, refs = refs[: len(loaded)], refs[len(loaded) :]
+        out_rooms, load_sems, store_sems = refs[: len(shapes)], refs[-2], refs[-1]
+        section = lax.axis_index("section")
+
+        def load(i, choice):
+            source = ins[2 * i + choice] if i < len(pairs) else ins[len(pairs) + i]
+            return pltpu.make_async_copy(
+                source.at[pl.ds(*spans[i])], rooms[i], load_sems.at[i]
+            )
+
+        for i in range(len(loaded)):
+            if i < len(pairs):
+
+                @pl.when(section == 0)
+                def _():
+                    load(i, 0).start()
+
+                @pl.when(section != 0)
+                def _():
+                    load(i, 1).start()
+
+            else:
+                load(i, 0).start()
+        stores = []
+
+        def fetch(i):
+            load(i, 0).wait()
+            return rooms[i]
+
+        for i, room in enumerate(finish(fetch, out_rooms)):
+            copy = pltpu.make_async_copy(room, outs[i], store_sems.at[i])
+            copy.start()
+            stores.append(copy)
+        for copy in stores:
+            copy.wait()
 
     hold = pl.BlockSpec(memory_space=pl.ANY)
     return pl.pallas_call(
         kernel,
-        grid=(steps,),
-        in_specs=[hold] * len(carrier.ins),
-        out_specs=[hold] * len(carrier.outs),
-        out_shape=carrier.outs,
-        scratch_shapes=carrier.scratch,
-        compiler_params=pltpu.CompilerParams(vmem_limit_bytes=VMEM, **carrier.params),
-        name="carry_alone",
-    )(*carrier.ins)
+        in_specs=[hold] * len(arrays),
+        out_specs=[hold] * len(shapes),
+        out_shape=[jax.ShapeDtypeStruct(*s) for s in shapes],
+        scratch_shapes=[pltpu.VMEM(a.shape, a.dtype) for a in loaded]
+        + [pltpu.VMEM(*s) for s in shapes]
+        + [pltpu.SemaphoreType.DMA((len(loaded),)), pltpu.SemaphoreType.DMA((len(shapes),))],
+        compiler_params=pltpu.CompilerParams(vmem_limit_bytes=VMEM),
+        name="lay_out",
+    )(*arrays)
 
 
 def open_up(tokens, qkv, norm, block, collective):
     _, rows, width = tokens.shape
     part = qkv.shape[-1]
     score = LOG2E / math.sqrt(width // HEADS)
+    count = min(block, rows)
+    pieces = rows // count
 
     def kernel(tokens_ref, qkv_ref, norm_ref, *refs):
         x_out, w_out, n_out, q_out, own_out, other_out = refs[:6]
-        x, low, w, n, q, kv = refs[6:12]
-        row_sems, weight_sems, norm_sems, store_sems, kv_sems = (
-            refs[12:15],
-            refs[15:16],
+        x, w, n, q, kv = refs[6:11]
+        row_sems_, weight_sems, norm_sems, store_sems, kv_sems = (
+            refs[11:14],
+            refs[14:15],
+            refs[15],
             refs[16],
             refs[17],
-            refs[18],
         )
         section, _, _ = spots()
         greet([*GROUP, 0])
-        rows_in = spread_rows(tokens_ref, x, row_sems)
+        rows_in = spread_rows(tokens_ref, x, row_sems_, pieces=pieces)
         weight = WeightCopies(qkv_ref, w, weight_sems[0])
         weight.start()
         rows_in.start()
@@ -1510,19 +1729,15 @@
         )
         norm_kept.start()
         norm_near.start()
-        stores = []
+        stores, kv_copies = [], []
 
         def save(source, target):
             copy = pltpu.make_async_copy(source, target, store_sems.at[len(stores)])
             copy.start()
             stores.append(copy)
 
-        kv_copies = []
-
-        def project(side, k):
-            def step(i, carry):
-                own = pl.ds(pl.multiple_of(i * block, block), block)
-                rows_low = low[own, :] if side == 0 else x[1, own, :]
+        def project(side, own, rows_low):
+            for k in range(2):
 
                 def product(m):
                     return dot_nn(rows_low, w[side, k, m * width : (m + 1) * width, :])
@@ -1530,21 +1745,6 @@
                 q[side, k, own, :] = (product(0) * score).astype(BF16)
                 kv[side, k, 0, own, :] = product(1).astype(BF16)
                 kv[side, k, 1, own, :] = product(2).astype(BF16)
-                return carry
-
-            lax.fori_loop(0, rows // block, step, 0)
-            spot = 2 * (2 * side + k)
-            copy = remote(
-                kv.at[side, k],
-                other_out.at[side, k],
-                kv_sems.at[spot],
-                kv_sems.at[spot + 1],
-                where_is("near"),
-            )
-            copy.start()
-            kv_copies.append(copy)
-            save(kv.at[side, k], own_out.at[side, k])
-            save(q.at[side, k], q_out.at[side, k])
 
         norm_kept.wait()
         norm_near.wait()
@@ -1553,22 +1753,27 @@
         weight.forward_last(0)
         weight.finish()
         save(w, w_out)
-        rows_in.wait_arrival(0)
-        save(x.at[0], x_out.at[0])
-
-        def settle(i, carry):
-            own = pl.ds(pl.multiple_of(i * block, block), block)
-            unit, _ = standardize(x[0, own, :].astype(F32))
-            low[own, :] = affine(unit, n.at[0], 2).astype(BF16)
-            return carry
-
-        lax.fori_loop(0, rows // block, settle, 0)
-        project(0, 0)
-        project(0, 1)
-        rows_in.wait_arrival(1)
-        save(x.at[1], x_out.at[1])
-        project(1, 0)
-        project(1, 1)
+        for i in range(pieces):
+            own = slice(i * count, (i + 1) * count)
+            for side in range(2):
+                rows_in.wait_arrival(2 * i + side)
+                rows_low = x[side, own, :]
+                if side == 0:
+                    unit, _ = standardize(rows_low.astype(F32))
+                    rows_low = affine(unit, n.at[0], 2).astype(BF16)
+                project(side, own, rows_low)
+                copy = remote(
+                    kv.at[side, :, :, own, :],
+                    other_out.at[side, :, :, own, :],
+                    kv_sems.at[0, 2 * i + side],
+                    kv_sems.at[1, 2 * i + side],
+                    where_is("near"),
+                )
+                copy.start()
+                kv_copies.append(copy)
+                save(x.at[side, own, :], x_out.at[side, own, :])
+                save(kv.at[side, :, :, own, :], own_out.at[side, :, :, own, :])
+                save(q.at[side, :, own, :], q_out.at[side, :, own, :])
         rows_in.wait_sent()
         for copy in kv_copies + stores:
             copy.wait()
@@ -1586,14 +1791,13 @@
         in_specs=[hold] * 3,
         out_specs=[hold] * 6,
         out_shape=[jax.ShapeDtypeStruct(*s) for s in shapes + shapes[-1:]],
-        scratch_shapes=[pltpu.VMEM(*shapes[0]), pltpu.VMEM((rows, width), BF16)]
-        + [pltpu.VMEM(*s) for s in shapes[1:]]
-        + ROW_SEMS
+        scratch_shapes=[pltpu.VMEM(*s) for s in shapes]
+        + row_sems(pieces)
         + [WeightCopies.sems(1)]
         + [
             pltpu.SemaphoreType.DMA((3,)),
-            pltpu.SemaphoreType.DMA((12,)),
-            pltpu.SemaphoreType.DMA((8,)),
+            pltpu.SemaphoreType.DMA((6 * pieces + 2,)),
+            pltpu.SemaphoreType.DMA((2, 2 * pieces)),
         ],
         compiler_params=pltpu.CompilerParams(
             vmem_limit_bytes=VMEM, collective_id=collective, has_side_effects=True
@@ -1802,9 +2006,6 @@
     def hops(*steps):
         return list(steps[:levels]) + list(steps[3 : 3 + levels])
 
-    def swap(value):
-        return lax.ppermute(value, "section", [(0, 1), (1, 0)])
-
     def flat(weight):
         return weight.reshape(-1, weight.shape[-1])
 
@@ -1844,7 +2045,7 @@
     )
     cross = cross.reshape(2, 2, *cross_proj.shape[1:])
     enc_mix, dec_mix = At(mix, 0), At(mix, 1)
-    encoded, memory, enc_first, enc_third = encoder_forward(
+    encoded, memory, enc_first, enc_third, pushed = encoder_forward(
         enc_x,
         enc_mix,
         enc_norm_in,
@@ -1852,8 +2053,9 @@
         parts(up, 0),
         parts(down, 0),
         parts(cross, 0),
-    )
-    memory = [memory, swap(memory)]
+        8,
+    )
+    memory = [memory, pushed]
     cross_q, dec_first = decoder_middle(
         dec_x, dec_mix, dec_norm_in, parts(out, 1), parts(cross, 1)
     )
@@ -1882,7 +2084,7 @@
         cross_mix_grad,
         cross_lse,
         cross_span,
-        chunk,
+        2 * chunk,
         Carry(
             [
                 Reduce(ffn_dec, 256, [0, 1, 2, 3], [1, 2], "chip"),
@@ -1937,80 +2139,88 @@
         2,
     )
     ffn_dec, ffn_dec_other, ffn_enc, ffn_enc_other, sides, _, encoded, decoded = moved
-    target_grad, dec_qkv = input_back(
-        dec_x,
-        dec_first_grad,
-        At(q_grad, 1),
-        [At(g, 1) for g in kv_grads],
-        dec_norm_in,
-        parts(qkv, 1),
-        False,
-        [],
-    )
-    source_grad, enc_qkv = input_back(
-        enc_x,
-        enc_first_grad,
-        At(q_grad, 0),
-        [At(g, 0) for g in kv_grads],
-        enc_norm_in,
-        parts(qkv, 0),
-        True,
+    tail = (
+        ([2, 2, 2, 2, 2, 3], [1, 2, *hops(1, 1, 1, 1, 1, 2)]),
+        ([4, 4, 4, 4, 4, 4, 4], [1, 2, *hops(1, 1, 1, 1, 1, 1)]),
+        (8, 6),
+        8 + 2 * levels,
+    )
+    enc_last, enc_other, dec_last, dec_other, source_grad, target_grad = close_down(
+        x,
+        [enc_first_grad, dec_first_grad],
+        q_grad,
+        kv_grads,
+        norm,
+        qkv,
         [enc_norm, dec_norm, mid_norm],
-    )
-    enc_last, enc_other, dec_last, dec_other, source_grad, target_grad = carry_alone(
+        tail,
+        7,
+    )
+
+    half = 3 * width // 2
+    units = ffn_up.shape[-1]
+
+    def columns(source, row, count, target, to):
+        wide = source.shape[-1]
+        for h in range(2):
+            target[to : to + count, h * wide : (h + 1) * wide] = source[
+                row + h * count : row + (h + 1) * count, :
+            ].astype(F32)
+
+    def finish(fetch, rooms):
+        grads, result, up, down, first, second, side, norm_part = range(8)
+        room = fetch(grads)
+        for row in range(2):
+            rooms[0][row] = room[row].astype(F32)
+        yield rooms[0]
+        yield fetch(result)
+        columns(fetch(up), 0, width, rooms[2], 0)
+        yield rooms[2]
+        rooms[3][...] = fetch(down)[...].astype(F32)
+        yield rooms[3]
+        room = fetch(side)
+        columns(room, 0, width // 2, rooms[4], 0)
+        yield rooms[4]
+        rooms[5][...] = room[width:, :].astype(F32)
+        yield rooms[5]
+        columns(fetch(first), 0, half, rooms[6], 0)
+        columns(fetch(second), 0, half, rooms[6], half)
+        yield rooms[6]
+        rooms[7][...] = fetch(norm_part)[...].astype(F32)
+        yield rooms[7]
+
+    part = qkv.shape[-1]
+    token_grad, result, up_grad, down_grad, out_grad, cross_grad, qkv_grad, norm_grad = lay_out(
         [
-            Reduce(
-                enc_qkv,
-                2 * PAIR,
-                [0, 1, 2, 2, 3, 3, 4],
-                [2, 2, *hops(1, 1, 1, 1, 1, 2)],
-            ),
-            Reduce(
-                dec_qkv,
-                2 * PAIR,
-                [0, 1, 1, 3, 4, 4],
-                [2, 2, *hops(1, 1, 1, 1, 1, 2)],
-            ),
-            ReturnRows(source_grad, 0, 6),
-            ReturnRows(target_grad, 1, 7),
+            (source_grad, target_grad),
+            (encoded, decoded),
+            (ffn_enc, ffn_dec_other),
+            (ffn_enc_other, ffn_dec),
+            (enc_last, dec_other),
+            (enc_other, dec_last),
         ],
-        10 + 2 * levels,
-        8,
-    )
-
-    half = 3 * width // 2
-    up_grad = jnp.where(is_first, ffn_enc, ffn_dec_other).astype(F32)
-    down_grad = jnp.where(is_first, ffn_enc_other, ffn_dec).astype(F32)
-    up_grad = jnp.concatenate(jnp.split(up_grad, 2, axis=0), axis=1)
-
-    def columns(halves):
-        return jnp.concatenate([halves[:half], halves[half : 2 * half]], axis=1)
-
-    qkv_grad = jnp.concatenate(
+        [(sides, 0, sides.shape[0]), (enc_last, 2 * half, 32)],
         [
-            jnp.where(is_first, columns(enc_last), columns(dec_other)),
-            jnp.where(is_first, columns(enc_other), columns(dec_last)),
+            ((2, rows, width), F32),
+            ((2, rows, width), BF16),
+            ((width, units), F32),
+            ((units, width), F32),
+            ((part, width), F32),
+            ((2 * width, part), F32),
+            ((2 * half, part), F32),
+            ((32, PAIR), F32),
         ],
-        axis=0,
-    )
-    qkv_grad = qkv_grad.astype(F32).reshape(self_qkv.shape)
-    sides = sides.astype(F32)
-    out_grad = jnp.concatenate([sides[: width // 2], sides[width // 2 : width]], axis=1)
-    cross_grad = sides[width:].reshape(cross_proj.shape)
-    norm_grad = enc_last[2 * half : 2 * half + 24].astype(F32).reshape(norms.shape)
-
-    def by_side(source, target):
-        return jnp.where(is_first, source, target)
-
+        finish,
+    )
     return (
-        by_side(encoded, decoded)[None],
-        by_side(source_grad, target_grad).astype(F32)[None],
-        qkv_grad,
+        result[None],
+        token_grad[None],
+        qkv_grad.reshape(self_qkv.shape),
         out_grad[None],
-        cross_grad,
+        cross_grad.reshape(cross_proj.shape),
         up_grad[None],
         down_grad[None],
-        norm_grad,
+        norm_grad[:24].reshape(norms.shape),
     )
 
 

time: 484 us -> 452 us (0.934)
  Pallas kernels: 446 us -> 434 us
  other arithmetic: 11.4 us -> 1.19 us
  local copies, waits for them, and re-layouts: 9.92 us -> 2.68 us
    pallas_call x1 -> x2, Pallas kernels: 45.3 us -> 61.7 us  [the longest x1 54.8 us: close_down(): pl.pallas_call(kernel, in_specs=[hold] * len(arrays) + [vmem] * len(norm_...]
    pallas_call x7 -> x5, Pallas kernels: 97.5 us -> 83 us  [row_call(): pl.pallas_call(kernel, grid=(rows // block,), in_specs=[blocked(a, dim) f...]
    pallas_call x2, Pallas kernels: 176 us -> 166 us  [attend_back(): pl.pallas_call(kernel, grid=(pairs,), in_specs=[pl.BlockSpec(memory_space...]
    broadcast_in_dim x5 -> x0, other arithmetic: 7.65 us -> none  [the longest x1 2.29 us: local_fast(): by_side(source_grad, target_grad).astype(F32)[None]]
    pallas_call x1, Pallas kernels: 45.4 us -> 39.6 us  [open_up(): pl.pallas_call(kernel, in_specs=[hold] * 3, out_specs=[hold] * 6, out_sha...]
    unnamed x26 -> x0, local copies, waits for them, and re-layouts: 5.57 us -> none
  transfers between devices with their start and end apart: 1 -> 0, of which waited for: 0 -> 0; matrix products, arithmetic and copies ran while one was open for 0% -> 0% of each run, Pallas kernels for 1% -> 0%
where the time goes in v6:
time: 452 us; the launch traced here: 447 us
  Pallas kernels  434 us (96%)
  between operations  10 us (2%)
    pallas_call x2, Pallas kernels, attend_back(): pl.pallas_call(kernel, grid=(pairs,), in_specs=[pl.BlockSpec(memory_space...  166 us
    pallas_call x5, Pallas kernels, row_call(): pl.pallas_call(kernel, grid=(rows // block,), in_specs=[blocked(a, dim) f...  83 us
    pallas_call x2, Pallas kernels, attend(): pl.pallas_call(kernel, grid=(pairs,), in_specs=[pl.BlockSpec(memory_space...  82.8 us
    pallas_call x1, Pallas kernels, close_down(): pl.pallas_call(kernel, in_specs=[hold] * len(arrays) + [vmem] * len(norm_...  54.8 us
    pallas_call x1, Pallas kernels, open_up(): pl.pallas_call(kernel, in_specs=[hold] * 3, out_specs=[hold] * 6, out_sha...  39.6 us

profile of v6, /device:TPU:0, one launch (start us, length us, event | category | flops | bytes accessed | tf_op | source)
XLA Modules:
  0.0 447.4 jit_solution(3583566750003849436)
XLA Ops:
  0.6 1.4 constant_dynamic-slice_fusion.1
  11.1 0.1 add_bitcast_fusion
  11.1 0.6 add_bitcast_fusion.2.span_ref
  11.7 0.5 pad_add_fusion.span_ref
  12.3 39.6 %open_up.1 = (bf16[2,1024,512]{2,1,0:T(8,128)(2,1)}, bf16[2,2,1536,256]{3,2,1,0:T(8,128)(2,1)}, f32[2,3,2,512]{3,2,1,0:T(2,128)}, bf16[2,2,1024,256]{3,2,1,0:T(8...) custom-call(bf16[2,1024,512]{2,1,0:T(8,128)(2,1)} %bitcast.46, ...), custom_call_target="tpu_custom_call" | custom-call | tf_op jit(solution)/shard_map/open_up/pallas_call | solution.py:1789
  51.9 55.4 %attend.2 = (bf16[2,2,1024,256]{3,2,1,0:T(8,128)(2,1)}, f32[2,1024,512]{2,1,0:T(8,128)}, bf16[2,2,256,512]{3,2,1,0:T(8,128)(2,1)}, bf16[2,2,512,1024]{3,2,1,0:T(...) custom-call(s32[2,4]{1,0:T(2,128)} %pad_add_fusion.span_ref, ...), custom_call_target="tpu_custom_call" | custom-call | flops 34359738368 | bytes 16777216 | tf_op jit(solution)/shard_map/attend/pallas_call | solution.py:840
  107.3 4.9 %decoder_middle.1 = (bf16[2,1024,256]{2,1,0:T(8,128)(2,1)}, f32[1024,512]{1,0:T(8,128)}) custom-call(bf16[2,1024,512]{2,1,0:T(8,128)(2,1)} %get-tuple-element.75.refs_0_, bf16[2,2,1024,256]{3,2,1,0:T(8,128)(2,1)} %get-tuple-element.79.refs_1_.refs_2_.refs_5_.mix_ref, f32[2,3,2,512]{3,2,1,0:T(2,128)} %get-tuple-element.80.refs_2_.refs_3_.refs_4_.refs_6_, ...), custom_call_target="tpu_custom_call" | custom-call | flops 1073741824 | bytes 3682304 | tf_op jit(solution)/shard_map/decoder_middle/pallas_call | solution.py:199
  112.2 15.3 %encoder_forward.1 = (bf16[1024,512]{1,0:T(8,128)(2,1)}, bf16[2,2,1024,256]{3,2,1,0:T(8,128)(2,1)}, f32[1024,512]{1,0:T(8,128)}, f32[1024,512]{1,0:T(8,128)}, bf16[2,2,1024,256]{3,2,1,0:T(8,128)(2,1)}) custom-call(bf16[2,1024,512]{2,1,0:T(8,128)(2,1)} %get-tuple-element.75.refs_0_, ...), custom_call_target="tpu_custom_call" | custom-call | flops 5905580032 | bytes 7876608 | tf_op jit(solution)/shard_map/encoder_forward/pallas_call | solution.py:199
  127.5 27.4 %attend.3 = (bf16[2,1024,256]{2,1,0:T(8,128)(2,1)}, f32[1024,512]{1,0:T(8,128)}, bf16[2,1024,512]{2,1,0:T(8,128)(2,1)}) custom-call(s32[1,4]{1,0:T(1,128)} %add_bitcast_fusion.2.span_ref, bf16[2,1024,256]{2,1,0:T(8,128)(2,1)} %get-tuple-element.87.q_ref, bf16[2,2,1024,256]{3,2,1,0:T(8,128)(2,1)} %get-tuple-element.88.refs_0_, ...), custom_call_target="tpu_custom_call" | custom-call | flops 17179869184 | bytes 8388608 | tf_op jit(solution)/shard_map/attend/pallas_call | solution.py:840
  154.9 25.7 %decoder_turn.1 = (bf16[1024,512]{1,0:T(8,128)(2,1)}, f32[1024,512]{1,0:T(8,128)}, bf16[2,1024,256]{2,1,0:T(8,128)(2,1)}, bf16[2,512,256]{2,1,0:T(8,128)(2,1)}, ...) custom-call(f32[1024,512]{1,0:T(8,128)} %get-tuple-element.91.refs_0_, ...), custom_call_target="tpu_custom_call" | custom-call | flops 14495514624 | bytes 9449472 | tf_op jit(solution)/shard_map/decoder_turn/pallas_call | solution.py:199
  180.6 53.6 %attend_back.2 = (bf16[2,1024,256]{2,1,0:T(8,128)(2,1)}, bf16[2,2,1024,256]{3,2,1,0:T(8,128)(2,1)}, bf16[2,2,1024,256]{3,2,1,0:T(8,128)(2,1)}, bf16[1024,512]{1,0:T(8,128)(2,1)}, bf16[2,1024,512]{2,1,0:T(8,128)(2,1)}) custom-call(s32[1,4]{1,0:T(1,128)} %add_bitcast_fusion.2.span_ref, bf16[2,1024,256]{2,1,0:T(8,128)(2,1)} %get-tuple-element.87.q_ref, ...), custom_call_target="tpu_custom_call" | custom-call | flops 42949672960 | bytes 16777216 | tf_op jit(solution)/shard_map/attend_back/pallas_call | solution.py:1000
  234.2 8.0 %decoder_middle_back.1 = (f32[1024,512]{1,0:T(8,128)}, bf16[2,2,1024,256]{3,2,1,0:T(8,128)(2,1)}, bf16[2,512,256]{2,1,0:T(8,128)(2,1)}, bf16[2,256,512]{2,1,0:T(8,128)(2,1)}, f32[3,2,512]{2,1,0:T(2,128)}) custom-call(f32[1024,512]{1,0:T(8,128)} %get-tuple-element.91.refs_0_, f32[1024,512]{1,0:T(8,128)} %get-tuple-element.99.refs_1_, ...), custom_call_target="tpu_custom_call" | custom-call | flops 2147483648 | bytes 7876608 | tf_op jit(solution)/shard_map/decoder_middle_back/pallas_call | solution.py:199
  242.2 29.1 %encoder_back.1 = (f32[1024,512]{1,0:T(8,128)}, bf16[2,2,1024,256]{3,2,1,0:T(8,128)(2,1)}, bf16[2,2,1024,512]{3,2,1,0:T(8,128)(2,1)}, bf16[2,2,1536,256]{3,2,1,0:T(8,128)(2,1)}, f32[3,2,512]{2,1,0:T(2,128)}) custom-call(f32[1024,512]{1,0:T(8,128)} %get-tuple-element.85.refs_0_, ...), custom_call_target="tpu_custom_call", output_to_operand_aliasing={{1}: (18, {})} | custom-call | flops 13958643712 | bytes 17838080 | tf_op jit(solution)/shard_map/encoder_back/pallas_call | solution.py:199
  271.3 112.8 %attend_back.3 = (bf16[2,2,1024,256]{3,2,1,0:T(8,128)(2,1)}, bf16[2,2,2,1024,256]{4,3,2,1,0:T(8,128)(2,1)}, bf16[2,2,2,1024,256]{4,3,2,1,0:T(8,128)(2,1)}, bf16[...) custom-call(s32[2,4]{1,0:T(2,128)} %pad_add_fusion.span_ref, ...), custom_call_target="tpu_custom_call" | custom-call | flops 85899345920 | bytes 33554432 | tf_op jit(solution)/shard_map/attend_back/pallas_call | solution.py:1000
  384.1 54.8 %close_down.1 = (bf16[1792,128]{1,0:T(8,128)(2,1)}, bf16[1792,128]{1,0:T(8,128)(2,1)}, bf16[1536,128]{1,0:T(8,128)(2,1)}, bf16[1536,128]{1,0:T(8,128)(2,1)}, bf1...) custom-call(bf16[2,1024,512]{2,1,0:T(8,128)(2,1)} %get-tuple-element.75.refs_0_, ...), custom_call_target="tpu_custom_call" | custom-call | tf_op jit(solution)/shard_map/close_down/pallas_call | solution.py:1631
  439.0 6.9 %lay_out.1 = (f32[2,1024,512]{2,1,0:T(8,128)}, bf16[2,1024,512]{2,1,0:T(8,128)(2,1)}, f32[512,1024]{1,0:T(8,128)}, f32[1024,512]{1,0:T(8,128)}, f32[256,512]{1,0...) custom-call(bf16[2,1024,512]{2,1,0:T(8,128)(2,1)} %get-tuple-element.121.refs_0_, ...), custom_call_target="tpu_custom_call" | custom-call | tf_op jit(solution)/shard_map/lay_out/pallas_call | solution.py:1690
  445.9 0.7 slice.24
  446.6 0.6 reshape.55

commit v7 on v6

--- a/solution.py
+++ b/solution.py
@@ -735,6 +735,23 @@
         value_o[own, :] = jnp.where(low, 1.0, values).astype(BF16)
 
 
+class Lengths:
+    def __init__(self, lengths, asking=None, answering=None):
+        self.lengths, self.asking, self.answering = lengths, asking, answering
+
+    def span(self, ref, side, rows):
+        section, _, tensor = spots()
+        asks, answers = [
+            [ref[side if own is None else own, tensor, j] for j in range(2)]
+            for own in (self.asking, self.answering)
+        ]
+        paired = asks[1] > 0
+        second = paired & (section * rows >= asks[0])
+        begin = jnp.where(second, answers[0], 0)
+        end = jnp.where(second | jnp.logical_not(paired), answers[0] + answers[1], answers[0])
+        return [begin, end, section * rows, (1 - section) * rows]
+
+
 class Pairs:
     def __init__(self, query):
         self.sides = query.shape[:-3]
@@ -772,8 +789,10 @@
             (*none, self.rows, PAIR), lambda i: (*self.side(i), 0, i % self.per_side)
         )
 
-    def span(self, span_ref, i):
+    def span(self, span, span_ref, i):
         side = i // self.per_side if self.sides else 0
+        if isinstance(span, Lengths):
+            return span.span(span_ref, side, self.rows)
         return [span_ref[side, j] for j in range(span_ref.shape[1])]
 
 
@@ -800,8 +819,8 @@
             carrier.run(place, slot, slots, pairs * slots, carry_ins, carry_outs, refs[4:])
 
         carry(0)
-        span = heads_of.span(span_ref, pl.program_id(0))
-        widen_keys(span, kv_refs, key_e, key_o, value_e, value_o, rows)
+        seen = heads_of.span(span, span_ref, pl.program_id(0))
+        widen_keys(seen, kv_refs, key_e, key_o, value_e, value_o, rows)
         lane = lax.broadcasted_iota(jnp.int32, (block, PAIR), 1)
         low = lane < HALF
         units = []
@@ -853,7 +872,8 @@
             transcendentals=0,
         ),
         name="attend",
-    )(span, query.array, *[piece.array for piece in kv_pieces], *carrier.ins)
+    )(
+        span.lengths if isinstance(span, Lengths) else span, query.array, *[piece.array for piece in kv_pieces], *carrier.ins)
 
 
 def attend_back(
@@ -888,8 +908,8 @@
             carrier.run(pair, slot, slots, pairs * slots, carry_ins, carry_outs, refs)
 
         carry(0)
-        span = heads_of.span(span_ref, pl.program_id(0))
-        widen_keys(span, kv_refs, key_e, key_o, value_e, value_o, rows)
+        seen = heads_of.span(span, span_ref, pl.program_id(0))
+        widen_keys(seen, kv_refs, key_e, key_o, value_e, value_o, rows)
         for g, kv_ref in enumerate(kv_refs):
             key_t[:, g * rows : (g + 1) * rows] = kv_ref[0].T
         lane = lax.broadcasted_iota(jnp.int32, (rows, PAIR), 1)
@@ -1021,7 +1041,7 @@
         ),
         name="attend_back",
     )(
-        span,
+        span.lengths if isinstance(span, Lengths) else span,
         query.array,
         mix.array,
         mix_grad.array,
@@ -1994,10 +2014,8 @@
 
 
 def local_fast(tokens, lengths, self_qkv, self_out, cross_proj, ffn_up, ffn_down, norms, cotangent):
-    section, tensor = lax.axis_index("section"), lax.axis_index("tensor")
     _, row_count, rows, width = tokens.shape
     assert row_count == 2
-    is_first = section == 0
     block = min(256, rows)
     query_block = min(256, rows)
     chunk = 256
@@ -2009,17 +2027,7 @@
     def flat(weight):
         return weight.reshape(-1, weight.shape[-1])
 
-    def span_of(query_side, key_side):
-        own = lax.dynamic_index_in_dim(lengths, tensor, 1, keepdims=False)
-        asks, answers = own[query_side], own[key_side]
-        paired = asks[1] > 0
-        second = paired & (section * rows >= asks[0])
-        begin = jnp.where(second, answers[0], 0)
-        end = jnp.where(second | ~paired, answers[0] + answers[1], answers[0])
-        return jnp.stack([begin, end, section * rows, (1 - section) * rows]).astype(jnp.int32)
-
-    spans = jnp.stack([span_of(0, 0), span_of(1, 1), span_of(1, 0)])
-    self_spans, cross_span = spans[:2], spans[2:]
+    self_spans, cross_span = Lengths(lengths), Lengths(lengths, 1, 0)
     x, qkv, norm, q, *kv = open_up(tokens[0], flat(self_qkv), norms[0], block, 1)
     qkv = qkv.reshape(2, 2, *self_qkv.shape[1:])
 
@@ -2034,14 +2042,13 @@
         query_block,
         Carry(
             [
-                SpreadWeight(self_out[0], [3], [5]),
-                SpreadWeight(ffn_up[0], [4, 6], [7, 9]),
-                SpreadWeight(flat(cross_proj), [8], [11]),
-                SpreadWeight(ffn_down[0], [10, 12], [13, 15]),
+                SpreadWeight(self_out[0], [1], [3]),
+                SpreadWeight(ffn_up[0], [2, 3], [4, 5]),
+                SpreadWeight(flat(cross_proj), [4], [6]),
+                SpreadWeight(ffn_down[0], [5, 6], [7, 7]),
             ],
             2,
         ),
-        2,
     )
     cross = cross.reshape(2, 2, *cross_proj.shape[1:])
     enc_mix, dec_mix = At(mix, 0), At(mix, 1)
@@ -2065,7 +2072,6 @@
         cross_span,
         query_block,
         Carry([SpreadRows(cotangent[0], (1,))], 4),
-        2,
     )
     decoded, second_grad, cross_mix_grad, cross_out_grad, ffn_dec, dec_norm = decoder_turn(
         dec_first,
@@ -2186,7 +2192,15 @@
         columns(fetch(first), 0, half, rooms[6], 0)
         columns(fetch(second), 0, half, rooms[6], half)
         yield rooms[6]
-        rooms[7][...] = fetch(norm_part)[...].astype(F32)
+        lines = fetch(norm_part)[...].astype(F32)
+        wide = width // PAIR
+        for slot in range(3):
+            for i in range(2):
+                for h in range(wide):
+                    line = (2 * slot + i) * wide + h
+                    rooms[7][slot, i : i + 1, h * PAIR : (h + 1) * PAIR] = lines[
+                        line : line + 1, :
+                    ]
         yield rooms[7]
 
     part = qkv.shape[-1]
@@ -2208,7 +2222,7 @@
             ((part, width), F32),
             ((2 * width, part), F32),
             ((2 * half, part), F32),
-            ((32, PAIR), F32),
+            (norms.shape[1:], F32),
         ],
         finish,
     )
@@ -2220,7 +2234,7 @@
         cross_grad.reshape(cross_proj.shape),
         up_grad[None],
         down_grad[None],
-        norm_grad[:24].reshape(norms.shape),
+        norm_grad[None],
     )
 
 

time: 452 us -> 436 us (0.965)
  between operations: 10 us -> 0.96 us
where the time goes in v7:
time: 436 us; the launch traced here: 432 us
  Pallas kernels  431 us (99%)
    pallas_call x2, Pallas kernels, attend_back(): pl.pallas_call(kernel, grid=(pairs,), in_specs=[pl.BlockSpec(memory_space...  166 us
    pallas_call x5, Pallas kernels, row_call(): pl.pallas_call(kernel, grid=(rows // block,), in_specs=[blocked(a, dim) f...  83 us
    pallas_call x2, Pallas kernels, attend(): pl.pallas_call(kernel, grid=(pairs,), in_specs=[pl.BlockSpec(memory_space...  80.2 us
    pallas_call x1, Pallas kernels, close_down(): pl.pallas_call(kernel, in_specs=[hold] * len(arrays) + [vmem] * len(norm_...  55.2 us
    pallas_call x1, Pallas kernels, open_up(): pl.pallas_call(kernel, in_specs=[hold] * 3, out_specs=[hold] * 6, out_sha...  39.7 us

profile of v7, /device:TPU:0, one launch (start us, length us, event | category | flops | bytes accessed | tf_op | source)
XLA Modules:
  0.0 432.3 jit_solution(15731396828659241237)
XLA Ops:
  0.6 39.7 %open_up.1 = (bf16[2,1024,512]{2,1,0:T(8,128)(2,1)}, bf16[2,2,1536,256]{3,2,1,0:T(8,128)(2,1)}, f32[2,3,2,512]{3,2,1,0:T(2,128)}, bf16[2,2,1024,256]{3,2,1,0:T(8...) custom-call(bf16[2,1024,512]{2,1,0:T(8,128)(2,1)} %bitcast.29, ...), custom_call_target="tpu_custom_call" | custom-call | tf_op jit(solution)/shard_map/open_up/pallas_call | solution.py:1809
  40.3 54.7 %attend.2 = (bf16[2,2,1024,256]{3,2,1,0:T(8,128)(2,1)}, f32[2,1024,512]{2,1,0:T(8,128)}, bf16[2,2,256,512]{3,2,1,0:T(8,128)(2,1)}, bf16[2,2,512,1024]{3,2,1,0:T(...) custom-call(s32[2,2,2]{2,1,0:T(2,128)} %span_ref.7, ...), custom_call_target="tpu_custom_call" | custom-call | flops 34359738368 | bytes 16777216 | tf_op jit(solution)/shard_map/attend/pallas_call | solution.py:859
  95.0 4.9 %decoder_middle.1 = (bf16[2,1024,256]{2,1,0:T(8,128)(2,1)}, f32[1024,512]{1,0:T(8,128)}) custom-call(bf16[2,1024,512]{2,1,0:T(8,128)(2,1)} %get-tuple-element.75.refs_0_, bf16[2,2,1024,256]{3,2,1,0:T(8,128)(2,1)} %get-tuple-element.79.refs_1_.refs_2_.refs_5_.mix_ref, f32[2,3,2,512]{3,2,1,0:T(2,128)} %get-tuple-element.80.refs_2_.refs_3_.refs_4_.refs_6_, ...), custom_call_target="tpu_custom_call" | custom-call | flops 1073741824 | bytes 3682304 | tf_op jit(solution)/shard_map/decoder_middle/pallas_call | solution.py:199
  100.0 15.3 %encoder_forward.1 = (bf16[1024,512]{1,0:T(8,128)(2,1)}, bf16[2,2,1024,256]{3,2,1,0:T(8,128)(2,1)}, f32[1024,512]{1,0:T(8,128)}, f32[1024,512]{1,0:T(8,128)}, bf16[2,2,1024,256]{3,2,1,0:T(8,128)(2,1)}) custom-call(bf16[2,1024,512]{2,1,0:T(8,128)(2,1)} %get-tuple-element.75.refs_0_, ...), custom_call_target="tpu_custom_call" | custom-call | flops 5905580032 | bytes 7876608 | tf_op jit(solution)/shard_map/encoder_forward/pallas_call | solution.py:199
  115.2 25.5 %attend.3 = (bf16[2,1024,256]{2,1,0:T(8,128)(2,1)}, f32[1024,512]{1,0:T(8,128)}, bf16[2,1024,512]{2,1,0:T(8,128)(2,1)}) custom-call(s32[2,2,2]{2,1,0:T(2,128)} %span_ref.7, bf16[2,1024,256]{2,1,0:T(8,128)(2,1)} %get-tuple-element.87.q_ref, bf16[2,2,1024,256]{3,2,1,0:T(8,128)(2,1)} %get-tuple-element.88.refs_0_, ...), custom_call_target="tpu_custom_call" | custom-call | flops 17179869184 | bytes 8388608 | tf_op jit(solution)/shard_map/attend/pallas_call | solution.py:859
  140.8 25.7 %decoder_turn.1 = (bf16[1024,512]{1,0:T(8,128)(2,1)}, f32[1024,512]{1,0:T(8,128)}, bf16[2,1024,256]{2,1,0:T(8,128)(2,1)}, bf16[2,512,256]{2,1,0:T(8,128)(2,1)}, ...) custom-call(f32[1024,512]{1,0:T(8,128)} %get-tuple-element.91.refs_0_, ...), custom_call_target="tpu_custom_call" | custom-call | flops 14495514624 | bytes 9449472 | tf_op jit(solution)/shard_map/decoder_turn/pallas_call | solution.py:199
  166.4 53.6 %attend_back.2 = (bf16[2,1024,256]{2,1,0:T(8,128)(2,1)}, bf16[2,2,1024,256]{3,2,1,0:T(8,128)(2,1)}, bf16[2,2,1024,256]{3,2,1,0:T(8,128)(2,1)}, bf16[1024,512]{1,0:T(8,128)(2,1)}, bf16[2,1024,512]{2,1,0:T(8,128)(2,1)}) custom-call(s32[2,2,2]{2,1,0:T(2,128)} %span_ref.7, bf16[2,1024,256]{2,1,0:T(8,128)(2,1)} %get-tuple-element.87.q_ref, ...), custom_call_target="tpu_custom_call" | custom-call | flops 42949672960 | bytes 16777216 | tf_op jit(solution)/shard_map/attend_back/pallas_call | solution.py:1020
  220.0 8.0 %decoder_middle_back.1 = (f32[1024,512]{1,0:T(8,128)}, bf16[2,2,1024,256]{3,2,1,0:T(8,128)(2,1)}, bf16[2,512,256]{2,1,0:T(8,128)(2,1)}, bf16[2,256,512]{2,1,0:T(8,128)(2,1)}, f32[3,2,512]{2,1,0:T(2,128)}) custom-call(f32[1024,512]{1,0:T(8,128)} %get-tuple-element.91.refs_0_, f32[1024,512]{1,0:T(8,128)} %get-tuple-element.99.refs_1_, ...), custom_call_target="tpu_custom_call" | custom-call | flops 2147483648 | bytes 7876608 | tf_op jit(solution)/shard_map/decoder_middle_back/pallas_call | solution.py:199
  228.0 29.1 %encoder_back.1 = (f32[1024,512]{1,0:T(8,128)}, bf16[2,2,1024,256]{3,2,1,0:T(8,128)(2,1)}, bf16[2,2,1024,512]{3,2,1,0:T(8,128)(2,1)}, bf16[2,2,1536,256]{3,2,1,0:T(8,128)(2,1)}, f32[3,2,512]{2,1,0:T(2,128)}) custom-call(f32[1024,512]{1,0:T(8,128)} %get-tuple-element.85.refs_0_, ...), custom_call_target="tpu_custom_call", output_to_operand_aliasing={{1}: (18, {})} | custom-call | flops 13958643712 | bytes 17838080 | tf_op jit(solution)/shard_map/encoder_back/pallas_call | solution.py:199
  257.2 112.8 %attend_back.3 = (bf16[2,2,1024,256]{3,2,1,0:T(8,128)(2,1)}, bf16[2,2,2,1024,256]{4,3,2,1,0:T(8,128)(2,1)}, bf16[2,2,2,1024,256]{4,3,2,1,0:T(8,128)(2,1)}, bf16[...) custom-call(s32[2,2,2]{2,1,0:T(2,128)} %span_ref.7, ...), custom_call_target="tpu_custom_call" | custom-call | flops 85899345920 | bytes 33554432 | tf_op jit(solution)/shard_map/attend_back/pallas_call | solution.py:1020
  370.0 55.2 %close_down.1 = (bf16[1792,128]{1,0:T(8,128)(2,1)}, bf16[1792,128]{1,0:T(8,128)(2,1)}, bf16[1536,128]{1,0:T(8,128)(2,1)}, bf16[1536,128]{1,0:T(8,128)(2,1)}, bf1...) custom-call(bf16[2,1024,512]{2,1,0:T(8,128)(2,1)} %get-tuple-element.75.refs_0_, ...), custom_call_target="tpu_custom_call" | custom-call | tf_op jit(solution)/shard_map/close_down/pallas_call | solution.py:1651
  425.2 6.9 %lay_out.1 = (f32[2,1024,512]{2,1,0:T(8,128)}, bf16[2,1024,512]{2,1,0:T(8,128)(2,1)}, f32[512,1024]{1,0:T(8,128)}, f32[1024,512]{1,0:T(8,128)}, f32[256,512]{1,0...) custom-call(bf16[2,1024,512]{2,1,0:T(8,128)(2,1)} %get-tuple-element.121.refs_0_, ...), custom_call_target="tpu_custom_call" | custom-call | tf_op jit(solution)/shard_map/lay_out/pallas_call | solution.py:1710

commit v8 on v7

--- a/solution.py
+++ b/solution.py
@@ -851,6 +851,7 @@
                 lse_ref[own, :] = top + LOG2E * jnp.log(weight)
                 mixed = jnp.where(low, sums[u - 1], sums[u])
                 out_ref[own, :] = (mixed / pltpu.roll(weight, HALF, 1)).astype(BF16)
+        carry(slots)
 
     query_spec, kv_spec = heads_of.query_spec, heads_of.kv_spec
     lse_spec = heads_of.lse_spec()
@@ -1005,6 +1006,8 @@
             def _():
                 for i in range(pairs):
                     swap(i).wait()
+
+        carry(slots)
 
     query_spec, kv_spec = heads_of.query_spec, heads_of.kv_spec
     lse_spec = heads_of.lse_spec()
@@ -1115,12 +1118,20 @@
             ins, outs, scratch = ins[i:], outs[o:], scratch[s:]
         for step, rank, action in sorted(events, key=lambda event: event[:2]):
             assert 0 <= step < steps
-            plan.setdefault(step, []).append(action)
+            plan.setdefault(steps if rank == LAST else step, []).append(action)
         return plan
 
     def run(self, place, slot, slots, steps, ins, outs, scratch):
         for step, actions in self.plan(steps, ins, outs, scratch).items():
-            if step % slots == slot:
+            if step == steps:
+                if slot == slots:
+
+                    @pl.when(place == steps // slots - 1)
+                    def _():
+                        for action in actions:
+                            action()
+
+            elif step % slots == slot:
 
                 @pl.when(place == step // slots)
                 def _():
@@ -1234,19 +1245,55 @@
 
 class SpreadRows:
     peers = GROUP
-    staged = True
 
     def __init__(self, array, sides, begin=0):
         self.ins, self.sides, self.begin = [array], sides, begin
         self.outs = [jax.ShapeDtypeStruct(array.shape, array.dtype)]
-        self.scratch = row_sems() + [pltpu.VMEM(array.shape[-2:], array.dtype)]
-
-    def make(self, ins, outs, scratch):
-        return spread_rows(ins[0], outs[0], scratch[:3], self.sides, scratch[3])
+        self.scratch = [
+            *row_sems(),
+            pltpu.VMEM(array.shape, array.dtype),
+            pltpu.SemaphoreType.DMA((2,)),
+        ]
+
+    def events(self, steps, ins, outs, scratch):
+        room, sems = scratch[3], scratch[4]
+
+        def make():
+            return spread_rows(ins[0], room, scratch[:3], self.sides)
+
+        def store(side):
+            return pltpu.make_async_copy(room.at[side], outs[0].at[side], sems.at[side])
+
+        def arrive():
+            rows = make()
+            for i, side in enumerate(self.sides):
+                rows.wait_arrival(i)
+                store(side).start()
+
+        def finish():
+            for side in self.sides:
+                store(side).wait()
+            make().wait_sent()
+
+        return [
+            (self.begin, 1, lambda: make().start()),
+            (steps - 1, 1, arrive),
+            (steps - 1, LAST, finish),
+        ]
+
+
+class ReturnRows:
+    peers = GROUP
+
+    def __init__(self, array, side, begin=0, staged=True):
+        self.ins, self.side, self.begin, self.staged = [array], side, begin, staged
+        self.outs = [jax.ShapeDtypeStruct((2, *array.shape), array.dtype)]
+        self.scratch = row_sems() + [pltpu.VMEM(array.shape, array.dtype)] * staged
 
     def events(self, steps, ins, outs, scratch):
         def make():
-            return self.make(ins, outs, scratch)
+            room = scratch[3] if self.staged else None
+            return return_rows(ins[0], outs[0], scratch[:3], self.side, room)
 
         def finish():
             rows = make()
@@ -1258,17 +1305,6 @@
         if self.staged:
             events.append((self.begin + 1, 1, lambda: make().keep_on()))
         return events
-
-
-class ReturnRows(SpreadRows):
-    def __init__(self, array, side, begin=0, staged=True):
-        self.ins, self.side, self.begin, self.staged = [array], side, begin, staged
-        self.outs = [jax.ShapeDtypeStruct((2, *array.shape), array.dtype)]
-        self.scratch = row_sems() + [pltpu.VMEM(array.shape, array.dtype)] * staged
-
-    def make(self, ins, outs, scratch):
-        room = scratch[3] if len(scratch) > 3 else None
-        return return_rows(ins[0], outs[0], scratch[:3], self.side, room)
 
 
 class WeightCopies:
@@ -1624,7 +1660,7 @@
                     ]
                     norm_lines(sides, into, parts, 2 * half)
 
-        for step in range(steps):
+        for step in range(steps + 1):
             for action in plan.get(step, []):
                 action()
             if step < 2 * halves:

time: 436 us -> 433 us (level)
  no operation moved by 1% of the time
where the time goes in v8:
time: 433 us; the launch traced here: 429 us
  Pallas kernels  428 us (99%)
    pallas_call x2, Pallas kernels, attend_back(): pl.pallas_call(kernel, grid=(pairs,), in_specs=[pl.BlockSpec(memory_space...  164 us
    pallas_call x5, Pallas kernels, row_call(): pl.pallas_call(kernel, grid=(rows // block,), in_specs=[blocked(a, dim) f...  83 us
    pallas_call x2, Pallas kernels, attend(): pl.pallas_call(kernel, grid=(pairs,), in_specs=[pl.BlockSpec(memory_space...  79.4 us
    pallas_call x1, Pallas kernels, close_down(): pl.pallas_call(kernel, in_specs=[hold] * len(arrays) + [vmem] * len(norm_...  55.5 us
    pallas_call x1, Pallas kernels, open_up(): pl.pallas_call(kernel, in_specs=[hold] * 3, out_specs=[hold] * 6, out_sha...  39.7 us

profile of v8, /device:TPU:0, one launch (start us, length us, event | category | flops | bytes accessed | tf_op | source)
XLA Modules:
  0.0 429.3 jit_solution(4095810717328282621)
XLA Ops:
  0.6 39.7 %open_up.1 = (bf16[2,1024,512]{2,1,0:T(8,128)(2,1)}, bf16[2,2,1536,256]{3,2,1,0:T(8,128)(2,1)}, f32[2,3,2,512]{3,2,1,0:T(2,128)}, bf16[2,2,1024,256]{3,2,1,0:T(8...) custom-call(bf16[2,1024,512]{2,1,0:T(8,128)(2,1)} %bitcast.29, ...), custom_call_target="tpu_custom_call" | custom-call | tf_op jit(solution)/shard_map/open_up/pallas_call | solution.py:1845
  40.3 53.8 %attend.2 = (bf16[2,2,1024,256]{3,2,1,0:T(8,128)(2,1)}, f32[2,1024,512]{2,1,0:T(8,128)}, bf16[2,2,256,512]{3,2,1,0:T(8,128)(2,1)}, bf16[2,2,512,1024]{3,2,1,0:T(...) custom-call(s32[2,2,2]{2,1,0:T(2,128)} %span_ref.7, ...), custom_call_target="tpu_custom_call" | custom-call | flops 34359738368 | bytes 16777216 | tf_op jit(solution)/shard_map/attend/pallas_call | solution.py:860
  94.1 4.9 %decoder_middle.1 = (bf16[2,1024,256]{2,1,0:T(8,128)(2,1)}, f32[1024,512]{1,0:T(8,128)}) custom-call(bf16[2,1024,512]{2,1,0:T(8,128)(2,1)} %get-tuple-element.75.refs_0_, bf16[2,2,1024,256]{3,2,1,0:T(8,128)(2,1)} %get-tuple-element.79.refs_1_.refs_2_.refs_5_.mix_ref, f32[2,3,2,512]{3,2,1,0:T(2,128)} %get-tuple-element.80.refs_2_.refs_3_.refs_4_.refs_6_, ...), custom_call_target="tpu_custom_call" | custom-call | flops 1073741824 | bytes 3682304 | tf_op jit(solution)/shard_map/decoder_middle/pallas_call | solution.py:199
  99.0 15.3 %encoder_forward.1 = (bf16[1024,512]{1,0:T(8,128)(2,1)}, bf16[2,2,1024,256]{3,2,1,0:T(8,128)(2,1)}, f32[1024,512]{1,0:T(8,128)}, f32[1024,512]{1,0:T(8,128)}, bf16[2,2,1024,256]{3,2,1,0:T(8,128)(2,1)}) custom-call(bf16[2,1024,512]{2,1,0:T(8,128)(2,1)} %get-tuple-element.75.refs_0_, ...), custom_call_target="tpu_custom_call" | custom-call | flops 5905580032 | bytes 7876608 | tf_op jit(solution)/shard_map/encoder_forward/pallas_call | solution.py:199
  114.3 25.6 %attend.3 = (bf16[2,1024,256]{2,1,0:T(8,128)(2,1)}, f32[1024,512]{1,0:T(8,128)}, bf16[2,1024,512]{2,1,0:T(8,128)(2,1)}) custom-call(s32[2,2,2]{2,1,0:T(2,128)} %span_ref.7, bf16[2,1024,256]{2,1,0:T(8,128)(2,1)} %get-tuple-element.87.q_ref, bf16[2,2,1024,256]{3,2,1,0:T(8,128)(2,1)} %get-tuple-element.88.refs_0_, ...), custom_call_target="tpu_custom_call" | custom-call | flops 17179869184 | bytes 8388608 | tf_op jit(solution)/shard_map/attend/pallas_call | solution.py:860
  139.9 25.7 %decoder_turn.1 = (bf16[1024,512]{1,0:T(8,128)(2,1)}, f32[1024,512]{1,0:T(8,128)}, bf16[2,1024,256]{2,1,0:T(8,128)(2,1)}, bf16[2,512,256]{2,1,0:T(8,128)(2,1)}, ...) custom-call(f32[1024,512]{1,0:T(8,128)} %get-tuple-element.91.refs_0_, ...), custom_call_target="tpu_custom_call" | custom-call | flops 14495514624 | bytes 9449472 | tf_op jit(solution)/shard_map/decoder_turn/pallas_call | solution.py:199
  165.6 53.5 %attend_back.2 = (bf16[2,1024,256]{2,1,0:T(8,128)(2,1)}, bf16[2,2,1024,256]{3,2,1,0:T(8,128)(2,1)}, bf16[2,2,1024,256]{3,2,1,0:T(8,128)(2,1)}, bf16[1024,512]{1,0:T(8,128)(2,1)}, bf16[2,1024,512]{2,1,0:T(8,128)(2,1)}) custom-call(s32[2,2,2]{2,1,0:T(2,128)} %span_ref.7, bf16[2,1024,256]{2,1,0:T(8,128)(2,1)} %get-tuple-element.87.q_ref, ...), custom_call_target="tpu_custom_call" | custom-call | flops 42949672960 | bytes 16777216 | tf_op jit(solution)/shard_map/attend_back/pallas_call | solution.py:1023
  219.1 8.0 %decoder_middle_back.1 = (f32[1024,512]{1,0:T(8,128)}, bf16[2,2,1024,256]{3,2,1,0:T(8,128)(2,1)}, bf16[2,512,256]{2,1,0:T(8,128)(2,1)}, bf16[2,256,512]{2,1,0:T(8,128)(2,1)}, f32[3,2,512]{2,1,0:T(2,128)}) custom-call(f32[1024,512]{1,0:T(8,128)} %get-tuple-element.91.refs_0_, f32[1024,512]{1,0:T(8,128)} %get-tuple-element.99.refs_1_, ...), custom_call_target="tpu_custom_call" | custom-call | flops 2147483648 | bytes 7876608 | tf_op jit(solution)/shard_map/decoder_middle_back/pallas_call | solution.py:199
  227.1 29.1 %encoder_back.1 = (f32[1024,512]{1,0:T(8,128)}, bf16[2,2,1024,256]{3,2,1,0:T(8,128)(2,1)}, bf16[2,2,1024,512]{3,2,1,0:T(8,128)(2,1)}, bf16[2,2,1536,256]{3,2,1,0:T(8,128)(2,1)}, f32[3,2,512]{2,1,0:T(2,128)}) custom-call(f32[1024,512]{1,0:T(8,128)} %get-tuple-element.85.refs_0_, ...), custom_call_target="tpu_custom_call", output_to_operand_aliasing={{1}: (18, {})} | custom-call | flops 13958643712 | bytes 17838080 | tf_op jit(solution)/shard_map/encoder_back/pallas_call | solution.py:199
  256.2 110.4 %attend_back.3 = (bf16[2,2,1024,256]{3,2,1,0:T(8,128)(2,1)}, bf16[2,2,2,1024,256]{4,3,2,1,0:T(8,128)(2,1)}, bf16[2,2,2,1024,256]{4,3,2,1,0:T(8,128)(2,1)}, bf16[...) custom-call(s32[2,2,2]{2,1,0:T(2,128)} %span_ref.7, ...), custom_call_target="tpu_custom_call" | custom-call | flops 85899345920 | bytes 33554432 | tf_op jit(solution)/shard_map/attend_back/pallas_call | solution.py:1023
  366.6 55.5 %close_down.1 = (bf16[1792,128]{1,0:T(8,128)(2,1)}, bf16[1792,128]{1,0:T(8,128)(2,1)}, bf16[1536,128]{1,0:T(8,128)(2,1)}, bf16[1536,128]{1,0:T(8,128)(2,1)}, bf1...) custom-call(bf16[2,1024,512]{2,1,0:T(8,128)(2,1)} %get-tuple-element.75.refs_0_, ...), custom_call_target="tpu_custom_call" | custom-call | tf_op jit(solution)/shard_map/close_down/pallas_call | solution.py:1687
  422.2 6.9 %lay_out.1 = (f32[2,1024,512]{2,1,0:T(8,128)}, bf16[2,1024,512]{2,1,0:T(8,128)(2,1)}, f32[512,1024]{1,0:T(8,128)}, f32[1024,512]{1,0:T(8,128)}, f32[256,512]{1,0...) custom-call(bf16[2,1024,512]{2,1,0:T(8,128)(2,1)} %get-tuple-element.121.refs_0_, ...), custom_call_target="tpu_custom_call" | custom-call | tf_op jit(solution)/shard_map/lay_out/pallas_call | solution.py:1746

commit v9 on v8

--- a/solution.py
+++ b/solution.py
@@ -2182,10 +2182,10 @@
     )
     ffn_dec, ffn_dec_other, ffn_enc, ffn_enc_other, sides, _, encoded, decoded = moved
     tail = (
-        ([2, 2, 2, 2, 2, 3], [1, 2, *hops(1, 1, 1, 1, 1, 2)]),
-        ([4, 4, 4, 4, 4, 4, 4], [1, 2, *hops(1, 1, 1, 1, 1, 1)]),
-        (8, 6),
-        8 + 2 * levels,
+        ([2, 2, 2, 2, 3, 2], [1, 3, *hops(1, 1, 1, 1, 1, 3)]),
+        ([4, 4, 4, 4, 5, 5, 5], [1, 2, *hops(1, 1, 1, 1, 1, 2)]),
+        (7, 6),
+        10 + 2 * levels,
     )
     enc_last, enc_other, dec_last, dec_other, source_grad, target_grad = close_down(
         x,

time: 433 us -> 433 us (level)
  no operation moved by 1% of the time
where the time goes in v9:
time: 433 us; the launch traced here: 429 us
  Pallas kernels  428 us (99%)
    pallas_call x2, Pallas kernels, attend_back(): pl.pallas_call(kernel, grid=(pairs,), in_specs=[pl.BlockSpec(memory_space...  164 us
    pallas_call x5, Pallas kernels, row_call(): pl.pallas_call(kernel, grid=(rows // block,), in_specs=[blocked(a, dim) f...  83 us
    pallas_call x2, Pallas kernels, attend(): pl.pallas_call(kernel, grid=(pairs,), in_specs=[pl.BlockSpec(memory_space...  79.4 us
    pallas_call x1, Pallas kernels, close_down(): pl.pallas_call(kernel, in_specs=[hold] * len(arrays) + [vmem] * len(norm_...  55.5 us
    pallas_call x1, Pallas kernels, open_up(): pl.pallas_call(kernel, in_specs=[hold] * 3, out_specs=[hold] * 6, out_sha...  39.7 us

profile of v9, /device:TPU:0, one launch (start us, length us, event | category | flops | bytes accessed | tf_op | source)
XLA Modules:
  0.0 429.3 jit_solution(1838487980914087791)
XLA Ops:
  0.6 39.7 %open_up.1 = (bf16[2,1024,512]{2,1,0:T(8,128)(2,1)}, bf16[2,2,1536,256]{3,2,1,0:T(8,128)(2,1)}, f32[2,3,2,512]{3,2,1,0:T(2,128)}, bf16[2,2,1024,256]{3,2,1,0:T(8...) custom-call(bf16[2,1024,512]{2,1,0:T(8,128)(2,1)} %bitcast.29, ...), custom_call_target="tpu_custom_call" | custom-call | tf_op jit(solution)/shard_map/open_up/pallas_call | solution.py:1845
  40.3 53.8 %attend.2 = (bf16[2,2,1024,256]{3,2,1,0:T(8,128)(2,1)}, f32[2,1024,512]{2,1,0:T(8,128)}, bf16[2,2,256,512]{3,2,1,0:T(8,128)(2,1)}, bf16[2,2,512,1024]{3,2,1,0:T(...) custom-call(s32[2,2,2]{2,1,0:T(2,128)} %span_ref.7, ...), custom_call_target="tpu_custom_call" | custom-call | flops 34359738368 | bytes 16777216 | tf_op jit(solution)/shard_map/attend/pallas_call | solution.py:860
  94.1 4.9 %decoder_middle.1 = (bf16[2,1024,256]{2,1,0:T(8,128)(2,1)}, f32[1024,512]{1,0:T(8,128)}) custom-call(bf16[2,1024,512]{2,1,0:T(8,128)(2,1)} %get-tuple-element.75.refs_0_, bf16[2,2,1024,256]{3,2,1,0:T(8,128)(2,1)} %get-tuple-element.79.refs_1_.refs_2_.refs_5_.mix_ref, f32[2,3,2,512]{3,2,1,0:T(2,128)} %get-tuple-element.80.refs_2_.refs_3_.refs_4_.refs_6_, ...), custom_call_target="tpu_custom_call" | custom-call | flops 1073741824 | bytes 3682304 | tf_op jit(solution)/shard_map/decoder_middle/pallas_call | solution.py:199
  99.0 15.3 %encoder_forward.1 = (bf16[1024,512]{1,0:T(8,128)(2,1)}, bf16[2,2,1024,256]{3,2,1,0:T(8,128)(2,1)}, f32[1024,512]{1,0:T(8,128)}, f32[1024,512]{1,0:T(8,128)}, bf16[2,2,1024,256]{3,2,1,0:T(8,128)(2,1)}) custom-call(bf16[2,1024,512]{2,1,0:T(8,128)(2,1)} %get-tuple-element.75.refs_0_, ...), custom_call_target="tpu_custom_call" | custom-call | flops 5905580032 | bytes 7876608 | tf_op jit(solution)/shard_map/encoder_forward/pallas_call | solution.py:199
  114.3 25.6 %attend.3 = (bf16[2,1024,256]{2,1,0:T(8,128)(2,1)}, f32[1024,512]{1,0:T(8,128)}, bf16[2,1024,512]{2,1,0:T(8,128)(2,1)}) custom-call(s32[2,2,2]{2,1,0:T(2,128)} %span_ref.7, bf16[2,1024,256]{2,1,0:T(8,128)(2,1)} %get-tuple-element.87.q_ref, bf16[2,2,1024,256]{3,2,1,0:T(8,128)(2,1)} %get-tuple-element.88.refs_0_, ...), custom_call_target="tpu_custom_call" | custom-call | flops 17179869184 | bytes 8388608 | tf_op jit(solution)/shard_map/attend/pallas_call | solution.py:860
  139.9 25.7 %decoder_turn.1 = (bf16[1024,512]{1,0:T(8,128)(2,1)}, f32[1024,512]{1,0:T(8,128)}, bf16[2,1024,256]{2,1,0:T(8,128)(2,1)}, bf16[2,512,256]{2,1,0:T(8,128)(2,1)}, ...) custom-call(f32[1024,512]{1,0:T(8,128)} %get-tuple-element.91.refs_0_, ...), custom_call_target="tpu_custom_call" | custom-call | flops 14495514624 | bytes 9449472 | tf_op jit(solution)/shard_map/decoder_turn/pallas_call | solution.py:199
  165.6 53.5 %attend_back.2 = (bf16[2,1024,256]{2,1,0:T(8,128)(2,1)}, bf16[2,2,1024,256]{3,2,1,0:T(8,128)(2,1)}, bf16[2,2,1024,256]{3,2,1,0:T(8,128)(2,1)}, bf16[1024,512]{1,0:T(8,128)(2,1)}, bf16[2,1024,512]{2,1,0:T(8,128)(2,1)}) custom-call(s32[2,2,2]{2,1,0:T(2,128)} %span_ref.7, bf16[2,1024,256]{2,1,0:T(8,128)(2,1)} %get-tuple-element.87.q_ref, ...), custom_call_target="tpu_custom_call" | custom-call | flops 42949672960 | bytes 16777216 | tf_op jit(solution)/shard_map/attend_back/pallas_call | solution.py:1023
  219.1 8.0 %decoder_middle_back.1 = (f32[1024,512]{1,0:T(8,128)}, bf16[2,2,1024,256]{3,2,1,0:T(8,128)(2,1)}, bf16[2,512,256]{2,1,0:T(8,128)(2,1)}, bf16[2,256,512]{2,1,0:T(8,128)(2,1)}, f32[3,2,512]{2,1,0:T(2,128)}) custom-call(f32[1024,512]{1,0:T(8,128)} %get-tuple-element.91.refs_0_, f32[1024,512]{1,0:T(8,128)} %get-tuple-element.99.refs_1_, ...), custom_call_target="tpu_custom_call" | custom-call | flops 2147483648 | bytes 7876608 | tf_op jit(solution)/shard_map/decoder_middle_back/pallas_call | solution.py:199
  227.1 29.1 %encoder_back.1 = (f32[1024,512]{1,0:T(8,128)}, bf16[2,2,1024,256]{3,2,1,0:T(8,128)(2,1)}, bf16[2,2,1024,512]{3,2,1,0:T(8,128)(2,1)}, bf16[2,2,1536,256]{3,2,1,0:T(8,128)(2,1)}, f32[3,2,512]{2,1,0:T(2,128)}) custom-call(f32[1024,512]{1,0:T(8,128)} %get-tuple-element.85.refs_0_, ...), custom_call_target="tpu_custom_call", output_to_operand_aliasing={{1}: (18, {})} | custom-call | flops 13958643712 | bytes 17838080 | tf_op jit(solution)/shard_map/encoder_back/pallas_call | solution.py:199
  256.2 110.4 %attend_back.3 = (bf16[2,2,1024,256]{3,2,1,0:T(8,128)(2,1)}, bf16[2,2,2,1024,256]{4,3,2,1,0:T(8,128)(2,1)}, bf16[2,2,2,1024,256]{4,3,2,1,0:T(8,128)(2,1)}, bf16[...) custom-call(s32[2,2,2]{2,1,0:T(2,128)} %span_ref.7, ...), custom_call_target="tpu_custom_call" | custom-call | flops 85899345920 | bytes 33554432 | tf_op jit(solution)/shard_map/attend_back/pallas_call | solution.py:1023
  366.6 55.5 %close_down.1 = (bf16[1792,128]{1,0:T(8,128)(2,1)}, bf16[1792,128]{1,0:T(8,128)(2,1)}, bf16[1536,128]{1,0:T(8,128)(2,1)}, bf16[1536,128]{1,0:T(8,128)(2,1)}, bf1...) custom-call(bf16[2,1024,512]{2,1,0:T(8,128)(2,1)} %get-tuple-element.75.refs_0_, ...), custom_call_target="tpu_custom_call" | custom-call | tf_op jit(solution)/shard_map/close_down/pallas_call | solution.py:1687
  422.2 6.9 %lay_out.1 = (f32[2,1024,512]{2,1,0:T(8,128)}, bf16[2,1024,512]{2,1,0:T(8,128)(2,1)}, f32[512,1024]{1,0:T(8,128)}, f32[1024,512]{1,0:T(8,128)}, f32[256,512]{1,0...) custom-call(bf16[2,1024,512]{2,1,0:T(8,128)(2,1)} %get-tuple-element.121.refs_0_, ...), custom_call_target="tpu_custom_call" | custom-call | tf_op jit(solution)/shard_map/lay_out/pallas_call | solution.py:1746
